TPU v7x, 32 devices: a whole 2x2x4 slice. The times are simulated.
32 devices in a mesh: shard: 4 (over z), replica: 2 (over x), ctx: 4 (over y, core).
Axes of the slice: x: 2, y: 2, z: 4, core: 2. Of those that a mesh axis runs over, the one named last changes fastest.
Arguments:
- tokens: bfloat16 [64, 512, 1088], P(('shard', 'replica'), 'ctx'), may hold values from -6 to 6
- cotangent: bfloat16 [64, 512, 1088], P(('shard', 'replica'), 'ctx'), may hold values from -6 to 6
- block_order: int32 [4], replicated, may hold values from 0 to 3, each once
- ln1_gain: bfloat16 [1088], P('shard'), may hold values from 0.5 to 1.5
- ln1_bias: bfloat16 [1088], P('shard'), may hold values from -3 to 3
- qkv_weight: bfloat16 [1088, 3264], P('shard'), may hold values from -0.1875 to 0.1875
- q_bias: bfloat16 [1088], P('shard'), may hold values from -3 to 3
- v_bias: bfloat16 [1088], P('shard'), may hold values from -3 to 3
- out_weight: bfloat16 [1088, 1088], P('shard'), may hold values from -0.75 to 0.75
- out_bias: bfloat16 [1088], P('shard'), may hold values from -3 to 3
- ln2_gain: bfloat16 [1088], P('shard'), may hold values from 0.5 to 1.5
- ln2_bias: bfloat16 [1088], P('shard'), may hold values from -3 to 3
- fc_weight: bfloat16 [1088, 4352], P('shard'), may hold values from -0.1875 to 0.1875
- fc_bias: bfloat16 [4352], P('shard'), may hold values from -3 to 3
- proj_weight: bfloat16 [4352, 1088], P('shard'), may hold values from -0.09375 to 0.09375
- proj_bias: bfloat16 [1088], P('shard'), may hold values from -3 to 3
Outputs:
- layer_out: bfloat16 [64, 512, 1088], P(('shard', 'replica'), 'ctx')
- input_grad: float32 [64, 512, 1088], P(('shard', 'replica'), 'ctx')
- ln1_gain_grad: float32 [1088], P('shard')
- ln1_bias_grad: float32 [1088], P('shard')
- qkv_weight_grad: float32 [1088, 3264], P('shard')
- q_bias_grad: float32 [1088], P('shard')
- v_bias_grad: float32 [1088], P('shard')
- out_weight_grad: float32 [1088, 1088], P('shard')
- out_bias_grad: float32 [1088], P('shard')
- ln2_gain_grad: float32 [1088], P('shard')
- ln2_bias_grad: float32 [1088], P('shard')
- fc_weight_grad: float32 [1088, 4352], P('shard')
- fc_bias_grad: float32 [4352], P('shard')
- proj_weight_grad: float32 [4352, 1088], P('shard')
- proj_bias_grad: float32 [1088], P('shard')
Inputs may be any that keep to these rules, and one draw needn't show every extreme that they name: A permutation: the index c of ctx holds positions block_order[c] * 128 to block_order[c] * 128 + 127 of each of its sequences.
All inputs are finite; a program needn't handle non-finite values.
Results may differ from a plain program's by a relative error of at most 0.018.
Values may be sent and summed in bfloat16 or wider, within the bound.
No kernel may reach another device: no remote copies, remote signals or barrier semaphores. Data moves between devices by JAX's collectives and lax.ppermute only.
A program may use at most 384 MiB of HBM per device.

v0:
```python
import jax
import jax.numpy as jnp
from jax import lax
from jax.sharding import PartitionSpec as P

HEAD_DIM = 64


epsilon = 1e-05


def normalize(values, gain_vec, shift_vec):
    centred = values - jnp.mean(values, axis=-1, keepdims=True)
    inverse = lax.rsqrt(jnp.mean(centred * centred, axis=-1, keepdims=True) + epsilon)
    standard = centred * inverse
    return (standard * gain_vec + shift_vec, standard, inverse)


def normalize_back(grad_out, standard, inverse, gain_vec):
    scaled = grad_out * gain_vec
    grad_in = inverse * (
        scaled
        - jnp.mean(scaled, axis=-1, keepdims=True)
        - standard * jnp.mean(scaled * standard, axis=-1, keepdims=True)
    )
    return (grad_in, jnp.sum(grad_out * standard, axis=0), jnp.sum(grad_out, axis=0))


def forward_dot(left, right):
    return jnp.dot(left, right, preferred_element_type=jnp.float32)


def transpose_dot(left, right):
    return lax.dot_general(
        left, right, (((0,), (0,)), ((), ())), preferred_element_type=jnp.float32
    )


def backward_dot(left, right):
    return lax.dot_general(
        left, right, (((1,), (1,)), ((), ())), preferred_element_type=jnp.float32
    )


def heads_major(rows, seq_count, length, num_heads, head_dim):
    return rows.reshape(seq_count, length, num_heads, head_dim).transpose(0, 2, 1, 3)


def rows_major(heads, row_total, model_width):
    return heads.transpose(0, 2, 1, 3).reshape(row_total, model_width)


def score_block(query_heads, key_heads, allowed):
    raw_scores = jnp.einsum(
        "shqe,shke->shqk", query_heads, key_heads, preferred_element_type=jnp.float32
    )
    scores = jnp.where(allowed, raw_scores * query_heads.shape[-1] ** (-0.5), -1e30)
    top_score = jnp.max(scores, axis=-1, keepdims=True)
    log_total = top_score + jnp.log(jnp.sum(jnp.exp(scores - top_score), axis=-1, keepdims=True))
    return jnp.exp(scores - log_total)


def per_device(
    tokens,
    cotangent,
    block_order,
    ln1_gain,
    ln1_bias,
    qkv_weight,
    q_bias,
    v_bias,
    out_weight,
    out_bias,
    ln2_gain,
    ln2_bias,
    fc_weight,
    fc_bias,
    proj_weight,
    proj_bias,
):
    seq_count, local_len, model_width = tokens.shape
    tok_rows = seq_count * local_len
    head_dim = HEAD_DIM
    num_heads = model_width // head_dim
    full_len = local_len * lax.axis_size("ctx")
    (
        g_one,
        b_one,
        w_qkv,
        bias_q,
        bias_v,
        w_out,
        bias_out,
        g_two,
        b_two,
        w_fc,
        bias_fc,
        w_proj,
        bias_proj,
    ) = (
        lax.all_gather(ln1_gain, "shard", axis=0, tiled=True),
        lax.all_gather(ln1_bias, "shard", axis=0, tiled=True),
        lax.all_gather(qkv_weight, "shard", axis=0, tiled=True),
        lax.all_gather(q_bias, "shard", axis=0, tiled=True),
        lax.all_gather(v_bias, "shard", axis=0, tiled=True),
        lax.all_gather(out_weight, "shard", axis=0, tiled=True),
        lax.all_gather(out_bias, "shard", axis=0, tiled=True),
        lax.all_gather(ln2_gain, "shard", axis=0, tiled=True),
        lax.all_gather(ln2_bias, "shard", axis=0, tiled=True),
        lax.all_gather(fc_weight, "shard", axis=0, tiled=True),
        lax.all_gather(fc_bias, "shard", axis=0, tiled=True),
        lax.all_gather(proj_weight, "shard", axis=0, tiled=True),
        lax.all_gather(proj_bias, "shard", axis=0, tiled=True),
    )
    own_block = lax.dynamic_slice_in_dim(block_order, lax.axis_index("ctx"), 1)[0]
    local_pos = own_block * local_len + jnp.arange(local_len, dtype=jnp.int32)
    key_pos = (
        block_order[:, None] * local_len + jnp.arange(local_len, dtype=jnp.int32)[None, :]
    ).reshape(-1)
    allowed = key_pos[None, :] <= local_pos[:, None]
    inputs = tokens.reshape(tok_rows, model_width).astype(jnp.float32)
    normed_one, standard_one, inverse_one = normalize(
        inputs, g_one.astype(jnp.float32), b_one.astype(jnp.float32)
    )
    low_one = normed_one.astype(jnp.bfloat16)
    triple_weight = w_qkv.reshape(model_width, 3, model_width)
    joined = jnp.einsum("td,dcx->ctx", low_one, triple_weight, preferred_element_type=jnp.float32)
    queries = (joined[0] + bias_q.astype(jnp.float32)).astype(jnp.bfloat16)
    own_keys = joined[1].astype(jnp.bfloat16)
    own_values = (joined[2] + bias_v.astype(jnp.float32)).astype(jnp.bfloat16)
    key_rows, value_rows = (
        lax.all_gather(
            own_keys.reshape(seq_count, local_len, model_width), "ctx", axis=1, tiled=True
        ),
        lax.all_gather(
            own_values.reshape(seq_count, local_len, model_width), "ctx", axis=1, tiled=True
        ),
    )
    query_heads = heads_major(queries, seq_count, local_len, num_heads, head_dim)
    key_heads = heads_major(key_rows, seq_count, full_len, num_heads, head_dim)
    value_heads = heads_major(value_rows, seq_count, full_len, num_heads, head_dim)
    soft_weights = score_block(query_heads, key_heads, allowed)
    low_weights = soft_weights.astype(jnp.bfloat16)
    attended = jnp.einsum(
        "shqk,shke->shqe", low_weights, value_heads, preferred_element_type=jnp.float32
    )
    attended = rows_major(attended.astype(jnp.bfloat16), tok_rows, model_width)
    middle = inputs + (forward_dot(attended, w_out) + bias_out.astype(jnp.float32))
    normed_two, standard_two, inverse_two = normalize(
        middle, g_two.astype(jnp.float32), b_two.astype(jnp.float32)
    )
    low_two = normed_two.astype(jnp.bfloat16)
    hidden = forward_dot(low_two, w_fc) + bias_fc.astype(jnp.float32)
    activated, gelu_pull = jax.vjp(lambda pre_act: jax.nn.gelu(pre_act, approximate=True), hidden)
    low_act = activated.astype(jnp.bfloat16)
    outputs = middle + (forward_dot(low_act, w_proj) + bias_proj.astype(jnp.float32))
    g_one, w_qkv, w_out, g_two, w_fc, w_proj = (
        lax.all_gather(ln1_gain, "shard", axis=0, tiled=True),
        lax.all_gather(qkv_weight, "shard", axis=0, tiled=True),
        lax.all_gather(out_weight, "shard", axis=0, tiled=True),
        lax.all_gather(ln2_gain, "shard", axis=0, tiled=True),
        lax.all_gather(fc_weight, "shard", axis=0, tiled=True),
        lax.all_gather(proj_weight, "shard", axis=0, tiled=True),
    )
    triple_weight = w_qkv.reshape(model_width, 3, model_width)
    low_grad_out = cotangent.reshape(tok_rows, model_width)
    grad_out = low_grad_out.astype(jnp.float32)
    grad_proj = transpose_dot(low_act, low_grad_out)
    grad_proj_bias = jnp.sum(grad_out, axis=0)
    grad_act = backward_dot(low_grad_out, w_proj)
    grad_hidden = gelu_pull(grad_act)[0].astype(jnp.bfloat16)
    grad_fc = transpose_dot(low_two, grad_hidden)
    grad_fc_bias = jnp.sum(grad_hidden.astype(jnp.float32), axis=0)
    grad_two = backward_dot(grad_hidden, w_fc)
    grad_norm_two, grad_g_two, grad_b_two = normalize_back(
        grad_two, standard_two, inverse_two, g_two.astype(jnp.float32)
    )
    grad_middle = grad_out + grad_norm_two
    low_grad_middle = grad_middle.astype(jnp.bfloat16)
    grad_out_weight = transpose_dot(attended, low_grad_middle)
    grad_out_bias = jnp.sum(low_grad_middle.astype(jnp.float32), axis=0)
    grad_attended = backward_dot(low_grad_middle, w_out).astype(jnp.bfloat16)
    grad_att_heads = heads_major(grad_attended, seq_count, local_len, num_heads, head_dim)
    back_weights = score_block(query_heads, key_heads, allowed)
    low_back_weights = back_weights.astype(jnp.bfloat16)
    grad_weights = jnp.einsum(
        "shqe,shke->shqk", grad_att_heads, value_heads, preferred_element_type=jnp.float32
    )
    grad_scores = back_weights * (
        grad_weights - jnp.sum(back_weights * grad_weights, axis=-1, keepdims=True)
    )
    low_grad_scores = (grad_scores * head_dim ** (-0.5)).astype(jnp.bfloat16)
    grad_queries = jnp.einsum(
        "shqk,shke->shqe", low_grad_scores, key_heads, preferred_element_type=jnp.float32
    )
    grad_queries = rows_major(grad_queries.astype(jnp.bfloat16), tok_rows, model_width)
    key_terms = jnp.einsum(
        "shqk,shqe->shke", low_grad_scores, query_heads, preferred_element_type=jnp.float32
    )
    value_terms = jnp.einsum(
        "shqk,shqe->shke", low_back_weights, grad_att_heads, preferred_element_type=jnp.float32
    )
    grad_keys, grad_values = (
        lax.psum_scatter(
            rows_major(key_terms, seq_count * full_len, model_width)
            .reshape(seq_count, full_len, model_width)
            .astype(jnp.bfloat16),
            "ctx",
            scatter_dimension=1,
            tiled=True,
        ).astype(jnp.float32),
        lax.psum_scatter(
            rows_major(value_terms, seq_count * full_len, model_width)
            .reshape(seq_count, full_len, model_width)
            .astype(jnp.bfloat16),
            "ctx",
            scatter_dimension=1,
            tiled=True,
        ).astype(jnp.float32),
    )
    low_grad_keys = grad_keys.reshape(tok_rows, model_width).astype(jnp.bfloat16)
    low_grad_values = grad_values.reshape(tok_rows, model_width).astype(jnp.bfloat16)
    grad_joined = jnp.stack([grad_queries, low_grad_keys, low_grad_values], axis=0)
    grad_qkv = jnp.einsum(
        "td,ctx->dcx", low_one, grad_joined, preferred_element_type=jnp.float32
    ).reshape(model_width, 3 * model_width)
    grad_q_bias = jnp.sum(grad_queries.astype(jnp.float32), axis=0)
    grad_v_bias = jnp.sum(low_grad_values.astype(jnp.float32), axis=0)
    grad_one = jnp.einsum(
        "ctx,dcx->td", grad_joined, triple_weight, preferred_element_type=jnp.float32
    )
    grad_norm_one, grad_g_one, grad_b_one = normalize_back(
        grad_one, standard_one, inverse_one, g_one.astype(jnp.float32)
    )
    grad_inputs = grad_middle + grad_norm_one
    owned = (
        lax.psum_scatter(
            grad_g_one.astype(jnp.bfloat16), "shard", scatter_dimension=0, tiled=True
        ).astype(jnp.float32),
        lax.psum_scatter(
            grad_b_one.astype(jnp.bfloat16), "shard", scatter_dimension=0, tiled=True
        ).astype(jnp.float32),
        lax.psum_scatter(
            grad_qkv.astype(jnp.bfloat16), "shard", scatter_dimension=0, tiled=True
        ).astype(jnp.float32),
        lax.psum_scatter(
            grad_q_bias.astype(jnp.bfloat16), "shard", scatter_dimension=0, tiled=True
        ).astype(jnp.float32),
        lax.psum_scatter(
            grad_v_bias.astype(jnp.bfloat16), "shard", scatter_dimension=0, tiled=True
        ).astype(jnp.float32),
        lax.psum_scatter(
            grad_out_weight.astype(jnp.bfloat16), "shard", scatter_dimension=0, tiled=True
        ).astype(jnp.float32),
        lax.psum_scatter(
            grad_out_bias.astype(jnp.bfloat16), "shard", scatter_dimension=0, tiled=True
        ).astype(jnp.float32),
        lax.psum_scatter(
            grad_g_two.astype(jnp.bfloat16), "shard", scatter_dimension=0, tiled=True
        ).astype(jnp.float32),
        lax.psum_scatter(
            grad_b_two.astype(jnp.bfloat16), "shard", scatter_dimension=0, tiled=True
        ).astype(jnp.float32),
        lax.psum_scatter(
            grad_fc.astype(jnp.bfloat16), "shard", scatter_dimension=0, tiled=True
        ).astype(jnp.float32),
        lax.psum_scatter(
            grad_fc_bias.astype(jnp.bfloat16), "shard", scatter_dimension=0, tiled=True
        ).astype(jnp.float32),
        lax.psum_scatter(
            grad_proj.astype(jnp.bfloat16), "shard", scatter_dimension=0, tiled=True
        ).astype(jnp.float32),
        lax.psum_scatter(
            grad_proj_bias.astype(jnp.bfloat16), "shard", scatter_dimension=0, tiled=True
        ).astype(jnp.float32),
    )
    summed = (
        lax.psum(owned[0].astype(jnp.bfloat16), ("replica", "ctx")).astype(jnp.float32),
        lax.psum(owned[1].astype(jnp.bfloat16), ("replica", "ctx")).astype(jnp.float32),
        lax.psum(owned[2].astype(jnp.bfloat16), ("replica", "ctx")).astype(jnp.float32),
        lax.psum(owned[3].astype(jnp.bfloat16), ("replica", "ctx")).astype(jnp.float32),
        lax.psum(owned[4].astype(jnp.bfloat16), ("replica", "ctx")).astype(jnp.float32),
        lax.psum(owned[5].astype(jnp.bfloat16), ("replica", "ctx")).astype(jnp.float32),
        lax.psum(owned[6].astype(jnp.bfloat16), ("replica", "ctx")).astype(jnp.float32),
        lax.psum(owned[7].astype(jnp.bfloat16), ("replica", "ctx")).astype(jnp.float32),
        lax.psum(owned[8].astype(jnp.bfloat16), ("replica", "ctx")).astype(jnp.float32),
        lax.psum(owned[9].astype(jnp.bfloat16), ("replica", "ctx")).astype(jnp.float32),
        lax.psum(owned[10].astype(jnp.bfloat16), ("replica", "ctx")).astype(jnp.float32),
        lax.psum(owned[11].astype(jnp.bfloat16), ("replica", "ctx")).astype(jnp.float32),
        lax.psum(owned[12].astype(jnp.bfloat16), ("replica", "ctx")).astype(jnp.float32),
    )
    return (
        outputs.astype(jnp.bfloat16).reshape(seq_count, local_len, model_width),
        grad_inputs.reshape(seq_count, local_len, model_width),
        summed[0],
        summed[1],
        summed[2],
        summed[3],
        summed[4],
        summed[5],
        summed[6],
        summed[7],
        summed[8],
        summed[9],
        summed[10],
        summed[11],
        summed[12],
    )


def solution(mesh):
    return jax.shard_map(
        per_device,
        mesh=mesh,
        in_specs=(
            P(("shard", "replica"), "ctx", None),
            P(("shard", "replica"), "ctx", None),
            P(),
            P("shard"),
            P("shard"),
            P("shard", None),
            P("shard"),
            P("shard"),
            P("shard", None),
            P("shard"),
            P("shard"),
            P("shard"),
            P("shard", None),
            P("shard"),
            P("shard", None),
            P("shard"),
        ),
        out_specs=(
            P(("shard", "replica"), "ctx", None),
            P(("shard", "replica"), "ctx", None),
            P("shard"),
            P("shard"),
            P("shard", None),
            P("shard"),
            P("shard"),
            P("shard", None),
            P("shard"),
            P("shard"),
            P("shard"),
            P("shard", None),
            P("shard"),
            P("shard", None),
            P("shard"),
        ),
        check_vma=False,
    )
```

profile of v0, /device:TPU:0, one launch (start us, length us, event | category | flops | bytes accessed | tf_op | source)
XLA Modules:
  0.0 1705.2 jit_solution(8097793054759129918)
XLA Ops:
  17.6 29.4 %all-reduce.21 = (bf16[1088]{0:T(1024)(128)(2,1)S(1)}, bf16[1088]{0:T(1024)(128)(2,1)S(1)}, bf16[1088]{0:T(1024)(128)(2,1)S(1)}, bf16[1088]{0:T(1024)(128)(2,1)S...) all-reduce(bf16[1088]{0:T(1024)(128)(2,1)S(1)} %dynamic-update-slic, ...), channel_id=1, replica_groups=mesh['shard'=4,'replica'=2,'ctx'=4] {'shard'}, use_global_device_ids=true, to_apply=%add.2 | all-reduce | flops 11968 | bytes 47872
  51.8 7.3 copy.59
  59.1 4.7 reshape.302
  63.8 80.6 %all-gather.7.cloned.1.call-done = bf16[1088,3264]{1,0:T(8,128)(2,1)} async-done(((bf16[272,3264]{1,0:T(8,128)(2,1)}), bf16[1088,3264]{1,0:T(8,128)(2,1)}) %all-gather.7.cloned.1.call-update) | async-done | bytes 7102480 | tf_op jit(solution)/shard_map/all_gather | solution.py:103
  144.5 11.2 copy.60
  155.6 11.8 convolution_bitcast_fusion
  167.4 4.8 copy-done.6
  175.3 7.2 slice_bitcast_fusion.1
  183.6 4.0 fusion.46
  191.0 5.5 copy.86
  196.6 39.2 %all-gather.9.cloned.1.call-done = bf16[8,512,1088]{1,0,2:T(8,128)(2,1)} async-done(((bf16[8,128,1088]{1,0,2:T(8,128)(2,1)}), bf16[8,512,1088]{1,0,2:T(8,128)(2,1)}) %all-gather.9.cloned.1.call-update) | async-done | bytes 8912912 | tf_op jit(solution)/shard_map/all_gather | solution.py:132
  235.7 11.0 copy.62
  246.7 53.7 %all-gather.11.cloned.1.call-done = bf16[8,512,1088]{1,0,2:T(8,128)(2,1)} async-done(((bf16[8,128,1088]{1,0,2:T(8,128)(2,1)}), bf16[8,512,1088]{1,0,2:T(8,128)(2,1)}) %all-gather.11.cloned.1.call-update) | async-done | bytes 8912912 | tf_op jit(solution)/shard_map/all_gather | solution.py:135
  300.4 10.3 copy.63
  310.7 19.4 %fusion.2 = (f32[8,17,128]{2,1,0:T(8,128)S(1)}, f32[8,17,128,512]{3,2,1,0:T(8,128)}) fusion(pred[128,512]{1,0:T(8,128)(4,1)S(1)} %broadcast_compare_fusion, bf16[8,17,512,64]{2,3,1,0:T(8,128)(2,1)} %bitcast.191, f32[8,128,17,64]{1,0,3,2:T(8,128)} %bitcast.189, f32[17,64]{1,0:T(8,128)S(1)} %reshape.256), kind=kOutput, calls=%fused_computation.7 | convolution fusion | flops 1169800192 | bytes 49160448 | tf_op jit(solution)/shard_map/shqe,shke->shqk/dot_general | solution.py:54
  330.0 15.6 exponential_reduce_fusion
  345.7 18.3 %convert_bitcast_fusion.2 = bf16[8,128,17,64]{1,3,2,0:T(8,128)(2,1)} fusion(bf16[8,17,512,64]{2,3,1,0:T(8,128)(2,1)} %bitcast.195, f32[8,17,128,512]{3,2,1,0:T(8,128)} %get-tuple-element.110, f32[8,17,128]{2,1,0:T(8,128)S(1)} %log_add_fusion, pred[128,512]{1,0:T(8,128)(4,1)S(1)} %broadcast_compare_fusion), kind=kOutput, calls=%fused_computation.89 | convolution fusion | flops 1177616384 | bytes 46927872 | tf_op jit(solution)/shard_map/shqk,shke->shqe/dot_general | solution.py:144
  364.0 5.2 copy.64
  369.2 5.9 fusion.101
  377.7 144.6 %all-gather.15.cloned.1.call-done = bf16[1088,4352]{1,0:T(8,128)(2,1)} async-done(((bf16[272,4352]{1,0:T(8,128)(2,1)}), bf16[1088,4352]{1,0:T(8,128)(2,1)}) %all-gather.15.cloned.1.call-update) | async-done | bytes 9469968 | tf_op jit(solution)/shard_map/all_gather | solution.py:110
  522.3 20.7 %fusion.99 = f32[1024,4352]{1,0:T(8,128)} fusion(bf16[1088,4352]{1,0:T(8,128)(2,1)} %all-gather.15.cloned.1.call-done, f32[1024,1088]{0,1:T(8,128)} %copy-done.3, f32[1088]{0:T(1024)S(1)} %convert_element_type.258, f32[1088]{0:T(1024)S(1)} %convert_element_type.257, f32[1024]{0:T(1024)S(1)} %add_rsqrt_fusion, f32[1024]{0:T(1024)S(1)} %broadcast_multiply_fusion.4), kind=kOutput, calls=%fused_computation.131 | convolution fusion | flops 9702801408 | bytes 31769088 | tf_op jit(solution)/shard_map/dot_general | solution.py:30
  543.0 155.4 %all-gather.17.cloned.1.call-done = bf16[4352,1088]{1,0:T(8,128)(2,1)} async-done(((bf16[1088,1088]{1,0:T(8,128)(2,1)}), bf16[4352,1088]{1,0:T(8,128)(2,1)}) %all-gather.17.cloned.1.call-update) | async-done | bytes 9469968 | tf_op jit(solution)/shard_map/all_gather | solution.py:112
  698.4 25.5 %fusion.105 = (bf16[4352]{0:T(1024)(128)(2,1)}, bf16[1024,4352]{1,0:T(8,128)(2,1)}) fusion(f32[1024,4352]{1,0:T(8,128)} %fusion.99, f32[4352]{0:T(1024)S(1)} %convert_element_type.260, bf16[4352,1088]{1,0:T(8,128)(2,1)} %all-gather.17.cloned.1.call-done, bf16[8,128,1088]{1,2,0:T(8,128)(2,1)S(1)} %copy-done.7), kind=kOutput, calls=%fused_computation.135 | convolution fusion | flops 9795268608 | bytes 38462976 | tf_op jit(solution)/shard_map/dot_general | solution.py:40
  723.8 19.2 %multiply_reduce_fusion.1 = (bf16[1088]{0:T(1024)(128)(2,1)}, f32[1024]{0:T(1024)S(1)}, f32[1024]{0:T(1024)S(1)}, bf16[1088]{0:T(1024)(128)(2,1)}, f32[1024,1088]{0,1:T(8,128)S(1)}) fusion(f32[1024,1088]{0,1:T(8,128)} %copy-done.3, f32[1024]{0:T(1024)S(1)} %add_rsqrt_fusion, f32[1024]{0:T(1024)S(1)} %broadcast_multiply_fusion.4, ...), kind=kOutput, calls=%fused_computation.63 | convolution fusion | flops 9707253760 | bytes 27320832 | tf_op jit(solution)/shard_map/dot_general | solution.py:40
  749.6 17.9 %convolution_convert_fusion.4 = bf16[8,17,512,64]{2,3,1,0:T(8,128)(2,1)} fusion(bf16[8,128,17,64]{1,0,3,2:T(8,128)(2,1)S(1)} %bitcast.199, f32[8,17,128,512]{3,2,1,0:T(8,128)} %get-tuple-element.110, f32[8,17,128]{2,1,0:T(8,128)S(1)} %log_add_fusion, pred[128,512]{1,0:T(8,128)(4,1)S(1)} %broadcast_compare_fusion), kind=kOutput, calls=%fused_computation.38 | convolution fusion | flops 1180958720 | bytes 46927872 | tf_op jit(solution)/shard_map/shqk,shqe->shke/dot_general | solution.py:200
  767.5 12.9 copy.76
  780.4 15.0 reshape.307
  796.1 4.6 fusion.135
  800.7 24.1 %fusion.64 = f32[8,17,128,512]{3,2,1,0:T(8,128)} fusion(bf16[8,17,512,64]{2,3,1,0:T(8,128)(2,1)} %bitcast.196, bf16[8,128,17,64]{1,0,3,2:T(8,128)(2,1)} %bitcast.200), kind=kOutput, calls=%fused_computation.86 | convolution fusion | flops 1140850688 | bytes 46792704 | tf_op jit(solution)/shard_map/shqe,shke->shqk/dot_general | solution.py:186
  824.8 117.8 %fusion.35 = bf16[8,17,512,64]{2,3,1,0:T(8,128)(2,1)} fusion(f32[8,17,128,512]{3,2,1,0:T(8,128)} %fusion.64, f32[8,17,128,512]{3,2,1,0:T(8,128)} %get-tuple-element.110, f32[8,17,128]{2,1,0:T(8,128)S(1)} %log_add_fusion, pred[128,512]{1,0:T(8,128)(4,1)S(1)} %broadcast_compare_fusion, bf16[8,17,128,64]{2,3,1,0:T(8,128)(2,1)} %fusion.135), kind=kOutput, calls=%fused_computation.37 | convolution fusion | flops 1243366912 | bytes 82579456 | tf_op jit(solution)/shard_map/shqk,shqe->shke/dot_general | solution.py:197
  942.7 12.9 copy.74
  955.6 15.0 reshape.305
  970.7 7.7 convolution_convert_fusion.3
  978.4 19.3 %convolution_convert_fusion.1 = bf16[1088,4352]{1,0:T(8,128)(2,1)} fusion(bf16[1024,4352]{1,0:T(8,128)(2,1)} %get-tuple-element.118, f32[1024,1088]{0,1:T(8,128)} %copy-done.3, f32[1088]{0:T(1024)S(1)} %copy-done.30, f32[1088]{0:T(1024)S(1)} %convert_element_type.257, f32[1024]{0:T(1024)S(1)} %add_rsqrt_fusion, f32[1024]{0:T(1024)S(1)} %broadcast_multiply_fusion.4), kind=kOutput, calls=%fused_computation.11 | convolution fusion | flops 9707536384 | bytes 22856192 | tf_op jit(solution)/shard_map/dot_general | solution.py:34
  998.4 21.9 %convolution_convert_fusion = bf16[4352,1088]{1,0:T(8,128)(2,1)} fusion(f32[1024,4352]{1,0:T(8,128)} %fusion.99, f32[4352]{0:T(1024)S(1)} %copy-done.22, bf16[8,128,1088]{1,2,0:T(8,128)(2,1)S(1)} %copy-done.7), kind=kOutput, calls=%fused_computation.10 | convolution fusion | flops 9746530304 | bytes 29541376 | tf_op jit(solution)/shard_map/dot_general | solution.py:34
  1020.4 114.6 %fusion.102 = (bf16[17,64]{1,0:T(8,128)(2,1)S(1)}, bf16[8,128,17,64]{1,3,2,0:T(8,128)(2,1)}) fusion(bf16[8,17,512,64]{2,3,1,0:T(8,128)(2,1)} %bitcast.192, f32[8,17,128,512]{3,2,1,0:T(8,128)} %fusion.64, f32[8,17,128,512]{3,2,1,0:T(8,128)} %get-tuple-element.110, f32[8,17,128]{2,1,0:T(8,128)S(1)} %log_add_fusion, ...), kind=kOutput, calls=%fused_computation.134 | convolution fusion | flops 1241137664 | bytes 82581632 | tf_op jit(solution)/shard_map/shqk,shke->shqe/dot_general | solution.py:193
  1150.9 4.7 convert_element_type.278
  1162.4 4.7 convert_element_type.274
  1172.1 13.6 convolution_convert_fusion.2
  1191.5 14.9 fusion.48
  1206.4 19.1 %all-reduce.20 = (bf16[1088]{0:T(1024)(128)(2,1)S(1)}, bf16[1088]{0:T(1024)(128)(2,1)S(1)}, bf16[1088]{0:T(1024)(128)(2,1)S(1)}, bf16[1088]{0:T(1024)(128)(2,1)S...) all-reduce(bf16[1088]{0:T(1024)(128)(2,1)S(1)} %dynamic-update-slic, ...), channel_id=1, replica_groups=mesh['shard'=4,'replica'=2,'ctx'=4] {'shard'}, use_global_device_ids=true, to_apply=%add.8 | all-reduce | flops 14144 | bytes 56576
  1226.3 23.8 %all-reduce.18 = (bf16[272]{0:T(512)(128)(2,1)S(1)}, bf16[272]{0:T(512)(128)(2,1)S(1)}, bf16[272]{0:T(512)(128)(2,1)S(1)}, bf16[272]{0:T(512)(128)(2,1)S(1)}, bf...) all-reduce(bf16[272]{0:T(512)(128)(2,1)S(1)} %dynamic-slice.10, ...), channel_id=1, replica_groups=mesh['shard'=4,'replica'=2,'ctx'=4] {'replica','ctx'}, use_global_device_ids=true, to_apply=%region_15.16 | all-reduce | flops 3264 | bytes 13056 | tf_op jit(solution)/shard_map/psum | solution.py:278
  1254.7 8.6 reduce-scatter.15.cloned.1.call-done
  1263.3 174.0 %reduce-scatter.17.cloned.1.call-done = bf16[1088,1088]{1,0:T(8,128)(2,1)} async-done(((bf16[4352,1088]{1,0:T(8,128)(2,1)}), bf16[1088,1088]{1,0:T(8,128)(2,1)}) %reduce-scatter.17.cloned.1.call-update) | async-done | bytes 2367504 | tf_op jit(solution)/shard_map/reduce_scatter | solution.py:270
  1437.3 129.5 %reduce-scatter.11.cloned.1.call-done = bf16[272,3264]{1,0:T(8,128)(2,1)} async-done(((bf16[1088,3264]{1,0:T(8,128)(2,1)}), bf16[272,3264]{1,0:T(8,128)(2,1)}) %reduce-scatter.11.cloned.1.call-update) | async-done | bytes 1775632 | tf_op jit(solution)/shard_map/reduce_scatter | solution.py:243
  1566.8 23.0 %fusion.75 = bf16[136,8,8,128]{3,2,1,0:T(8,128)(2,1)S(1)} fusion(f32[1024,1088]{0,1:T(8,128)} %copy-done.3, f32[1088]{0:T(1024)S(1)} %convert_element_type.262, bf16[4352,1088]{1,0:T(8,128)(2,1)} %all-gather.17.cloned.1.call-done, f32[1024,4352]{1,0:T(8,128)} %fusion.99, f32[4352]{0:T(1024)S(1)} %copy-done.22), kind=kOutput, calls=%fused_computation.97 | convolution fusion | flops 9745137664 | bytes 34002176 | tf_op jit(solution)/shard_map/dot_general | solution.py:30
  1592.9 4.8 copy_bitcast_fusion
  1597.7 89.5 %all-reduce.24.cloned.1.call-done = (bf16[272,3264]{1,0:T(8,128)(2,1)}, bf16[272,1088]{1,0:T(8,128)(2,1)}, bf16[272,4352]{1,0:T(8,128)(2,1)}, bf16[1088,1088]{1,0:T(8,128)(2,1)}) async-done(((bf16[272,3264]{1,0:T(8,128)(2,1)}, bf16[272,1088]{1,0:T(8,128)(2,1)}, bf16[272,4352]{1,0:T(8,128)(2,1)}, bf16[1088,1088]{1,0:T(8,128)(2,1)}), (bf16[272,3264]{1,0:T(8,128)(2,1)}, bf16[272,1088]{1,0:T(8,128)(2,1)}, ...) | async-done | bytes 7102480 | tf_op jit(solution)/shard_map/psum | solution.py:280
  (187 shorter events, 83.1 us)
Async XLA Ops:
  7.2 42.5 %copy-start = (bf16[8,128,1088]{1,2,0:T(8,128)(2,1)S(1)}, bf16[8,128,1088]{1,2,0:T(8,128)(2,1)}, u32[]{:S(2)}) copy-start(bf16[8,128,1088]{1,2,0:T(8,128)(2,1)} %param.16) | copy-start | bytes 6684676
  7.2 137.3 %all-gather.7.cloned.1.call-start = ((), (), s32[]{:S(2)}) async-start(), calls=%async_computation.6 | async-start | bytes 9052160 | tf_op jit(solution)/shard_map/all_gather | solution.py:103
  7.9 227.8 %all-gather.9.cloned.1.call-start = ((), (), s32[]{:S(2)}) async-start(), calls=%async_computation.7 | async-start | bytes 11141120 | tf_op jit(solution)/shard_map/all_gather | solution.py:132
  47.1 4.7 copy-start.15
  47.1 4.7 copy-start.19
  49.6 1.2 copy-start.17
  50.8 0.9 copy-start.24
  167.4 4.8 copy-start.6
  174.8 125.6 %all-gather.11.cloned.1.call-start = ((), (), s32[]{:S(2)}) async-start(), calls=%async_computation.8 | async-start | bytes 11141120 | tf_op jit(solution)/shard_map/all_gather | solution.py:135
  187.6 1.9 copy-start.35
  187.7 181.5 %all-gather.13.cloned.1.call-start = ((), (), s32[]{:S(2)}) async-start(), calls=%async_computation.9 | async-start | bytes 3133440 | tf_op jit(solution)/shard_map/all_gather | solution.py:106
  188.2 334.0 %all-gather.15.cloned.1.call-start = ((), (), s32[]{:S(2)}) async-start(), calls=%async_computation.10 | async-start | bytes 11837440 | tf_op jit(solution)/shard_map/all_gather | solution.py:110
  188.8 509.5 %all-gather.17.cloned.1.call-start = ((), (), s32[]{:S(2)}) async-start(), calls=%async_computation.11 | async-start | bytes 12533760 | tf_op jit(solution)/shard_map/all_gather | solution.py:112
  189.4 954.7 %reduce-scatter.21.cloned.1.call-start = ((), (), s32[]{:S(2)}) async-start(), calls=%async_computation.17 | async-start | bytes 11141120
  189.5 121.2 %copy-start.13 = (f32[17,64]{1,0:T(8,128)}, f32[17,64]{1,0:T(8,128)S(1)}, u32[]{:S(2)}) copy-start(f32[17,64]{1,0:T(8,128)S(1)} %reshape.256) | copy-start | bytes 13060
  189.5 332.8 %copy-start.29 = (f32[1088]{0:T(1024)}, f32[1088]{0:T(1024)S(1)}, u32[]{:S(2)}) copy-start(f32[1088]{0:T(1024)S(1)} %convert_element_type.258) | copy-start | bytes 13060
  189.6 508.8 %copy-start.21 = (f32[4352]{0:T(1024)}, f32[4352]{0:T(1024)S(1)}, u32[]{:S(2)}) copy-start(f32[4352]{0:T(1024)S(1)} %convert_element_type.260) | copy-start | bytes 52228
  375.0 2.1 copy-start.3
  377.7 320.7 %copy-start.7 = (bf16[8,128,1088]{1,2,0:T(8,128)(2,1)S(1)}, bf16[8,128,1088]{1,2,0:T(8,128)(2,1)}, u32[]{:S(2)}) copy-start(bf16[8,128,1088]{1,2,0:T(8,128)(2,1)} %param.17) | copy-start | bytes 6684676
  723.8 19.2 %copy-start.4 = (f32[1024,1088]{0,1:T(8,128)S(1)}, f32[1024,1088]{0,1:T(8,128)}, u32[]{:S(2)}) copy-start(f32[1024,1088]{0,1:T(8,128)} %copy-done.3) | copy-start | bytes 13369348
  743.1 2.6 copy-start.34
  745.7 3.3 copy-start.5
  749.6 17.9 %copy-start.8 = (bf16[136,8,8,128]{3,2,1,0:T(8,128)(2,1)}, bf16[136,8,8,128]{3,2,1,0:T(8,128)(2,1)S(1)}, u32[]{:S(2)}) copy-start(bf16[136,8,8,128]{3,2,1,0:T(8,128)(2,1)S(1)} %copy.90) | copy-start | bytes 6684676
  795.4 360.2 %reduce-scatter.19.cloned.1.call-start = ((), (), s32[]{:S(2)}) async-start(), calls=%async_computation.16 | async-start | bytes 11141120
  970.6 7.8 copy-start.30
  970.6 284.1 %reduce-scatter.13.cloned.1.call-start = ((), (), s32[]{:S(2)}) async-start(), calls=%async_computation.13 | async-start | bytes 3133440 | tf_op jit(solution)/shard_map/reduce_scatter | solution.py:252
  978.3 285.0 %reduce-scatter.15.cloned.1.call-start = ((), (), s32[]{:S(2)}) async-start(), calls=%async_computation.14 | async-start | bytes 11837440 | tf_op jit(solution)/shard_map/reduce_scatter | solution.py:264
  997.7 0.7 copy-start.22
  997.7 439.6 %reduce-scatter.17.cloned.1.call-start = ((), (), s32[]{:S(2)}) async-start(), calls=%async_computation.15 | async-start | bytes 12533760 | tf_op jit(solution)/shard_map/reduce_scatter | solution.py:270
  1020.4 546.4 %reduce-scatter.11.cloned.1.call-start = ((), (), s32[]{:S(2)}) async-start(), calls=%async_computation.12 | async-start | bytes 9052160 | tf_op jit(solution)/shard_map/reduce_scatter | solution.py:243
  1147.8 7.8 copy-start.2
  1167.0 3.4 copy-start.9
  1167.0 5.0 copy-start.1
  1167.0 5.0 copy-start.16
  1167.0 5.0 copy-start.18
  1167.1 5.0 copy-start.20
  1167.1 5.0 copy-start.25
  1185.7 3.4 copy-start.33
  1185.7 5.8 copy-start.26
  1185.7 5.8 copy-start.27
  1185.7 501.5 %all-reduce.24.cloned.1.call-start = ((), (), s32[]{:S(2)}) async-start(), calls=%async_computation.18 | async-start | bytes 14622720 | tf_op jit(solution)/shard_map/psum | solution.py:280
  1191.5 14.9 copy-start.23
  1191.5 14.9 copy-start.28
  1191.5 14.9 copy-start.31
  1191.5 14.9 copy-start.32
  1589.7 3.2 copy-start.10
  1687.2 5.9 copy-start.12
  1693.1 2.8 copy-start.11
  (1 other events, 0.7 us)
Sparse Core Ops, SparseCore 0:
  9.6 134.8 all-gather.6
  174.9 60.7 all-gather.8
  237.9 62.4 all-gather.10
  301.8 52.9 all-gather.12
  356.2 166.0 all-gather.14
  523.7 174.6 all-gather.16
  795.6 73.2 reduce-scatter.20
  970.7 73.2 reduce-scatter.18
  1046.9 50.5 reduce-scatter.12
  1099.9 163.3 reduce-scatter.14
  1265.8 171.4 reduce-scatter.16
  1439.6 127.1 reduce-scatter.10
  1570.5 116.7 all-reduce.23
where the time goes:
time: 1720 us; the launch traced here: 1710 us
  waiting for transfers between devices  877 us (51%)
  matrix products  499 us (29%)
  local copies, waits for them, and re-layouts  180 us (10%)
  blocking collectives  72.4 us (4%)
  other arithmetic  57.3 us (3%)
  between operations  17.8 us (1%)
    reduce_scatter x1, waiting for transfers between devices, per_device(): lax.psum_scatter(grad_proj.astype(jnp.bfloat16), 'shard', scatter_dimensi...  174 us
    all_gather x1, waiting for transfers between devices, per_device(): lax.all_gather(proj_weight, 'shard', axis=0, tiled=True)  155 us
    all_gather x1, waiting for transfers between devices, per_device(): lax.all_gather(fc_weight, 'shard', axis=0, tiled=True)  145 us
    reduce_scatter x1, waiting for transfers between devices, per_device(): lax.psum_scatter(grad_qkv.astype(jnp.bfloat16), 'shard', scatter_dimensio...  129 us
    dot_general x1, matrix products, per_device(): jnp.einsum('shqk,shqe->shke', low_grad_scores, query_heads, preferred_ele...  118 us
    dot_general x1, matrix products, per_device(): jnp.einsum('shqk,shke->shqe', low_grad_scores, key_heads, preferred_eleme...  115 us
    unnamed x114, local copies, waits for them, and re-layouts  105 us
    psum x1, waiting for transfers between devices, per_device(): lax.psum(owned[2].astype(jnp.bfloat16), ('replica', 'ctx'))  89.5 us
  transfers between devices with their start and end apart: 13, of which 9 were waited for; matrix products, arithmetic and copies ran while one was open for 35% of the time, Pallas kernels for 0%

commit v1 on v0

v1 whole, which is shorter than its diff:
```python
import functools

import jax
import jax.numpy as jnp
from jax import lax
from jax.experimental import pallas as pl
from jax.experimental.pallas import tpu as pltpu
from jax.sharding import PartitionSpec as P

HEAD_DIM = 64
EPSILON = 1e-05
LANES = 128
UNITS = 8
VMEM_LIMIT = 48 * 1024 * 1024

BF16 = jnp.bfloat16
F32 = jnp.float32


def dot_nn(left, right):
    return lax.dot_general(left, right, (((1,), (0,)), ((), ())), preferred_element_type=F32)


def dot_nt(left, right):
    return lax.dot_general(left, right, (((1,), (1,)), ((), ())), preferred_element_type=F32)


def dot_tn(left, right):
    return lax.dot_general(left, right, (((0,), (0,)), ((), ())), preferred_element_type=F32)


def head_lanes(shape, which):
    lane = lax.broadcasted_iota(jnp.int32, shape, 1)
    return (lane < HEAD_DIM) if which == 0 else (lane >= HEAD_DIM)


def only_valid(values, width):
    if width % LANES == 0:
        return values
    lane = lax.broadcasted_iota(jnp.int32, values.shape, 1) + pl.program_id(1) * LANES
    return jnp.where(lane < width, values, jnp.zeros_like(values))


def causal(rows, columns):
    key_at = lax.broadcasted_iota(jnp.int32, (rows, columns), 0)
    query_at = lax.broadcasted_iota(jnp.int32, (rows, columns), 1)
    return key_at <= query_at


def attention_forward_kernel(tile, width, q_ref, k_ref, v_ref, o_ref, lse_ref):
    length = q_ref.shape[2]
    keys = only_valid(k_ref[0, 0], width)
    values_t = v_ref[0, 0].astype(F32).T.astype(BF16)
    diagonal = causal(tile, tile)
    for start in range(0, length, tile):
        queries = q_ref[0, 0, start : start + tile, :] * jnp.asarray(HEAD_DIM**-0.5, BF16)
        pieces = []
        for which in range(2):
            masked_q = jnp.where(head_lanes(queries.shape, which), queries, jnp.zeros_like(queries))
            scores = dot_nt(keys[: start + tile], masked_q)
            blocks = []
            if start > 0:
                blocks.append(scores[:start])
            blocks.append(jnp.where(diagonal, scores[start:], -1e30))
            top = functools.reduce(
                jnp.maximum, [jnp.max(block, axis=0, keepdims=True) for block in blocks]
            )
            weights = [jnp.exp(block - top) for block in blocks]
            total = sum(jnp.sum(weight, axis=0, keepdims=True) for weight in weights)
            low = jnp.concatenate([weight.astype(BF16) for weight in weights], axis=0)
            rows = values_t[which * HEAD_DIM : (which + 1) * HEAD_DIM, : start + tile]
            pieces.append(dot_nn(rows, low) * (1.0 / total))
            lse_ref[0, 0, which : which + 1, start : start + tile] = top + jnp.log(total)
        mixed_t = jnp.concatenate(pieces, axis=0)
        o_ref[0, start : start + tile, :] = mixed_t.T.astype(BF16)


def attention_backward_kernel(
    tile, width, q_ref, k_ref, v_ref, o_ref, do_ref, lse_ref, out_ref, dk_acc, dv_acc
):
    length = q_ref.shape[2]
    keys = only_valid(k_ref[0, 0], width)
    values = only_valid(v_ref[0, 0], width)
    keys_t = keys.astype(F32).T.astype(BF16)
    diagonal = causal(tile, tile)
    for start in range(0, length, tile):
        stop = start + tile
        queries = q_ref[0, 0, start:stop, :] * jnp.asarray(HEAD_DIM**-0.5, BF16)
        grads = do_ref[0, start:stop, :]
        product_t = (grads.astype(F32) * o_ref[0, start:stop, :].astype(F32)).T
        lanes = head_lanes(queries.shape, 0)
        key_lanes = head_lanes((stop, LANES), 0)
        dq_parts, dk_parts, dv_parts = [], [], []
        for which in range(2):
            mine = head_lanes(queries.shape, which)
            masked_q = jnp.where(mine, queries, jnp.zeros_like(queries))
            masked_g = jnp.where(mine, grads, jnp.zeros_like(grads))
            delta = jnp.sum(
                product_t[which * HEAD_DIM : (which + 1) * HEAD_DIM], axis=0, keepdims=True
            )
            lse = lse_ref[0, 0, which : which + 1, start:stop]
            scores = dot_nt(keys[:stop], masked_q)
            grad_weights = dot_nt(values[:stop], masked_g)
            weights = jnp.exp(scores - lse)
            if start > 0:
                weights = jnp.concatenate(
                    [weights[:start], jnp.where(diagonal, weights[start:], 0.0)], axis=0
                )
            else:
                weights = jnp.where(diagonal, weights, 0.0)
            low_scores = (weights * (grad_weights - delta)).astype(BF16)
            dv_parts.append(dot_nn(weights.astype(BF16), grads))
            dk_parts.append(dot_nn(low_scores, queries))
            dq_parts.append(
                dot_nn(keys_t[which * HEAD_DIM : (which + 1) * HEAD_DIM, :stop], low_scores)
            )
        dq_t = jnp.concatenate(dq_parts, axis=0) * (HEAD_DIM**-0.5)
        out_ref[0, 0, start:stop, :] = dq_t.T.astype(BF16)
        dk = jnp.where(key_lanes, dk_parts[0], dk_parts[1])
        dv = jnp.where(key_lanes, dv_parts[0], dv_parts[1])
        if start > 0:
            dk_acc[:start] += dk[:start]
            dv_acc[:start] += dv[:start]
        dk_acc[start:stop] = dk[start:]
        dv_acc[start:stop] = dv[start:]
    out_ref[1, 0] = dk_acc[...].astype(BF16)
    out_ref[2, 0] = dv_acc[...].astype(BF16)


def attention_tile(length):
    return 256 if length % 256 == 0 else 128


def attention_forward(joined):
    _, seqs, length, width = joined.shape
    pairs = pl.cdiv(width, LANES)
    spec = lambda which: pl.BlockSpec((1, 1, length, LANES), lambda s, h: (which, s, 0, h))
    return pl.pallas_call(
        functools.partial(attention_forward_kernel, attention_tile(length), width),
        grid=(seqs, pairs),
        in_specs=[spec(0), spec(1), spec(2)],
        out_specs=[
            pl.BlockSpec((1, length, LANES), lambda s, h: (s, 0, h)),
            pl.BlockSpec((1, 1, 8, length), lambda s, h: (s, h, 0, 0)),
        ],
        out_shape=[
            jax.ShapeDtypeStruct((seqs, length, width), BF16),
            jax.ShapeDtypeStruct((seqs, pairs, 8, length), F32),
        ],
        compiler_params=pltpu.CompilerParams(vmem_limit_bytes=VMEM_LIMIT),
        cost_estimate=pl.CostEstimate(
            flops=seqs * pairs * 8 * length * length * LANES,
            bytes_accessed=8 * seqs * length * width,
            transcendentals=seqs * pairs * 2 * length * length,
        ),
    )(joined, joined, joined)


def attention_backward(joined, mixed, grad_mixed, lse):
    _, seqs, length, width = joined.shape
    pairs = pl.cdiv(width, LANES)
    spec = lambda which: pl.BlockSpec((1, 1, length, LANES), lambda s, h: (which, s, 0, h))
    rows = pl.BlockSpec((1, length, LANES), lambda s, h: (s, 0, h))
    return pl.pallas_call(
        functools.partial(attention_backward_kernel, attention_tile(length), width),
        grid=(seqs, pairs),
        in_specs=[
            spec(0),
            spec(1),
            spec(2),
            rows,
            rows,
            pl.BlockSpec((1, 1, 8, length), lambda s, h: (s, h, 0, 0)),
        ],
        out_specs=pl.BlockSpec((3, 1, length, LANES), lambda s, h: (0, s, 0, h)),
        out_shape=jax.ShapeDtypeStruct((3, seqs, length, width), BF16),
        scratch_shapes=[pltpu.VMEM((length, LANES), F32), pltpu.VMEM((length, LANES), F32)],
        compiler_params=pltpu.CompilerParams(vmem_limit_bytes=VMEM_LIMIT),
        cost_estimate=pl.CostEstimate(
            flops=seqs * pairs * 20 * length * length * LANES,
            bytes_accessed=16 * seqs * length * width,
            transcendentals=seqs * pairs * 2 * length * length,
        ),
    )(joined, joined, joined, mixed, grad_mixed, lse)


def standardize(values):
    centred = values - jnp.mean(values, axis=-1, keepdims=True)
    inverse = lax.rsqrt(jnp.mean(centred * centred, axis=-1, keepdims=True) + EPSILON)
    return centred * inverse, inverse


def normalize_back(grad_out, standard, inverse, gain_vec):
    scaled = grad_out * gain_vec
    grad_in = inverse * (
        scaled
        - jnp.mean(scaled, axis=-1, keepdims=True)
        - standard * jnp.mean(scaled * standard, axis=-1, keepdims=True)
    )
    return grad_in, jnp.sum(grad_out * standard, axis=0), jnp.sum(grad_out, axis=0)


def swap_pairs(count, offset):
    return [(index, index ^ offset) for index in range(count)]


def to_sequences(values, block_order, count):
    seqs, local, width = values.shape
    own = lax.axis_index("ctx")
    share = seqs // count
    out = jnp.zeros((share, count, local, width), values.dtype)
    for offset in range(count):
        other = own ^ offset
        piece = lax.dynamic_slice_in_dim(values, other * share, share, axis=0)
        if offset:
            piece = lax.ppermute(piece, "ctx", swap_pairs(count, offset))
        place = lax.dynamic_index_in_dim(block_order, other, keepdims=False)
        out = lax.dynamic_update_slice(out, piece[:, None], (0, place, 0, 0))
    return out


def to_blocks(values, block_order, count):
    share, _, local, width = values.shape
    own = lax.axis_index("ctx")
    out = jnp.zeros((share * count, local, width), values.dtype)
    for offset in range(count):
        other = own ^ offset
        place = lax.dynamic_index_in_dim(block_order, other, keepdims=False)
        piece = lax.dynamic_slice(values, (0, place, 0, 0), (share, 1, local, width))[:, 0]
        if offset:
            piece = lax.ppermute(piece, "ctx", swap_pairs(count, offset))
        out = lax.dynamic_update_slice(out, piece, (other * share, 0, 0))
    return out


def per_device(
    tokens,
    cotangent,
    block_order,
    ln1_gain,
    ln1_bias,
    qkv_weight,
    q_bias,
    v_bias,
    out_weight,
    out_bias,
    ln2_gain,
    ln2_bias,
    fc_weight,
    fc_bias,
    proj_weight,
    proj_bias,
):
    seq_count, local_len, width = tokens.shape
    owned_rows = ln1_gain.shape[0]
    shards = width // owned_rows
    half = owned_rows // 2
    wide = fc_weight.shape[1] // width
    count = lax.axis_size("ctx")
    rows = seq_count * local_len
    spread = ("replica", "ctx")
    others = ()
    if UNITS % (lax.axis_size("replica") * count):
        spread, others = ("ctx",), ("replica",)
    parts = 1
    for axis in spread:
        parts *= lax.axis_size(axis)
    units = UNITS // parts
    everyone = ("shard",) + spread
    part = lax.axis_index(spread)

    def take_units(blocks):
        flat = blocks.reshape(UNITS * half, width)
        return lax.dynamic_slice_in_dim(flat, part * units * half, units * half, axis=0)

    def gather(chunk):
        full = lax.all_gather(chunk, everyone, axis=0, tiled=False)
        return full.reshape(shards, parts, chunk.shape[0], width)

    def to_matrices(gathered):
        blocks = gathered.reshape(shards, 4, owned_rows, width)
        return blocks.transpose(1, 0, 2, 3).reshape(4, width, width)

    vectors = jnp.concatenate(
        [ln1_gain, ln1_bias, q_bias, v_bias, out_bias, ln2_gain, ln2_bias, proj_bias, fc_bias]
    )
    vector_rows = vectors.shape[0] // width
    vector_pad = -vector_rows % 8
    vector_tile = jnp.pad(vectors.reshape(vector_rows, width), ((0, vector_pad), (0, 0)))
    blocks_a = jnp.concatenate(
        [qkv_weight.reshape(owned_rows, 3, width).transpose(1, 0, 2), out_weight[None]], axis=0
    )
    blocks_b = fc_weight.reshape(owned_rows, wide, width).transpose(1, 0, 2)
    chunk_a = jnp.concatenate([take_units(blocks_a), vector_tile], axis=0)
    gathered_a = gather(chunk_a)
    gathered_b = gather(take_units(blocks_b))
    gathered_c = gather(take_units(proj_weight.reshape(4, owned_rows, width)))
    used = units * half
    matrices_a = to_matrices(gathered_a[:, :, :used])
    w_qkv, w_out = matrices_a[:3], matrices_a[3]
    w_fc = to_matrices(gathered_b)
    w_proj = gathered_c.reshape(wide, width, width)
    vector_part = gathered_a[:, 0, used : used + vector_rows].reshape(shards, vector_rows * width)
    vector_part = vector_part.astype(F32)
    small = vector_part[:, : 8 * owned_rows].reshape(shards, 8, owned_rows)
    small = small.transpose(1, 0, 2).reshape(8, width)
    g_one, b_one, bias_q, bias_v, bias_out, g_two, b_two, bias_proj = [small[i] for i in range(8)]
    bias_fc = vector_part[:, 8 * owned_rows :].reshape(wide, 1, width)

    low_inputs = to_sequences(tokens, block_order, count).reshape(rows, width)
    low_grad_out = to_sequences(cotangent, block_order, count).reshape(rows, width)
    share = seq_count // count
    full_len = count * local_len

    inputs = low_inputs.astype(F32)
    standard_one, inverse_one = standardize(inputs)
    low_one = (standard_one * g_one + b_one).astype(BF16)
    joined = jnp.einsum("td,cdx->ctx", low_one, w_qkv, preferred_element_type=F32)
    bias_qkv = jnp.stack([bias_q, jnp.zeros_like(bias_q), bias_v])[:, None]
    joined = (joined + bias_qkv).astype(BF16).reshape(3, share, full_len, width)
    mixed, lse = attention_forward(joined)
    attended = mixed.reshape(rows, width)
    middle = inputs + (dot_nn(attended, w_out) + bias_out)
    standard_two, inverse_two = standardize(middle)
    low_two = (standard_two * g_two + b_two).astype(BF16)
    hidden = jnp.einsum("td,cdx->ctx", low_two, w_fc, preferred_element_type=F32) + bias_fc
    activated, gelu_pull = jax.vjp(lambda pre_act: jax.nn.gelu(pre_act, approximate=True), hidden)
    low_act = activated.astype(BF16)
    outputs = middle + (
        jnp.einsum("ctx,cxd->td", low_act, w_proj, preferred_element_type=F32) + bias_proj
    )
    layer_out = to_blocks(
        outputs.astype(BF16).reshape(share, count, local_len, width), block_order, count
    )

    def reduce_units(grads):
        owned = lax.psum_scatter(grads, everyone, scatter_dimension=0, tiled=False)
        if others:
            owned = lax.psum(owned, others)
        return lax.all_gather(owned, spread, axis=0, tiled=False)

    def from_matrices(grads):
        blocks = grads.reshape(4, shards, owned_rows, width).transpose(1, 0, 2, 3)
        return blocks.reshape(shards * parts, units * half, width)

    grad_out = low_grad_out.astype(F32)
    grad_proj = jnp.einsum("ctx,td->cxd", low_act, low_grad_out, preferred_element_type=F32)
    owned_proj = reduce_units(grad_proj.astype(BF16).reshape(shards * parts, units * half, width))
    grad_proj_bias = jnp.sum(grad_out, axis=0)
    grad_act = jnp.einsum("td,cxd->ctx", low_grad_out, w_proj, preferred_element_type=F32)
    grad_hidden = gelu_pull(grad_act)[0].astype(BF16)
    grad_fc = jnp.einsum("td,ctx->cdx", low_two, grad_hidden, preferred_element_type=F32)
    owned_fc = reduce_units(from_matrices(grad_fc.astype(BF16)))
    grad_fc_bias = jnp.sum(grad_hidden.astype(F32), axis=1)
    grad_two = jnp.einsum("ctx,cdx->td", grad_hidden, w_fc, preferred_element_type=F32)
    grad_norm_two, grad_g_two, grad_b_two = normalize_back(
        grad_two, standard_two, inverse_two, g_two
    )
    grad_middle = grad_out + grad_norm_two
    low_grad_middle = grad_middle.astype(BF16)
    grad_out_weight = dot_tn(attended, low_grad_middle)
    grad_out_bias = jnp.sum(low_grad_middle.astype(F32), axis=0)
    grad_attended = dot_nt(low_grad_middle, w_out).astype(BF16)
    grad_joined = attention_backward(
        joined, mixed, grad_attended.reshape(share, full_len, width), lse
    ).reshape(3, rows, width)
    grad_qkv = jnp.einsum("td,ctx->cdx", low_one, grad_joined, preferred_element_type=F32)
    grad_q_bias = jnp.sum(grad_joined[0].astype(F32), axis=0)
    grad_v_bias = jnp.sum(grad_joined[2].astype(F32), axis=0)
    grad_one = jnp.einsum("ctx,cdx->td", grad_joined, w_qkv, preferred_element_type=F32)
    grad_norm_one, grad_g_one, grad_b_one = normalize_back(
        grad_one, standard_one, inverse_one, g_one
    )
    input_grad = to_blocks(
        (grad_middle + grad_norm_one).astype(BF16).reshape(share, count, local_len, width),
        block_order,
        count,
    ).astype(F32)

    small_grads = jnp.stack(
        [
            grad_g_one,
            grad_b_one,
            grad_q_bias,
            grad_v_bias,
            grad_out_bias,
            grad_g_two,
            grad_b_two,
            grad_proj_bias,
        ]
    )
    vector_grads = jnp.concatenate(
        [
            small_grads.reshape(8, shards, owned_rows)
            .transpose(1, 0, 2)
            .reshape(shards, 8 * owned_rows),
            grad_fc_bias.reshape(shards, owned_rows * wide),
        ],
        axis=1,
    ).astype(BF16)
    vector_tile = vector_grads.reshape(shards, parts, 1, -1)
    piece = vector_tile.shape[-1]
    vector_tile = jnp.pad(vector_tile, ((0, 0), (0, 0), (0, 7), (0, width - piece)))
    grads_a = jnp.concatenate([grad_qkv.astype(BF16), grad_out_weight.astype(BF16)[None]], axis=0)
    grads_a = jnp.concatenate(
        [from_matrices(grads_a), vector_tile.reshape(shards * parts, 8, width)], axis=1
    )
    owned_a = reduce_units(grads_a)
    owned_vectors = owned_a[:, used, :piece].reshape(-1).astype(F32)
    vec = [owned_vectors[i * owned_rows : (i + 1) * owned_rows] for i in range(8)]
    fc_bias_grad = owned_vectors[8 * owned_rows :]
    owned_blocks = owned_a[:, :used].reshape(4, owned_rows, width)
    qkv_grad = owned_blocks[:3].transpose(1, 0, 2).reshape(owned_rows, 3 * width).astype(F32)
    fc_grad = (
        owned_fc.reshape(wide, owned_rows, width)
        .transpose(1, 0, 2)
        .reshape(owned_rows, wide * width)
        .astype(F32)
    )
    return (
        layer_out,
        input_grad,
        vec[0],
        vec[1],
        qkv_grad,
        vec[2],
        vec[3],
        owned_blocks[3].astype(F32),
        vec[4],
        vec[5],
        vec[6],
        fc_grad,
        fc_bias_grad,
        owned_proj.reshape(wide * owned_rows, width).astype(F32),
        vec[7],
    )


def solution(mesh):
    vector, matrix = P("shard"), P("shard", None)
    rows = P(("shard", "replica"), "ctx", None)
    weights = (
        vector,
        vector,
        matrix,
        vector,
        vector,
        matrix,
        vector,
        vector,
        vector,
        matrix,
        vector,
        matrix,
        vector,
    )
    return jax.shard_map(
        per_device,
        mesh=mesh,
        in_specs=(rows, rows, P()) + weights,
        out_specs=(rows, rows) + weights,
        check_vma=False,
    )
```

time: 1720 us -> 1080 us (0.63)
  waiting for transfers between devices: 877 us -> 290 us
  matrix products: 499 us -> 187 us
  local copies, waits for them, and re-layouts: 180 us -> 414 us
  blocking collectives: 72.4 us -> 0 us
  Pallas kernels: 0 us -> 57.7 us
    all_gather x6, waiting for transfers between devices: 474 us -> 63.7 us  [the longest x3 63.7 us: reduce_units(): return lax.all_gather(owned, spread, axis=0, tiled=False)]
    dot_general x18 -> x12, matrix products: 499 us -> 187 us  [the longest x1 28.6 us: per_device(): jnp.einsum('td,cxd->ctx', low_grad_out, w_proj, preferred_element_type=F32)]
    dynamic_update_slice x0 -> x16, local copies, waits for them, and re-layouts: none -> 211 us  [the longest x8 202 us: to_sequences(): out = lax.dynamic_update_slice(out, piece[:, None], (0, place, 0, 0))]
    reduce_scatter x4 -> x1, waiting for transfers between devices: 312 us -> 105 us  [reduce_units(): owned = lax.psum_scatter(grads, everyone, scatter_dimension=0, tiled=False)]
    unnamed x15 -> x11, waiting for transfers between devices: 2.41 us -> 110 us
    unnamed x114 -> x83, local copies, waits for them, and re-layouts: 105 us -> 7.89 us
    psum x1 -> x0, waiting for transfers between devices: 89.5 us -> none  [per_device(): lax.psum(owned[2].astype(jnp.bfloat16), ('replica', 'ctx'))]
    pallas_call x0 -> x2, Pallas kernels: none -> 57.7 us  [the longest x1 29.9 us: attention_forward(): pl.pallas_call(functools.partial(attention_forward_kernel, attention_tile...]
  transfers between devices with their start and end apart: 13 -> 21, of which waited for: 9 -> 6; matrix products, arithmetic and copies ran while one was open for 35% -> 55% of each run, Pallas kernels for 0% -> 5%
where the time goes in v1:
time: 1080 us; the launch traced here: 1060 us
  local copies, waits for them, and re-layouts  414 us (38%)
  waiting for transfers between devices  290 us (27%)
  matrix products  187 us (17%)
  other arithmetic  71.7 us (7%)
  Pallas kernels  57.7 us (5%)
  between operations  22.9 us (2%)
  starting transfers between devices  11.9 us (1%)
    dynamic_update_slice x8, local copies, waits for them, and re-layouts, to_sequences(): out = lax.dynamic_update_slice(out, piece[:, None], (0, place, 0, 0))  202 us
    unnamed x11, waiting for transfers between devices  110 us
    reduce_scatter x1, waiting for transfers between devices, reduce_units(): owned = lax.psum_scatter(grads, everyone, scatter_dimension=0, tiled=False)  105 us
    all_gather x3, waiting for transfers between devices, reduce_units(): return lax.all_gather(owned, spread, axis=0, tiled=False)  63.7 us
    broadcast_in_dim x8, local copies, waits for them, and re-layouts, to_sequences(): out = lax.dynamic_update_slice(out, piece[:, None], (0, place, 0, 0))  44.7 us
    pallas_call x1, Pallas kernels, attention_forward(): pl.pallas_call(functools.partial(attention_forward_kernel, attention_tile...  29.9 us
    dot_general x1, matrix products, per_device(): jnp.einsum('td,cxd->ctx', low_grad_out, w_proj, preferred_element_type=F32)  28.6 us
    pallas_call x1, Pallas kernels, attention_backward(): pl.pallas_call(functools.partial(attention_backward_kernel, attention_til...  27.7 us
  transfers between devices with their start and end apart: 21, of which 6 were waited for; matrix products, arithmetic and copies ran while one was open for 55% of the time, Pallas kernels for 5%

profile of v1, /device:TPU:0, one launch (start us, length us, event | category | flops | bytes accessed | tf_op | source)
XLA Modules:
  0.0 1055.3 jit_solution(3819266965531145335)
XLA Ops:
  7.4 6.4 reshape.301
  21.3 5.7 reshape.293
  43.5 11.9 %collective-permute-done.2 = bf16[2,128,1088]{1,2,0:T(8,128)(2,1)} collective-permute-done((bf16[2,128,1088]{1,2,0:T(8,128)(2,1)S(1)}, bf16[2,128,1088]{1,2,0:T(8,128)(2,1)}, u32[]{:S(2)}, u32[]{:S(2)}) %collective-permute-start.2) | collective-permute-done | bytes 557088 | tf_op jit(solution)/shard_map/ppermute | solution.py:216
  63.9 7.7 copy.121
  79.6 24.4 %dynamic_update_slice.48 = bf16[2,4,128,1088]{2,1,0,3:T(4,128)(2,1)S(1)} dynamic-update-slice(bf16[2,4,128,1088]{2,1,0,3:T(4,128)(2,1)S(1)} %broadcast.130.clone, bf16[2,1,128,1088]{2,1,0,3:T(2,128)(2,1)} %copy.121, s32[]{:T(128)} %constant.72.clone.1, s32[]{:T(128)S(6)} %select_n.80, s32[]{:T(128)} %constant.72.clone.1, s32[]{:T(128)} %constant.72.clone.1) | dynamic-update-slice | bytes 1114116 | tf_op jit(solution)/shard_map/dynamic_update_slice | solution.py:218
  105.7 26.6 %dynamic_update_slice.56 = bf16[2,4,128,1088]{2,1,0,3:T(4,128)(2,1)} dynamic-update-slice(bf16[2,4,128,1088]{2,1,0,3:T(4,128)(2,1)} %broadcast.130.clone.1, bf16[2,1,128,1088]{2,1,0,3:T(2,128)(2,1)S(1)} %copy.138, s32[]{:T(128)} %constant.72.clone.1, s32[]{:T(128)S(6)} %select_n.80, s32[]{:T(128)} %constant.72.clone.1, s32[]{:T(128)} %constant.72.clone.1) | dynamic-update-slice | bytes 1114116 | tf_op jit(solution)/shard_map/dynamic_update_slice | solution.py:218
  137.0 5.5 copy.122
  142.5 5.6 copy.123
  148.1 5.5 copy.141
  153.6 5.5 copy.139
  164.6 26.7 %dynamic_update_slice.57 = bf16[2,4,128,1088]{2,1,0,3:T(4,128)(2,1)} dynamic-update-slice(bf16[2,4,128,1088]{2,1,0,3:T(4,128)(2,1)} %dynamic_update_slice.56, bf16[2,1,128,1088]{2,1,0,3:T(2,128)(2,1)} %copy.139, s32[]{:T(128)} %constant.72.clone.1, s32[]{:T(128)S(6)} %select_n.83, s32[]{:T(128)} %constant.72.clone.1, s32[]{:T(128)} %constant.72.clone.1) | dynamic-update-slice | bytes 1114116 | tf_op jit(solution)/shard_map/dynamic_update_slice | solution.py:218
  191.4 26.8 %dynamic_update_slice.58 = bf16[2,4,128,1088]{2,1,0,3:T(4,128)(2,1)} dynamic-update-slice(bf16[2,4,128,1088]{2,1,0,3:T(4,128)(2,1)} %dynamic_update_slice.57, bf16[2,1,128,1088]{2,1,0,3:T(2,128)(2,1)} %copy.140, s32[]{:T(128)} %constant.72.clone.1, s32[]{:T(128)S(6)} %select_n.86, s32[]{:T(128)} %constant.72.clone.1, s32[]{:T(128)} %constant.72.clone.1) | dynamic-update-slice | bytes 1114116 | tf_op jit(solution)/shard_map/dynamic_update_slice | solution.py:218
  218.1 26.7 %dynamic_update_slice.59 = bf16[2,4,128,1088]{2,1,0,3:T(4,128)(2,1)} dynamic-update-slice(bf16[2,4,128,1088]{2,1,0,3:T(4,128)(2,1)} %dynamic_update_slice.58, bf16[2,1,128,1088]{2,1,0,3:T(2,128)(2,1)} %copy.141, s32[]{:T(128)} %constant.72.clone.1, s32[]{:T(128)S(6)} %select_n.89, s32[]{:T(128)} %constant.72.clone.1, s32[]{:T(128)} %constant.72.clone.1) | dynamic-update-slice | bytes 1114116 | tf_op jit(solution)/shard_map/dynamic_update_slice | solution.py:218
  249.7 24.4 %dynamic_update_slice.49 = bf16[2,4,128,1088]{2,1,0,3:T(4,128)(2,1)S(1)} dynamic-update-slice(bf16[2,4,128,1088]{2,1,0,3:T(4,128)(2,1)S(1)} %dynamic_update_slice.48, bf16[2,1,128,1088]{2,1,0,3:T(2,128)(2,1)} %copy.122, s32[]{:T(128)} %constant.72.clone.1, s32[]{:T(128)S(6)} %select_n.83, s32[]{:T(128)} %constant.72.clone.1, s32[]{:T(128)} %constant.72.clone.1) | dynamic-update-slice | bytes 1114116 | tf_op jit(solution)/shard_map/dynamic_update_slice | solution.py:218
  274.1 24.4 %dynamic_update_slice.50 = bf16[2,4,128,1088]{2,1,0,3:T(4,128)(2,1)S(1)} dynamic-update-slice(bf16[2,4,128,1088]{2,1,0,3:T(4,128)(2,1)S(1)} %dynamic_update_slice.49, bf16[2,1,128,1088]{2,1,0,3:T(2,128)(2,1)} %copy.123, s32[]{:T(128)} %constant.72.clone.1, s32[]{:T(128)S(6)} %select_n.86, s32[]{:T(128)} %constant.72.clone.1, s32[]{:T(128)} %constant.72.clone.1) | dynamic-update-slice | bytes 1114116 | tf_op jit(solution)/shard_map/dynamic_update_slice | solution.py:218
  298.5 22.4 %dynamic_update_slice.51 = bf16[2,4,128,1088]{2,1,0,3:T(4,128)(2,1)S(1)} dynamic-update-slice(bf16[2,4,128,1088]{2,1,0,3:T(4,128)(2,1)S(1)} %dynamic_update_slice.50, bf16[2,1,128,1088]{2,1,0,3:T(2,128)(2,1)S(1)} %copy.124, s32[]{:T(128)} %constant.72.clone.1, s32[]{:T(128)S(6)} %select_n.89, s32[]{:T(128)} %constant.72.clone.1, s32[]{:T(128)} %constant.72.clone.1) | dynamic-update-slice | bytes 1114116 | tf_op jit(solution)/shard_map/dynamic_update_slice | solution.py:218
  326.9 8.3 copy.131
  335.3 8.4 slice.138
  348.1 6.7 slice.139
  372.6 10.8 %fusion.11 = bf16[3,1024,1088]{1,2,0:T(8,128)(2,1)} fusion(f32[3,1088]{1,0:T(4,128)S(1)} %pad_maximum_fusion.4, bf16[3,1088,1088]{2,1,0:T(8,128)(2,1)S(1)} %bitcast.217, bf16[1024,1088,1]{0,1,2:T(8,128)(2,1)S(1)} %reshape.330), kind=kOutput, calls=%fused_computation.24 | convolution fusion | flops 7279607808 | bytes 16028416 | tf_op jit(solution)/shard_map/td,cdx->ctx/dot_general | solution.py:318
  383.3 9.5 copy.129
  392.8 29.9 %shard_map.271 = (bf16[2,512,1088]{2,1,0:T(8,128)(2,1)S(1)}, f32[2,9,8,512]{3,2,1,0:T(8,128)S(1)}) custom-call(bf16[3,2,512,1088]{3,2,1,0:T(8,128)(2,1)} %bitcast.195, bf16[3,2,512,1088]{3,2,1,0:T(8,128)(2,1)} %bitcast.196, bf16[3,2,512,1088]{3,2,1,0:T(8,128)(2,1)} %bitcast.197), custom_call_target="tpu_custom_call" | custom-call | flops 4831838208 | bytes 8912896 | tf_op jit(solution)/shard_map/pallas_call | solution.py:138
  422.8 5.7 fusion.31
  430.7 18.5 %convolution_add_fusion = f32[4,1088,1024]{2,1,0:T(8,128)} fusion(bf16[4,1088,1088]{2,1,0:T(8,128)(2,1)} %bitcast.210, f32[4,1088]{1,0:T(4,128)S(1)} %slice-done.2, f32[1024,1088]{0,1:T(8,128)S(1)} %get-tuple-element.68, f32[1088]{0:T(1024)S(1)} %add.215, f32[1088]{0:T(1024)S(1)} %mul.196, f32[1024]{0:T(1024)S(1)} %add_rsqrt_fusion, ...), kind=kOutput, calls=%fused_computation.4 | convolution fusion | flops 9707257856 | bytes 31786496 | tf_op jit(solution)/shard_map/td,cdx->ctx/dot_general | solution.py:326
  449.2 28.6 %fusion.32 = (bf16[4,1088]{1,0:T(4,128)(2,1)S(1)}, bf16[4,1024,1088]{1,2,0:T(8,128)(2,1)}) fusion(f32[4,1088,1024]{2,1,0:T(8,128)} %convolution_add_fusion, bf16[4,1088,1088]{2,1,0:T(8,128)(2,1)} %bitcast.240, bf16[1024,1088,1]{0,1,2:T(8,128)(2,1)S(1)} %copy-done.14), kind=kOutput, calls=%fused_computation.132 | convolution fusion | flops 9790812160 | bytes 38445568 | tf_op jit(solution)/shard_map/td,cxd->ctx/dot_general | solution.py:350
  477.8 17.6 %convolution_convert_fusion.1 = bf16[4,1088,1088]{1,2,0:T(8,128)(2,1)} fusion(bf16[4,1024,1088]{1,2,0:T(8,128)(2,1)} %get-tuple-element.72, f32[1024,1088]{0,1:T(8,128)} %copy-done.6, f32[1088]{0:T(1024)S(1)} %add.215, f32[1088]{0:T(1024)S(1)} %mul.196, f32[1024]{0:T(1024)S(1)} %add_rsqrt_fusion, f32[1024]{0:T(1024)S(1)} %broadcast_multiply_fusion.4), kind=kOutput, calls=%fused_computation.1 | convolution fusion | flops 9707536384 | bytes 22856192 | tf_op jit(solution)/shard_map/td,ctx->cdx/dot_general | solution.py:352
  495.4 8.4 copy.154
  508.5 8.2 reduce.8
  516.7 22.6 %convolution_convert_fusion = bf16[4,1088,1088]{2,1,0:T(8,128)(2,1)} fusion(bf16[1024,1088,1]{0,1,2:T(8,128)(2,1)} %reshape.333, f32[4,1088,1024]{2,1,0:T(8,128)} %convolution_add_fusion), kind=kOutput, calls=%fused_computation | convolution fusion | flops 9742073856 | bytes 29523968 | tf_op jit(solution)/shard_map/ctx,td->cxd/dot_general | solution.py:347
  539.4 19.3 %fusion.14 = (bf16[1088]{0:T(1024)(128)(2,1)S(1)}, f32[1024]{0:T(1024)S(1)}, f32[1024]{0:T(1024)S(1)}, bf16[1088]{0:T(1024)(128)(2,1)S(1)}, f32[1024,1088,1]{0,1,2:T(8,128)}) fusion(f32[1024,1088]{0,1:T(8,128)} %copy-done.6, f32[1024]{0:T(1024)S(1)} %add_rsqrt_fusion, f32[1024]{0:T(1024)S(1)} %broadcast_multiply_fusion.4, f32[1088]{0:T(1024)S(1)} %mul.196, ...), kind=kOutput, calls=%fused_computation.36 | convolution fusion | flops 9707253760 | bytes 27320832 | tf_op jit(solution)/shard_map/ctx,cdx->td/dot_general | solution.py:355
  559.0 7.5 convert_reduce_fusion.1
  566.6 7.6 convolution_convert_fusion.4
  578.8 27.7 %shard_map.272 = bf16[3,2,512,1088]{3,2,1,0:T(8,128)(2,1)} custom-call(bf16[3,2,512,1088]{3,2,1,0:T(8,128)(2,1)} %bitcast.198, bf16[3,2,512,1088]{3,2,1,0:T(8,128)(2,1)} %bitcast.199, bf16[3,2,512,1088]{3,2,1,0:T(8,128)(2,1)} %bitcast.200, bf16[2,512,1088]{2,1,0:T(8,128)(2,1)S(1)} %copy-done.3, bf16[2,512,1088]{2,1,0:T(8,128)(2,1)S(1)} %bitcast.192, ...), custom_call_target="tpu_custom_call" | custom-call | flops 12079595520 | bytes 17825792 | tf_op jit(solution)/shard_map/pallas_call | solution.py:164
  606.5 16.2 %fusion.13 = (bf16[1088]{0:T(1024)(128)(2,1)S(1)}, f32[1024]{0:T(1024)S(1)}, f32[1024]{0:T(1024)S(1)}, bf16[1088]{0:T(1024)(128)(2,1)S(1)}, f32[1024,1088,1]{0,1,2:T(8,128)}) fusion(f32[1024,1088]{0,1:T(8,128)} %reshape.315, f32[1024]{0:T(1024)S(1)} %bitcast.235, f32[1024]{0:T(1024)S(1)} %bitcast.237, f32[1088]{0:T(1024)S(1)} %copy-done.20, ...), kind=kOutput, calls=%fused_computation.32 | convolution fusion | flops 7282946048 | bytes 22725120 | tf_op jit(solution)/shard_map/ctx,cdx->td/dot_general | solution.py:370
  627.0 7.1 convolution_convert_fusion.3
  634.1 13.4 %convolution_convert_fusion.2 = bf16[3,1088,1088]{1,2,0:T(8,128)(2,1)} fusion(bf16[1024,1088,1]{0,1,2:T(8,128)(2,1)S(1)} %copy-done.13, bf16[3,1024,1088]{2,1,0:T(8,128)(2,1)} %bitcast.224), kind=kOutput, calls=%fused_computation.19 | convolution fusion | flops 7276474368 | bytes 16015360 | tf_op jit(solution)/shard_map/td,ctx->cdx/dot_general | solution.py:367
  647.5 8.2 pad_maximum_fusion.1
  655.7 10.3 pad_maximum_fusion
  666.9 108.8 %reduce-scatter.12.cloned.1.call-done = bf16[1,136,1088]{2,1,0:T(8,128)(2,1)} async-done(((bf16[32,136,1088]{2,1,0:T(8,128)(2,1)}), bf16[1,136,1088]{2,1,0:T(8,128)(2,1)}) %reduce-scatter.12.cloned.1.call-update) | async-done | bytes 295952
  775.8 19.1 %fusion.16 = bf16[1024,1088]{0,1:T(8,128)(2,1)} fusion(f32[1024,1088]{0,1:T(8,128)} %copy-done.6, bf16[4,1088,1088]{2,1,0:T(8,128)(2,1)} %bitcast.241, f32[1088]{0:T(1024)S(1)} %add.223, f32[4,1088,1024]{2,1,0:T(8,128)} %convolution_add_fusion), kind=kOutput, calls=%fused_computation.39 | convolution fusion | flops 9740681216 | bytes 33984768 | tf_op jit(solution)/shard_map/ctx,cxd->td/dot_general | solution.py:330
  799.3 7.8 add_convert_fusion.1
  812.5 13.2 %constant_dynamic-slice_fusion = (bf16[2,1,128,1088]{2,1,0,3:T(2,128)(2,1)S(1)}, bf16[2,1,128,1088]{2,1,0,3:T(2,128)(2,1)S(1)}, bf16[2,1,128,1088]{2,1,0,3:T(2,1...) fusion(bf16[2,4,128,1088]{2,1,0,3:T(4,128)(2,1)} %reshape.308, ...), kind=kLoop, calls=%fused_computation.88 | loop fusion | bytes 8912912 | tf_op jit(solution)/shard_map/dynamic_slice | solution.py:229
  832.9 105.1 %reduce-scatter.8.cloned.1.call-done = bf16[1,144,1088]{2,1,0:T(8,128)(2,1)} async-done(((bf16[32,144,1088]{2,1,0:T(8,128)(2,1)}), bf16[1,144,1088]{2,1,0:T(8,128)(2,1)}) %reduce-scatter.8.cloned.1.call-update) | async-done | bytes 313360 | tf_op jit(solution)/shard_map/reduce_scatter | solution.py:337
  951.6 17.2 %all-gather.12.cloned.1.call-done = bf16[8,136,1088]{2,1,0:T(8,128)(2,1)} async-done(((bf16[1,136,1088]{2,1,0:T(8,128)(2,1)}), bf16[8,136,1088]{2,1,0:T(8,128)(2,1)}) %all-gather.12.cloned.1.call-update) | async-done | bytes 2367504 | tf_op jit(solution)/shard_map/all_gather | solution.py:340
  975.0 6.6 reshape.320
  981.6 18.6 %all-gather.14.cloned.1.call-done = bf16[8,136,1088]{2,1,0:T(8,128)(2,1)} async-done(((bf16[1,136,1088]{2,1,0:T(8,128)(2,1)}), bf16[8,136,1088]{2,1,0:T(8,128)(2,1)}) %all-gather.14.cloned.1.call-update) | async-done | bytes 2367504 | tf_op jit(solution)/shard_map/all_gather | solution.py:340
  1004.6 27.9 %all-gather.10.cloned.1.call-done = bf16[8,144,1088]{2,1,0:T(8,128)(2,1)} async-done(((bf16[1,144,1088]{2,1,0:T(8,128)(2,1)}), bf16[8,144,1088]{2,1,0:T(8,128)(2,1)}) %all-gather.10.cloned.1.call-update) | async-done | bytes 2506768 | tf_op jit(solution)/shard_map/all_gather | solution.py:340
  1041.8 6.5 reshape.318
  (229 shorter events, 144.4 us)
Async XLA Ops:
  7.2 25.8 %copy-start = (bf16[1088,1088]{1,0:T(8,128)(2,1)S(1)}, bf16[1088,1088]{1,0:T(8,128)(2,1)}, u32[]{:S(2)}) copy-start(bf16[1088,1088]{1,0:T(8,128)(2,1)} %param.30) | copy-start | bytes 7102468
  7.2 319.7 %all-gather.18.cloned.1.call-start = ((), (), s32[]{:S(2)}) async-start(), calls=%async_computation.8 | async-start | bytes 10340352 | tf_op jit(solution)/shard_map/all_gather | solution.py:277
  7.3 11.8 %copy-start.27 = (bf16[1088]{0:T(1024)(128)(2,1)S(1)}, bf16[1088]{0:T(1024)(128)(2,1)}, u32[]{:S(2)}) copy-start(bf16[1088]{0:T(1024)(128)(2,1)} %param.29) | copy-start | bytes 6532
  7.3 11.8 %copy-start.28 = (bf16[272]{0:T(512)(128)(2,1)S(1)}, bf16[272]{0:T(512)(128)(2,1)}, u32[]{:S(2)}) copy-start(bf16[272]{0:T(512)(128)(2,1)} %param.19) | copy-start | bytes 1636
  7.3 11.8 %copy-start.29 = (bf16[272]{0:T(512)(128)(2,1)S(1)}, bf16[272]{0:T(512)(128)(2,1)}, u32[]{:S(2)}) copy-start(bf16[272]{0:T(512)(128)(2,1)} %param.20) | copy-start | bytes 1636
  7.3 11.8 %copy-start.30 = (bf16[272]{0:T(512)(128)(2,1)S(1)}, bf16[272]{0:T(512)(128)(2,1)}, u32[]{:S(2)}) copy-start(bf16[272]{0:T(512)(128)(2,1)} %param.22) | copy-start | bytes 1636
  7.3 11.8 %copy-start.31 = (bf16[272]{0:T(512)(128)(2,1)S(1)}, bf16[272]{0:T(512)(128)(2,1)}, u32[]{:S(2)}) copy-start(bf16[272]{0:T(512)(128)(2,1)} %param.23) | copy-start | bytes 1636
  7.3 11.8 %copy-start.32 = (bf16[272]{0:T(512)(128)(2,1)S(1)}, bf16[272]{0:T(512)(128)(2,1)}, u32[]{:S(2)}) copy-start(bf16[272]{0:T(512)(128)(2,1)} %param.25) | copy-start | bytes 1636
  7.3 11.8 %copy-start.33 = (bf16[272]{0:T(512)(128)(2,1)S(1)}, bf16[272]{0:T(512)(128)(2,1)}, u32[]{:S(2)}) copy-start(bf16[272]{0:T(512)(128)(2,1)} %param.26) | copy-start | bytes 1636
  7.3 11.8 %copy-start.34 = (bf16[272]{0:T(512)(128)(2,1)S(1)}, bf16[272]{0:T(512)(128)(2,1)}, u32[]{:S(2)}) copy-start(bf16[272]{0:T(512)(128)(2,1)} %param.27) | copy-start | bytes 1636
  7.3 11.8 %copy-start.35 = (bf16[272]{0:T(512)(128)(2,1)S(1)}, bf16[272]{0:T(512)(128)(2,1)}, u32[]{:S(2)}) copy-start(bf16[272]{0:T(512)(128)(2,1)} %param.31) | copy-start | bytes 1636
  7.3 12.0 %copy-start.16 = (bf16[272,1088]{1,0:T(8,128)(2,1)S(1)}, bf16[272,1088]{1,0:T(8,128)(2,1)}, u32[]{:S(2)}) copy-start(bf16[272,1088]{1,0:T(8,128)(2,1)} %param.24) | copy-start | bytes 1775620
  19.0 316.3 %all-gather.16.cloned.1.call-start = ((), (), s32[]{:S(2)}) async-start(), calls=%async_computation.7 | async-start | bytes 10948608 | tf_op jit(solution)/shard_map/all_gather | solution.py:277
  32.9 416.2 %all-gather.20.cloned.1.call-start = ((), (), s32[]{:S(2)}) async-start(), calls=%async_computation.9 | async-start | bytes 10340352 | tf_op jit(solution)/shard_map/all_gather | solution.py:277
  33.8 632.3 %reduce-scatter.10.cloned.1.call-start = ((), (), s32[]{:S(2)}) async-start(), calls=%async_computation.10 | async-start | bytes 10340352
  33.9 24.3 %copy-start.26 = (s32[4]{0:T(128)S(1)}, s32[4]{0:T(128)}, u32[]{:S(2)}) copy-start(s32[4]{0:T(128)} %param.18) | copy-start | bytes 52
  36.7 18.7 %collective-permute-start.2 = (bf16[2,128,1088]{1,2,0:T(8,128)(2,1)S(1)}, bf16[2,128,1088]{1,2,0:T(8,128)(2,1)}, u32[]{:S(2)}, u32[]{:S(2)}) collective-permute-start(bf16[2,128,1088]{1,2,0:T(8,128)(2,1)S(1)} %get-tuple-element.51), channel_id=1, source_target_pairs={{0,3},{1,2},{2,1},{3,0},{4,7},{5,6},{6,5},{7,4},{8,11},{9,10},{10,... | collective-permute-start | bytes 1671176 | tf_op jit(solution)/shard_map/ppermute | solution.py:216
  39.2 97.8 %collective-permute-start = (bf16[2,128,1088]{1,2,0:T(8,128)(2,1)}, bf16[2,128,1088]{1,2,0:T(8,128)(2,1)}, u32[]{:S(2)}, u32[]{:S(2)}) collective-permute-start(bf16[2,128,1088]{1,2,0:T(8,128)(2,1)} %get-tuple-element.52), channel_id=1, source_target_pairs={{0,1},{1,0},{2,3},{3,2},{4,5},{5,4},{6,7},{7,6},{8,9},{9,8},{10,11... | collective-permute-start | bytes 1671176 | tf_op jit(solution)/shard_map/ppermute | solution.py:216
  39.9 102.6 %collective-permute-start.1 = (bf16[2,128,1088]{1,2,0:T(8,128)(2,1)}, bf16[2,128,1088]{1,2,0:T(8,128)(2,1)}, u32[]{:S(2)}, u32[]{:S(2)}) collective-permute-start(bf16[2,128,1088]{1,2,0:T(8,128)(2,1)} %get-tuple-element.54), channel_id=1, source_target_pairs={{0,2},{1,3},{2,0},{3,1},{4,6},{5,7},{6,4},{7,5},{8,10},{9,11},{10,... | collective-permute-start | bytes 1671176 | tf_op jit(solution)/shard_map/ppermute | solution.py:216
  41.3 106.8 %collective-permute-start.8 = (bf16[2,128,1088]{1,2,0:T(8,128)(2,1)}, bf16[2,128,1088]{1,2,0:T(8,128)(2,1)}, u32[]{:S(2)}, u32[]{:S(2)}) collective-permute-start(bf16[2,128,1088]{1,2,0:T(8,128)(2,1)} %get-tuple-element.43), channel_id=1, source_target_pairs={{0,3},{1,2},{2,1},{3,0},{4,7},{5,6},{6,5},{7,4},{8,11},{9,10},{10,... | collective-permute-start | bytes 1671176 | tf_op jit(solution)/shard_map/ppermute | solution.py:216
  42.7 110.9 %collective-permute-start.6 = (bf16[2,128,1088]{1,2,0:T(8,128)(2,1)}, bf16[2,128,1088]{1,2,0:T(8,128)(2,1)}, u32[]{:S(2)}, u32[]{:S(2)}) collective-permute-start(bf16[2,128,1088]{1,2,0:T(8,128)(2,1)} %get-tuple-element.44), channel_id=1, source_target_pairs={{0,1},{1,0},{2,3},{3,2},{4,5},{5,4},{6,7},{7,6},{8,9},{9,8},{10,11... | collective-permute-start | bytes 1671176 | tf_op jit(solution)/shard_map/ppermute | solution.py:216
  55.4 103.7 %collective-permute-start.7 = (bf16[2,128,1088]{1,2,0:T(8,128)(2,1)}, bf16[2,128,1088]{1,2,0:T(8,128)(2,1)}, u32[]{:S(2)}, u32[]{:S(2)}) collective-permute-start(bf16[2,128,1088]{1,2,0:T(8,128)(2,1)} %get-tuple-element.46), channel_id=1, source_target_pairs={{0,2},{1,3},{2,0},{3,1},{4,6},{5,7},{6,4},{7,5},{8,10},{9,11},{10,... | collective-permute-start | bytes 1671176 | tf_op jit(solution)/shard_map/ppermute | solution.py:216
  325.3 30.9 %copy-start.21 = (f32[2,4,128]{2,1,0:T(4,128)}, f32[2,4,128]{2,1,0:T(4,128)S(1)}, u32[]{:S(2)}) copy-start(f32[2,4,128]{2,1,0:T(4,128)S(1)} %broadcast_multiply_fusion.5) | copy-start | bytes 12292
  326.9 29.3 %copy-start.23 = (f32[2,4,128]{2,1,0:T(4,128)}, f32[2,4,128]{2,1,0:T(4,128)S(1)}, u32[]{:S(2)}) copy-start(f32[2,4,128]{2,1,0:T(4,128)S(1)} %add_rsqrt_fusion.1) | copy-start | bytes 12292
  344.7 10.1 copy-start.18
  355.9 9.1 copy-start.19
  383.3 39.4 %slice-start = ((s8[4456448]{0:T(1024)(128)(4,1)}), s8[262144]{0:T(1024)(128)(4,1)S(1)}, s32[]{:S(2)}) async-start(s8[4456448]{0:T(1024)(128)(4,1)} %bitcast.206), calls=%async_computation.12 | async-start | bytes 524288
  392.8 30.0 %slice-start.1 = ((s8[4456448]{0:T(1024)(128)(4,1)}), s8[4194304]{0:T(1024)(128)(4,1)S(1)}, s32[]{:S(2)}) async-start(s8[4456448]{0:T(1024)(128)(4,1)} %bitcast.206), calls=%async_computation.13 | async-start | bytes 8388608
  430.7 18.5 %copy-start.14 = (bf16[1024,1088,1]{0,1,2:T(8,128)(2,1)S(1)}, bf16[1024,1088,1]{0,1,2:T(8,128)(2,1)}, u32[]{:S(2)}) copy-start(bf16[1024,1088,1]{0,1,2:T(8,128)(2,1)} %reshape.333) | copy-start | bytes 6684676
  503.9 271.9 %reduce-scatter.12.cloned.1.call-start = ((), (), s32[]{:S(2)}) async-start(), calls=%async_computation.11 | async-start | bytes 10340352
  539.4 19.6 %copy-start.7 = (bf16[1024,1088]{0,1:T(8,128)(2,1)S(1)}, bf16[1024,1088]{0,1:T(8,128)(2,1)}, u32[]{:S(2)}) copy-start(bf16[1024,1088]{0,1:T(8,128)(2,1)} %reshape.305) | copy-start | bytes 6684676
  539.4 398.6 %reduce-scatter.8.cloned.1.call-start = ((), (), s32[]{:S(2)}) async-start(), calls=%async_computation.3 | async-start | bytes 10948608 | tf_op jit(solution)/shard_map/reduce_scatter | solution.py:337
  578.8 27.7 %copy-start.20 = (f32[1088]{0:T(1024)S(1)}, f32[1088]{0:T(1024)}, u32[]{:S(2)}) copy-start(f32[1088]{0:T(1024)} %copy-done.19) | copy-start | bytes 13060
  578.8 27.7 %copy-start.22 = (f32[2,4,128]{2,1,0:T(4,128)S(1)}, f32[2,4,128]{2,1,0:T(4,128)}, u32[]{:S(2)}) copy-start(f32[2,4,128]{2,1,0:T(4,128)} %copy-done.21) | copy-start | bytes 12292
  578.8 27.7 %copy-start.24 = (f32[2,4,128]{2,1,0:T(4,128)S(1)}, f32[2,4,128]{2,1,0:T(4,128)}, u32[]{:S(2)}) copy-start(f32[2,4,128]{2,1,0:T(4,128)} %copy-done.23) | copy-start | bytes 12292
  627.0 7.2 copy-start.13
  634.1 13.4 %copy-start.10 = (bf16[1088,1088]{1,0:T(8,128)(2,1)S(1)}, bf16[1088,1088]{1,0:T(8,128)(2,1)}, u32[]{:S(2)}) copy-start(bf16[1088,1088]{1,0:T(8,128)(2,1)} %convolution_convert_fusion.3) | copy-start | bytes 7102468
  666.1 302.7 %all-gather.12.cloned.1.call-start = ((), (), s32[]{:S(2)}) async-start(), calls=%async_computation.5 | async-start | bytes 2820096 | tf_op jit(solution)/shard_map/all_gather | solution.py:340
  666.8 333.5 %all-gather.14.cloned.1.call-start = ((), (), s32[]{:S(2)}) async-start(), calls=%async_computation.6 | async-start | bytes 2820096 | tf_op jit(solution)/shard_map/all_gather | solution.py:340
  775.8 256.7 %all-gather.10.cloned.1.call-start = ((), (), s32[]{:S(2)}) async-start(), calls=%async_computation.4 | async-start | bytes 2985984 | tf_op jit(solution)/shard_map/all_gather | solution.py:340
  827.5 112.1 %copy-start.9 = (bf16[2,1,128,1088]{2,1,0,3:T(2,128)(2,1)S(1)}, bf16[2,1,128,1088]{2,1,0,3:T(2,128)(2,1)}, u32[]{:S(2)}) copy-start(bf16[2,1,128,1088]{2,1,0,3:T(2,128)(2,1)} %get-tuple-element.73) | copy-start | bytes 1671172
  829.5 120.1 %collective-permute-start.5 = (bf16[2,128,1088]{1,2,0:T(8,128)(2,1)S(1)}, bf16[2,128,1088]{1,2,0:T(8,128)(2,1)}, u32[]{:S(2)}, u32[]{:S(2)}) collective-permute-start(bf16[2,128,1088]{1,2,0:T(8,128)(2,1)S(1)} %bitcast.231), channel_id=1, source_target_pairs={{0,3},{1,2},{2,1},{3,0},{4,7},{5,6},{6,5},{7,4},{8,11},{9,10},{10,... | collective-permute-start | bytes 1671176 | tf_op jit(solution)/shard_map/ppermute | solution.py:231
  829.6 118.2 %collective-permute-start.4 = (bf16[2,128,1088]{1,2,0:T(8,128)(2,1)S(1)}, bf16[2,128,1088]{1,2,0:T(8,128)(2,1)}, u32[]{:S(2)}, u32[]{:S(2)}) collective-permute-start(bf16[2,128,1088]{1,2,0:T(8,128)(2,1)S(1)} %bitcast.232), channel_id=1, source_target_pairs={{0,2},{1,3},{2,0},{3,1},{4,6},{5,7},{6,4},{7,5},{8,10},{9,11},{10,... | collective-permute-start | bytes 1671176 | tf_op jit(solution)/shard_map/ppermute | solution.py:231
  831.0 110.0 %collective-permute-start.9 = (bf16[2,128,1088]{1,2,0:T(8,128)(2,1)}, bf16[2,128,1088]{1,2,0:T(8,128)(2,1)}, u32[]{:S(2)}, u32[]{:S(2)}) collective-permute-start(bf16[2,128,1088]{1,2,0:T(8,128)(2,1)} %bitcast.186), channel_id=1, source_target_pairs={{0,1},{1,0},{2,3},{3,2},{4,5},{5,4},{6,7},{7,6},{8,9},{9,8},{10,11... | collective-permute-start | bytes 1671176 | tf_op jit(solution)/shard_map/ppermute | solution.py:231
  831.5 110.8 %collective-permute-start.10 = (bf16[2,128,1088]{1,2,0:T(8,128)(2,1)}, bf16[2,128,1088]{1,2,0:T(8,128)(2,1)}, u32[]{:S(2)}, u32[]{:S(2)}) collective-permute-start(bf16[2,128,1088]{1,2,0:T(8,128)(2,1)} %bitcast.185), channel_id=1, source_target_pairs={{0,2},{1,3},{2,0},{3,1},{4,6},{5,7},{6,4},{7,5},{8,10},{9,11},{10,... | collective-permute-start | bytes 1671176 | tf_op jit(solution)/shard_map/ppermute | solution.py:231
  832.8 110.6 %collective-permute-start.11 = (bf16[2,128,1088]{1,2,0:T(8,128)(2,1)}, bf16[2,128,1088]{1,2,0:T(8,128)(2,1)}, u32[]{:S(2)}, u32[]{:S(2)}) collective-permute-start(bf16[2,128,1088]{1,2,0:T(8,128)(2,1)} %bitcast.184), channel_id=1, source_target_pairs={{0,3},{1,2},{2,1},{3,0},{4,7},{5,6},{6,5},{7,4},{8,11},{9,10},{10,... | collective-permute-start | bytes 1671176 | tf_op jit(solution)/shard_map/ppermute | solution.py:231
  941.0 5.9 collective-permute-start.3
  1037.6 10.7 %copy-start.1 = (bf16[1088,1088]{1,0:T(8,128)(2,1)S(1)}, bf16[1088,1088]{1,0:T(8,128)(2,1)}, u32[]{:S(2)}) copy-start(bf16[1088,1088]{1,0:T(8,128)(2,1)} %param.30) | copy-start | bytes 7102468
  (12 other events, 39.8 us)
Sparse Core Ops, SparseCore 0:
  19.1 107.1 all-gather.17
  129.3 85.6 all-gather.15
  217.8 83.1 all-gather.19
  504.0 133.6 reduce-scatter.9
  643.6 132.0 reduce-scatter.11
  781.7 156.2 reduce-scatter.7
  939.9 28.8 all-gather.11
  970.6 29.6 all-gather.13
  1002.2 30.2 all-gather.9

commit v2 on v1

v2 whole, which is shorter than its diff:
```python
import functools

import jax
import jax.numpy as jnp
from jax import lax
from jax.experimental import pallas as pl
from jax.experimental.layout import Layout, with_layout_constraint
from jax.experimental.pallas import tpu as pltpu
from jax.sharding import PartitionSpec as P

HEAD_DIM = 64
EPSILON = 1e-05
LANES = 128
VMEM_LIMIT = 48 * 1024 * 1024

BF16 = jnp.bfloat16
F32 = jnp.float32


def dot_nn(left, right):
    return lax.dot_general(left, right, (((1,), (0,)), ((), ())), preferred_element_type=F32)


def dot_nt(left, right):
    return lax.dot_general(left, right, (((1,), (1,)), ((), ())), preferred_element_type=F32)


def dot_tn(left, right):
    return lax.dot_general(left, right, (((0,), (0,)), ((), ())), preferred_element_type=F32)


def head_lanes(shape, which):
    lane = lax.broadcasted_iota(jnp.int32, shape, 1)
    return (lane < HEAD_DIM) if which == 0 else (lane >= HEAD_DIM)


def only_valid(values, width):
    if width % LANES == 0:
        return values
    lane = lax.broadcasted_iota(jnp.int32, values.shape, 1) + pl.program_id(1) * LANES
    return jnp.where(lane < width, values, jnp.zeros_like(values))


def sorted_rows(ref, lead, order_ref, first, last):
    return jnp.concatenate([ref[lead + (order_ref[i], 0)] for i in range(first, last)], axis=0)


def store_rows(ref, lead, order_ref, first, rows):
    local = ref.shape[-2]
    for i in range(rows.shape[0] // local):
        ref[lead + (order_ref[first + i], 0)] = rows[i * local : (i + 1) * local]


def causal(rows, columns):
    key_at = lax.broadcasted_iota(jnp.int32, (rows, columns), 0)
    query_at = lax.broadcasted_iota(jnp.int32, (rows, columns), 1)
    return key_at <= query_at


def attention_forward_kernel(blocks, width, order_ref, q_ref, k_ref, v_ref, o_ref, lse_ref):
    count, local = k_ref.shape[1], k_ref.shape[3]
    tile = blocks * local
    keys = only_valid(sorted_rows(k_ref, (0,), order_ref, 0, count), width)
    values_t = sorted_rows(v_ref, (0,), order_ref, 0, count).astype(F32).T.astype(BF16)
    diagonal = causal(tile, tile)
    for first in range(0, count, blocks):
        start, stop = first * local, (first + blocks) * local
        queries = sorted_rows(q_ref, (0,), order_ref, first, first + blocks)
        queries = queries * jnp.asarray(HEAD_DIM**-0.5, BF16)
        pieces = []
        for which in range(2):
            masked_q = jnp.where(head_lanes(queries.shape, which), queries, jnp.zeros_like(queries))
            scores = dot_nt(keys[:stop], masked_q)
            tiles = []
            if start > 0:
                tiles.append(scores[:start])
            tiles.append(jnp.where(diagonal, scores[start:], -1e30))
            top = functools.reduce(
                jnp.maximum, [jnp.max(block, axis=0, keepdims=True) for block in tiles]
            )
            weights = [jnp.exp(block - top) for block in tiles]
            total = sum(jnp.sum(weight, axis=0, keepdims=True) for weight in weights)
            low = jnp.concatenate([weight.astype(BF16) for weight in weights], axis=0)
            rows = values_t[which * HEAD_DIM : (which + 1) * HEAD_DIM, :stop]
            pieces.append(dot_nn(rows, low) * (1.0 / total))
            lse_ref[0, 0, which : which + 1, start:stop] = top + jnp.log(total)
        mixed_t = jnp.concatenate(pieces, axis=0)
        store_rows(o_ref, (), order_ref, first, mixed_t.T.astype(BF16))


def attention_backward_kernel(
    blocks,
    width,
    order_ref,
    q_ref,
    k_ref,
    v_ref,
    o_ref,
    do_ref,
    lse_ref,
    out_ref,
    dk_acc,
    dv_acc,
):
    count, local = k_ref.shape[1], k_ref.shape[3]
    tile = blocks * local
    keys = only_valid(sorted_rows(k_ref, (0,), order_ref, 0, count), width)
    values = only_valid(sorted_rows(v_ref, (0,), order_ref, 0, count), width)
    keys_t = keys.astype(F32).T.astype(BF16)
    diagonal = causal(tile, tile)
    for first in range(0, count, blocks):
        start, stop = first * local, (first + blocks) * local
        queries = sorted_rows(q_ref, (0,), order_ref, first, first + blocks)
        queries = queries * jnp.asarray(HEAD_DIM**-0.5, BF16)
        grads = sorted_rows(do_ref, (), order_ref, first, first + blocks)
        mixed = sorted_rows(o_ref, (), order_ref, first, first + blocks)
        product_t = (grads.astype(F32) * mixed.astype(F32)).T
        key_lanes = head_lanes((stop, LANES), 0)
        dq_parts, dk_parts, dv_parts = [], [], []
        for which in range(2):
            mine = head_lanes(queries.shape, which)
            masked_q = jnp.where(mine, queries, jnp.zeros_like(queries))
            masked_g = jnp.where(mine, grads, jnp.zeros_like(grads))
            delta = jnp.sum(
                product_t[which * HEAD_DIM : (which + 1) * HEAD_DIM], axis=0, keepdims=True
            )
            lse = lse_ref[0, 0, which : which + 1, start:stop]
            scores = dot_nt(keys[:stop], masked_q)
            grad_weights = dot_nt(values[:stop], masked_g)
            weights = jnp.exp(scores - lse)
            if start > 0:
                weights = jnp.concatenate(
                    [weights[:start], jnp.where(diagonal, weights[start:], 0.0)], axis=0
                )
            else:
                weights = jnp.where(diagonal, weights, 0.0)
            low_scores = (weights * (grad_weights - delta)).astype(BF16)
            dv_parts.append(dot_nn(weights.astype(BF16), grads))
            dk_parts.append(dot_nn(low_scores, queries))
            dq_parts.append(
                dot_nn(keys_t[which * HEAD_DIM : (which + 1) * HEAD_DIM, :stop], low_scores)
            )
        dq_t = jnp.concatenate(dq_parts, axis=0) * (HEAD_DIM**-0.5)
        store_rows(out_ref, (0,), order_ref, first, dq_t.T.astype(BF16))
        dk = jnp.where(key_lanes, dk_parts[0], dk_parts[1])
        dv = jnp.where(key_lanes, dv_parts[0], dv_parts[1])
        if start > 0:
            dk_acc[:start] += dk[:start]
            dv_acc[:start] += dv[:start]
        dk_acc[start:stop] = dk[start:]
        dv_acc[start:stop] = dv[start:]
    store_rows(out_ref, (1,), order_ref, 0, dk_acc[...].astype(BF16))
    store_rows(out_ref, (2,), order_ref, 0, dv_acc[...].astype(BF16))


def query_blocks(count):
    return 2 if count % 2 == 0 else 1


def attention_forward(joined, order):
    _, count, seqs, local, width = joined.shape
    length = count * local
    pairs = pl.cdiv(width, LANES)
    spec = lambda which: pl.BlockSpec(
        (1, count, 1, local, LANES), lambda s, h, order: (which, 0, s, 0, h)
    )
    return pl.pallas_call(
        functools.partial(attention_forward_kernel, query_blocks(count), width),
        grid_spec=pltpu.PrefetchScalarGridSpec(
            num_scalar_prefetch=1,
            grid=(seqs, pairs),
            in_specs=[spec(0), spec(1), spec(2)],
            out_specs=[
                pl.BlockSpec((count, 1, local, LANES), lambda s, h, order: (0, s, 0, h)),
                pl.BlockSpec((1, 1, 8, length), lambda s, h, order: (s, h, 0, 0)),
            ],
        ),
        out_shape=[
            jax.ShapeDtypeStruct((count, seqs, local, width), BF16),
            jax.ShapeDtypeStruct((seqs, pairs, 8, length), F32),
        ],
        compiler_params=pltpu.CompilerParams(vmem_limit_bytes=VMEM_LIMIT),
        cost_estimate=pl.CostEstimate(
            flops=seqs * pairs * 16 * length * length * LANES,
            bytes_accessed=8 * seqs * length * width,
            transcendentals=seqs * pairs * 2 * length * length,
        ),
    )(order, joined, joined, joined)


def attention_backward(joined, mixed, grad_mixed, lse, order):
    _, count, seqs, local, width = joined.shape
    length = count * local
    pairs = pl.cdiv(width, LANES)
    spec = lambda which: pl.BlockSpec(
        (1, count, 1, local, LANES), lambda s, h, order: (which, 0, s, 0, h)
    )
    rows = pl.BlockSpec((count, 1, local, LANES), lambda s, h, order: (0, s, 0, h))
    return pl.pallas_call(
        functools.partial(attention_backward_kernel, query_blocks(count), width),
        grid_spec=pltpu.PrefetchScalarGridSpec(
            num_scalar_prefetch=1,
            grid=(seqs, pairs),
            in_specs=[
                spec(0),
                spec(1),
                spec(2),
                rows,
                rows,
                pl.BlockSpec((1, 1, 8, length), lambda s, h, order: (s, h, 0, 0)),
            ],
            out_specs=pl.BlockSpec(
                (3, count, 1, local, LANES), lambda s, h, order: (0, 0, s, 0, h)
            ),
            scratch_shapes=[pltpu.VMEM((length, LANES), F32), pltpu.VMEM((length, LANES), F32)],
        ),
        out_shape=jax.ShapeDtypeStruct(joined.shape, BF16),
        compiler_params=pltpu.CompilerParams(vmem_limit_bytes=VMEM_LIMIT),
        cost_estimate=pl.CostEstimate(
            flops=seqs * pairs * 20 * length * length * LANES,
            bytes_accessed=16 * seqs * length * width,
            transcendentals=seqs * pairs * 2 * length * length,
        ),
    )(order, joined, joined, joined, mixed, grad_mixed, lse)


def standardize(values):
    centred = values - jnp.mean(values, axis=-1, keepdims=True)
    inverse = lax.rsqrt(jnp.mean(centred * centred, axis=-1, keepdims=True) + EPSILON)
    return centred * inverse, inverse


def normalize_back(grad_out, standard, inverse, gain_vec):
    scaled = grad_out * gain_vec
    grad_in = inverse * (
        scaled
        - jnp.mean(scaled, axis=-1, keepdims=True)
        - standard * jnp.mean(scaled * standard, axis=-1, keepdims=True)
    )
    return grad_in, jnp.sum(grad_out * standard, axis=0), jnp.sum(grad_out, axis=0)


def row_major(values):
    return with_layout_constraint(values, Layout(major_to_minor=tuple(range(values.ndim))))


def swap(values, axis, offset):
    count = lax.axis_size(axis)
    return lax.ppermute(values, axis, [(index, index ^ offset) for index in range(count)])


def pick(bit, on_zero, on_one):
    return jnp.where(bit == 0, on_zero, on_one)


def to_sequences(values, count):
    seqs, local, width = values.shape
    own = lax.axis_index("ctx")
    parts = values.reshape(count, seqs // count, local, width)
    pieces = []
    for offset in range(count):
        piece = lax.dynamic_index_in_dim(parts, own ^ offset, keepdims=False)
        pieces.append(swap(piece, "ctx", offset) if offset else piece)
    return row_major(jnp.stack(pieces))


def to_blocks(values, kind):
    count, share, local, width = values.shape
    own = lax.axis_index("ctx")
    out = row_major(jnp.zeros((count, share, local, width), kind))
    for offset in range(count):
        piece = swap(values[offset], "ctx", offset) if offset else values[0]
        out = lax.dynamic_update_index_in_dim(out, piece.astype(kind), own ^ offset, 0)
    return row_major(out).reshape(count * share, local, width)


class Windows:
    def __init__(self, owned_rows):
        tiles = owned_rows // 16
        self.start = tiles // 2 * 16
        self.size = owned_rows - self.start
        ctx = lax.axis_index("ctx")
        self.core = ctx % 2
        self.y = ctx // 2
        self.x = lax.axis_index("replica")

    def rows(self, values):
        return pick(
            self.core, values[..., : self.size, :], values[..., self.start :, :]
        )

    def other_rows(self, values):
        return pick(
            self.core, values[..., self.start :, :], values[..., : self.size, :]
        )

    def block(self, blocks):
        return pick(
            self.x,
            pick(self.y, blocks[0], blocks[1]),
            pick(self.y, blocks[2], blocks[3]),
        )


def assemble_kernel(groups, start, size, here_ref, *refs):
    arrays, out_ref, sem = refs[:-2], refs[-2], refs[-1]
    x, y, core = here_ref[0], here_ref[1], here_ref[2]
    for turn in range(2):
        copies = []
        row = pl.multiple_of((core ^ turn) * start, 16)
        for (places, first), ref in zip(groups, arrays[turn * len(groups) :]):
            for i, (dx, dy) in enumerate(places):
                for s in range(ref.shape[1]):
                    copies.append(
                        pltpu.make_async_copy(
                            ref.at[i, s, pl.ds(0, size), :],
                            out_ref.at[
                                2 * (x ^ dx) + (y ^ dy), first + s, pl.ds(row, size), :
                            ],
                            sem.at[len(copies)],
                        )
                    )
        for copy in copies:
            copy.start()
        for copy in copies:
            copy.wait()


def assemble(win, groups, own, other, owned_rows, shards):
    width = own[0].shape[-1]
    here = jnp.stack([win.x, win.y, win.core]).astype(jnp.int32)
    most = sum(len(places) * array.shape[1] for (places, _), array in zip(groups, own))
    return pl.pallas_call(
        functools.partial(assemble_kernel, groups, win.start, win.size),
        in_specs=[pl.BlockSpec(memory_space=pltpu.SMEM)]
        + [pl.BlockSpec(memory_space=pl.ANY)] * (2 * len(groups)),
        out_specs=pl.BlockSpec(memory_space=pl.ANY),
        out_shape=jax.ShapeDtypeStruct((4, shards, owned_rows, width), BF16),
        scratch_shapes=[pltpu.SemaphoreType.DMA((most,))],
        cost_estimate=pl.CostEstimate(
            flops=0, bytes_accessed=16 * shards * owned_rows * width, transcendentals=0
        ),
    )(here, *own, *other)


def spread_weights(win, mine, owned_rows):
    shards = mine.shape[0]
    if shards % 2:
        first = jnp.stack([mine, swap(mine, "replica", 1)])
        own = [first, swap(first, "ctx", 2)]
        groups = ((((0, 0), (1, 0)), 0), (((0, 1), (1, 1)), 0))
    else:
        half = shards // 2
        low, high = mine[:half], mine[half:]
        first = jnp.stack([low, swap(low, "replica", 1)])
        second = jnp.stack([high, swap(high, "ctx", 2)])
        own = [first, second, swap(first, "ctx", 2), swap(second, "replica", 1)]
        groups = (
            (((0, 0), (1, 0)), 0),
            (((0, 0), (0, 1)), half),
            (((0, 1), (1, 1)), 0),
            (((1, 0), (1, 1)), half),
        )
    other = [swap(array, "ctx", 1) for array in own]
    return assemble(win, groups, own, other, owned_rows, shards)


def add_pair(kept, received):
    return (kept.astype(F32) + received.astype(F32)).astype(BF16)


def reduce_blocks(win, grads):
    shards = grads.shape[1]
    half = shards // 2
    both = add_pair(win.rows(grads), swap(win.other_rows(grads), "ctx", 1))
    x_kept = pick(win.x, both[:2, :half], both[2:, :half])
    x_sent = pick(win.x, both[2:, :half], both[:2, :half])
    y_kept = pick(win.y, both[0::2, half:], both[1::2, half:])
    y_sent = pick(win.y, both[1::2, half:], both[0::2, half:])
    low = add_pair(x_kept, swap(x_sent, "replica", 1))
    high = add_pair(y_kept, swap(y_sent, "ctx", 2))
    low_sum = add_pair(
        pick(win.y, low[0], low[1]), swap(pick(win.y, low[1], low[0]), "ctx", 2)
    )
    high_sum = add_pair(
        pick(win.x, high[0], high[1]), swap(pick(win.x, high[1], high[0]), "replica", 1)
    )
    return jnp.concatenate([low_sum, high_sum], axis=0)


def reduce_vectors(values):
    values = add_pair(values, swap(values, "ctx", 1))
    values = add_pair(values, swap(values, "replica", 1))
    return add_pair(values, swap(values, "ctx", 2))


def per_device(
    tokens,
    cotangent,
    block_order,
    ln1_gain,
    ln1_bias,
    qkv_weight,
    q_bias,
    v_bias,
    out_weight,
    out_bias,
    ln2_gain,
    ln2_bias,
    fc_weight,
    fc_bias,
    proj_weight,
    proj_bias,
):
    seq_count, local_len, width = tokens.shape
    owned_rows = ln1_gain.shape[0]
    shards = width // owned_rows
    wide = fc_weight.shape[1] // width
    count = lax.axis_size("ctx")
    rows = seq_count * local_len
    pairwise = lax.axis_size("replica") == 2 and count == 4 and shards % 2 == 0
    win = Windows(owned_rows)

    vectors = jnp.concatenate(
        [ln1_gain, ln1_bias, q_bias, v_bias, out_bias, ln2_gain, ln2_bias, proj_bias, fc_bias]
    )
    vector_rows = vectors.shape[0] // width
    vector_tile = jnp.pad(vectors.reshape(vector_rows, width), ((0, -vector_rows % 16), (0, 0)))
    column = lambda values, i: values[:, i * width : (i + 1) * width]
    blocks_a = [column(qkv_weight, i) for i in range(3)] + [out_weight]
    blocks_b = [column(fc_weight, i) for i in range(wide)]
    blocks_c = [proj_weight[i * owned_rows : (i + 1) * owned_rows] for i in range(wide)]

    def gather_z(values):
        return lax.all_gather(values, "shard", axis=0, tiled=False)

    if pairwise:
        mine = [win.rows(win.block(blocks)) for blocks in (blocks_a, blocks_b, blocks_c)]
        part_a = gather_z(jnp.concatenate([mine[0], vector_tile], axis=0))
        part_b, part_c = gather_z(mine[1]), gather_z(mine[2])
        vector_part = part_a[:, win.size : win.size + vector_rows]
        full_a = spread_weights(win, part_a[:, : win.size], owned_rows)
        full_b = spread_weights(win, part_b, owned_rows)
        full_c = spread_weights(win, part_c, owned_rows)
    else:
        vector_part = gather_z(vector_tile)[:, :vector_rows]
        full_a, full_b, full_c = [
            gather_z(jnp.stack(blocks)).transpose(1, 0, 2, 3)
            for blocks in (blocks_a, blocks_b, blocks_c)
        ]
    matrices_a = full_a.reshape(4, width, width)
    w_qkv, w_out = matrices_a[:3], matrices_a[3]
    w_fc = full_b.reshape(wide, width, width)
    w_proj = full_c.transpose(1, 0, 2, 3).reshape(wide, width, width)
    vector_part = vector_part.reshape(shards, vector_rows * width).astype(F32)
    small = vector_part[:, : 8 * owned_rows].reshape(shards, 8, owned_rows)
    small = small.transpose(1, 0, 2).reshape(8, width)
    g_one, b_one, bias_q, bias_v, bias_out, g_two, b_two, bias_proj = [small[i] for i in range(8)]
    bias_fc = vector_part[:, 8 * owned_rows :].reshape(wide, 1, width)

    low_inputs = to_sequences(tokens, count).reshape(rows, width)
    low_grad_out = to_sequences(cotangent, count).reshape(rows, width)
    share = seq_count // count
    blocked = (count, share, local_len, width)
    index = jnp.arange(count, dtype=jnp.int32)
    held_by = jnp.sum(jnp.where(block_order[None, :] == index[:, None], index[None, :], 0), axis=1)
    order = (held_by ^ lax.axis_index("ctx")).astype(jnp.int32)

    inputs = low_inputs.astype(F32)
    standard_one, inverse_one = standardize(inputs)
    low_one = (standard_one * g_one + b_one).astype(BF16)
    joined = jnp.einsum("td,cdx->ctx", low_one, w_qkv, preferred_element_type=F32)
    bias_qkv = jnp.stack([bias_q, jnp.zeros_like(bias_q), bias_v])[:, None]
    joined = (joined + bias_qkv).astype(BF16).reshape((3,) + blocked)
    mixed, lse = attention_forward(joined, order)
    attended = mixed.reshape(rows, width)
    middle = inputs + (dot_nn(attended, w_out) + bias_out)
    standard_two, inverse_two = standardize(middle)
    low_two = (standard_two * g_two + b_two).astype(BF16)
    hidden = jnp.einsum("td,cdx->ctx", low_two, w_fc, preferred_element_type=F32) + bias_fc
    activated, gelu_pull = jax.vjp(lambda pre_act: jax.nn.gelu(pre_act, approximate=True), hidden)
    low_act = activated.astype(BF16)
    outputs = middle + (
        jnp.einsum("ctx,cxd->td", low_act, w_proj, preferred_element_type=F32) + bias_proj
    )
    layer_out = to_blocks(row_major(outputs.astype(BF16).reshape(blocked)), BF16)

    def reduce_units(grads, extra=None):
        if pairwise:
            sums = reduce_blocks(win, grads)
            if extra is not None:
                sums = jnp.concatenate([sums, reduce_vectors(extra)], axis=1)
            sums = lax.psum_scatter(sums, "shard", scatter_dimension=0, tiled=False)
            full = spread_weights(win, sums[None, : win.size], owned_rows)[:, 0]
            return full, sums[win.size :]
        rest = ("replica", "ctx")
        full = lax.psum_scatter(grads, "shard", scatter_dimension=1, tiled=False)
        full = lax.psum(full, rest)
        if extra is not None:
            extra = lax.psum_scatter(extra, "shard", scatter_dimension=0, tiled=False)
            extra = lax.psum(extra, rest)
        return full, extra

    def by_shard(grads):
        return grads.astype(BF16).reshape(4, shards, owned_rows, width)

    grad_out = low_grad_out.astype(F32)
    grad_proj = jnp.einsum("ctx,td->cxd", low_act, low_grad_out, preferred_element_type=F32)
    owned_proj, _ = reduce_units(by_shard(grad_proj).transpose(1, 0, 2, 3))
    grad_proj_bias = jnp.sum(grad_out, axis=0)
    grad_act = jnp.einsum("td,cxd->ctx", low_grad_out, w_proj, preferred_element_type=F32)
    grad_hidden = gelu_pull(grad_act)[0].astype(BF16)
    grad_fc = jnp.einsum("td,ctx->cdx", low_two, grad_hidden, preferred_element_type=F32)
    owned_fc, _ = reduce_units(by_shard(grad_fc))
    grad_fc_bias = jnp.sum(grad_hidden.astype(F32), axis=1)
    grad_two = jnp.einsum("ctx,cdx->td", grad_hidden, w_fc, preferred_element_type=F32)
    grad_norm_two, grad_g_two, grad_b_two = normalize_back(
        grad_two, standard_two, inverse_two, g_two
    )
    grad_middle = grad_out + grad_norm_two
    low_grad_middle = grad_middle.astype(BF16)
    grad_out_weight = dot_tn(attended, low_grad_middle)
    grad_out_bias = jnp.sum(low_grad_middle.astype(F32), axis=0)
    grad_attended = dot_nt(low_grad_middle, w_out).astype(BF16)
    grad_joined = attention_backward(
        joined, mixed, grad_attended.reshape(blocked), lse, order
    ).reshape(3, rows, width)
    grad_qkv = jnp.einsum("td,ctx->cdx", low_one, grad_joined, preferred_element_type=F32)
    grads_a = jnp.concatenate([grad_qkv.astype(BF16), grad_out_weight.astype(BF16)[None]], axis=0)
    grad_q_bias = jnp.sum(grad_joined[0].astype(F32), axis=0)
    grad_v_bias = jnp.sum(grad_joined[2].astype(F32), axis=0)
    grad_one = jnp.einsum("ctx,cdx->td", grad_joined, w_qkv, preferred_element_type=F32)
    grad_norm_one, grad_g_one, grad_b_one = normalize_back(
        grad_one, standard_one, inverse_one, g_one
    )
    input_grad = to_blocks(
        row_major((grad_middle + grad_norm_one).astype(BF16).reshape(blocked)), F32
    )

    small_grads = jnp.stack(
        [
            grad_g_one,
            grad_b_one,
            grad_q_bias,
            grad_v_bias,
            grad_out_bias,
            grad_g_two,
            grad_b_two,
            grad_proj_bias,
        ]
    )
    vector_grads = jnp.concatenate(
        [
            small_grads.reshape(8, shards, owned_rows)
            .transpose(1, 0, 2)
            .reshape(shards, 8 * owned_rows),
            grad_fc_bias.reshape(shards, owned_rows * wide),
        ],
        axis=1,
    ).astype(BF16)
    vector_grads = jnp.pad(
        vector_grads.reshape(shards, vector_rows, width),
        ((0, 0), (0, -vector_rows % 16), (0, 0)),
    )
    owned_a, owned_vectors = reduce_units(by_shard(grads_a), vector_grads)
    owned_vectors = owned_vectors[:vector_rows].reshape(-1).astype(F32)
    vec = [owned_vectors[i * owned_rows : (i + 1) * owned_rows] for i in range(8)]
    qkv_grad = jnp.concatenate([owned_a[i] for i in range(3)], axis=1).astype(F32)
    fc_grad = jnp.concatenate([owned_fc[i] for i in range(wide)], axis=1).astype(F32)
    return (
        layer_out,
        input_grad,
        vec[0],
        vec[1],
        qkv_grad,
        vec[2],
        vec[3],
        owned_a[3].astype(F32),
        vec[4],
        vec[5],
        vec[6],
        fc_grad,
        owned_vectors[8 * owned_rows :],
        owned_proj.reshape(wide * owned_rows, width).astype(F32),
        vec[7],
    )


def solution(mesh):
    vector, matrix = P("shard"), P("shard", None)
    rows = P(("shard", "replica"), "ctx", None)
    weights = (
        vector,
        vector,
        matrix,
        vector,
        vector,
        matrix,
        vector,
        vector,
        vector,
        matrix,
        vector,
        matrix,
        vector,
    )
    return jax.shard_map(
        per_device,
        mesh=mesh,
        in_specs=(rows, rows, P()) + weights,
        out_specs=(rows, rows) + weights,
        check_vma=False,
    )
```

time: 1080 us -> 2100 us (1.94)
  Pallas kernels: 57.7 us -> 1280 us
  local copies, waits for them, and re-layouts: 414 us -> 155 us
  other arithmetic: 71.7 us -> 123 us
  starting transfers between devices: 11.9 us -> 46.7 us
    pallas_call x2 -> x8, Pallas kernels: 57.7 us -> 1280 us  [the longest x6 1220 us: assemble(): pl.pallas_call(functools.partial(assemble_kernel, groups, win.start, win....]
    ppermute x12 -> x66, waiting for transfers between devices: 11.9 us -> 224 us  [swap(): lax.ppermute(values, axis, [(index, index ^ offset) for index in range(co...]
    dynamic_update_slice x16 -> x3, local copies, waits for them, and re-layouts: 211 us -> 1.36 us  [to_blocks(): lax.dynamic_update_index_in_dim(out, piece.astype(kind), own ^ offset, 0)]
    unnamed x11 -> x6, waiting for transfers between devices: 110 us -> 0.1 us
    reduce_scatter x1 -> x3, waiting for transfers between devices: 105 us -> 18.1 us  [reduce_units(): sums = lax.psum_scatter(sums, 'shard', scatter_dimension=0, tiled=False)]
    broadcast_in_dim x9 -> x2, local copies, waits for them, and re-layouts: 46.7 us -> 2.85 us  [to_blocks(): out = row_major(jnp.zeros((count, share, local, width), kind))]
    ppermute x12 -> x66, starting transfers between devices: 11.5 us -> 46.2 us  [swap(): lax.ppermute(values, axis, [(index, index ^ offset) for index in range(co...]
    convert_element_type x7 -> x22, other arithmetic: 15.6 us -> 47.3 us  [the longest x15 29.7 us: add_pair(): return (kept.astype(F32) + received.astype(F32)).astype(BF16)]
  transfers between devices with their start and end apart: 21 -> 72, of which waited for: 6 -> 28; matrix products, arithmetic and copies ran while one was open for 55% -> 12% of each run, Pallas kernels for 5% -> 39%
where the time goes in v2:
time: 2100 us; the launch traced here: 2080 us
  Pallas kernels  1280 us (61%)
  waiting for transfers between devices  284 us (14%)
  matrix products  176 us (8%)
  local copies, waits for them, and re-layouts  155 us (7%)
  other arithmetic  123 us (6%)
  starting transfers between devices  46.7 us (2%)
    pallas_call x6, Pallas kernels, assemble(): pl.pallas_call(functools.partial(assemble_kernel, groups, win.start, win....  1220 us
    ppermute x66, waiting for transfers between devices, swap(): lax.ppermute(values, axis, [(index, index ^ offset) for index in range(co...  224 us
    ppermute x66, starting transfers between devices, swap(): lax.ppermute(values, axis, [(index, index ^ offset) for index in range(co...  46.2 us
  transfers between devices with their start and end apart: 72, of which 28 were waited for; matrix products, arithmetic and copies ran while one was open for 12% of the time, Pallas kernels for 39%

profile of v2, /device:TPU:0, one launch (start us, length us, event | category | flops | bytes accessed | tf_op | source)
XLA Modules:
  0.0 2083.3 jit_solution(13732438936891681652)
XLA Ops:
  34.9 11.0 all-gather.11.cloned.1.call-done
  54.5 25.0 %all-gather.9.cloned.1.call-done = bf16[576,1088]{1,0:T(8,128)(2,1)} async-done(((bf16[144,1088]{1,0:T(8,128)(2,1)}), bf16[576,1088]{1,0:T(8,128)(2,1)}) %all-gather.9.cloned.1.call-update) | async-done | bytes 1253392 | tf_op jit(solution)/shard_map/all_gather | solution.py:435
  90.7 5.4 collective-permute-done.32
  97.6 10.5 collective-permute-done.31
  109.9 5.7 all-gather.7.cloned.1.call-done
  132.2 22.1 %collective-permute-done.3 = bf16[2,144,1088]{2,1,0:T(8,128)(2,1)} collective-permute-done((bf16[2,144,1088]{2,1,0:T(8,128)(2,1)}, bf16[2,144,1088]{2,1,0:T(8,128)(2,1)}, u32[]{:S(2)}, u32[]{:S(2)}) %collective-permute-start.3) | collective-permute-done | bytes 626720 | tf_op jit(solution)/shard_map/ppermute | solution.py:249
  154.2 10.8 collective-permute-done.4
  169.6 6.0 copy.184
  200.7 25.3 %collective-permute-done.5.refs_2_ = bf16[2,2,144,1088]{3,2,1,0:T(8,128)(2,1)} collective-permute-done((bf16[2,2,144,1088]{3,2,1,0:T(8,128)(2,1)}, bf16[2,2,144,1088]{3,2,1,0:T(8,128)(2,1)}, u32[]{:S(2)}, u32[]{:S(2)}) %collective-permute-start.5) | collective-permute-done | bytes 1253408 | tf_op jit(solution)/shard_map/ppermute | solution.py:249
  232.2 324.6 %shard_map.274 = bf16[4,4,272,1088]{3,2,1,0:T(8,128)(2,1)} custom-call(s32[3]{0:T(128)} %pad_add_fusion.here_ref, bf16[2,2,144,1088]{3,2,1,0:T(8,128)(2,1)} %pad_maximum_fusion.8.refs_0_, bf16[2,2,144,1088]{3,2,1,0:T(8,128)(2,1)} %pad_maximum_fusion.9.refs_1_, bf16[2,2,144,1088]{3,2,1,0:T(8,128)(2,1)} %collective-permute-done.21.refs_2_, ...), custom_call_target="tpu_custom_call" | custom-call | bytes 18939904 | tf_op jit(solution)/shard_map/pallas_call | solution.py:333
  556.9 8.4 copy.186
  565.3 324.6 %shard_map.273 = bf16[4,4,272,1088]{3,2,1,0:T(8,128)(2,1)} custom-call(s32[3]{0:T(128)} %pad_add_fusion.here_ref, bf16[2,2,144,1088]{3,2,1,0:T(8,128)(2,1)} %pad_maximum_fusion.6.refs_0_, bf16[2,2,144,1088]{3,2,1,0:T(8,128)(2,1)} %pad_maximum_fusion.7.refs_1_, bf16[2,2,144,1088]{3,2,1,0:T(8,128)(2,1)} %collective-permute-done.13.refs_2_, ...), custom_call_target="tpu_custom_call" | custom-call | bytes 18939904 | tf_op jit(solution)/shard_map/pallas_call | solution.py:333
  890.0 324.6 %shard_map.271 = bf16[4,4,272,1088]{3,2,1,0:T(8,128)(2,1)} custom-call(s32[3]{0:T(128)} %pad_add_fusion.here_ref, bf16[2,2,144,1088]{3,2,1,0:T(8,128)(2,1)} %pad_maximum_fusion.4.refs_0_, bf16[2,2,144,1088]{3,2,1,0:T(8,128)(2,1)} %pad_maximum_fusion.5.refs_1_, bf16[2,2,144,1088]{3,2,1,0:T(8,128)(2,1)} %collective-permute-done.5.refs_2_, ...), custom_call_target="tpu_custom_call" | custom-call | bytes 18939904 | tf_op jit(solution)/shard_map/pallas_call | solution.py:333
  1223.5 11.3 fusion.12
  1234.8 9.4 copy.183
  1244.2 30.5 %shard_map.272 = (bf16[4,2,128,1088]{3,2,1,0:T(8,128)(2,1)S(1)}, f32[2,9,8,512]{3,2,1,0:T(8,128)S(1)}) custom-call(s32[4]{0:T(128)S(1)} %broadcast_xor_fusion.order_ref, bf16[3,4,2,128,1088]{4,3,2,1,0:T(8,128)(2,1)} %bitcast.304, bf16[3,4,2,128,1088]{4,3,2,1,0:T(8,128)(2,1)} %bitcast.305, bf16[3,4,2,128,1088]{4,3,2,1,0:T(8,128)(2,1)} %bitcast.306), custom_call_target="tpu_custom_call" | custom-call | flops 9663676416 | bytes 8912896 | tf_op jit(solution)/shard_map/pallas_call | solution.py:167
  1274.8 6.3 fusion.43
  1281.9 19.9 convolution_add_fusion
  1301.8 24.3 %fusion.44 = (bf16[4,1088]{1,0:T(4,128)(2,1)}, bf16[4,1024,1088]{1,2,0:T(8,128)(2,1)}) fusion(f32[4,1088,1024]{2,1,0:T(8,128)} %convolution_add_fusion, bf16[4,1088,1088]{2,1,0:T(8,128)(2,1)} %bitcast.287, bf16[1024,1088,1]{1,0,2:T(8,128)(2,1)S(1)} %bitcast.298), kind=kOutput, calls=%fused_computation.199 | convolution fusion | flops 9790812160 | bytes 38445568 | tf_op jit(solution)/shard_map/td,cxd->ctx/dot_general | solution.py:511
  1326.1 18.1 fusion.16
  1360.0 29.1 %shard_map.275 = bf16[3,4,2,128,1088]{4,3,2,1,0:T(8,128)(2,1)} custom-call(s32[4]{0:T(128)S(1)} %broadcast_xor_fusion.order_ref, bf16[3,4,2,128,1088]{4,3,2,1,0:T(8,128)(2,1)} %bitcast.307, bf16[3,4,2,128,1088]{4,3,2,1,0:T(8,128)(2,1)} %bitcast.308, bf16[3,4,2,128,1088]{4,3,2,1,0:T(8,128)(2,1)} %bitcast.309, bf16[4,2,128,1088]{3,2,1,0:T(8,128)(2,1)S(1)} %copy-done.1, ...), custom_call_target="tpu_custom_call" | custom-call | flops 12079595520 | bytes 17825792 | tf_op jit(solution)/shard_map/pallas_call | solution.py:199
  1392.6 13.8 fusion.11
  1406.3 16.9 convolution_convert_fusion.1
  1423.2 21.6 %convolution_convert_fusion = bf16[4,1088,1088]{2,1,0:T(8,128)(2,1)} fusion(bf16[1024,1088,1]{1,0,2:T(8,128)(2,1)S(1)} %bitcast.299, f32[4,1088,1024]{2,1,0:T(8,128)} %convolution_add_fusion), kind=kOutput, calls=%fused_computation | convolution fusion | flops 9742073856 | bytes 29523968 | tf_op jit(solution)/shard_map/ctx,td->cxd/dot_general | solution.py:508
  1444.9 19.0 fusion.18
  1472.0 15.7 fusion.15
  1489.3 7.5 broadcast_select_fusion.1
  1502.4 5.6 add_convert_fusion.5
  1508.0 8.5 copy.233
  1516.6 7.0 broadcast_select_fusion
  1544.6 7.1 add_convert_fusion.2
  1568.0 17.0 collective-permute-done.49
  1585.9 11.2 collective-permute-done.51
  1600.8 14.7 collective-permute-done.58
  1616.3 11.2 collective-permute-done.60
  1631.8 10.9 collective-permute-done.50
  1645.2 14.9 collective-permute-done.37
  1661.1 11.1 collective-permute-done.39
  1672.9 5.8 add_convert_fusion.12
  1680.3 7.0 collective-permute-done.59
  1691.1 9.4 collective-permute-done.40
  1735.9 18.1 reduce-scatter.4.cloned.1.call-done
  1763.2 6.0 copy.218
  1780.0 11.5 collective-permute-done.54.refs_1_
  1792.0 12.2 collective-permute-done.45.refs_1_
  1804.2 83.3 %shard_map.278 = bf16[4,1,272,1088]{3,2,1,0:T(8,128)(2,1)} custom-call(s32[3]{0:T(128)} %pad_add_fusion.here_ref, bf16[2,1,144,1088]{3,2,1,0:T(8,128)(2,1)} %pad_maximum_fusion.14.refs_0_, bf16[2,1,144,1088]{3,2,1,0:T(8,128)(2,1)} %collective-permute-done.63.refs_1_, bf16[2,1,144,1088]{3,2,1,0:T(8,128)(2,1)} %copy-done.29, ...), custom_call_target="tpu_custom_call" | custom-call | bytes 4734976 | tf_op jit(solution)/shard_map/pallas_call | solution.py:333
  1891.9 83.3 %shard_map.277 = bf16[4,1,272,1088]{3,2,1,0:T(8,128)(2,1)} custom-call(s32[3]{0:T(128)} %pad_add_fusion.here_ref, bf16[2,1,144,1088]{3,2,1,0:T(8,128)(2,1)} %copy-done.19, bf16[2,1,144,1088]{3,2,1,0:T(8,128)(2,1)} %copy-done.28, bf16[2,1,144,1088]{3,2,1,0:T(8,128)(2,1)} %collective-permute-done.55.refs_2_, ...), custom_call_target="tpu_custom_call" | custom-call | bytes 4734976 | tf_op jit(solution)/shard_map/pallas_call | solution.py:333
  1984.9 83.3 %shard_map.276 = bf16[4,1,272,1088]{3,2,1,0:T(8,128)(2,1)} custom-call(s32[3]{0:T(128)} %pad_add_fusion.here_ref, bf16[2,1,144,1088]{3,2,1,0:T(8,128)(2,1)} %copy-done.17, bf16[2,1,144,1088]{3,2,1,0:T(8,128)(2,1)} %collective-permute-done.45.refs_1_, bf16[2,1,144,1088]{3,2,1,0:T(8,128)(2,1)} %collective-permute-done.46.refs_2_, ...), custom_call_target="tpu_custom_call" | custom-call | bytes 4734976 | tf_op jit(solution)/shard_map/pallas_call | solution.py:333
  (427 shorter events, 280.6 us)
Async XLA Ops:
  7.2 38.8 %all-gather.11.cloned.1.call-start = ((), (), s32[]{:S(2)}) async-start(), calls=%async_computation.8 | async-start | bytes 1658880 | tf_op jit(solution)/shard_map/all_gather | solution.py:435
  10.1 69.4 %all-gather.9.cloned.1.call-start = ((), (), s32[]{:S(2)}) async-start(), calls=%async_computation.7 | async-start | bytes 1658880 | tf_op jit(solution)/shard_map/all_gather | solution.py:435
  11.4 104.1 %all-gather.7.cloned.1.call-start = ((), (), s32[]{:S(2)}) async-start(), calls=%async_computation.6 | async-start | bytes 1843200 | tf_op jit(solution)/shard_map/all_gather | solution.py:435
  14.4 1719.4 %reduce-scatter.6.cloned.1.call-start = ((), (), s32[]{:S(2)}) async-start(), calls=%async_computation.4 | async-start | bytes 1658880 | tf_op jit(solution)/shard_map/reduce_scatter | solution.py:493
  27.5 53.4 %collective-permute-start.2 = (bf16[2,128,1088]{1,2,0:T(8,128)(2,1)}, bf16[2,128,1088]{1,2,0:T(8,128)(2,1)}, u32[]{:S(2)}, u32[]{:S(2)}) collective-permute-start(bf16[2,128,1088]{1,2,0:T(8,128)(2,1)} %bitcast.5), channel_id=1, source_target_pairs={{0,3},{1,2},{2,1},{3,0},{4,7},{5,6},{6,5},{7,4},{8,11},{9,10},{10,... | collective-permute-start | bytes 1671176 | tf_op jit(solution)/shard_map/ppermute | solution.py:249
  32.1 55.7 %collective-permute-start.1 = (bf16[2,128,1088]{1,2,0:T(8,128)(2,1)}, bf16[2,128,1088]{1,2,0:T(8,128)(2,1)}, u32[]{:S(2)}, u32[]{:S(2)}) collective-permute-start(bf16[2,128,1088]{1,2,0:T(8,128)(2,1)} %bitcast.3), channel_id=1, source_target_pairs={{0,2},{1,3},{2,0},{3,1},{4,6},{5,7},{6,4},{7,5},{8,10},{9,11},{10,... | collective-permute-start | bytes 1671176 | tf_op jit(solution)/shard_map/ppermute | solution.py:249
  34.8 54.4 %collective-permute-start = (bf16[2,128,1088]{1,2,0:T(8,128)(2,1)}, bf16[2,128,1088]{1,2,0:T(8,128)(2,1)}, u32[]{:S(2)}, u32[]{:S(2)}) collective-permute-start(bf16[2,128,1088]{1,2,0:T(8,128)(2,1)} %bitcast.1), channel_id=1, source_target_pairs={{0,1},{1,0},{2,3},{3,2},{4,5},{5,4},{6,7},{7,6},{8,9},{9,8},{10,11... | collective-permute-start | bytes 1671176 | tf_op jit(solution)/shard_map/ppermute | solution.py:249
  48.2 33.1 %collective-permute-start.19 = (bf16[2,144,1088]{2,1,0:T(8,128)(2,1)}, bf16[2,144,1088]{2,1,0:T(8,128)(2,1)}, u32[]{:S(2)}, u32[]{:S(2)}) collective-permute-start(bf16[2,144,1088]{2,1,0:T(8,128)(2,1)} %bitcast.34), channel_id=1, source_target_pairs={{0,4},{4,0},{1,5},{5,1},{2,6},{6,2},{3,7},{7,3},{8,12},{12,8},{9,1... | collective-permute-start | bytes 1880072 | tf_op jit(solution)/shard_map/ppermute | solution.py:249
  49.7 32.9 %collective-permute-start.20 = (bf16[2,144,1088]{2,1,0:T(8,128)(2,1)S(1)}, bf16[2,144,1088]{2,1,0:T(8,128)(2,1)}, u32[]{:S(2)}, u32[]{:S(2)}) collective-permute-start(bf16[2,144,1088]{2,1,0:T(8,128)(2,1)S(1)} %bitcast.315), channel_id=1, source_target_pairs={{0,2},{1,3},{2,0},{3,1},{4,6},{5,7},{6,4},{7,5},{8,10},{9,11},{10,... | collective-permute-start | bytes 1880072 | tf_op jit(solution)/shard_map/ppermute | solution.py:249
  87.7 30.7 %collective-permute-start.11 = (bf16[2,144,1088]{2,1,0:T(8,128)(2,1)S(1)}, bf16[2,144,1088]{2,1,0:T(8,128)(2,1)S(1)}, u32[]{:S(2)}, u32[]{:S(2)}) collective-permute-start(bf16[2,144,1088]{2,1,0:T(8,128)(2,1)S(1)} %bitcast.313), channel_id=1, source_target_pairs={{0,4},{4,0},{1,5},{5,1},{2,6},{6,2},{3,7},{7,3},{8,12},{12,8},{9,1... | collective-permute-start | bytes 1880072 | tf_op jit(solution)/shard_map/ppermute | solution.py:249
  89.2 33.2 %collective-permute-start.12 = (bf16[2,144,1088]{2,1,0:T(8,128)(2,1)S(1)}, bf16[2,144,1088]{2,1,0:T(8,128)(2,1)}, u32[]{:S(2)}, u32[]{:S(2)}) collective-permute-start(bf16[2,144,1088]{2,1,0:T(8,128)(2,1)S(1)} %bitcast.311), channel_id=1, source_target_pairs={{0,2},{1,3},{2,0},{3,1},{4,6},{5,7},{6,4},{7,5},{8,10},{9,11},{10,... | collective-permute-start | bytes 1880072 | tf_op jit(solution)/shard_map/ppermute | solution.py:249
  96.1 69.2 %collective-permute-start.21 = (bf16[2,2,144,1088]{3,2,1,0:T(8,128)(2,1)}, bf16[2,2,144,1088]{3,2,1,0:T(8,128)(2,1)}, u32[]{:S(2)}, u32[]{:S(2)}) collective-permute-start(bf16[2,2,144,1088]{3,2,1,0:T(8,128)(2,1)} %pad_maximum_fusion.8.refs_0_), channel_id=1, source_target_pairs={{0,2},{1,3},{2,0},{3,1},{4,6},{5,7},{6,4},{7,5},{8,10},{9,11},{10,... | collective-permute-start | bytes 3760136 | tf_op jit(solution)/shard_map/ppermute | solution.py:249
  108.1 58.8 %collective-permute-start.23 = (bf16[2,2,144,1088]{3,2,1,0:T(8,128)(2,1)}, bf16[2,2,144,1088]{3,2,1,0:T(8,128)(2,1)}, u32[]{:S(2)}, u32[]{:S(2)}) collective-permute-start(bf16[2,2,144,1088]{3,2,1,0:T(8,128)(2,1)} %pad_maximum_fusion.8.refs_0_), channel_id=1, source_target_pairs={{0,1},{1,0},{2,3},{3,2},{4,5},{5,4},{6,7},{7,6},{8,9},{9,8},{10,11... | collective-permute-start | bytes 3760136 | tf_op jit(solution)/shard_map/ppermute | solution.py:249
  108.3 57.2 %collective-permute-start.22 = (bf16[2,2,144,1088]{3,2,1,0:T(8,128)(2,1)}, bf16[2,2,144,1088]{3,2,1,0:T(8,128)(2,1)}, u32[]{:S(2)}, u32[]{:S(2)}) collective-permute-start(bf16[2,2,144,1088]{3,2,1,0:T(8,128)(2,1)} %pad_maximum_fusion.9.refs_1_), channel_id=1, source_target_pairs={{0,4},{4,0},{1,5},{5,1},{2,6},{6,2},{3,7},{7,3},{8,12},{12,8},{9,1... | collective-permute-start | bytes 3760136 | tf_op jit(solution)/shard_map/ppermute | solution.py:249
  118.5 35.8 %collective-permute-start.3 = (bf16[2,144,1088]{2,1,0:T(8,128)(2,1)}, bf16[2,144,1088]{2,1,0:T(8,128)(2,1)}, u32[]{:S(2)}, u32[]{:S(2)}) collective-permute-start(bf16[2,144,1088]{2,1,0:T(8,128)(2,1)} %get-tuple-element.169), channel_id=1, source_target_pairs={{0,4},{4,0},{1,5},{5,1},{2,6},{6,2},{3,7},{7,3},{8,12},{12,8},{9,1... | collective-permute-start | bytes 1880072 | tf_op jit(solution)/shard_map/ppermute | solution.py:249
  122.4 42.6 %collective-permute-start.4 = (bf16[2,144,1088]{2,1,0:T(8,128)(2,1)}, bf16[2,144,1088]{2,1,0:T(8,128)(2,1)}, u32[]{:S(2)}, u32[]{:S(2)}) collective-permute-start(bf16[2,144,1088]{2,1,0:T(8,128)(2,1)} %get-tuple-element.168), channel_id=1, source_target_pairs={{0,2},{1,3},{2,0},{3,1},{4,6},{5,7},{6,4},{7,5},{8,10},{9,11},{10,... | collective-permute-start | bytes 1880072 | tf_op jit(solution)/shard_map/ppermute | solution.py:249
  154.2 39.9 %collective-permute-start.24 = (bf16[2,2,144,1088]{3,2,1,0:T(8,128)(2,1)}, bf16[2,2,144,1088]{3,2,1,0:T(8,128)(2,1)}, u32[]{:S(2)}, u32[]{:S(2)}) collective-permute-start(bf16[2,2,144,1088]{3,2,1,0:T(8,128)(2,1)} %pad_maximum_fusion.9.refs_1_), channel_id=1, source_target_pairs={{0,1},{1,0},{2,3},{3,2},{4,5},{5,4},{6,7},{7,6},{8,9},{9,8},{10,11... | collective-permute-start | bytes 3760136 | tf_op jit(solution)/shard_map/ppermute | solution.py:249
  165.1 31.4 %collective-permute-start.13 = (bf16[2,2,144,1088]{3,2,1,0:T(8,128)(2,1)}, bf16[2,2,144,1088]{3,2,1,0:T(8,128)(2,1)}, u32[]{:S(2)}, u32[]{:S(2)}) collective-permute-start(bf16[2,2,144,1088]{3,2,1,0:T(8,128)(2,1)} %pad_maximum_fusion.6.refs_0_), channel_id=1, source_target_pairs={{0,2},{1,3},{2,0},{3,1},{4,6},{5,7},{6,4},{7,5},{8,10},{9,11},{10,... | collective-permute-start | bytes 3760136 | tf_op jit(solution)/shard_map/ppermute | solution.py:249
  165.3 32.7 %collective-permute-start.15 = (bf16[2,2,144,1088]{3,2,1,0:T(8,128)(2,1)}, bf16[2,2,144,1088]{3,2,1,0:T(8,128)(2,1)}, u32[]{:S(2)}, u32[]{:S(2)}) collective-permute-start(bf16[2,2,144,1088]{3,2,1,0:T(8,128)(2,1)} %pad_maximum_fusion.6.refs_0_), channel_id=1, source_target_pairs={{0,1},{1,0},{2,3},{3,2},{4,5},{5,4},{6,7},{7,6},{8,9},{9,8},{10,11... | collective-permute-start | bytes 3760136 | tf_op jit(solution)/shard_map/ppermute | solution.py:249
  165.4 32.5 %collective-permute-start.14 = (bf16[2,2,144,1088]{3,2,1,0:T(8,128)(2,1)}, bf16[2,2,144,1088]{3,2,1,0:T(8,128)(2,1)}, u32[]{:S(2)}, u32[]{:S(2)}) collective-permute-start(bf16[2,2,144,1088]{3,2,1,0:T(8,128)(2,1)} %pad_maximum_fusion.7.refs_1_), channel_id=1, source_target_pairs={{0,4},{4,0},{1,5},{5,1},{2,6},{6,2},{3,7},{7,3},{8,12},{12,8},{9,1... | collective-permute-start | bytes 3760136 | tf_op jit(solution)/shard_map/ppermute | solution.py:249
  166.9 31.6 %collective-permute-start.16 = (bf16[2,2,144,1088]{3,2,1,0:T(8,128)(2,1)}, bf16[2,2,144,1088]{3,2,1,0:T(8,128)(2,1)}, u32[]{:S(2)}, u32[]{:S(2)}) collective-permute-start(bf16[2,2,144,1088]{3,2,1,0:T(8,128)(2,1)} %pad_maximum_fusion.7.refs_1_), channel_id=1, source_target_pairs={{0,1},{1,0},{2,3},{3,2},{4,5},{5,4},{6,7},{7,6},{8,9},{9,8},{10,11... | collective-permute-start | bytes 3760136 | tf_op jit(solution)/shard_map/ppermute | solution.py:249
  194.1 31.8 %collective-permute-start.5 = (bf16[2,2,144,1088]{3,2,1,0:T(8,128)(2,1)}, bf16[2,2,144,1088]{3,2,1,0:T(8,128)(2,1)}, u32[]{:S(2)}, u32[]{:S(2)}) collective-permute-start(bf16[2,2,144,1088]{3,2,1,0:T(8,128)(2,1)} %pad_maximum_fusion.4.refs_0_), channel_id=1, source_target_pairs={{0,2},{1,3},{2,0},{3,1},{4,6},{5,7},{6,4},{7,5},{8,10},{9,11},{10,... | collective-permute-start | bytes 3760136 | tf_op jit(solution)/shard_map/ppermute | solution.py:249
  196.5 30.9 %collective-permute-start.6 = (bf16[2,2,144,1088]{3,2,1,0:T(8,128)(2,1)}, bf16[2,2,144,1088]{3,2,1,0:T(8,128)(2,1)}, u32[]{:S(2)}, u32[]{:S(2)}) collective-permute-start(bf16[2,2,144,1088]{3,2,1,0:T(8,128)(2,1)} %pad_maximum_fusion.5.refs_1_), channel_id=1, source_target_pairs={{0,4},{4,0},{1,5},{5,1},{2,6},{6,2},{3,7},{7,3},{8,12},{12,8},{9,1... | collective-permute-start | bytes 3760136 | tf_op jit(solution)/shard_map/ppermute | solution.py:249
  198.0 29.9 %collective-permute-start.26 = (bf16[2,2,144,1088]{3,2,1,0:T(8,128)(2,1)}, bf16[2,2,144,1088]{3,2,1,0:T(8,128)(2,1)}, u32[]{:S(2)}, u32[]{:S(2)}) collective-permute-start(bf16[2,2,144,1088]{3,2,1,0:T(8,128)(2,1)} %collective-permute-done.22.refs_3_), channel_id=1, source_target_pairs={{0,1},{1,0},{2,3},{3,2},{4,5},{5,4},{6,7},{7,6},{8,9},{9,8},{10,11... | collective-permute-start | bytes 3760136 | tf_op jit(solution)/shard_map/ppermute | solution.py:249
  225.9 664.0 %collective-permute-start.7 = (bf16[2,2,144,1088]{3,2,1,0:T(8,128)(2,1)}, bf16[2,2,144,1088]{3,2,1,0:T(8,128)(2,1)}, u32[]{:S(2)}, u32[]{:S(2)}) collective-permute-start(bf16[2,2,144,1088]{3,2,1,0:T(8,128)(2,1)} %pad_maximum_fusion.4.refs_0_), channel_id=1, source_target_pairs={{0,1},{1,0},{2,3},{3,2},{4,5},{5,4},{6,7},{7,6},{8,9},{9,8},{10,11... | collective-permute-start | bytes 3760136 | tf_op jit(solution)/shard_map/ppermute | solution.py:249
  227.4 662.6 %collective-permute-start.8 = (bf16[2,2,144,1088]{3,2,1,0:T(8,128)(2,1)}, bf16[2,2,144,1088]{3,2,1,0:T(8,128)(2,1)}, u32[]{:S(2)}, u32[]{:S(2)}) collective-permute-start(bf16[2,2,144,1088]{3,2,1,0:T(8,128)(2,1)} %pad_maximum_fusion.5.refs_1_), channel_id=1, source_target_pairs={{0,1},{1,0},{2,3},{3,2},{4,5},{5,4},{6,7},{7,6},{8,9},{9,8},{10,11... | collective-permute-start | bytes 3760136 | tf_op jit(solution)/shard_map/ppermute | solution.py:249
  227.4 337.9 %collective-permute-start.18 = (bf16[2,2,144,1088]{3,2,1,0:T(8,128)(2,1)}, bf16[2,2,144,1088]{3,2,1,0:T(8,128)(2,1)}, u32[]{:S(2)}, u32[]{:S(2)}) collective-permute-start(bf16[2,2,144,1088]{3,2,1,0:T(8,128)(2,1)} %collective-permute-done.14.refs_3_), channel_id=1, source_target_pairs={{0,1},{1,0},{2,3},{3,2},{4,5},{5,4},{6,7},{7,6},{8,9},{9,8},{10,11... | collective-permute-start | bytes 3760136 | tf_op jit(solution)/shard_map/ppermute | solution.py:249
  227.9 662.1 %collective-permute-start.9 = (bf16[2,2,144,1088]{3,2,1,0:T(8,128)(2,1)}, bf16[2,2,144,1088]{3,2,1,0:T(8,128)(2,1)}, u32[]{:S(2)}, u32[]{:S(2)}) collective-permute-start(bf16[2,2,144,1088]{3,2,1,0:T(8,128)(2,1)} %collective-permute-done.5.refs_2_), channel_id=1, source_target_pairs={{0,1},{1,0},{2,3},{3,2},{4,5},{5,4},{6,7},{7,6},{8,9},{9,8},{10,11... | collective-permute-start | bytes 3760136 | tf_op jit(solution)/shard_map/ppermute | solution.py:249
  228.0 662.0 %collective-permute-start.10 = (bf16[2,2,144,1088]{3,2,1,0:T(8,128)(2,1)}, bf16[2,2,144,1088]{3,2,1,0:T(8,128)(2,1)}, u32[]{:S(2)}, u32[]{:S(2)}) collective-permute-start(bf16[2,2,144,1088]{3,2,1,0:T(8,128)(2,1)} %collective-permute-done.6.refs_3_), channel_id=1, source_target_pairs={{0,1},{1,0},{2,3},{3,2},{4,5},{5,4},{6,7},{7,6},{8,9},{9,8},{10,11... | collective-permute-start | bytes 3760136 | tf_op jit(solution)/shard_map/ppermute | solution.py:249
  1472.0 231.9 %collective-permute-start.27 = (bf16[2,128,1088]{1,2,0:T(8,128)(2,1)}, bf16[2,128,1088]{1,2,0:T(8,128)(2,1)}, u32[]{:S(2)}, u32[]{:S(2)}) collective-permute-start(bf16[2,128,1088]{1,2,0:T(8,128)(2,1)} %copy.189), channel_id=1, source_target_pairs={{0,1},{1,0},{2,3},{3,2},{4,5},{5,4},{6,7},{7,6},{8,9},{9,8},{10,11... | collective-permute-start | bytes 1671176 | tf_op jit(solution)/shard_map/ppermute | solution.py:249
  1488.8 39.0 %collective-permute-start.41 = (bf16[4,16,1088]{2,1,0:T(8,128)(2,1)S(1)}, bf16[4,16,1088]{2,1,0:T(8,128)(2,1)S(1)}, u32[]{:S(2)}, u32[]{:S(2)}) collective-permute-start(bf16[4,16,1088]{2,1,0:T(8,128)(2,1)S(1)} %pad.9), channel_id=1, source_target_pairs={{0,1},{1,0},{2,3},{3,2},{4,5},{5,4},{6,7},{7,6},{8,9},{9,8},{10,11... | collective-permute-start | bytes 417800 | tf_op jit(solution)/shard_map/ppermute | solution.py:249
  1496.8 47.3 %collective-permute-start.48 = (bf16[4,4,144,1088]{3,2,1,0:T(8,128)(2,1)}, bf16[4,4,144,1088]{3,2,1,0:T(8,128)(2,1)}, u32[]{:S(2)}, u32[]{:S(2)}) collective-permute-start(bf16[4,4,144,1088]{3,2,1,0:T(8,128)(2,1)} %broadcast_select_fusion.1), channel_id=1, source_target_pairs={{0,1},{1,0},{2,3},{3,2},{4,5},{5,4},{6,7},{7,6},{8,9},{9,8},{10,11... | collective-permute-start | bytes 15040520 | tf_op jit(solution)/shard_map/ppermute | solution.py:249
  1501.6 51.8 %collective-permute-start.36 = (bf16[4,4,144,1088]{3,2,1,0:T(8,128)(2,1)}, bf16[4,4,144,1088]{3,2,1,0:T(8,128)(2,1)}, u32[]{:S(2)}, u32[]{:S(2)}) collective-permute-start(bf16[4,4,144,1088]{3,2,1,0:T(8,128)(2,1)} %broadcast_select_fusion.2), channel_id=1, source_target_pairs={{0,1},{1,0},{2,3},{3,2},{4,5},{5,4},{6,7},{7,6},{8,9},{9,8},{10,11... | collective-permute-start | bytes 15040520 | tf_op jit(solution)/shard_map/ppermute | solution.py:249
  1527.7 32.0 %collective-permute-start.57 = (bf16[4,4,144,1088]{3,2,1,0:T(8,128)(2,1)}, bf16[4,4,144,1088]{3,2,1,0:T(8,128)(2,1)}, u32[]{:S(2)}, u32[]{:S(2)}) collective-permute-start(bf16[4,4,144,1088]{3,2,1,0:T(8,128)(2,1)} %broadcast_select_fusion), channel_id=1, source_target_pairs={{0,1},{1,0},{2,3},{3,2},{4,5},{5,4},{6,7},{7,6},{8,9},{9,8},{10,11... | collective-permute-start | bytes 15040520 | tf_op jit(solution)/shard_map/ppermute | solution.py:249
  1541.9 169.6 %collective-permute-start.28 = (bf16[2,128,1088]{1,2,0:T(8,128)(2,1)}, bf16[2,128,1088]{1,2,0:T(8,128)(2,1)}, u32[]{:S(2)}, u32[]{:S(2)}) collective-permute-start(bf16[2,128,1088]{1,2,0:T(8,128)(2,1)} %copy.191), channel_id=1, source_target_pairs={{0,2},{1,3},{2,0},{3,1},{4,6},{5,7},{6,4},{7,5},{8,10},{9,11},{10,... | collective-permute-start | bytes 1671176 | tf_op jit(solution)/shard_map/ppermute | solution.py:249
  1544.1 169.5 %collective-permute-start.29 = (bf16[2,128,1088]{1,2,0:T(8,128)(2,1)}, bf16[2,128,1088]{1,2,0:T(8,128)(2,1)}, u32[]{:S(2)}, u32[]{:S(2)}) collective-permute-start(bf16[2,128,1088]{1,2,0:T(8,128)(2,1)} %copy.193), channel_id=1, source_target_pairs={{0,3},{1,2},{2,1},{3,0},{4,7},{5,6},{6,5},{7,4},{8,11},{9,10},{10,... | collective-permute-start | bytes 1671176 | tf_op jit(solution)/shard_map/ppermute | solution.py:249
  1553.4 31.6 %collective-permute-start.49 = (bf16[2,2,144,1088]{3,2,1,0:T(8,128)(2,1)}, bf16[2,2,144,1088]{3,2,1,0:T(8,128)(2,1)}, u32[]{:S(2)}, u32[]{:S(2)}) collective-permute-start(bf16[2,2,144,1088]{3,2,1,0:T(8,128)(2,1)} %get-tuple-element.137), channel_id=1, source_target_pairs={{0,4},{4,0},{1,5},{5,1},{2,6},{6,2},{3,7},{7,3},{8,12},{12,8},{9,1... | collective-permute-start | bytes 3760136 | tf_op jit(solution)/shard_map/ppermute | solution.py:249
  1559.7 37.4 %collective-permute-start.51 = (bf16[2,2,144,1088]{3,2,1,0:T(8,128)(2,1)}, bf16[2,2,144,1088]{3,2,1,0:T(8,128)(2,1)S(1)}, u32[]{:S(2)}, u32[]{:S(2)}) collective-permute-start(bf16[2,2,144,1088]{3,2,1,0:T(8,128)(2,1)} %get-tuple-element.138), channel_id=1, source_target_pairs={{0,2},{1,3},{2,0},{3,1},{4,6},{5,7},{6,4},{7,5},{8,10},{9,11},{10,... | collective-permute-start | bytes 3760136 | tf_op jit(solution)/shard_map/ppermute | solution.py:249
  1585.0 30.4 %collective-permute-start.58 = (bf16[2,2,144,1088]{3,2,1,0:T(8,128)(2,1)S(1)}, bf16[2,2,144,1088]{3,2,1,0:T(8,128)(2,1)S(1)}, u32[]{:S(2)}, u32[]{:S(2)}) collective-permute-start(bf16[2,2,144,1088]{3,2,1,0:T(8,128)(2,1)S(1)} %get-tuple-element.133), channel_id=1, source_target_pairs={{0,4},{4,0},{1,5},{5,1},{2,6},{6,2},{3,7},{7,3},{8,12},{12,8},{9,1... | collective-permute-start | bytes 3760136 | tf_op jit(solution)/shard_map/ppermute | solution.py:249
  1597.1 30.4 %collective-permute-start.60 = (bf16[2,2,144,1088]{3,2,1,0:T(8,128)(2,1)S(1)}, bf16[2,2,144,1088]{3,2,1,0:T(8,128)(2,1)S(1)}, u32[]{:S(2)}, u32[]{:S(2)}) collective-permute-start(bf16[2,2,144,1088]{3,2,1,0:T(8,128)(2,1)S(1)} %get-tuple-element.134), channel_id=1, source_target_pairs={{0,2},{1,3},{2,0},{3,1},{4,6},{5,7},{6,4},{7,5},{8,10},{9,11},{10,... | collective-permute-start | bytes 3760136 | tf_op jit(solution)/shard_map/ppermute | solution.py:249
  1644.9 89.9 %reduce-scatter.8.cloned.1.call-start = ((), (), s32[]{:S(2)}) async-start(), calls=%async_computation.5 | async-start | bytes 1658880 | tf_op jit(solution)/shard_map/reduce_scatter | solution.py:493
  1688.9 65.1 %reduce-scatter.4.cloned.1.call-start = ((), (), s32[]{:S(2)}) async-start(), calls=%async_computation.3 | async-start | bytes 1843200 | tf_op jit(solution)/shard_map/reduce_scatter | solution.py:493
  1733.8 35.4 %collective-permute-start.53 = (bf16[1,144,1088]{2,1,0:T(8,128)(2,1)}, bf16[1,144,1088]{2,1,0:T(8,128)(2,1)}, u32[]{:S(2)}, u32[]{:S(2)}) collective-permute-start(bf16[1,144,1088]{2,1,0:T(8,128)(2,1)} %reduce-scatter.6.cloned.1.call-done), channel_id=1, source_target_pairs={{0,4},{4,0},{1,5},{5,1},{2,6},{6,2},{3,7},{7,3},{8,12},{12,8},{9,1... | collective-permute-start | bytes 940040 | tf_op jit(solution)/shard_map/ppermute | solution.py:249
  1772.0 32.2 %collective-permute-start.45 = (bf16[2,1,144,1088]{3,2,1,0:T(8,128)(2,1)S(1)}, bf16[2,1,144,1088]{3,2,1,0:T(8,128)(2,1)}, u32[]{:S(2)}, u32[]{:S(2)}) collective-permute-start(bf16[2,1,144,1088]{3,2,1,0:T(8,128)(2,1)S(1)} %pad_maximum_fusion.12.refs_0_), channel_id=1, source_target_pairs={{0,2},{1,3},{2,0},{3,1},{4,6},{5,7},{6,4},{7,5},{8,10},{9,11},{10,... | collective-permute-start | bytes 1880072 | tf_op jit(solution)/shard_map/ppermute | solution.py:249
  1779.5 112.3 %collective-permute-start.55 = (bf16[2,1,144,1088]{3,2,1,0:T(8,128)(2,1)S(1)}, bf16[2,1,144,1088]{3,2,1,0:T(8,128)(2,1)}, u32[]{:S(2)}, u32[]{:S(2)}) collective-permute-start(bf16[2,1,144,1088]{3,2,1,0:T(8,128)(2,1)S(1)} %pad_maximum_fusion.13.refs_0_), channel_id=1, source_target_pairs={{0,1},{1,0},{2,3},{3,2},{4,5},{5,4},{6,7},{7,6},{8,9},{9,8},{10,11... | collective-permute-start | bytes 1880072 | tf_op jit(solution)/shard_map/ppermute | solution.py:249
  1791.5 193.4 %collective-permute-start.46 = (bf16[2,1,144,1088]{3,2,1,0:T(8,128)(2,1)S(1)}, bf16[2,1,144,1088]{3,2,1,0:T(8,128)(2,1)}, u32[]{:S(2)}, u32[]{:S(2)}) collective-permute-start(bf16[2,1,144,1088]{3,2,1,0:T(8,128)(2,1)S(1)} %pad_maximum_fusion.12.refs_0_), channel_id=1, source_target_pairs={{0,1},{1,0},{2,3},{3,2},{4,5},{5,4},{6,7},{7,6},{8,9},{9,8},{10,11... | collective-permute-start | bytes 1880072 | tf_op jit(solution)/shard_map/ppermute | solution.py:249
  1791.5 100.3 %collective-permute-start.56 = (bf16[2,1,144,1088]{3,2,1,0:T(8,128)(2,1)S(1)}, bf16[2,1,144,1088]{3,2,1,0:T(8,128)(2,1)}, u32[]{:S(2)}, u32[]{:S(2)}) collective-permute-start(bf16[2,1,144,1088]{3,2,1,0:T(8,128)(2,1)S(1)} %collective-permute-done.54.refs_1_), channel_id=1, source_target_pairs={{0,1},{1,0},{2,3},{3,2},{4,5},{5,4},{6,7},{7,6},{8,9},{9,8},{10,11... | collective-permute-start | bytes 1880072 | tf_op jit(solution)/shard_map/ppermute | solution.py:249
  1804.2 180.7 %collective-permute-start.47 = (bf16[2,1,144,1088]{3,2,1,0:T(8,128)(2,1)}, bf16[2,1,144,1088]{3,2,1,0:T(8,128)(2,1)}, u32[]{:S(2)}, u32[]{:S(2)}) collective-permute-start(bf16[2,1,144,1088]{3,2,1,0:T(8,128)(2,1)} %collective-permute-done.45.refs_1_), channel_id=1, source_target_pairs={{0,1},{1,0},{2,3},{3,2},{4,5},{5,4},{6,7},{7,6},{8,9},{9,8},{10,11... | collective-permute-start | bytes 1880072 | tf_op jit(solution)/shard_map/ppermute | solution.py:249
  (90 other events, 2902.2 us)
Sparse Core Ops, SparseCore 0:
  10.2 35.6 all-gather.10
  47.5 31.9 all-gather.8
  81.1 34.4 all-gather.6
  1645.0 29.5 reduce-scatter.5
  1689.0 29.6 reduce-scatter.7
  1721.4 32.5 reduce-scatter.3

commit v3 on v2

--- a/solution.py
+++ b/solution.py
@@ -11,7 +11,7 @@
 HEAD_DIM = 64
 EPSILON = 1e-05
 LANES = 128
-VMEM_LIMIT = 48 * 1024 * 1024
+VMEM_LIMIT = 56 * 1024 * 1024
 
 BF16 = jnp.bfloat16
 F32 = jnp.float32
@@ -98,10 +98,9 @@
     o_ref,
     do_ref,
     lse_ref,
-    out_ref,
-    dk_acc,
-    dv_acc,
+    *refs,
 ):
+    out_ref, dk_acc, dv_acc = refs[-3:]
     count, local = k_ref.shape[1], k_ref.shape[3]
     tile = blocks * local
     keys = only_valid(sorted_rows(k_ref, (0,), order_ref, 0, count), width)
@@ -188,7 +187,7 @@
     )(order, joined, joined, joined)
 
 
-def attention_backward(joined, mixed, grad_mixed, lse, order):
+def attention_backward(joined, mixed, grad_mixed, lse, order, ties=()):
     _, count, seqs, local, width = joined.shape
     length = count * local
     pairs = pl.cdiv(width, LANES)
@@ -208,7 +207,8 @@
                 rows,
                 rows,
                 pl.BlockSpec((1, 1, 8, length), lambda s, h, order: (s, h, 0, 0)),
-            ],
+            ]
+            + [pl.BlockSpec(memory_space=pl.ANY)] * len(ties),
             out_specs=pl.BlockSpec(
                 (3, count, 1, local, LANES), lambda s, h, order: (0, 0, s, 0, h)
             ),
@@ -221,7 +221,7 @@
             bytes_accessed=16 * seqs * length * width,
             transcendentals=seqs * pairs * 2 * length * length,
         ),
-    )(order, joined, joined, joined, mixed, grad_mixed, lse)
+    )(order, joined, joined, joined, mixed, grad_mixed, lse, *ties)
 
 
 def standardize(values):
@@ -230,14 +230,156 @@
     return centred * inverse, inverse
 
 
-def normalize_back(grad_out, standard, inverse, gain_vec):
-    scaled = grad_out * gain_vec
-    grad_in = inverse * (
+def normalize_back(grad_out, standard, inverse, gain):
+    scaled = grad_out * gain
+    return inverse * (
         scaled
         - jnp.mean(scaled, axis=-1, keepdims=True)
         - standard * jnp.mean(scaled * standard, axis=-1, keepdims=True)
     )
-    return grad_in, jnp.sum(grad_out * standard, axis=0), jnp.sum(grad_out, axis=0)
+
+
+def add_row(sums_ref, row, values):
+    sums_ref[row : row + 1, :] += jnp.sum(values, axis=0, keepdims=True)
+
+
+def clear_first(sums_ref):
+    @pl.when(pl.program_id(0) == 0)
+    def _():
+        sums_ref[...] = jnp.zeros_like(sums_ref)
+
+
+G_ONE, B_ONE, BIAS_Q, BIAS_V, BIAS_OUT, G_TWO, B_TWO, BIAS_PROJ = range(8)
+
+
+def row(small_ref, index):
+    return small_ref[index : index + 1, :]
+
+
+def qkv_kernel(x_ref, w_ref, small_ref, joined_ref, low_ref):
+    standard, _ = standardize(x_ref[...].astype(F32))
+    low = (standard * row(small_ref, G_ONE) + row(small_ref, B_ONE)).astype(BF16)
+    low_ref[...] = low
+    for which, bias in enumerate((BIAS_Q, None, BIAS_V)):
+        out = dot_nn(low, w_ref[which])
+        if bias is not None:
+            out = out + row(small_ref, bias)
+        joined_ref[which] = out.astype(BF16)
+
+
+def attended_kernel(x_ref, o_ref, w_ref, small_ref, middle_ref, low_ref):
+    middle = x_ref[...].astype(F32) + dot_nn(o_ref[...], w_ref[0]) + row(small_ref, BIAS_OUT)
+    middle_ref[...] = middle
+    standard, _ = standardize(middle)
+    low_ref[...] = (standard * row(small_ref, G_TWO) + row(small_ref, B_TWO)).astype(BF16)
+
+
+def hidden_kernel(low_ref, w_ref, bias_ref, act_ref, slope_ref):
+    low = low_ref[...]
+    scale = 0.7978845608028654
+    for which in range(w_ref.shape[0]):
+        hidden = dot_nn(low, w_ref[which]) + bias_ref[which]
+        square = hidden * hidden
+        bent = jnp.tanh(scale * hidden * (1.0 + 0.044715 * square))
+        half = 0.5 * (1.0 + bent)
+        act_ref[which] = (hidden * half).astype(BF16)
+        slope = half + 0.5 * hidden * (1.0 - bent * bent) * (
+            scale * (1.0 + 3.0 * 0.044715 * square)
+        )
+        slope_ref[which] = slope.astype(BF16)
+
+
+def output_kernel(middle_ref, act_ref, w_ref, small_ref, out_ref):
+    total = middle_ref[...] + row(small_ref, BIAS_PROJ)
+    for which in range(w_ref.shape[0]):
+        total += dot_nn(act_ref[which], w_ref[which])
+    out_ref[...] = total.astype(BF16)
+
+
+def hidden_back_kernel(grad_ref, slope_ref, w_ref, *refs):
+    out_ref, sums_ref = refs[-2:]
+    clear_first(sums_ref)
+    grad = grad_ref[...]
+    for which in range(w_ref.shape[0]):
+        back = dot_nt(grad, w_ref[which]) * slope_ref[which].astype(F32)
+        low = back.astype(BF16)
+        out_ref[which] = low
+        add_row(sums_ref, which, low.astype(F32))
+
+
+def middle_back_kernel(hidden_ref, grad_ref, middle_ref, w_ref, out_w_ref, small_ref, *refs):
+    grad_middle_ref, low_ref, mixed_ref, sums_ref = refs[-4:]
+    clear_first(sums_ref)
+    grad_two = dot_nt(hidden_ref[0], w_ref[0])
+    for which in range(1, w_ref.shape[0]):
+        grad_two += dot_nt(hidden_ref[which], w_ref[which])
+    standard, inverse = standardize(middle_ref[...])
+    grad_out = grad_ref[...].astype(F32)
+    grad_middle = grad_out + normalize_back(grad_two, standard, inverse, row(small_ref, G_TWO))
+    low = grad_middle.astype(BF16)
+    grad_middle_ref[...] = grad_middle
+    low_ref[...] = low
+    mixed_ref[...] = dot_nt(low, out_w_ref[0]).astype(BF16)
+    add_row(sums_ref, G_TWO, grad_two * standard)
+    add_row(sums_ref, B_TWO, grad_two)
+    add_row(sums_ref, BIAS_OUT, low.astype(F32))
+    add_row(sums_ref, BIAS_PROJ, grad_out)
+
+
+def input_back_kernel(joined_ref, grad_middle_ref, x_ref, w_ref, small_ref, *refs):
+    out_ref, sums_ref = refs[-2:]
+    clear_first(sums_ref)
+    grad_one = dot_nt(joined_ref[0], w_ref[0])
+    for which in range(1, 3):
+        grad_one += dot_nt(joined_ref[which], w_ref[which])
+    standard, inverse = standardize(x_ref[...].astype(F32))
+    back = normalize_back(grad_one, standard, inverse, row(small_ref, G_ONE))
+    out_ref[...] = (grad_middle_ref[...] + back).astype(BF16)
+    add_row(sums_ref, G_ONE, grad_one * standard)
+    add_row(sums_ref, B_ONE, grad_one)
+    add_row(sums_ref, BIAS_Q, joined_ref[0].astype(F32))
+    add_row(sums_ref, BIAS_V, joined_ref[2].astype(F32))
+
+
+def by_rows(kernel, by_row, fixed, outs, sums=None, ties=(), tile=256):
+    rows, width = by_row[0].shape[-2:]
+    tile = tile if rows % tile == 0 else rows
+    whole = lambda shape, index: pl.BlockSpec(
+        shape, lambda i: index, pipeline_mode=pl.Buffered(buffer_count=1)
+    )
+    tiled = lambda lead: pl.BlockSpec(
+        tuple(lead) + (tile, width), lambda i: (0,) * len(lead) + (i, 0)
+    )
+    in_specs = [tiled(array.shape[:-2]) for array in by_row]
+    operands = list(by_row)
+    products = 0
+    for entry in fixed:
+        array, first, blocks = entry if isinstance(entry, tuple) else (entry, 0, entry.shape[0])
+        shape = (blocks,) + array.shape[1:]
+        in_specs.append(whole(shape, (first // blocks,) + (0,) * (array.ndim - 1)))
+        operands.append(array)
+        if array.dtype == BF16:
+            products += blocks
+    in_specs += [pl.BlockSpec(memory_space=pl.ANY)] * len(ties)
+    operands += list(ties)
+    out_specs = [tiled(lead) for lead, _ in outs]
+    out_shape = [jax.ShapeDtypeStruct(tuple(lead) + (rows, width), kind) for lead, kind in outs]
+    if sums:
+        out_specs.append(pl.BlockSpec((sums, width), lambda i: (0, 0)))
+        out_shape.append(jax.ShapeDtypeStruct((sums, width), F32))
+    moved = sum(array.size * array.dtype.itemsize for array in operands)
+    moved += sum(leaf.size * leaf.dtype.itemsize for leaf in out_shape)
+    return pl.pallas_call(
+        kernel,
+        grid=(rows // tile,),
+        in_specs=in_specs,
+        out_specs=out_specs,
+        out_shape=out_shape,
+        compiler_params=pltpu.CompilerParams(vmem_limit_bytes=VMEM_LIMIT),
+        cost_estimate=pl.CostEstimate(
+            flops=3 * rows * width * width * products, bytes_accessed=moved, transcendentals=0
+        ),
+    )(*operands)
 
 
 def row_major(values):
@@ -247,6 +389,10 @@
 def swap(values, axis, offset):
     count = lax.axis_size(axis)
     return lax.ppermute(values, axis, [(index, index ^ offset) for index in range(count)])
+
+
+def after(values, *earlier):
+    return lax.optimization_barrier((values, *earlier))
 
 
 def pick(bit, on_zero, on_one):
@@ -259,8 +405,8 @@
     parts = values.reshape(count, seqs // count, local, width)
     pieces = []
     for offset in range(count):
-        piece = lax.dynamic_index_in_dim(parts, own ^ offset, keepdims=False)
-        pieces.append(swap(piece, "ctx", offset) if offset else piece)
+        piece = row_major(lax.dynamic_index_in_dim(parts, own ^ offset, keepdims=False))
+        pieces.append(row_major(swap(piece, "ctx", offset)) if offset else piece)
     return row_major(jnp.stack(pieces))
 
 
@@ -269,7 +415,9 @@
     own = lax.axis_index("ctx")
     out = row_major(jnp.zeros((count, share, local, width), kind))
     for offset in range(count):
-        piece = swap(values[offset], "ctx", offset) if offset else values[0]
+        piece = row_major(values[offset])
+        if offset:
+            piece = row_major(swap(piece, "ctx", offset))
         out = lax.dynamic_update_index_in_dim(out, piece.astype(kind), own ^ offset, 0)
     return row_major(out).reshape(count * share, local, width)
 
@@ -302,90 +450,91 @@
         )
 
 
-def assemble_kernel(groups, start, size, here_ref, *refs):
-    arrays, out_ref, sem = refs[:-2], refs[-2], refs[-1]
+def assemble_kernel(groups, start, size, transposed, here_ref, *refs):
+    arrays, out_ref = refs[:-1], refs[-1]
     x, y, core = here_ref[0], here_ref[1], here_ref[2]
     for turn in range(2):
-        copies = []
         row = pl.multiple_of((core ^ turn) * start, 16)
         for (places, first), ref in zip(groups, arrays[turn * len(groups) :]):
             for i, (dx, dy) in enumerate(places):
+                block = 2 * (x ^ dx) + (y ^ dy)
                 for s in range(ref.shape[1]):
-                    copies.append(
-                        pltpu.make_async_copy(
-                            ref.at[i, s, pl.ds(0, size), :],
-                            out_ref.at[
-                                2 * (x ^ dx) + (y ^ dy), first + s, pl.ds(row, size), :
-                            ],
-                            sem.at[len(copies)],
-                        )
-                    )
-        for copy in copies:
-            copy.start()
-        for copy in copies:
-            copy.wait()
-
-
-def assemble(win, groups, own, other, owned_rows, shards):
+                    place = (first + s, block) if transposed else (block, first + s)
+                    out_ref[place + (pl.ds(row, size), slice(None))] = ref[
+                        i, s, :size, :
+                    ].astype(out_ref.dtype)
+
+
+def assemble(win, groups, own, other, owned_rows, shards, transposed, kind):
     width = own[0].shape[-1]
     here = jnp.stack([win.x, win.y, win.core]).astype(jnp.int32)
-    most = sum(len(places) * array.shape[1] for (places, _), array in zip(groups, own))
+    shape = (shards, 4, owned_rows, width) if transposed else (4, shards, owned_rows, width)
     return pl.pallas_call(
-        functools.partial(assemble_kernel, groups, win.start, win.size),
+        functools.partial(assemble_kernel, groups, win.start, win.size, transposed),
         in_specs=[pl.BlockSpec(memory_space=pltpu.SMEM)]
-        + [pl.BlockSpec(memory_space=pl.ANY)] * (2 * len(groups)),
-        out_specs=pl.BlockSpec(memory_space=pl.ANY),
-        out_shape=jax.ShapeDtypeStruct((4, shards, owned_rows, width), BF16),
-        scratch_shapes=[pltpu.SemaphoreType.DMA((most,))],
+        + [pl.BlockSpec(memory_space=pltpu.VMEM)] * (2 * len(groups)),
+        out_specs=pl.BlockSpec(memory_space=pltpu.VMEM),
+        out_shape=jax.ShapeDtypeStruct(shape, kind),
+        compiler_params=pltpu.CompilerParams(vmem_limit_bytes=VMEM_LIMIT),
         cost_estimate=pl.CostEstimate(
             flops=0, bytes_accessed=16 * shards * owned_rows * width, transcendentals=0
         ),
     )(here, *own, *other)
 
 
-def spread_weights(win, mine, owned_rows):
+def spread_weights(win, mine, owned_rows, transposed=False, kind=BF16):
     shards = mine.shape[0]
-    if shards % 2:
+    if shards == 1:
         first = jnp.stack([mine, swap(mine, "replica", 1)])
         own = [first, swap(first, "ctx", 2)]
         groups = ((((0, 0), (1, 0)), 0), (((0, 1), (1, 1)), 0))
     else:
-        half = shards // 2
-        low, high = mine[:half], mine[half:]
-        first = jnp.stack([low, swap(low, "replica", 1)])
-        second = jnp.stack([high, swap(high, "ctx", 2)])
+        split = max(shards // 4, 1)
+        low, high = mine[:split], mine[split:]
+        low_there, high_there = after(swap(low, "replica", 1), swap(high, "ctx", 2))
+        first = jnp.stack([low, low_there])
+        second = jnp.stack([high, high_there])
         own = [first, second, swap(first, "ctx", 2), swap(second, "replica", 1)]
         groups = (
             (((0, 0), (1, 0)), 0),
-            (((0, 0), (0, 1)), half),
+            (((0, 0), (0, 1)), split),
             (((0, 1), (1, 1)), 0),
-            (((1, 0), (1, 1)), half),
+            (((1, 0), (1, 1)), split),
         )
     other = [swap(array, "ctx", 1) for array in own]
-    return assemble(win, groups, own, other, owned_rows, shards)
+    return assemble(win, groups, own, other, owned_rows, shards, transposed, kind), own[-2:]
 
 
 def add_pair(kept, received):
     return (kept.astype(F32) + received.astype(F32)).astype(BF16)
 
 
+def corner(values):
+    return values[(0,) * (values.ndim - 2)][:16, :LANES]
+
+
 def reduce_blocks(win, grads):
     shards = grads.shape[1]
-    half = shards // 2
-    both = add_pair(win.rows(grads), swap(win.other_rows(grads), "ctx", 1))
-    x_kept = pick(win.x, both[:2, :half], both[2:, :half])
-    x_sent = pick(win.x, both[2:, :half], both[:2, :half])
-    y_kept = pick(win.y, both[0::2, half:], both[1::2, half:])
-    y_sent = pick(win.y, both[1::2, half:], both[0::2, half:])
-    low = add_pair(x_kept, swap(x_sent, "replica", 1))
-    high = add_pair(y_kept, swap(y_sent, "ctx", 2))
-    low_sum = add_pair(
-        pick(win.y, low[0], low[1]), swap(pick(win.y, low[1], low[0]), "ctx", 2)
-    )
-    high_sum = add_pair(
-        pick(win.x, high[0], high[1]), swap(pick(win.x, high[1], high[0]), "replica", 1)
-    )
-    return jnp.concatenate([low_sum, high_sum], axis=0)
+    split = shards - max(shards // 4, 1)
+    received = swap(win.other_rows(grads), "ctx", 1)
+    both = add_pair(win.rows(grads), received)
+    x_kept = pick(win.x, both[:2, :split], both[2:, :split])
+    x_sent = pick(win.x, both[2:, :split], both[:2, :split])
+    y_kept = pick(win.y, both[0::2, split:], both[1::2, split:])
+    y_sent = pick(win.y, both[1::2, split:], both[0::2, split:])
+    x_received, y_received = after(swap(x_sent, "replica", 1), swap(y_sent, "ctx", 2))
+    low = add_pair(x_kept, x_received)
+    high = add_pair(y_kept, y_received)
+    low_received = swap(pick(win.y, low[1], low[0]), "ctx", 2)
+    high_received = swap(pick(win.x, high[1], high[0]), "replica", 1)
+    low_sum = add_pair(pick(win.y, low[0], low[1]), low_received)
+    high_sum = add_pair(pick(win.x, high[0], high[1]), high_received)
+    marks = (
+        [corner(received)],
+        [corner(x_received), corner(y_received)],
+        [corner(low_received), corner(high_received)],
+    )
+    return jnp.concatenate([low_sum, high_sum], axis=0), marks
 
 
 def reduce_vectors(values):
@@ -434,31 +583,37 @@
     def gather_z(values):
         return lax.all_gather(values, "shard", axis=0, tiled=False)
 
+    low_inputs = to_sequences(tokens, count).reshape(rows, width)
+
     if pairwise:
         mine = [win.rows(win.block(blocks)) for blocks in (blocks_a, blocks_b, blocks_c)]
         part_a = gather_z(jnp.concatenate([mine[0], vector_tile], axis=0))
-        part_b, part_c = gather_z(mine[1]), gather_z(mine[2])
+        mine_b, part_a = after(mine[1], part_a)
+        part_b = gather_z(mine_b)
+        mine_c, part_b = after(mine[2], part_b)
+        part_c = gather_z(mine_c)
+        part_a, low_inputs = after(part_a, low_inputs)
         vector_part = part_a[:, win.size : win.size + vector_rows]
-        full_a = spread_weights(win, part_a[:, : win.size], owned_rows)
-        full_b = spread_weights(win, part_b, owned_rows)
-        full_c = spread_weights(win, part_c, owned_rows)
+        full_a, steps = spread_weights(win, part_a[:, : win.size], owned_rows)
+        part_b, *_ = after(part_b, *steps)
+        full_b, steps = spread_weights(win, part_b, owned_rows)
+        part_c, *_ = after(part_c, *steps)
+        full_c, steps = spread_weights(win, part_c, owned_rows, transposed=True)
+        cotangent, *_ = after(cotangent, *steps)
     else:
         vector_part = gather_z(vector_tile)[:, :vector_rows]
         full_a, full_b, full_c = [
-            gather_z(jnp.stack(blocks)).transpose(1, 0, 2, 3)
-            for blocks in (blocks_a, blocks_b, blocks_c)
+            gather_z(jnp.stack(blocks)) for blocks in (blocks_a, blocks_b, blocks_c)
         ]
-    matrices_a = full_a.reshape(4, width, width)
-    w_qkv, w_out = matrices_a[:3], matrices_a[3]
+        full_a, full_b = full_a.transpose(1, 0, 2, 3), full_b.transpose(1, 0, 2, 3)
+    w_a = full_a.reshape(4, width, width)
     w_fc = full_b.reshape(wide, width, width)
-    w_proj = full_c.transpose(1, 0, 2, 3).reshape(wide, width, width)
+    w_proj = full_c.reshape(wide, width, width)
     vector_part = vector_part.reshape(shards, vector_rows * width).astype(F32)
     small = vector_part[:, : 8 * owned_rows].reshape(shards, 8, owned_rows)
     small = small.transpose(1, 0, 2).reshape(8, width)
-    g_one, b_one, bias_q, bias_v, bias_out, g_two, b_two, bias_proj = [small[i] for i in range(8)]
     bias_fc = vector_part[:, 8 * owned_rows :].reshape(wide, 1, width)
 
-    low_inputs = to_sequences(tokens, count).reshape(rows, width)
     low_grad_out = to_sequences(cotangent, count).reshape(rows, width)
     share = seq_count // count
     blocked = (count, share, local_len, width)
@@ -466,89 +621,86 @@
     held_by = jnp.sum(jnp.where(block_order[None, :] == index[:, None], index[None, :], 0), axis=1)
     order = (held_by ^ lax.axis_index("ctx")).astype(jnp.int32)
 
-    inputs = low_inputs.astype(F32)
-    standard_one, inverse_one = standardize(inputs)
-    low_one = (standard_one * g_one + b_one).astype(BF16)
-    joined = jnp.einsum("td,cdx->ctx", low_one, w_qkv, preferred_element_type=F32)
-    bias_qkv = jnp.stack([bias_q, jnp.zeros_like(bias_q), bias_v])[:, None]
-    joined = (joined + bias_qkv).astype(BF16).reshape((3,) + blocked)
+    joined, low_one = by_rows(
+        qkv_kernel, [low_inputs], [(w_a, 0, 3), small], [((3,), BF16), ((), BF16)]
+    )
+    joined = joined.reshape((3,) + blocked)
     mixed, lse = attention_forward(joined, order)
     attended = mixed.reshape(rows, width)
-    middle = inputs + (dot_nn(attended, w_out) + bias_out)
-    standard_two, inverse_two = standardize(middle)
-    low_two = (standard_two * g_two + b_two).astype(BF16)
-    hidden = jnp.einsum("td,cdx->ctx", low_two, w_fc, preferred_element_type=F32) + bias_fc
-    activated, gelu_pull = jax.vjp(lambda pre_act: jax.nn.gelu(pre_act, approximate=True), hidden)
-    low_act = activated.astype(BF16)
-    outputs = middle + (
-        jnp.einsum("ctx,cxd->td", low_act, w_proj, preferred_element_type=F32) + bias_proj
-    )
-    layer_out = to_blocks(row_major(outputs.astype(BF16).reshape(blocked)), BF16)
+    middle, low_two = by_rows(
+        attended_kernel, [low_inputs, attended], [(w_a, 3, 1), small], [((), F32), ((), BF16)]
+    )
+    low_act, slope = by_rows(
+        hidden_kernel, [low_two], [w_fc, bias_fc], [((wide,), BF16), ((wide,), BF16)]
+    )
+    (outputs,) = by_rows(output_kernel, [middle, low_act], [w_proj, small], [((), BF16)])
+    layer_out = to_blocks(outputs.reshape(blocked), BF16)
 
     def reduce_units(grads, extra=None):
         if pairwise:
-            sums = reduce_blocks(win, grads)
+            sums, marks = reduce_blocks(win, grads)
             if extra is not None:
                 sums = jnp.concatenate([sums, reduce_vectors(extra)], axis=1)
             sums = lax.psum_scatter(sums, "shard", scatter_dimension=0, tiled=False)
-            full = spread_weights(win, sums[None, : win.size], owned_rows)[:, 0]
-            return full, sums[win.size :]
+            full = spread_weights(win, sums[None, : win.size], owned_rows, kind=F32)[0][:, 0]
+            return full, sums[win.size :], marks
         rest = ("replica", "ctx")
         full = lax.psum_scatter(grads, "shard", scatter_dimension=1, tiled=False)
         full = lax.psum(full, rest)
         if extra is not None:
             extra = lax.psum_scatter(extra, "shard", scatter_dimension=0, tiled=False)
             extra = lax.psum(extra, rest)
-        return full, extra
+        return full.astype(F32), extra, ((), (), ())
 
     def by_shard(grads):
         return grads.astype(BF16).reshape(4, shards, owned_rows, width)
 
-    grad_out = low_grad_out.astype(F32)
     grad_proj = jnp.einsum("ctx,td->cxd", low_act, low_grad_out, preferred_element_type=F32)
-    owned_proj, _ = reduce_units(by_shard(grad_proj).transpose(1, 0, 2, 3))
-    grad_proj_bias = jnp.sum(grad_out, axis=0)
-    grad_act = jnp.einsum("td,cxd->ctx", low_grad_out, w_proj, preferred_element_type=F32)
-    grad_hidden = gelu_pull(grad_act)[0].astype(BF16)
+    grad_proj = grad_proj.astype(BF16)
+    owned_proj, _, proj_marks = reduce_units(by_shard(grad_proj).transpose(1, 0, 2, 3))
+    grad_hidden, sums_hidden = by_rows(
+        hidden_back_kernel,
+        [low_grad_out, slope],
+        [w_proj],
+        [((wide,), BF16)],
+        sums=8,
+        ties=[corner(grad_proj)],
+    )
     grad_fc = jnp.einsum("td,ctx->cdx", low_two, grad_hidden, preferred_element_type=F32)
-    owned_fc, _ = reduce_units(by_shard(grad_fc))
-    grad_fc_bias = jnp.sum(grad_hidden.astype(F32), axis=1)
-    grad_two = jnp.einsum("ctx,cdx->td", grad_hidden, w_fc, preferred_element_type=F32)
-    grad_norm_two, grad_g_two, grad_b_two = normalize_back(
-        grad_two, standard_two, inverse_two, g_two
-    )
-    grad_middle = grad_out + grad_norm_two
-    low_grad_middle = grad_middle.astype(BF16)
-    grad_out_weight = dot_tn(attended, low_grad_middle)
-    grad_out_bias = jnp.sum(low_grad_middle.astype(F32), axis=0)
-    grad_attended = dot_nt(low_grad_middle, w_out).astype(BF16)
+    grad_fc = grad_fc.astype(BF16)
+    owned_fc, _, fc_marks = reduce_units(by_shard(grad_fc))
+    grad_middle, low_grad_middle, grad_mixed, sums_middle = by_rows(
+        middle_back_kernel,
+        [grad_hidden, low_grad_out, middle],
+        [w_fc, (w_a, 3, 1), small],
+        [((), F32), ((), BF16), ((), BF16)],
+        sums=8,
+        ties=[corner(grad_fc), *proj_marks[0]],
+    )
+    grad_out_weight = dot_tn(attended, low_grad_middle).astype(BF16)
     grad_joined = attention_backward(
-        joined, mixed, grad_attended.reshape(blocked), lse, order
+        joined,
+        mixed,
+        grad_mixed.reshape(blocked),
+        lse,
+        order,
+        ties=[*proj_marks[1], *fc_marks[0]],
     ).reshape(3, rows, width)
     grad_qkv = jnp.einsum("td,ctx->cdx", low_one, grad_joined, preferred_element_type=F32)
-    grads_a = jnp.concatenate([grad_qkv.astype(BF16), grad_out_weight.astype(BF16)[None]], axis=0)
-    grad_q_bias = jnp.sum(grad_joined[0].astype(F32), axis=0)
-    grad_v_bias = jnp.sum(grad_joined[2].astype(F32), axis=0)
-    grad_one = jnp.einsum("ctx,cdx->td", grad_joined, w_qkv, preferred_element_type=F32)
-    grad_norm_one, grad_g_one, grad_b_one = normalize_back(
-        grad_one, standard_one, inverse_one, g_one
-    )
-    input_grad = to_blocks(
-        row_major((grad_middle + grad_norm_one).astype(BF16).reshape(blocked)), F32
-    )
-
-    small_grads = jnp.stack(
-        [
-            grad_g_one,
-            grad_b_one,
-            grad_q_bias,
-            grad_v_bias,
-            grad_out_bias,
-            grad_g_two,
-            grad_b_two,
-            grad_proj_bias,
-        ]
-    )
+    grad_qkv = grad_qkv.astype(BF16)
+    grads_a = jnp.concatenate([grad_qkv, grad_out_weight[None]], axis=0)
+    grad_inputs, sums_input = by_rows(
+        input_back_kernel,
+        [grad_joined, grad_middle, low_inputs],
+        [(w_a, 0, 3), small],
+        [((), BF16)],
+        sums=8,
+        ties=[corner(grad_qkv), *proj_marks[2], *fc_marks[1]],
+    )
+    input_grad = to_blocks(grad_inputs.reshape(blocked), F32)
+
+    small_grads = sums_middle + sums_input
+    grad_fc_bias = sums_hidden[:wide]
     vector_grads = jnp.concatenate(
         [
             small_grads.reshape(8, shards, owned_rows)
@@ -562,11 +714,11 @@
         vector_grads.reshape(shards, vector_rows, width),
         ((0, 0), (0, -vector_rows % 16), (0, 0)),
     )
-    owned_a, owned_vectors = reduce_units(by_shard(grads_a), vector_grads)
+    owned_a, owned_vectors, _ = reduce_units(by_shard(grads_a), vector_grads)
     owned_vectors = owned_vectors[:vector_rows].reshape(-1).astype(F32)
     vec = [owned_vectors[i * owned_rows : (i + 1) * owned_rows] for i in range(8)]
-    qkv_grad = jnp.concatenate([owned_a[i] for i in range(3)], axis=1).astype(F32)
-    fc_grad = jnp.concatenate([owned_fc[i] for i in range(wide)], axis=1).astype(F32)
+    qkv_grad = jnp.concatenate([owned_a[i] for i in range(3)], axis=1)
+    fc_grad = jnp.concatenate([owned_fc[i] for i in range(wide)], axis=1)
     return (
         layer_out,
         input_grad,
@@ -575,13 +727,13 @@
         qkv_grad,
         vec[2],
         vec[3],
-        owned_a[3].astype(F32),
+        owned_a[3],
         vec[4],
         vec[5],
         vec[6],
         fc_grad,
         owned_vectors[8 * owned_rows :],
-        owned_proj.reshape(wide * owned_rows, width).astype(F32),
+        owned_proj.reshape(wide * owned_rows, width),
         vec[7],
     )
 

time: 2100 us -> 809 us (0.39)
  Pallas kernels: 1280 us -> 239 us
  matrix products: 176 us -> 47.1 us
  waiting for transfers between devices: 284 us -> 240 us
  other arithmetic: 123 us -> 82.9 us
  local copies, waits for them, and re-layouts: 155 us -> 120 us
    pallas_call x6, Pallas kernels: 1220 us -> 39.1 us  [assemble(): pl.pallas_call(functools.partial(assemble_kernel, groups, win.start, win....]
    pallas_call x0 -> x7, Pallas kernels: none -> 140 us  [by_rows(): pl.pallas_call(kernel, grid=(rows // tile,), in_specs=in_specs, out_specs...]
    dot_general x8 -> x0, matrix products: 119 us -> none  [the longest x1 24.3 us: per_device(): jnp.einsum('td,cxd->ctx', low_grad_out, w_proj, preferred_element_type=F32)]
    convert_element_type x5 -> x0, local copies, waits for them, and re-layouts: 25.5 us -> none  [the longest x1 9.43 us: per_device(): joined = (joined + bias_qkv).astype(BF16).reshape((3,) + blocked)]
    all_gather x3, waiting for transfers between devices: 41.8 us -> 17.5 us  [gather_z(): return lax.all_gather(values, 'shard', axis=0, tiled=False)]
    convert_element_type x7 -> x0, other arithmetic: 22.5 us -> none  [the longest x1 5.62 us: per_device(): (grad_middle + grad_norm_one).astype(BF16).reshape(blocked)]
  transfers between devices with their start and end apart: 72 -> 72, of which waited for: 28 -> 26; matrix products, arithmetic and copies ran while one was open for 12% -> 27% of each run, Pallas kernels for 39% -> 29%
where the time goes in v3:
time: 809 us; the launch traced here: 798 us
  waiting for transfers between devices  240 us (30%)
  Pallas kernels  239 us (30%)
  local copies, waits for them, and re-layouts  120 us (15%)
  other arithmetic  82.9 us (10%)
  starting transfers between devices  53.7 us (7%)
  matrix products  47.1 us (6%)
  between operations  15.5 us (2%)
    ppermute x66, waiting for transfers between devices, swap(): lax.ppermute(values, axis, [(index, index ^ offset) for index in range(co...  222 us
    pallas_call x7, Pallas kernels, by_rows(): pl.pallas_call(kernel, grid=(rows // tile,), in_specs=in_specs, out_specs...  140 us
    ppermute x66, starting transfers between devices, swap(): lax.ppermute(values, axis, [(index, index ^ offset) for index in range(co...  53.5 us
    pallas_call x6, Pallas kernels, assemble(): pl.pallas_call(functools.partial(assemble_kernel, groups, win.start, win....  39.1 us
    convert_element_type x18, other arithmetic, add_pair(): return (kept.astype(F32) + received.astype(F32)).astype(BF16)  34.8 us
    pallas_call x1, Pallas kernels, attention_forward(): pl.pallas_call(functools.partial(attention_forward_kernel, query_blocks(c...  31.1 us
    pallas_call x1, Pallas kernels, attention_backward(): pl.pallas_call(functools.partial(attention_backward_kernel, query_blocks(...  28.8 us
    unnamed x82, local copies, waits for them, and re-layouts  24.3 us
  transfers between devices with their start and end apart: 72, of which 26 were waited for; matrix products, arithmetic and copies ran while one was open for 27% of the time, Pallas kernels for 29%

profile of v3, /device:TPU:0, one launch (start us, length us, event | category | flops | bytes accessed | tf_op | source)
XLA Modules:
  0.0 798.1 jit_solution(102411450748444752)
XLA Ops:
  7.3 6.3 concatenate.36
  24.1 12.1 %collective-permute-done.1 = bf16[2,128,1088]{1,2,0:T(8,128)(2,1)} collective-permute-done((bf16[2,128,1088]{1,2,0:T(8,128)(2,1)}, bf16[2,128,1088]{1,2,0:T(8,128)(2,1)}, u32[]{:S(2)}, u32[]{:S(2)}) %collective-permute-start.1) | collective-permute-done | bytes 557088 | tf_op jit(solution)/shard_map/ppermute | solution.py:391
  38.9 7.7 collective-permute-done.2
  49.7 5.1 all-gather.7.cloned.1.call-done
  61.0 7.3 collective-permute-done.3
  68.2 11.0 %collective-permute-done.4 = bf16[3,144,1088]{2,1,0:T(8,128)(2,1)S(1)} collective-permute-done((bf16[3,144,1088]{2,1,0:T(8,128)(2,1)S(1)}, bf16[3,144,1088]{2,1,0:T(8,128)(2,1)S(1)}, u32[]{:S(2)}, u32[]{:S(2)}) %collective-permute-start.4) | collective-permute-done | bytes 940064 | tf_op jit(solution)/shard_map/ppermute | solution.py:391
  86.5 4.6 all-gather.9.cloned.1.call-done
  91.1 8.1 %collective-permute-done.5.refs_2_ = bf16[2,1,144,1088]{3,2,1,0:T(8,128)(2,1)} collective-permute-done((bf16[2,1,144,1088]{3,2,1,0:T(8,128)(2,1)}, bf16[2,1,144,1088]{3,2,1,0:T(8,128)(2,1)}, u32[]{:S(2)}, u32[]{:S(2)}) %collective-permute-start.5) | collective-permute-done | bytes 626720 | tf_op jit(solution)/shard_map/ppermute | solution.py:391
  99.2 25.4 %collective-permute-done.6.refs_3_ = bf16[2,3,144,1088]{3,2,1,0:T(8,128)(2,1)} collective-permute-done((bf16[2,3,144,1088]{3,2,1,0:T(8,128)(2,1)}, bf16[2,3,144,1088]{3,2,1,0:T(8,128)(2,1)}, u32[]{:S(2)}, u32[]{:S(2)}) %collective-permute-start.6) | collective-permute-done | bytes 1880096 | tf_op jit(solution)/shard_map/ppermute | solution.py:391
  130.7 5.9 collective-permute-done.11
  136.6 10.6 %collective-permute-done.12 = bf16[3,144,1088]{2,1,0:T(8,128)(2,1)S(1)} collective-permute-done((bf16[3,144,1088]{2,1,0:T(8,128)(2,1)S(1)}, bf16[3,144,1088]{2,1,0:T(8,128)(2,1)S(1)}, u32[]{:S(2)}, u32[]{:S(2)}) %collective-permute-start.12) | collective-permute-done | bytes 940064 | tf_op jit(solution)/shard_map/ppermute | solution.py:391
  155.0 7.8 all-gather.11.cloned.1.call-done
  165.4 26.2 %collective-permute-done.14.refs_3_ = bf16[2,3,144,1088]{3,2,1,0:T(8,128)(2,1)} collective-permute-done((bf16[2,3,144,1088]{3,2,1,0:T(8,128)(2,1)S(1)}, bf16[2,3,144,1088]{3,2,1,0:T(8,128)(2,1)}, u32[]{:S(2)}, u32[]{:S(2)}) %collective-permute-start.14) | collective-permute-done | bytes 1880096 | tf_op jit(solution)/shard_map/ppermute | solution.py:391
  202.5 8.8 %shard_map.271 = bf16[4,4,272,1088]{3,2,1,0:T(8,128)(2,1)} custom-call(s32[3]{0:T(128)} %pad_add_fusion.here_ref, bf16[2,1,144,1088]{3,2,1,0:T(8,128)(2,1)} %pad_maximum_fusion.9.refs_0_, bf16[2,3,144,1088]{3,2,1,0:T(8,128)(2,1)} %pad_maximum_fusion.3.refs_1_, bf16[2,1,144,1088]{3,2,1,0:T(8,128)(2,1)} %collective-permute-done.5.refs_2_, ...), custom_call_target="tpu_custom_call" | custom-call | bytes 18939904 | tf_op jit(solution)/shard_map/pallas_call | solution.py:472
  218.0 16.9 %shard_map.272 = (bf16[3,1024,1088]{2,1,0:T(8,128)(2,1)}, bf16[1024,1088]{1,0:T(8,128)(2,1)}) custom-call(bf16[1024,1088]{1,0:T(8,128)(2,1)} %bitcast.217, bf16[4,1088,1088]{2,1,0:T(8,128)(2,1)} %bitcast.205, f32[8,1088]{1,0:T(8,128)} %reshape.322.small_ref), custom_call_target="tpu_custom_call" | custom-call | flops 10909384704 | bytes 20645888 | tf_op jit(solution)/shard_map/pallas_call | solution.py:372
  237.5 31.1 %shard_map.273 = (bf16[4,2,128,1088]{3,2,1,0:T(8,128)(2,1)}, f32[2,9,8,512]{3,2,1,0:T(8,128)}) custom-call(s32[4]{0:T(128)} %broadcast_xor_fusion.order_ref, bf16[3,4,2,128,1088]{4,3,2,1,0:T(8,128)(2,1)} %bitcast.259, bf16[3,4,2,128,1088]{4,3,2,1,0:T(8,128)(2,1)} %bitcast.260, bf16[3,4,2,128,1088]{4,3,2,1,0:T(8,128)(2,1)} %bitcast.261), custom_call_target="tpu_custom_call" | custom-call | flops 9663676416 | bytes 8912896 | tf_op jit(solution)/shard_map/pallas_call | solution.py:166
  268.5 8.5 %shard_map.274 = (f32[1024,1088]{1,0:T(8,128)}, bf16[1024,1088]{1,0:T(8,128)(2,1)}) custom-call(bf16[1024,1088]{1,0:T(8,128)(2,1)} %bitcast.218, bf16[1024,1088]{1,0:T(8,128)(2,1)} %bitcast.238, bf16[4,1088,1088]{2,1,0:T(8,128)(2,1)} %bitcast.206, f32[8,1088]{1,0:T(8,128)} %reshape.322.small_ref), custom_call_target="tpu_custom_call" | custom-call | flops 3636461568 | bytes 20645888 | tf_op jit(solution)/shard_map/pallas_call | solution.py:372
  277.7 8.7 %shard_map.275 = bf16[4,4,272,1088]{3,2,1,0:T(8,128)(2,1)} custom-call(s32[3]{0:T(128)} %pad_add_fusion.here_ref, bf16[2,1,144,1088]{3,2,1,0:T(8,128)(2,1)} %copy-done.11, bf16[2,3,144,1088]{3,2,1,0:T(8,128)(2,1)} %copy-done.9, bf16[2,1,144,1088]{3,2,1,0:T(8,128)(2,1)} %copy-done.25, bf16[2,3,144,1088]{3,2,1,0:T(8,128)(2,1)} %collective-permute-done.14.refs_3_, ...), custom_call_target="tpu_custom_call" | custom-call | bytes 18939904 | tf_op jit(solution)/shard_map/pallas_call | solution.py:472
  289.9 27.8 %shard_map.276 = (bf16[4,1024,1088]{2,1,0:T(8,128)(2,1)}, bf16[4,1024,1088]{2,1,0:T(8,128)(2,1)}) custom-call(bf16[1024,1088]{1,0:T(8,128)(2,1)} %get-tuple-element.60.low_ref, bf16[4,1088,1088]{2,1,0:T(8,128)(2,1)} %bitcast.210, f32[4,1,1088]{2,1,0:T(1,128)} %reshape.326.bias_ref), custom_call_target="tpu_custom_call" | custom-call | flops 14545846272 | bytes 29541376 | tf_op jit(solution)/shard_map/pallas_call | solution.py:372
  322.5 14.4 %convolution_convert_fusion.1 = bf16[4,1088,1088]{2,1,0:T(8,128)(2,1)S(1)} fusion(bf16[4,1024,1088]{2,1,0:T(8,128)(2,1)} %get-tuple-element.66.act_ref, bf16[1024,1088,1]{1,0,2:T(8,128)(2,1)S(1)} %bitcast.235), kind=kOutput, calls=%fused_computation.1 | convolution fusion | flops 9701965824 | bytes 20611072 | tf_op jit(solution)/shard_map/ctx,td->cxd/dot_general | solution.py:658
  341.4 8.4 %copy.167 = bf16[4,4,272,1088]{3,2,0,1:T(8,128)(2,1)} copy(bf16[4,4,272,1088]{3,2,1,0:T(8,128)(2,1)} %bitcast.209) | data formatting | bytes 18939904 | tf_op jit(solution)/shard_map/reshape | solution.py:656
  349.9 7.0 broadcast_select_fusion.2
  356.9 8.6 %shard_map.277 = bf16[4,4,272,1088]{3,2,1,0:T(8,128)(2,1)} custom-call(s32[3]{0:T(128)} %pad_add_fusion.here_ref, bf16[2,1,144,1088]{3,2,1,0:T(8,128)(2,1)} %copy-done.12, bf16[2,3,144,1088]{3,2,1,0:T(8,128)(2,1)} %pad_maximum_fusion.5.refs_1_, bf16[2,1,144,1088]{3,2,1,0:T(8,128)(2,1)} %collective-permute-done.21.refs_2_, ...), custom_call_target="tpu_custom_call" | custom-call | bytes 18939904 | tf_op jit(solution)/shard_map/pallas_call | solution.py:472
  365.5 20.2 %shard_map.278 = bf16[1024,1088]{1,0:T(8,128)(2,1)} custom-call(f32[1024,1088]{1,0:T(8,128)} %get-tuple-element.59.middle_ref, bf16[4,1024,1088]{2,1,0:T(8,128)(2,1)} %get-tuple-element.66.act_ref, bf16[4,1088,1088]{2,1,0:T(8,128)(2,1)} %bitcast.212, f32[8,1088]{1,0:T(8,128)} %reshape.322.small_ref), custom_call_target="tpu_custom_call" | custom-call | flops 14545846272 | bytes 25102336 | tf_op jit(solution)/shard_map/pallas_call | solution.py:372
  391.7 20.9 %shard_map.279 = (bf16[4,1024,1088]{2,1,0:T(8,128)(2,1)}, f32[8,1088]{1,0:T(8,128)}) custom-call(bf16[1024,1088]{1,0:T(8,128)(2,1)} %bitcast.236, bf16[4,1024,1088]{2,1,0:T(8,128)(2,1)} %get-tuple-element.72.slope_ref, bf16[4,1088,1088]{2,1,0:T(8,128)(2,1)} %bitcast.213, bf16[16,128]{1,0:T(8,128)(2,1)} %slice.492.refs_0_), custom_call_target="tpu_custom_call" | custom-call | flops 14545846272 | bytes 29562880 | tf_op jit(solution)/shard_map/pallas_call | solution.py:372
  412.7 13.4 %convolution_convert_fusion = bf16[4,1088,1088]{1,2,0:T(8,128)(2,1)S(1)} fusion(bf16[4,1024,1088]{2,1,0:T(8,128)(2,1)} %get-tuple-element.73.hidden_ref, bf16[1024,1088]{1,0:T(8,128)(2,1)S(1)} %copy-done.33), kind=kOutput, calls=%fused_computation | convolution fusion | flops 9701965824 | bytes 20611072 | tf_op jit(solution)/shard_map/td,ctx->cdx/dot_general | solution.py:669
  440.9 6.6 add_convert_fusion.2
  451.0 27.0 %shard_map.280 = (f32[1024,1088]{1,0:T(8,128)}, bf16[1024,1088]{1,0:T(8,128)(2,1)}, bf16[1024,1088]{1,0:T(8,128)(2,1)}, f32[8,1088]{1,0:T(8,128)}) custom-call(bf16[4,1024,1088]{2,1,0:T(8,128)(2,1)} %get-tuple-element.73.hidden_ref, bf16[1024,1088]{1,0:T(8,128)(2,1)} %bitcast.237, f32[1024,1088]{1,0:T(8,128)} %get-tuple-element.59.middle_ref, ...), custom_call_target="tpu_custom_call" | custom-call | flops 18182307840 | bytes 43528192 | tf_op jit(solution)/shard_map/pallas_call | solution.py:372
  478.0 7.1 convolution_convert_fusion.3
  486.7 4.6 add_convert_fusion.1
  506.4 28.8 %shard_map.281 = bf16[3,4,2,128,1088]{4,3,2,1,0:T(8,128)(2,1)} custom-call(s32[4]{0:T(128)} %broadcast_xor_fusion.order_ref, bf16[3,4,2,128,1088]{4,3,2,1,0:T(8,128)(2,1)} %bitcast.262, bf16[3,4,2,128,1088]{4,3,2,1,0:T(8,128)(2,1)} %bitcast.263, bf16[3,4,2,128,1088]{4,3,2,1,0:T(8,128)(2,1)} %bitcast.264, bf16[4,2,128,1088]{3,2,1,0:T(8,128)(2,1)} %get-tuple-element.58.o_ref, ...), custom_call_target="tpu_custom_call" | custom-call | flops 12079595520 | bytes 17825792 | tf_op jit(solution)/shard_map/pallas_call | solution.py:198
  535.2 12.3 %convolution_convert_fusion.2 = bf16[3,1088,1088]{1,2,0:T(8,128)(2,1)S(1)} fusion(bf16[3,1024,1088]{2,1,0:T(8,128)(2,1)} %bitcast.265, bf16[1024,1088]{1,0:T(8,128)(2,1)S(1)} %copy-done.35), kind=kOutput, calls=%fused_computation.2 | convolution fusion | flops 7276474368 | bytes 16015360 | tf_op jit(solution)/shard_map/td,ctx->cdx/dot_general | solution.py:689
  563.8 18.6 %shard_map.282 = (bf16[1024,1088]{1,0:T(8,128)(2,1)}, f32[8,1088]{1,0:T(8,128)}) custom-call(bf16[3,1024,1088]{2,1,0:T(8,128)(2,1)} %bitcast.266, f32[1024,1088]{1,0:T(8,128)} %get-tuple-element.78.grad_middle_ref, bf16[1024,1088]{1,0:T(8,128)(2,1)} %bitcast.219, bf16[4,1088,1088]{2,1,0:T(8,128)(2,1)} %bitcast.208, f32[8,1088]{1,0:T(8,128)} %reshape.322.small_ref, ...), custom_call_target="tpu_custom_call" | custom-call | flops 10909384704 | bytes 25157632 | tf_op jit(solution)/shard_map/pallas_call | solution.py:372
  589.5 6.1 add_convert_fusion
  600.7 11.6 %collective-permute-done.56 = bf16[3,144,1088]{2,1,0:T(8,128)(2,1)S(1)} collective-permute-done((bf16[3,144,1088]{2,1,0:T(8,128)(2,1)S(1)}, bf16[3,144,1088]{2,1,0:T(8,128)(2,1)S(1)}, u32[]{:S(2)}, u32[]{:S(2)}) %collective-permute-start.56) | collective-permute-done | bytes 940064 | tf_op jit(solution)/shard_map/ppermute | solution.py:391
  614.0 15.1 %collective-permute-done.46 = bf16[2,1,144,1088]{3,2,1,0:T(8,128)(2,1)S(1)} collective-permute-done((bf16[2,1,144,1088]{3,2,1,0:T(8,128)(2,1)S(1)}, bf16[2,1,144,1088]{3,2,1,0:T(8,128)(2,1)S(1)}, u32[]{:S(2)}, u32[]{:S(2)}) %collective-permute-start.46) | collective-permute-done | bytes 626720 | tf_op jit(solution)/shard_map/ppermute | solution.py:391
  629.2 12.0 %collective-permute-done.45 = bf16[2,3,144,1088]{3,2,1,0:T(8,128)(2,1)} collective-permute-done((bf16[2,3,144,1088]{3,2,1,0:T(8,128)(2,1)S(1)}, bf16[2,3,144,1088]{3,2,1,0:T(8,128)(2,1)}, u32[]{:S(2)}, u32[]{:S(2)}) %collective-permute-start.45) | collective-permute-done | bytes 1880096 | tf_op jit(solution)/shard_map/ppermute | solution.py:391
  649.5 5.5 collective-permute-done.48
  655.1 15.0 %collective-permute-done.47 = bf16[3,144,1088]{2,1,0:T(8,128)(2,1)S(1)} collective-permute-done((bf16[3,144,1088]{2,1,0:T(8,128)(2,1)S(1)}, bf16[3,144,1088]{2,1,0:T(8,128)(2,1)S(1)}, u32[]{:S(2)}, u32[]{:S(2)}) %collective-permute-start.47) | collective-permute-done | bytes 940064 | tf_op jit(solution)/shard_map/ppermute | solution.py:391
  696.7 5.4 collective-permute-done.58
  712.8 12.0 %collective-permute-done.63.refs_1_ = bf16[2,1,144,1088]{3,2,1,0:T(8,128)(2,1)} collective-permute-done((bf16[2,1,144,1088]{3,2,1,0:T(8,128)(2,1)S(1)}, bf16[2,1,144,1088]{3,2,1,0:T(8,128)(2,1)}, u32[]{:S(2)}, u32[]{:S(2)}) %collective-permute-start.63) | collective-permute-done | bytes 626720 | tf_op jit(solution)/shard_map/ppermute | solution.py:391
  725.3 13.2 %collective-permute-done.59.refs_1_ = bf16[2,1,144,1088]{3,2,1,0:T(8,128)(2,1)S(1)} collective-permute-done((bf16[2,1,144,1088]{3,2,1,0:T(8,128)(2,1)S(1)}, bf16[2,1,144,1088]{3,2,1,0:T(8,128)(2,1)S(1)}, u32[]{:S(2)}, u32[]{:S(2)}) %collective-permute-start.59) | collective-permute-done | bytes 626720 | tf_op jit(solution)/shard_map/ppermute | solution.py:391
  742.6 6.0 copy.145
  748.5 4.3 shard_map.285
  752.9 4.4 shard_map.284
  763.3 5.8 concatenate.46
  769.1 5.2 collective-permute-done.53.refs_1_
  778.1 4.4 shard_map.283
  (346 shorter events, 219.0 us)
Async XLA Ops:
  7.2 47.6 %all-gather.7.cloned.1.call-start = ((), (), s32[]{:S(2)}) async-start(), calls=%async_computation.6 | async-start | bytes 1843200 | tf_op jit(solution)/shard_map/all_gather | solution.py:584
  16.3 74.8 %all-gather.9.cloned.1.call-start = ((), (), s32[]{:S(2)}) async-start(), calls=%async_computation.7 | async-start | bytes 1658880 | tf_op jit(solution)/shard_map/all_gather | solution.py:584
  22.4 24.1 %collective-permute-start.2 = (bf16[2,128,1088]{1,2,0:T(8,128)(2,1)}, bf16[2,128,1088]{1,2,0:T(8,128)(2,1)}, u32[]{:S(2)}, u32[]{:S(2)}) collective-permute-start(bf16[2,128,1088]{1,2,0:T(8,128)(2,1)} %get-tuple-element.172), channel_id=1, source_target_pairs={{0,3},{1,2},{2,1},{3,0},{4,7},{5,6},{6,5},{7,4},{8,11},{9,10},{10,... | collective-permute-start | bytes 1671176 | tf_op jit(solution)/shard_map/ppermute | solution.py:391
  60.9 101.9 %all-gather.11.cloned.1.call-start = ((), (), s32[]{:S(2)}) async-start(), calls=%async_computation.8 | async-start | bytes 1658880 | tf_op jit(solution)/shard_map/all_gather | solution.py:584
  80.7 43.8 %collective-permute-start.6 = (bf16[2,3,144,1088]{3,2,1,0:T(8,128)(2,1)}, bf16[2,3,144,1088]{3,2,1,0:T(8,128)(2,1)}, u32[]{:S(2)}, u32[]{:S(2)}) collective-permute-start(bf16[2,3,144,1088]{3,2,1,0:T(8,128)(2,1)} %pad_maximum_fusion.3.refs_1_), channel_id=1, source_target_pairs={{0,4},{4,0},{1,5},{5,1},{2,6},{6,2},{3,7},{7,3},{8,12},{12,8},{9,1... | collective-permute-start | bytes 5640200 | tf_op jit(solution)/shard_map/ppermute | solution.py:391
  130.7 554.1 %reduce-scatter.8.cloned.1.call-start = ((), (), s32[]{:S(2)}) async-start(), calls=%async_computation.5 | async-start | bytes 1658880 | tf_op jit(solution)/shard_map/reduce_scatter | solution.py:644
  149.7 42.0 %collective-permute-start.14 = (bf16[2,3,144,1088]{3,2,1,0:T(8,128)(2,1)S(1)}, bf16[2,3,144,1088]{3,2,1,0:T(8,128)(2,1)}, u32[]{:S(2)}, u32[]{:S(2)}) collective-permute-start(bf16[2,3,144,1088]{3,2,1,0:T(8,128)(2,1)S(1)} %pad_maximum_fusion.4.refs_1_), channel_id=1, source_target_pairs={{0,4},{4,0},{1,5},{5,1},{2,6},{6,2},{3,7},{7,3},{8,12},{12,8},{9,1... | collective-permute-start | bytes 5640200 | tf_op jit(solution)/shard_map/ppermute | solution.py:391
  153.8 48.2 %collective-permute-start.8 = (bf16[2,3,144,1088]{3,2,1,0:T(8,128)(2,1)}, bf16[2,3,144,1088]{3,2,1,0:T(8,128)(2,1)}, u32[]{:S(2)}, u32[]{:S(2)}) collective-permute-start(bf16[2,3,144,1088]{3,2,1,0:T(8,128)(2,1)} %pad_maximum_fusion.3.refs_1_), channel_id=1, source_target_pairs={{0,1},{1,0},{2,3},{3,2},{4,5},{5,4},{6,7},{7,6},{8,9},{9,8},{10,11... | collective-permute-start | bytes 5640200 | tf_op jit(solution)/shard_map/ppermute | solution.py:391
  153.8 48.4 %collective-permute-start.10 = (bf16[2,3,144,1088]{3,2,1,0:T(8,128)(2,1)}, bf16[2,3,144,1088]{3,2,1,0:T(8,128)(2,1)}, u32[]{:S(2)}, u32[]{:S(2)}) collective-permute-start(bf16[2,3,144,1088]{3,2,1,0:T(8,128)(2,1)} %collective-permute-done.6.refs_3_), channel_id=1, source_target_pairs={{0,1},{1,0},{2,3},{3,2},{4,5},{5,4},{6,7},{7,6},{8,9},{9,8},{10,11... | collective-permute-start | bytes 5640200 | tf_op jit(solution)/shard_map/ppermute | solution.py:391
  155.0 42.8 %collective-permute-start.7 = (bf16[2,1,144,1088]{3,2,1,0:T(8,128)(2,1)}, bf16[2,1,144,1088]{3,2,1,0:T(8,128)(2,1)}, u32[]{:S(2)}, u32[]{:S(2)}) collective-permute-start(bf16[2,1,144,1088]{3,2,1,0:T(8,128)(2,1)} %pad_maximum_fusion.9.refs_0_), channel_id=1, source_target_pairs={{0,1},{1,0},{2,3},{3,2},{4,5},{5,4},{6,7},{7,6},{8,9},{9,8},{10,11... | collective-permute-start | bytes 1880072 | tf_op jit(solution)/shard_map/ppermute | solution.py:391
  201.7 34.2 %collective-permute-start.15 = (bf16[2,1,144,1088]{3,2,1,0:T(8,128)(2,1)}, bf16[2,1,144,1088]{3,2,1,0:T(8,128)(2,1)S(1)}, u32[]{:S(2)}, u32[]{:S(2)}) collective-permute-start(bf16[2,1,144,1088]{3,2,1,0:T(8,128)(2,1)} %copy-done.11), channel_id=1, source_target_pairs={{0,1},{1,0},{2,3},{3,2},{4,5},{5,4},{6,7},{7,6},{8,9},{9,8},{10,11... | collective-permute-start | bytes 1880072 | tf_op jit(solution)/shard_map/ppermute | solution.py:391
  202.0 75.2 %collective-permute-start.16 = (bf16[2,3,144,1088]{3,2,1,0:T(8,128)(2,1)S(1)}, bf16[2,3,144,1088]{3,2,1,0:T(8,128)(2,1)}, u32[]{:S(2)}, u32[]{:S(2)}) collective-permute-start(bf16[2,3,144,1088]{3,2,1,0:T(8,128)(2,1)S(1)} %pad_maximum_fusion.4.refs_1_), channel_id=1, source_target_pairs={{0,1},{1,0},{2,3},{3,2},{4,5},{5,4},{6,7},{7,6},{8,9},{9,8},{10,11... | collective-permute-start | bytes 5640200 | tf_op jit(solution)/shard_map/ppermute | solution.py:391
  202.3 74.8 %collective-permute-start.17 = (bf16[2,1,144,1088]{3,2,1,0:T(8,128)(2,1)}, bf16[2,1,144,1088]{3,2,1,0:T(8,128)(2,1)}, u32[]{:S(2)}, u32[]{:S(2)}) collective-permute-start(bf16[2,1,144,1088]{3,2,1,0:T(8,128)(2,1)} %copy-done.25), channel_id=1, source_target_pairs={{0,1},{1,0},{2,3},{3,2},{4,5},{5,4},{6,7},{7,6},{8,9},{9,8},{10,11... | collective-permute-start | bytes 1880072 | tf_op jit(solution)/shard_map/ppermute | solution.py:391
  211.3 66.4 %collective-permute-start.18 = (bf16[2,3,144,1088]{3,2,1,0:T(8,128)(2,1)}, bf16[2,3,144,1088]{3,2,1,0:T(8,128)(2,1)}, u32[]{:S(2)}, u32[]{:S(2)}) collective-permute-start(bf16[2,3,144,1088]{3,2,1,0:T(8,128)(2,1)} %collective-permute-done.14.refs_3_), channel_id=1, source_target_pairs={{0,1},{1,0},{2,3},{3,2},{4,5},{5,4},{6,7},{7,6},{8,9},{9,8},{10,11... | collective-permute-start | bytes 5640200 | tf_op jit(solution)/shard_map/ppermute | solution.py:391
  216.5 69.8 %collective-permute-start.22 = (bf16[2,3,144,1088]{3,2,1,0:T(8,128)(2,1)}, bf16[2,3,144,1088]{3,2,1,0:T(8,128)(2,1)S(1)}, u32[]{:S(2)}, u32[]{:S(2)}) collective-permute-start(bf16[2,3,144,1088]{3,2,1,0:T(8,128)(2,1)} %pad_maximum_fusion.5.refs_1_), channel_id=1, source_target_pairs={{0,4},{4,0},{1,5},{5,1},{2,6},{6,2},{3,7},{7,3},{8,12},{12,8},{9,1... | collective-permute-start | bytes 5640200 | tf_op jit(solution)/shard_map/ppermute | solution.py:391
  235.9 50.4 %collective-permute-start.21 = (bf16[2,1,144,1088]{3,2,1,0:T(8,128)(2,1)S(1)}, bf16[2,1,144,1088]{3,2,1,0:T(8,128)(2,1)}, u32[]{:S(2)}, u32[]{:S(2)}) collective-permute-start(bf16[2,1,144,1088]{3,2,1,0:T(8,128)(2,1)S(1)} %pad_maximum_fusion.11.refs_0_), channel_id=1, source_target_pairs={{0,2},{1,3},{2,0},{3,1},{4,6},{5,7},{6,4},{7,5},{8,10},{9,11},{10,... | collective-permute-start | bytes 1880072 | tf_op jit(solution)/shard_map/ppermute | solution.py:391
  277.1 79.8 %collective-permute-start.23 = (bf16[2,1,144,1088]{3,2,1,0:T(8,128)(2,1)S(1)}, bf16[2,1,144,1088]{3,2,1,0:T(8,128)(2,1)}, u32[]{:S(2)}, u32[]{:S(2)}) collective-permute-start(bf16[2,1,144,1088]{3,2,1,0:T(8,128)(2,1)S(1)} %pad_maximum_fusion.11.refs_0_), channel_id=1, source_target_pairs={{0,1},{1,0},{2,3},{3,2},{4,5},{5,4},{6,7},{7,6},{8,9},{9,8},{10,11... | collective-permute-start | bytes 1880072 | tf_op jit(solution)/shard_map/ppermute | solution.py:391
  277.2 79.7 %collective-permute-start.24 = (bf16[2,3,144,1088]{3,2,1,0:T(8,128)(2,1)}, bf16[2,3,144,1088]{3,2,1,0:T(8,128)(2,1)}, u32[]{:S(2)}, u32[]{:S(2)}) collective-permute-start(bf16[2,3,144,1088]{3,2,1,0:T(8,128)(2,1)} %pad_maximum_fusion.5.refs_1_), channel_id=1, source_target_pairs={{0,1},{1,0},{2,3},{3,2},{4,5},{5,4},{6,7},{7,6},{8,9},{9,8},{10,11... | collective-permute-start | bytes 5640200 | tf_op jit(solution)/shard_map/ppermute | solution.py:391
  287.7 30.3 %collective-permute-start.31 = (bf16[2,128,1088]{1,2,0:T(8,128)(2,1)}, bf16[2,128,1088]{1,2,0:T(8,128)(2,1)S(1)}, u32[]{:S(2)}, u32[]{:S(2)}) collective-permute-start(bf16[2,128,1088]{1,2,0:T(8,128)(2,1)} %get-tuple-element.166), channel_id=1, source_target_pairs={{0,2},{1,3},{2,0},{3,1},{4,6},{5,7},{6,4},{7,5},{8,10},{9,11},{10,... | collective-permute-start | bytes 1671176 | tf_op jit(solution)/shard_map/ppermute | solution.py:391
  288.3 30.1 %collective-permute-start.30 = (bf16[2,128,1088]{1,2,0:T(8,128)(2,1)}, bf16[2,128,1088]{1,2,0:T(8,128)(2,1)S(1)}, u32[]{:S(2)}, u32[]{:S(2)}) collective-permute-start(bf16[2,128,1088]{1,2,0:T(8,128)(2,1)} %get-tuple-element.167), channel_id=1, source_target_pairs={{0,1},{1,0},{2,3},{3,2},{4,5},{5,4},{6,7},{7,6},{8,9},{9,8},{10,11... | collective-permute-start | bytes 1671176 | tf_op jit(solution)/shard_map/ppermute | solution.py:391
  288.3 31.0 %collective-permute-start.32 = (bf16[2,128,1088]{1,2,0:T(8,128)(2,1)}, bf16[2,128,1088]{1,2,0:T(8,128)(2,1)}, u32[]{:S(2)}, u32[]{:S(2)}) collective-permute-start(bf16[2,128,1088]{1,2,0:T(8,128)(2,1)} %get-tuple-element.168), channel_id=1, source_target_pairs={{0,3},{1,2},{2,1},{3,0},{4,7},{5,6},{6,5},{7,4},{8,11},{9,10},{10,... | collective-permute-start | bytes 1671176 | tf_op jit(solution)/shard_map/ppermute | solution.py:391
  318.0 38.8 %collective-permute-start.25 = (bf16[2,1,144,1088]{3,2,1,0:T(8,128)(2,1)}, bf16[2,1,144,1088]{3,2,1,0:T(8,128)(2,1)}, u32[]{:S(2)}, u32[]{:S(2)}) collective-permute-start(bf16[2,1,144,1088]{3,2,1,0:T(8,128)(2,1)} %collective-permute-done.21.refs_2_), channel_id=1, source_target_pairs={{0,1},{1,0},{2,3},{3,2},{4,5},{5,4},{6,7},{7,6},{8,9},{9,8},{10,11... | collective-permute-start | bytes 1880072 | tf_op jit(solution)/shard_map/ppermute | solution.py:391
  318.4 38.4 %collective-permute-start.26 = (bf16[2,3,144,1088]{3,2,1,0:T(8,128)(2,1)}, bf16[2,3,144,1088]{3,2,1,0:T(8,128)(2,1)}, u32[]{:S(2)}, u32[]{:S(2)}) collective-permute-start(bf16[2,3,144,1088]{3,2,1,0:T(8,128)(2,1)} %copy-done.21), channel_id=1, source_target_pairs={{0,1},{1,0},{2,3},{3,2},{4,5},{5,4},{6,7},{7,6},{8,9},{9,8},{10,11... | collective-permute-start | bytes 5640200 | tf_op jit(solution)/shard_map/ppermute | solution.py:391
  356.8 82.1 %collective-permute-start.33 = (bf16[4,4,144,1088]{3,2,1,0:T(8,128)(2,1)}, bf16[4,4,144,1088]{3,2,1,0:T(8,128)(2,1)}, u32[]{:S(2)}, u32[]{:S(2)}) collective-permute-start(bf16[4,4,144,1088]{3,2,1,0:T(8,128)(2,1)} %broadcast_select_fusion.2), channel_id=1, source_target_pairs={{0,1},{1,0},{2,3},{3,2},{4,5},{5,4},{6,7},{7,6},{8,9},{9,8},{10,11... | collective-permute-start | bytes 15040520 | tf_op jit(solution)/shard_map/ppermute | solution.py:391
  389.9 44.0 %collective-permute-start.27 = (bf16[2,128,1088]{1,2,0:T(8,128)(2,1)}, bf16[2,128,1088]{1,2,0:T(8,128)(2,1)}, u32[]{:S(2)}, u32[]{:S(2)}) collective-permute-start(bf16[2,128,1088]{1,2,0:T(8,128)(2,1)} %copy.116), channel_id=1, source_target_pairs={{0,1},{1,0},{2,3},{3,2},{4,5},{5,4},{6,7},{7,6},{8,9},{9,8},{10,11... | collective-permute-start | bytes 1671176 | tf_op jit(solution)/shard_map/ppermute | solution.py:391
  390.4 44.9 %collective-permute-start.28 = (bf16[2,128,1088]{1,2,0:T(8,128)(2,1)S(1)}, bf16[2,128,1088]{1,2,0:T(8,128)(2,1)}, u32[]{:S(2)}, u32[]{:S(2)}) collective-permute-start(bf16[2,128,1088]{1,2,0:T(8,128)(2,1)S(1)} %copy.118), channel_id=1, source_target_pairs={{0,2},{1,3},{2,0},{3,1},{4,6},{5,7},{6,4},{7,5},{8,10},{9,11},{10,... | collective-permute-start | bytes 1671176 | tf_op jit(solution)/shard_map/ppermute | solution.py:391
  390.9 45.7 %collective-permute-start.29 = (bf16[2,128,1088]{1,2,0:T(8,128)(2,1)}, bf16[2,128,1088]{1,2,0:T(8,128)(2,1)}, u32[]{:S(2)}, u32[]{:S(2)}) collective-permute-start(bf16[2,128,1088]{1,2,0:T(8,128)(2,1)} %copy.120), channel_id=1, source_target_pairs={{0,3},{1,2},{2,1},{3,0},{4,7},{5,6},{6,5},{7,4},{8,11},{9,10},{10,... | collective-permute-start | bytes 1671176 | tf_op jit(solution)/shard_map/ppermute | solution.py:391
  432.8 52.3 %collective-permute-start.36 = (bf16[4,4,144,1088]{3,2,1,0:T(8,128)(2,1)}, bf16[4,4,144,1088]{3,2,1,0:T(8,128)(2,1)}, u32[]{:S(2)}, u32[]{:S(2)}) collective-permute-start(bf16[4,4,144,1088]{3,2,1,0:T(8,128)(2,1)} %broadcast_select_fusion.1), channel_id=1, source_target_pairs={{0,1},{1,0},{2,3},{3,2},{4,5},{5,4},{6,7},{7,6},{8,9},{9,8},{10,11... | collective-permute-start | bytes 15040520 | tf_op jit(solution)/shard_map/ppermute | solution.py:391
  448.4 48.3 %collective-permute-start.35 = (bf16[2,1,144,1088]{3,2,1,0:T(8,128)(2,1)}, bf16[2,1,144,1088]{3,2,1,0:T(8,128)(2,1)S(1)}, u32[]{:S(2)}, u32[]{:S(2)}) collective-permute-start(bf16[2,1,144,1088]{3,2,1,0:T(8,128)(2,1)} %broadcast_select_fusion.8), channel_id=1, source_target_pairs={{0,2},{1,3},{2,0},{3,1},{4,6},{5,7},{6,4},{7,5},{8,10},{9,11},{10,... | collective-permute-start | bytes 1880072 | tf_op jit(solution)/shard_map/ppermute | solution.py:391
  450.5 47.1 %collective-permute-start.34 = (bf16[2,3,144,1088]{3,2,1,0:T(8,128)(2,1)}, bf16[2,3,144,1088]{3,2,1,0:T(8,128)(2,1)S(1)}, u32[]{:S(2)}, u32[]{:S(2)}) collective-permute-start(bf16[2,3,144,1088]{3,2,1,0:T(8,128)(2,1)} %broadcast_select_fusion.5), channel_id=1, source_target_pairs={{0,4},{4,0},{1,5},{5,1},{2,6},{6,2},{3,7},{7,3},{8,12},{12,8},{9,1... | collective-permute-start | bytes 5640200 | tf_op jit(solution)/shard_map/ppermute | solution.py:391
  492.3 65.8 %collective-permute-start.40 = (bf16[2,1,144,1088]{3,2,1,0:T(8,128)(2,1)}, bf16[2,1,144,1088]{3,2,1,0:T(8,128)(2,1)}, u32[]{:S(2)}, u32[]{:S(2)}) collective-permute-start(bf16[2,1,144,1088]{3,2,1,0:T(8,128)(2,1)} %broadcast_select_fusion.7), channel_id=1, source_target_pairs={{0,2},{1,3},{2,0},{3,1},{4,6},{5,7},{6,4},{7,5},{8,10},{9,11},{10,... | collective-permute-start | bytes 1880072 | tf_op jit(solution)/shard_map/ppermute | solution.py:391
  495.3 62.8 %collective-permute-start.39 = (bf16[2,3,144,1088]{3,2,1,0:T(8,128)(2,1)}, bf16[2,3,144,1088]{3,2,1,0:T(8,128)(2,1)}, u32[]{:S(2)}, u32[]{:S(2)}) collective-permute-start(bf16[2,3,144,1088]{3,2,1,0:T(8,128)(2,1)} %broadcast_select_fusion.4), channel_id=1, source_target_pairs={{0,4},{4,0},{1,5},{5,1},{2,6},{6,2},{3,7},{7,3},{8,12},{12,8},{9,1... | collective-permute-start | bytes 5640200 | tf_op jit(solution)/shard_map/ppermute | solution.py:391
  504.9 50.2 %collective-permute-start.38 = (bf16[1,144,1088]{2,1,0:T(8,128)(2,1)S(1)}, bf16[1,144,1088]{2,1,0:T(8,128)(2,1)S(1)}, u32[]{:S(2)}, u32[]{:S(2)}) collective-permute-start(bf16[1,144,1088]{2,1,0:T(8,128)(2,1)S(1)} %select_bitcast_fusion.5), channel_id=1, source_target_pairs={{0,4},{4,0},{1,5},{5,1},{2,6},{6,2},{3,7},{7,3},{8,12},{12,8},{9,1... | collective-permute-start | bytes 940040 | tf_op jit(solution)/shard_map/ppermute | solution.py:391
  505.6 50.2 %collective-permute-start.37 = (bf16[3,144,1088]{2,1,0:T(8,128)(2,1)S(1)}, bf16[3,144,1088]{2,1,0:T(8,128)(2,1)S(1)}, u32[]{:S(2)}, u32[]{:S(2)}) collective-permute-start(bf16[3,144,1088]{2,1,0:T(8,128)(2,1)S(1)} %select_bitcast_fusion.2), channel_id=1, source_target_pairs={{0,2},{1,3},{2,0},{3,1},{4,6},{5,7},{6,4},{7,5},{8,10},{9,11},{10,... | collective-permute-start | bytes 2820104 | tf_op jit(solution)/shard_map/ppermute | solution.py:391
  555.1 34.4 %collective-permute-start.44 = (bf16[4,4,144,1088]{3,2,1,0:T(8,128)(2,1)}, bf16[4,4,144,1088]{3,2,1,0:T(8,128)(2,1)}, u32[]{:S(2)}, u32[]{:S(2)}) collective-permute-start(bf16[4,4,144,1088]{3,2,1,0:T(8,128)(2,1)} %broadcast_select_fusion), channel_id=1, source_target_pairs={{0,1},{1,0},{2,3},{3,2},{4,5},{5,4},{6,7},{7,6},{8,9},{9,8},{10,11... | collective-permute-start | bytes 15040520 | tf_op jit(solution)/shard_map/ppermute | solution.py:391
  558.1 127.7 %reduce-scatter.6.cloned.1.call-start = ((), (), s32[]{:S(2)}) async-start(), calls=%async_computation.4 | async-start | bytes 1658880 | tf_op jit(solution)/shard_map/reduce_scatter | solution.py:644
  562.2 36.0 %collective-permute-start.57 = (bf16[1,144,1088]{2,1,0:T(8,128)(2,1)S(1)}, bf16[1,144,1088]{2,1,0:T(8,128)(2,1)}, u32[]{:S(2)}, u32[]{:S(2)}) collective-permute-start(bf16[1,144,1088]{2,1,0:T(8,128)(2,1)S(1)} %select_bitcast_fusion.3), channel_id=1, source_target_pairs={{0,4},{4,0},{1,5},{5,1},{2,6},{6,2},{3,7},{7,3},{8,12},{12,8},{9,1... | collective-permute-start | bytes 940040 | tf_op jit(solution)/shard_map/ppermute | solution.py:391
  587.5 24.9 %collective-permute-start.56 = (bf16[3,144,1088]{2,1,0:T(8,128)(2,1)S(1)}, bf16[3,144,1088]{2,1,0:T(8,128)(2,1)S(1)}, u32[]{:S(2)}, u32[]{:S(2)}) collective-permute-start(bf16[3,144,1088]{2,1,0:T(8,128)(2,1)S(1)} %select_bitcast_fusion), channel_id=1, source_target_pairs={{0,2},{1,3},{2,0},{3,1},{4,6},{5,7},{6,4},{7,5},{8,10},{9,11},{10,... | collective-permute-start | bytes 2820104 | tf_op jit(solution)/shard_map/ppermute | solution.py:391
  595.8 45.3 %collective-permute-start.45 = (bf16[2,3,144,1088]{3,2,1,0:T(8,128)(2,1)S(1)}, bf16[2,3,144,1088]{3,2,1,0:T(8,128)(2,1)}, u32[]{:S(2)}, u32[]{:S(2)}) collective-permute-start(bf16[2,3,144,1088]{3,2,1,0:T(8,128)(2,1)S(1)} %broadcast_select_fusion.3), channel_id=1, source_target_pairs={{0,4},{4,0},{1,5},{5,1},{2,6},{6,2},{3,7},{7,3},{8,12},{12,8},{9,1... | collective-permute-start | bytes 5640200 | tf_op jit(solution)/shard_map/ppermute | solution.py:391
  597.4 51.1 %collective-permute-start.51 = (bf16[4,16,1088]{2,1,0:T(8,128)(2,1)S(1)}, bf16[4,16,1088]{2,1,0:T(8,128)(2,1)}, u32[]{:S(2)}, u32[]{:S(2)}) collective-permute-start(bf16[4,16,1088]{2,1,0:T(8,128)(2,1)S(1)} %add_convert_fusion.10), channel_id=1, source_target_pairs={{0,2},{1,3},{2,0},{3,1},{4,6},{5,7},{6,4},{7,5},{8,10},{9,11},{10,... | collective-permute-start | bytes 417800 | tf_op jit(solution)/shard_map/ppermute | solution.py:391
  599.4 29.8 %collective-permute-start.46 = (bf16[2,1,144,1088]{3,2,1,0:T(8,128)(2,1)S(1)}, bf16[2,1,144,1088]{3,2,1,0:T(8,128)(2,1)S(1)}, u32[]{:S(2)}, u32[]{:S(2)}) collective-permute-start(bf16[2,1,144,1088]{3,2,1,0:T(8,128)(2,1)S(1)} %broadcast_select_fusion.6), channel_id=1, source_target_pairs={{0,2},{1,3},{2,0},{3,1},{4,6},{5,7},{6,4},{7,5},{8,10},{9,11},{10,... | collective-permute-start | bytes 1880072 | tf_op jit(solution)/shard_map/ppermute | solution.py:391
  614.0 124.6 %reduce-scatter.4.cloned.1.call-start = ((), (), s32[]{:S(2)}) async-start(), calls=%async_computation.3 | async-start | bytes 1843200 | tf_op jit(solution)/shard_map/reduce_scatter | solution.py:644
  683.8 26.0 %collective-permute-start.43 = (bf16[2,128,1088]{1,2,0:T(8,128)(2,1)}, bf16[2,128,1088]{1,2,0:T(8,128)(2,1)}, u32[]{:S(2)}, u32[]{:S(2)}) collective-permute-start(bf16[2,128,1088]{1,2,0:T(8,128)(2,1)} %copy.141), channel_id=1, source_target_pairs={{0,3},{1,2},{2,1},{3,0},{4,7},{5,6},{6,5},{7,4},{8,11},{9,10},{10,... | collective-permute-start | bytes 1671176 | tf_op jit(solution)/shard_map/ppermute | solution.py:391
  695.7 29.1 %collective-permute-start.63 = (bf16[2,1,144,1088]{3,2,1,0:T(8,128)(2,1)S(1)}, bf16[2,1,144,1088]{3,2,1,0:T(8,128)(2,1)}, u32[]{:S(2)}, u32[]{:S(2)}) collective-permute-start(bf16[2,1,144,1088]{3,2,1,0:T(8,128)(2,1)S(1)} %pad_maximum_fusion.14.refs_0_), channel_id=1, source_target_pairs={{0,2},{1,3},{2,0},{3,1},{4,6},{5,7},{6,4},{7,5},{8,10},{9,11},{10,... | collective-permute-start | bytes 1880072 | tf_op jit(solution)/shard_map/ppermute | solution.py:391
  702.2 36.4 %collective-permute-start.59 = (bf16[2,1,144,1088]{3,2,1,0:T(8,128)(2,1)S(1)}, bf16[2,1,144,1088]{3,2,1,0:T(8,128)(2,1)S(1)}, u32[]{:S(2)}, u32[]{:S(2)}) collective-permute-start(bf16[2,1,144,1088]{3,2,1,0:T(8,128)(2,1)S(1)} %pad_maximum_fusion.13.refs_0_), channel_id=1, source_target_pairs={{0,2},{1,3},{2,0},{3,1},{4,6},{5,7},{6,4},{7,5},{8,10},{9,11},{10,... | collective-permute-start | bytes 1880072 | tf_op jit(solution)/shard_map/ppermute | solution.py:391
  712.2 36.3 %collective-permute-start.64 = (bf16[2,1,144,1088]{3,2,1,0:T(8,128)(2,1)S(1)}, bf16[2,1,144,1088]{3,2,1,0:T(8,128)(2,1)}, u32[]{:S(2)}, u32[]{:S(2)}) collective-permute-start(bf16[2,1,144,1088]{3,2,1,0:T(8,128)(2,1)S(1)} %pad_maximum_fusion.14.refs_0_), channel_id=1, source_target_pairs={{0,1},{1,0},{2,3},{3,2},{4,5},{5,4},{6,7},{7,6},{8,9},{9,8},{10,11... | collective-permute-start | bytes 1880072 | tf_op jit(solution)/shard_map/ppermute | solution.py:391
  724.8 23.7 %collective-permute-start.65 = (bf16[2,1,144,1088]{3,2,1,0:T(8,128)(2,1)}, bf16[2,1,144,1088]{3,2,1,0:T(8,128)(2,1)}, u32[]{:S(2)}, u32[]{:S(2)}) collective-permute-start(bf16[2,1,144,1088]{3,2,1,0:T(8,128)(2,1)} %collective-permute-done.63.refs_1_), channel_id=1, source_target_pairs={{0,1},{1,0},{2,3},{3,2},{4,5},{5,4},{6,7},{7,6},{8,9},{9,8},{10,11... | collective-permute-start | bytes 1880072 | tf_op jit(solution)/shard_map/ppermute | solution.py:391
  724.8 28.1 %collective-permute-start.60 = (bf16[2,1,144,1088]{3,2,1,0:T(8,128)(2,1)S(1)}, bf16[2,1,144,1088]{3,2,1,0:T(8,128)(2,1)}, u32[]{:S(2)}, u32[]{:S(2)}) collective-permute-start(bf16[2,1,144,1088]{3,2,1,0:T(8,128)(2,1)S(1)} %pad_maximum_fusion.13.refs_0_), channel_id=1, source_target_pairs={{0,1},{1,0},{2,3},{3,2},{4,5},{5,4},{6,7},{7,6},{8,9},{9,8},{10,11... | collective-permute-start | bytes 1880072 | tf_op jit(solution)/shard_map/ppermute | solution.py:391
  (63 other events, 797.4 us)
Sparse Core Ops, SparseCore 0:
  16.4 38.3 all-gather.6
  61.0 30.0 all-gather.8
  130.8 31.9 all-gather.10
  558.2 35.3 reduce-scatter.7
  614.1 34.5 reduce-scatter.5
  671.9 37.4 reduce-scatter.3

commit v4 on v3

--- a/solution.py
+++ b/solution.py
@@ -12,6 +12,7 @@
 EPSILON = 1e-05
 LANES = 128
 VMEM_LIMIT = 56 * 1024 * 1024
+COST_SCALE = 8
 
 BF16 = jnp.bfloat16
 F32 = jnp.float32
@@ -180,9 +181,9 @@
         ],
         compiler_params=pltpu.CompilerParams(vmem_limit_bytes=VMEM_LIMIT),
         cost_estimate=pl.CostEstimate(
-            flops=seqs * pairs * 16 * length * length * LANES,
-            bytes_accessed=8 * seqs * length * width,
-            transcendentals=seqs * pairs * 2 * length * length,
+            flops=seqs * pairs * 16 * length * length * LANES // COST_SCALE,
+            bytes_accessed=8 * seqs * length * width // COST_SCALE,
+            transcendentals=0,
         ),
     )(order, joined, joined, joined)
 
@@ -217,9 +218,9 @@
         out_shape=jax.ShapeDtypeStruct(joined.shape, BF16),
         compiler_params=pltpu.CompilerParams(vmem_limit_bytes=VMEM_LIMIT),
         cost_estimate=pl.CostEstimate(
-            flops=seqs * pairs * 20 * length * length * LANES,
-            bytes_accessed=16 * seqs * length * width,
-            transcendentals=seqs * pairs * 2 * length * length,
+            flops=seqs * pairs * 20 * length * length * LANES // COST_SCALE,
+            bytes_accessed=16 * seqs * length * width // COST_SCALE,
+            transcendentals=0,
         ),
     )(order, joined, joined, joined, mixed, grad_mixed, lse, *ties)
 
@@ -267,7 +268,8 @@
         joined_ref[which] = out.astype(BF16)
 
 
-def attended_kernel(x_ref, o_ref, w_ref, small_ref, middle_ref, low_ref):
+def attended_kernel(x_ref, o_ref, w_ref, small_ref, *refs):
+    middle_ref, low_ref = refs[-2:]
     middle = x_ref[...].astype(F32) + dot_nn(o_ref[...], w_ref[0]) + row(small_ref, BIAS_OUT)
     middle_ref[...] = middle
     standard, _ = standardize(middle)
@@ -289,7 +291,8 @@
         slope_ref[which] = slope.astype(BF16)
 
 
-def output_kernel(middle_ref, act_ref, w_ref, small_ref, out_ref):
+def output_kernel(middle_ref, act_ref, w_ref, small_ref, *refs):
+    out_ref = refs[-1]
     total = middle_ref[...] + row(small_ref, BIAS_PROJ)
     for which in range(w_ref.shape[0]):
         total += dot_nn(act_ref[which], w_ref[which])
@@ -377,7 +380,9 @@
         out_shape=out_shape,
         compiler_params=pltpu.CompilerParams(vmem_limit_bytes=VMEM_LIMIT),
         cost_estimate=pl.CostEstimate(
-            flops=3 * rows * width * width * products, bytes_accessed=moved, transcendentals=0
+            flops=3 * rows * width * width * products // COST_SCALE,
+            bytes_accessed=moved // COST_SCALE,
+            transcendentals=0,
         ),
     )(*operands)
 
@@ -395,27 +400,40 @@
     return lax.optimization_barrier((values, *earlier))
 
 
+def held(values, *earlier):
+    wrong = jnp.zeros((), jnp.bool_)
+    for array in earlier:
+        entry = array[(0,) * array.ndim]
+        wrong = wrong | (entry != entry)
+    return jnp.where(wrong, jnp.zeros_like(values), values)
+
+
 def pick(bit, on_zero, on_one):
     return jnp.where(bit == 0, on_zero, on_one)
 
 
-def to_sequences(values, count):
+def to_sequences(values, count, *earlier):
     seqs, local, width = values.shape
     own = lax.axis_index("ctx")
     parts = values.reshape(count, seqs // count, local, width)
     pieces = []
     for offset in range(count):
-        piece = row_major(lax.dynamic_index_in_dim(parts, own ^ offset, keepdims=False))
-        pieces.append(row_major(swap(piece, "ctx", offset)) if offset else piece)
+        piece = lax.dynamic_index_in_dim(parts, own ^ offset, keepdims=False)
+        if earlier:
+            piece = held(piece, *earlier)
+        pieces.append(swap(piece, "ctx", offset) if offset else piece)
     return row_major(jnp.stack(pieces))
 
 
-def to_blocks(values, kind):
+def to_blocks(values, kind, *earlier):
     count, share, local, width = values.shape
     own = lax.axis_index("ctx")
     out = row_major(jnp.zeros((count, share, local, width), kind))
     for offset in range(count):
-        piece = row_major(values[offset])
+        piece = values[offset]
+        if earlier:
+            piece = held(piece, *earlier)
+        piece = row_major(piece)
         if offset:
             piece = row_major(swap(piece, "ctx", offset))
         out = lax.dynamic_update_index_in_dim(out, piece.astype(kind), own ^ offset, 0)
@@ -482,27 +500,36 @@
     )(here, *own, *other)
 
 
-def spread_weights(win, mine, owned_rows, transposed=False, kind=BF16):
+def spread_chips(mine, hold=()):
     shards = mine.shape[0]
     if shards == 1:
         first = jnp.stack([mine, swap(mine, "replica", 1)])
-        own = [first, swap(first, "ctx", 2)]
-        groups = ((((0, 0), (1, 0)), 0), (((0, 1), (1, 1)), 0))
-    else:
-        split = max(shards // 4, 1)
-        low, high = mine[:split], mine[split:]
-        low_there, high_there = after(swap(low, "replica", 1), swap(high, "ctx", 2))
-        first = jnp.stack([low, low_there])
-        second = jnp.stack([high, high_there])
-        own = [first, second, swap(first, "ctx", 2), swap(second, "replica", 1)]
-        groups = (
-            (((0, 0), (1, 0)), 0),
-            (((0, 0), (0, 1)), split),
-            (((0, 1), (1, 1)), 0),
-            (((1, 0), (1, 1)), split),
-        )
-    other = [swap(array, "ctx", 1) for array in own]
-    return assemble(win, groups, own, other, owned_rows, shards, transposed, kind), own[-2:]
+        return [first, swap(first, "ctx", 2)]
+    split = shards // 2
+    low, high = mine[:split], mine[split:]
+    low_there, high_there = after(swap(low, "replica", 1), swap(high, "ctx", 2))
+    first = held(jnp.stack([low, low_there]), *hold)
+    second = held(jnp.stack([high, high_there]), *hold)
+    return [first, second, swap(first, "ctx", 2), swap(second, "replica", 1)]
+
+
+def chip_groups(shards):
+    if shards == 1:
+        return ((((0, 0), (1, 0)), 0), (((0, 1), (1, 1)), 0))
+    return (
+        (((0, 0), (1, 0)), 0),
+        (((0, 0), (0, 1)), shards // 2),
+        (((0, 1), (1, 1)), 0),
+        (((1, 0), (1, 1)), shards // 2),
+    )
+
+
+def spread_cores(own):
+    return [swap(array, "ctx", 1) for array in own]
+
+
+def place(win, own, other, owned_rows, shards, transposed=False, kind=BF16):
+    return assemble(win, chip_groups(shards), own, other, owned_rows, shards, transposed, kind)
 
 
 def add_pair(kept, received):
@@ -513,34 +540,53 @@
     return values[(0,) * (values.ndim - 2)][:16, :LANES]
 
 
-def reduce_blocks(win, grads):
-    shards = grads.shape[1]
-    split = shards - max(shards // 4, 1)
+def reduce_first(win, grads, transposed):
+    shards = grads.shape[0 if transposed else 1]
+    split = shards // 2
+
+    def part(values, blocks, which):
+        return values[which, blocks] if transposed else values[blocks, which]
+
+    lower, upper = slice(None, split), slice(split, None)
+    entry = lambda values, i: values[:, i] if transposed else values[i]
     received = swap(win.other_rows(grads), "ctx", 1)
     both = add_pair(win.rows(grads), received)
-    x_kept = pick(win.x, both[:2, :split], both[2:, :split])
-    x_sent = pick(win.x, both[2:, :split], both[:2, :split])
-    y_kept = pick(win.y, both[0::2, split:], both[1::2, split:])
-    y_sent = pick(win.y, both[1::2, split:], both[0::2, split:])
-    x_received, y_received = after(swap(x_sent, "replica", 1), swap(y_sent, "ctx", 2))
-    low = add_pair(x_kept, x_received)
-    high = add_pair(y_kept, y_received)
-    low_received = swap(pick(win.y, low[1], low[0]), "ctx", 2)
-    high_received = swap(pick(win.x, high[1], high[0]), "replica", 1)
-    low_sum = add_pair(pick(win.y, low[0], low[1]), low_received)
-    high_sum = add_pair(pick(win.x, high[0], high[1]), high_received)
-    marks = (
-        [corner(received)],
-        [corner(x_received), corner(y_received)],
-        [corner(low_received), corner(high_received)],
-    )
-    return jnp.concatenate([low_sum, high_sum], axis=0), marks
+    by_x = [part(both, slice(2 * i, 2 * i + 2), lower) for i in range(2)]
+    by_y = [part(both, slice(i, None, 2), upper) for i in range(2)]
+    x_sent = row_major(pick(win.x, by_x[1], by_x[0]))
+    y_sent = row_major(pick(win.y, by_y[1], by_y[0]))
+    x_received, y_received = after(
+        row_major(swap(x_sent, "replica", 1)), row_major(swap(y_sent, "ctx", 2))
+    )
+    low = row_major(add_pair(pick(win.x, *by_x), x_received))
+    high = row_major(add_pair(pick(win.y, *by_y), y_received))
+    low, high = [entry(low, i) for i in range(2)], [entry(high, i) for i in range(2)]
+    return (low, high), [corner(x_sent), corner(y_sent)]
+
+
+def reduce_second(win, halves, *earlier):
+    low, high = halves
+    low_sent, high_sent = pick(win.y, low[1], low[0]), pick(win.x, high[1], high[0])
+    if earlier:
+        low_sent, high_sent = held(low_sent, *earlier), held(high_sent, *earlier)
+    low_received, high_received = after(
+        swap(low_sent, "ctx", 2), swap(high_sent, "replica", 1)
+    )
+    low_sum = add_pair(pick(win.y, *low), low_received)
+    high_sum = add_pair(pick(win.x, *high), high_received)
+    sums = jnp.concatenate([low_sum, high_sum], axis=0)
+    return sums, [corner(low_sent), corner(high_sent)], [corner(sums)]
 
 
 def reduce_vectors(values):
     values = add_pair(values, swap(values, "ctx", 1))
     values = add_pair(values, swap(values, "replica", 1))
-    return add_pair(values, swap(values, "ctx", 2))
+    values = add_pair(values, swap(values, "ctx", 2))
+    step = 1
+    while step < lax.axis_size("shard"):
+        values = add_pair(values, swap(values, "shard", step))
+        step *= 2
+    return values
 
 
 def per_device(
@@ -567,7 +613,7 @@
     wide = fc_weight.shape[1] // width
     count = lax.axis_size("ctx")
     rows = seq_count * local_len
-    pairwise = lax.axis_size("replica") == 2 and count == 4 and shards % 2 == 0
+    pairwise = lax.axis_size("replica") == 2 and count == 4 and shards == 4
     win = Windows(owned_rows)
 
     vectors = jnp.concatenate(
@@ -587,19 +633,17 @@
 
     if pairwise:
         mine = [win.rows(win.block(blocks)) for blocks in (blocks_a, blocks_b, blocks_c)]
-        part_a = gather_z(jnp.concatenate([mine[0], vector_tile], axis=0))
-        mine_b, part_a = after(mine[1], part_a)
+        part_a = gather_z(mine[0])
+        mine_b, part_a = after(jnp.concatenate([mine[1], vector_tile], axis=0), part_a)
         part_b = gather_z(mine_b)
         mine_c, part_b = after(mine[2], part_b)
         part_c = gather_z(mine_c)
         part_a, low_inputs = after(part_a, low_inputs)
-        vector_part = part_a[:, win.size : win.size + vector_rows]
-        full_a, steps = spread_weights(win, part_a[:, : win.size], owned_rows)
-        part_b, *_ = after(part_b, *steps)
-        full_b, steps = spread_weights(win, part_b, owned_rows)
-        part_c, *_ = after(part_c, *steps)
-        full_c, steps = spread_weights(win, part_c, owned_rows, transposed=True)
-        cotangent, *_ = after(cotangent, *steps)
+        own_a = spread_chips(part_a)
+        other_a = spread_cores(own_a)
+        full_a = place(win, own_a, other_a, owned_rows, shards)
+        vector_part = part_b[:, win.size : win.size + vector_rows]
+        own_b = spread_chips(held(part_b[:, : win.size], *own_a[-2:]), hold=other_a)
     else:
         vector_part = gather_z(vector_tile)[:, :vector_rows]
         full_a, full_b, full_c = [
@@ -607,14 +651,11 @@
         ]
         full_a, full_b = full_a.transpose(1, 0, 2, 3), full_b.transpose(1, 0, 2, 3)
     w_a = full_a.reshape(4, width, width)
-    w_fc = full_b.reshape(wide, width, width)
-    w_proj = full_c.reshape(wide, width, width)
     vector_part = vector_part.reshape(shards, vector_rows * width).astype(F32)
     small = vector_part[:, : 8 * owned_rows].reshape(shards, 8, owned_rows)
     small = small.transpose(1, 0, 2).reshape(8, width)
     bias_fc = vector_part[:, 8 * owned_rows :].reshape(wide, 1, width)
 
-    low_grad_out = to_sequences(cotangent, count).reshape(rows, width)
     share = seq_count // count
     blocked = (count, share, local_len, width)
     index = jnp.arange(count, dtype=jnp.int32)
@@ -625,57 +666,86 @@
         qkv_kernel, [low_inputs], [(w_a, 0, 3), small], [((3,), BF16), ((), BF16)]
     )
     joined = joined.reshape((3,) + blocked)
+    if pairwise:
+        other_b = spread_cores(own_b)
+        full_b = place(win, own_b, other_b, owned_rows, shards)
+        own_c = spread_chips(held(part_c, joined, *own_b[-2:]), hold=other_b)
+        steps = [corner(array[1]) for array in own_c[:2]]
+    else:
+        steps = []
     mixed, lse = attention_forward(joined, order)
     attended = mixed.reshape(rows, width)
     middle, low_two = by_rows(
-        attended_kernel, [low_inputs, attended], [(w_a, 3, 1), small], [((), F32), ((), BF16)]
-    )
+        attended_kernel,
+        [low_inputs, attended],
+        [(w_a, 3, 1), small],
+        [((), F32), ((), BF16)],
+        ties=steps,
+    )
+    w_fc = full_b.reshape(wide, width, width)
     low_act, slope = by_rows(
         hidden_kernel, [low_two], [w_fc, bias_fc], [((wide,), BF16), ((wide,), BF16)]
     )
-    (outputs,) = by_rows(output_kernel, [middle, low_act], [w_proj, small], [((), BF16)])
-    layer_out = to_blocks(outputs.reshape(blocked), BF16)
-
-    def reduce_units(grads, extra=None):
-        if pairwise:
-            sums, marks = reduce_blocks(win, grads)
-            if extra is not None:
-                sums = jnp.concatenate([sums, reduce_vectors(extra)], axis=1)
-            sums = lax.psum_scatter(sums, "shard", scatter_dimension=0, tiled=False)
-            full = spread_weights(win, sums[None, : win.size], owned_rows, kind=F32)[0][:, 0]
-            return full, sums[win.size :], marks
-        rest = ("replica", "ctx")
+    if pairwise:
+        full_c = place(win, own_c, spread_cores(own_c), owned_rows, shards, transposed=True)
+    w_proj = full_c.reshape(wide, width, width)
+    low_grad_out = to_sequences(cotangent, count, *(own_b[-2:] if pairwise else ()))
+    if pairwise:
+        low_grad_out = held(low_grad_out, *own_c[-2:])
+    low_grad_out = low_grad_out.reshape(rows, width)
+
+    def finish_units(sums, *earlier):
+        sums = lax.psum_scatter(sums, "shard", scatter_dimension=0, tiled=False)
+        own = spread_chips(held(sums[None], *earlier))
+        return place(win, own, spread_cores(own), owned_rows, 1, kind=F32)[:, 0]
+
+    def reduce_whole(grads, transposed=False):
+        if transposed:
+            grads = grads.transpose(1, 0, 2, 3)
         full = lax.psum_scatter(grads, "shard", scatter_dimension=1, tiled=False)
-        full = lax.psum(full, rest)
-        if extra is not None:
-            extra = lax.psum_scatter(extra, "shard", scatter_dimension=0, tiled=False)
-            extra = lax.psum(extra, rest)
-        return full.astype(F32), extra, ((), (), ())
+        return lax.psum(full, ("replica", "ctx")).astype(F32)
+
+    def start_units(grads, transposed=False):
+        if not pairwise:
+            return grads, ((), (), ())
+        halves, first = reduce_first(win, grads, transposed)
+        sums, second, last = reduce_second(win, halves)
+        return sums, (first, second, last)
 
     def by_shard(grads):
         return grads.astype(BF16).reshape(4, shards, owned_rows, width)
 
     grad_proj = jnp.einsum("ctx,td->cxd", low_act, low_grad_out, preferred_element_type=F32)
     grad_proj = grad_proj.astype(BF16)
-    owned_proj, _, proj_marks = reduce_units(by_shard(grad_proj).transpose(1, 0, 2, 3))
+    partial_proj, proj_marks = start_units(by_shard(grad_proj), transposed=True)
+    (outputs,) = by_rows(
+        output_kernel,
+        [middle, low_act],
+        [w_proj, small],
+        [((), BF16)],
+        ties=[corner(grad_proj)],
+    )
     grad_hidden, sums_hidden = by_rows(
         hidden_back_kernel,
         [low_grad_out, slope],
         [w_proj],
         [((wide,), BF16)],
         sums=8,
-        ties=[corner(grad_proj)],
+        ties=[corner(outputs), *proj_marks[0]],
     )
     grad_fc = jnp.einsum("td,ctx->cdx", low_two, grad_hidden, preferred_element_type=F32)
     grad_fc = grad_fc.astype(BF16)
-    owned_fc, _, fc_marks = reduce_units(by_shard(grad_fc))
+    partial_fc, fc_marks = start_units(by_shard(grad_fc))
     grad_middle, low_grad_middle, grad_mixed, sums_middle = by_rows(
         middle_back_kernel,
         [grad_hidden, low_grad_out, middle],
         [w_fc, (w_a, 3, 1), small],
         [((), F32), ((), BF16), ((), BF16)],
         sums=8,
-        ties=[corner(grad_fc), *proj_marks[0]],
+        ties=[corner(grad_fc), *proj_marks[1]],
+    )
+    layer_out = to_blocks(
+        outputs.reshape(blocked), BF16, low_grad_middle, *proj_marks[2], *fc_marks[0]
     )
     grad_out_weight = dot_tn(attended, low_grad_middle).astype(BF16)
     grad_joined = attention_backward(
@@ -684,20 +754,26 @@
         grad_mixed.reshape(blocked),
         lse,
         order,
-        ties=[*proj_marks[1], *fc_marks[0]],
+        ties=[corner(grad_out_weight), *proj_marks[2], *fc_marks[0]],
     ).reshape(3, rows, width)
     grad_qkv = jnp.einsum("td,ctx->cdx", low_one, grad_joined, preferred_element_type=F32)
     grad_qkv = grad_qkv.astype(BF16)
     grads_a = jnp.concatenate([grad_qkv, grad_out_weight[None]], axis=0)
+    partial_a, mark = by_shard(grads_a), ()
+    if pairwise:
+        halves, mark = reduce_first(win, partial_a, False)
     grad_inputs, sums_input = by_rows(
         input_back_kernel,
         [grad_joined, grad_middle, low_inputs],
         [(w_a, 0, 3), small],
         [((), BF16)],
         sums=8,
-        ties=[corner(grad_qkv), *proj_marks[2], *fc_marks[1]],
-    )
-    input_grad = to_blocks(grad_inputs.reshape(blocked), F32)
+        ties=[corner(grad_qkv), *mark, *fc_marks[2]],
+    )
+    if pairwise:
+        partial_a, _, _ = reduce_second(win, halves, grad_inputs)
+    earlier = (partial_a,) if pairwise else ()
+    input_grad = to_blocks(grad_inputs.reshape(blocked), F32, *earlier)
 
     small_grads = sums_middle + sums_input
     grad_fc_bias = sums_hidden[:wide]
@@ -714,7 +790,22 @@
         vector_grads.reshape(shards, vector_rows, width),
         ((0, 0), (0, -vector_rows % 16), (0, 0)),
     )
-    owned_a, owned_vectors, _ = reduce_units(by_shard(grads_a), vector_grads)
+    if pairwise:
+        owned_proj = finish_units(partial_proj, grad_joined)
+        owned_a = finish_units(partial_a)
+        owned_fc = finish_units(partial_fc, partial_a)
+        owned_vectors = lax.dynamic_index_in_dim(
+            reduce_vectors(held(vector_grads, partial_a)),
+            lax.axis_index("shard"),
+            keepdims=False,
+        )
+    else:
+        owned_proj = reduce_whole(partial_proj, transposed=True)
+        owned_a, owned_fc = reduce_whole(partial_a), reduce_whole(partial_fc)
+        owned_vectors = lax.psum_scatter(
+            vector_grads, "shard", scatter_dimension=0, tiled=False
+        )
+        owned_vectors = lax.psum(owned_vectors, ("replica", "ctx"))
     owned_vectors = owned_vectors[:vector_rows].reshape(-1).astype(F32)
     vec = [owned_vectors[i * owned_rows : (i + 1) * owned_rows] for i in range(8)]
     qkv_grad = jnp.concatenate([owned_a[i] for i in range(3)], axis=1)

time: 809 us -> 792 us (0.979)
  waiting for transfers between devices: 240 us -> 160 us
  between operations: 15.5 us -> 44.1 us
  local copies, waits for them, and re-layouts: 120 us -> 146 us
  other arithmetic: 82.9 us -> 93.3 us
    ppermute x66 -> x68, waiting for transfers between devices: 222 us -> 159 us  [swap(): lax.ppermute(values, axis, [(index, index ^ offset) for index in range(co...]
    slice x2 -> x23, local copies, waits for them, and re-layouts: 4.72 us -> 24.3 us  [the longest x22 23.4 us: held(): entry = array[(0,) * array.ndim]]
    all_gather x3, waiting for transfers between devices: 17.5 us -> 0.01 us  [gather_z(): return lax.all_gather(values, 'shard', axis=0, tiled=False)]
    select_n x0 -> x15, other arithmetic: none -> 16.7 us  [held(): return jnp.where(wrong, jnp.zeros_like(values), values)]
    reshape x1 -> x0, local copies, waits for them, and re-layouts: 8.43 us -> none  [by_shard(): return grads.astype(BF16).reshape(4, shards, owned_rows, width)]
    another operation x7 -> x3, local copies, waits for them, and re-layouts: 12.2 us -> 3.99 us  [the longest x2 3.71 us: spread_chips(): second = held(jnp.stack([high, high_there]), *hold)]
    unnamed x82 -> x114, local copies, waits for them, and re-layouts: 24.3 us -> 31.6 us
    ppermute x66 -> x68, starting transfers between devices: 53.5 us -> 55.4 us  [swap(): lax.ppermute(values, axis, [(index, index ^ offset) for index in range(co...]
  transfers between devices with their start and end apart: 72 -> 74, of which waited for: 26 -> 29; matrix products, arithmetic and copies ran while one was open for 27% -> 29% of each run, Pallas kernels for 29% -> 30%
where the time goes in v4:
time: 792 us; the launch traced here: 784 us
  Pallas kernels  238 us (30%)
  waiting for transfers between devices  160 us (20%)
  local copies, waits for them, and re-layouts  146 us (18%)
  other arithmetic  93.3 us (12%)
  starting transfers between devices  56.2 us (7%)
  matrix products  46.2 us (6%)
  between operations  44.1 us (6%)
    ppermute x68, waiting for transfers between devices, swap(): lax.ppermute(values, axis, [(index, index ^ offset) for index in range(co...  159 us
    pallas_call x7, Pallas kernels, by_rows(): pl.pallas_call(kernel, grid=(rows // tile,), in_specs=in_specs, out_specs...  139 us
    ppermute x68, starting transfers between devices, swap(): lax.ppermute(values, axis, [(index, index ^ offset) for index in range(co...  55.4 us
    pallas_call x6, Pallas kernels, assemble(): pl.pallas_call(functools.partial(assemble_kernel, groups, win.start, win....  38.9 us
    convert_element_type x16, other arithmetic, add_pair(): return (kept.astype(F32) + received.astype(F32)).astype(BF16)  35.7 us
    unnamed x114, local copies, waits for them, and re-layouts  31.6 us
    pallas_call x1, Pallas kernels, attention_forward(): pl.pallas_call(functools.partial(attention_forward_kernel, query_blocks(c...  31 us
    pallas_call x1, Pallas kernels, attention_backward(): pl.pallas_call(functools.partial(attention_backward_kernel, query_blocks(...  28.8 us
  transfers between devices with their start and end apart: 74, of which 29 were waited for; matrix products, arithmetic and copies ran while one was open for 29% of the time, Pallas kernels for 30%

profile of v4, /device:TPU:0, one launch (start us, length us, event | category | flops | bytes accessed | tf_op | source)
XLA Modules:
  0.0 783.8 jit_solution(10029861966324840965)
XLA Ops:
  22.8 4.9 concatenate.33
  33.6 10.7 %collective-permute-done.1 = bf16[2,128,1088]{1,2,0:T(8,128)(2,1)} collective-permute-done((bf16[2,128,1088]{1,2,0:T(8,128)(2,1)}, bf16[2,128,1088]{1,2,0:T(8,128)(2,1)}, u32[]{:S(2)}, u32[]{:S(2)}) %collective-permute-start.1) | collective-permute-done | bytes 557088 | tf_op jit(solution)/shard_map/ppermute | solution.py:396
  54.2 13.3 %collective-permute-done.3 = bf16[2,144,1088]{2,1,0:T(8,128)(2,1)S(1)} collective-permute-done((bf16[2,144,1088]{2,1,0:T(8,128)(2,1)}, bf16[2,144,1088]{2,1,0:T(8,128)(2,1)S(1)}, u32[]{:S(2)}, u32[]{:S(2)}) %collective-permute-start.3) | collective-permute-done | bytes 626720 | tf_op jit(solution)/shard_map/ppermute | solution.py:396
  76.4 24.5 %collective-permute-done.7.refs_2_ = bf16[2,2,144,1088]{3,2,1,0:T(8,128)(2,1)} collective-permute-done((bf16[2,2,144,1088]{3,2,1,0:T(8,128)(2,1)S(1)}, bf16[2,2,144,1088]{3,2,1,0:T(8,128)(2,1)}, u32[]{:S(2)}, u32[]{:S(2)}) %collective-permute-start.7) | collective-permute-done | bytes 1253408 | tf_op jit(solution)/shard_map/ppermute | solution.py:396
  117.9 8.8 %collective-permute-done.11 = bf16[2,144,1088]{2,1,0:T(8,128)(2,1)} collective-permute-done((bf16[2,144,1088]{2,1,0:T(8,128)(2,1)}, bf16[2,144,1088]{2,1,0:T(8,128)(2,1)}, u32[]{:S(2)}, u32[]{:S(2)}) %collective-permute-start.11) | collective-permute-done | bytes 626720 | tf_op jit(solution)/shard_map/ppermute | solution.py:396
  140.6 8.6 %shard_map.271 = bf16[4,4,272,1088]{3,2,1,0:T(8,128)(2,1)} custom-call(s32[3]{0:T(128)} %pad_add_fusion.here_ref, bf16[2,2,144,1088]{3,2,1,0:T(8,128)(2,1)} %copy-done.20, bf16[2,2,144,1088]{3,2,1,0:T(8,128)(2,1)} %copy-done.21, bf16[2,2,144,1088]{3,2,1,0:T(8,128)(2,1)} %collective-permute-done.7.refs_2_, ...), custom_call_target="tpu_custom_call" | custom-call | bytes 18939904 | tf_op jit(solution)/shard_map/pallas_call | solution.py:490
  149.2 16.7 %shard_map.272 = (bf16[3,1024,1088]{2,1,0:T(8,128)(2,1)}, bf16[1024,1088]{1,0:T(8,128)(2,1)}) custom-call(bf16[1024,1088]{1,0:T(8,128)(2,1)} %bitcast.262, bf16[4,1088,1088]{2,1,0:T(8,128)(2,1)} %bitcast.242, f32[8,1088]{1,0:T(8,128)} %reshape.266.small_ref), custom_call_target="tpu_custom_call" | custom-call | flops 1363673088 | bytes 2580736 | tf_op jit(solution)/shard_map/pallas_call | solution.py:375
  207.2 31.0 %shard_map.273 = (bf16[4,2,128,1088]{3,2,1,0:T(8,128)(2,1)}, f32[2,9,8,512]{3,2,1,0:T(8,128)}) custom-call(s32[4]{0:T(128)} %broadcast_xor_fusion.order_ref, bf16[3,4,2,128,1088]{4,3,2,1,0:T(8,128)(2,1)} %bitcast.236, bf16[3,4,2,128,1088]{4,3,2,1,0:T(8,128)(2,1)} %bitcast.237, bf16[3,4,2,128,1088]{4,3,2,1,0:T(8,128)(2,1)} %bitcast.238), custom_call_target="tpu_custom_call" | custom-call | flops 1207959552 | bytes 1114112 | tf_op jit(solution)/shard_map/pallas_call | solution.py:167
  245.2 8.6 %shard_map.275 = bf16[4,4,272,1088]{3,2,1,0:T(8,128)(2,1)} custom-call(s32[3]{0:T(128)} %pad_add_fusion.here_ref, bf16[2,2,144,1088]{3,2,1,0:T(8,128)(2,1)} %copy-done.19, bf16[2,2,144,1088]{3,2,1,0:T(8,128)(2,1)} %maximum_select_fusion.2.refs_1_, bf16[2,2,144,1088]{3,2,1,0:T(8,128)(2,1)} %collective-permute-done.15.refs_2_, ...), custom_call_target="tpu_custom_call" | custom-call | bytes 18939904 | tf_op jit(solution)/shard_map/pallas_call | solution.py:490
  253.7 8.5 %shard_map.274 = (f32[1024,1088]{1,0:T(8,128)}, bf16[1024,1088]{1,0:T(8,128)(2,1)}) custom-call(bf16[1024,1088]{1,0:T(8,128)(2,1)} %bitcast.263, bf16[1024,1088]{1,0:T(8,128)(2,1)} %bitcast.273, bf16[4,1088,1088]{2,1,0:T(8,128)(2,1)} %bitcast.243, f32[8,1088]{1,0:T(8,128)} %reshape.266.small_ref, bf16[16,128]{1,0:T(8,128)(2,1)} %slice.654.refs_0_, ...), custom_call_target="tpu_custom_call" | custom-call | flops 454557696 | bytes 2581760 | tf_op jit(solution)/shard_map/pallas_call | solution.py:375
  262.3 27.8 %shard_map.276 = (bf16[4,1024,1088]{2,1,0:T(8,128)(2,1)}, bf16[4,1024,1088]{2,1,0:T(8,128)(2,1)}) custom-call(bf16[1024,1088]{1,0:T(8,128)(2,1)} %get-tuple-element.69.low_ref, bf16[4,1088,1088]{2,1,0:T(8,128)(2,1)} %bitcast.246, f32[4,1,1088]{2,1,0:T(1,128)} %reshape.272.bias_ref), custom_call_target="tpu_custom_call" | custom-call | flops 1818230784 | bytes 3692672 | tf_op jit(solution)/shard_map/pallas_call | solution.py:375
  295.6 15.4 %convolution_convert_fusion.1 = bf16[4,1088,1088]{2,1,0:T(8,128)(2,1)S(1)} fusion(bf16[4,1024,1088]{2,1,0:T(8,128)(2,1)} %get-tuple-element.72.act_ref, bf16[1024,1088,1]{1,0,2:T(8,128)(2,1)S(1)} %bitcast.268), kind=kOutput, calls=%fused_computation.1 | convolution fusion | flops 9701965824 | bytes 20611072 | tf_op jit(solution)/shard_map/ctx,td->cxd/dot_general | solution.py:718
  320.6 6.1 collective-permute-done.26.refs_4_
  326.7 5.7 collective-permute-done.27.refs_5_
  333.8 8.6 %shard_map.277 = bf16[4,4,272,1088]{3,2,1,0:T(8,128)(2,1)} custom-call(s32[3]{0:T(128)} %pad_add_fusion.here_ref, bf16[2,2,144,1088]{3,2,1,0:T(8,128)(2,1)} %copy-done.15, bf16[2,2,144,1088]{3,2,1,0:T(8,128)(2,1)} %copy-done.17, bf16[2,2,144,1088]{3,2,1,0:T(8,128)(2,1)} %collective-permute-done.21.refs_2_, ...), custom_call_target="tpu_custom_call" | custom-call | bytes 18939904 | tf_op jit(solution)/shard_map/pallas_call | solution.py:490
  342.5 19.8 %shard_map.278 = bf16[1024,1088]{1,0:T(8,128)(2,1)} custom-call(f32[1024,1088]{1,0:T(8,128)} %get-tuple-element.71.middle_ref, bf16[4,1024,1088]{2,1,0:T(8,128)(2,1)} %get-tuple-element.72.act_ref, bf16[4,1088,1088]{2,1,0:T(8,128)(2,1)} %bitcast.248, f32[8,1088]{1,0:T(8,128)} %reshape.266.small_ref, bf16[16,128]{1,0:T(8,128)(2,1)} %slice.659.refs_0_), custom_call_target="tpu_custom_call" | custom-call | flops 1818230784 | bytes 3138304 | tf_op jit(solution)/shard_map/pallas_call | solution.py:375
  363.5 6.6 add_convert_fusion.2
  377.3 20.9 %shard_map.279 = (bf16[4,1024,1088]{2,1,0:T(8,128)(2,1)}, f32[8,1088]{1,0:T(8,128)}) custom-call(bf16[1024,1088]{1,0:T(8,128)(2,1)} %bitcast.269, bf16[4,1024,1088]{2,1,0:T(8,128)(2,1)} %get-tuple-element.70.slope_ref, bf16[4,1088,1088]{2,1,0:T(8,128)(2,1)} %bitcast.249, bf16[16,128]{1,0:T(8,128)(2,1)} %slice.660.refs_0_, bf16[16,128]{1,0:T(8,128)(2,1)} %slice.666.refs_1_, ...), custom_call_target="tpu_custom_call" | custom-call | flops 1818230784 | bytes 3696384 | tf_op jit(solution)/shard_map/pallas_call | solution.py:375
  398.3 13.7 %convolution_convert_fusion = bf16[4,1088,1088]{1,2,0:T(8,128)(2,1)S(1)} fusion(bf16[4,1024,1088]{2,1,0:T(8,128)(2,1)} %get-tuple-element.73.hidden_ref, bf16[1024,1088]{1,0:T(8,128)(2,1)S(1)} %copy-done.33), kind=kOutput, calls=%fused_computation | convolution fusion | flops 9701965824 | bytes 20611072 | tf_op jit(solution)/shard_map/td,ctx->cdx/dot_general | solution.py:736
  413.0 3.3 broadcast_select_fusion.1
  418.1 4.3 add_convert_fusion.7
  423.8 27.0 %shard_map.280 = (f32[1024,1088]{1,0:T(8,128)}, bf16[1024,1088]{1,0:T(8,128)(2,1)}, bf16[1024,1088]{1,0:T(8,128)(2,1)}, f32[8,1088]{1,0:T(8,128)}) custom-call(bf16[4,1024,1088]{2,1,0:T(8,128)(2,1)} %get-tuple-element.73.hidden_ref, bf16[1024,1088]{1,0:T(8,128)(2,1)} %bitcast.270, f32[1024,1088]{1,0:T(8,128)} %get-tuple-element.71.middle_ref, ...), custom_call_target="tpu_custom_call" | custom-call | flops 2272788480 | bytes 5441536 | tf_op jit(solution)/shard_map/pallas_call | solution.py:375
  455.7 4.8 convolution_convert_fusion.3
  461.2 9.8 %collective-permute-done.33 = bf16[2,144,1088]{2,1,0:T(8,128)(2,1)S(1)} collective-permute-done((bf16[2,144,1088]{2,1,0:T(8,128)(2,1)S(1)}, bf16[2,144,1088]{2,1,0:T(8,128)(2,1)S(1)}, u32[]{:S(2)}, u32[]{:S(2)}) %collective-permute-start.33) | collective-permute-done | bytes 626720 | tf_op jit(solution)/shard_map/ppermute | solution.py:396
  476.5 7.0 add_convert_fusion.1
  501.7 28.8 %shard_map.281 = bf16[3,4,2,128,1088]{4,3,2,1,0:T(8,128)(2,1)} custom-call(s32[4]{0:T(128)} %broadcast_xor_fusion.order_ref, bf16[3,4,2,128,1088]{4,3,2,1,0:T(8,128)(2,1)} %bitcast.239, bf16[3,4,2,128,1088]{4,3,2,1,0:T(8,128)(2,1)} %bitcast.240, bf16[3,4,2,128,1088]{4,3,2,1,0:T(8,128)(2,1)} %bitcast.241, bf16[4,2,128,1088]{3,2,1,0:T(8,128)(2,1)} %get-tuple-element.68.o_ref, ...), custom_call_target="tpu_custom_call" | custom-call | flops 1509949440 | bytes 2228224 | tf_op jit(solution)/shard_map/pallas_call | solution.py:199
  533.0 12.3 %convolution_convert_fusion.2 = bf16[3,1088,1088]{1,2,0:T(8,128)(2,1)S(1)} fusion(bf16[3,1024,1088]{2,1,0:T(8,128)(2,1)} %bitcast.266, bf16[1024,1088]{1,0:T(8,128)(2,1)S(1)} %copy-done.49), kind=kOutput, calls=%fused_computation.2 | convolution fusion | flops 7276474368 | bytes 16015360 | tf_op jit(solution)/shard_map/td,ctx->cdx/dot_general | solution.py:759
  552.7 7.0 broadcast_select_fusion
  569.3 10.6 %collective-permute-done.65.refs_1_ = bf16[2,1,144,1088]{3,2,1,0:T(8,128)(2,1)} collective-permute-done((bf16[2,1,144,1088]{3,2,1,0:T(8,128)(2,1)}, bf16[2,1,144,1088]{3,2,1,0:T(8,128)(2,1)}, u32[]{:S(2)}, u32[]{:S(2)}) %collective-permute-start.65) | collective-permute-done | bytes 626720 | tf_op jit(solution)/shard_map/ppermute | solution.py:396
  580.4 4.3 add_convert_fusion.4
  587.3 3.7 collective-permute-done.38
  595.6 4.4 copy.167
  600.0 4.5 shard_map.285
  612.5 4.4 add_convert_fusion
  623.8 18.6 %shard_map.282 = (bf16[1024,1088]{1,0:T(8,128)(2,1)}, f32[8,1088]{1,0:T(8,128)}) custom-call(bf16[3,1024,1088]{2,1,0:T(8,128)(2,1)} %bitcast.267, f32[1024,1088]{1,0:T(8,128)} %get-tuple-element.82.grad_middle_ref, bf16[1024,1088]{1,0:T(8,128)(2,1)} %bitcast.264, bf16[4,1088,1088]{2,1,0:T(8,128)(2,1)} %bitcast.245, f32[8,1088]{1,0:T(8,128)} %reshape.266.small_ref, ...), custom_call_target="tpu_custom_call" | custom-call | flops 1363673088 | bytes 3144192 | tf_op jit(solution)/shard_map/pallas_call | solution.py:375
  644.9 5.2 collective-permute-done.40
  657.5 13.6 %collective-permute-done.46 = bf16[2,144,1088]{2,1,0:T(8,128)(2,1)} collective-permute-done((bf16[2,144,1088]{2,1,0:T(8,128)(2,1)}, bf16[2,144,1088]{2,1,0:T(8,128)(2,1)}, u32[]{:S(2)}, u32[]{:S(2)}) %collective-permute-start.46) | collective-permute-done | bytes 626720 | tf_op jit(solution)/shard_map/ppermute | solution.py:396
  693.3 7.3 collective-permute-done.52
  702.4 8.4 %collective-permute-done.53 = bf16[4,16,1088]{2,1,0:T(8,128)(2,1)S(1)} collective-permute-done((bf16[4,16,1088]{2,1,0:T(8,128)(2,1)S(1)}, bf16[4,16,1088]{2,1,0:T(8,128)(2,1)S(1)}, u32[]{:S(2)}, u32[]{:S(2)}) %collective-permute-start.53) | collective-permute-done | bytes 139296 | tf_op jit(solution)/shard_map/ppermute | solution.py:396
  714.2 5.5 collective-permute-done.54
  729.0 7.5 collective-permute-done.56
  740.2 6.0 copy.168
  747.6 4.3 shard_map.284
  754.0 4.2 slice_bitcast_fusion.3
  758.2 5.8 concatenate.42
  764.0 4.3 shard_map.283
  768.3 4.3 slice_bitcast_fusion.7
  772.6 4.1 concatenate.40
  (421 shorter events, 243.9 us)
Async XLA Ops:
  7.2 40.8 %all-gather.7.cloned.1.call-start = ((), (), s32[]{:S(2)}) async-start(), calls=%async_computation.6 | async-start | bytes 1658880 | tf_op jit(solution)/shard_map/all_gather | solution.py:630
  9.8 96.9 %all-gather.9.cloned.1.call-start = ((), (), s32[]{:S(2)}) async-start(), calls=%async_computation.7 | async-start | bytes 1843200 | tf_op jit(solution)/shard_map/all_gather | solution.py:630
  21.1 23.3 %collective-permute-start.1 = (bf16[2,128,1088]{1,2,0:T(8,128)(2,1)}, bf16[2,128,1088]{1,2,0:T(8,128)(2,1)}, u32[]{:S(2)}, u32[]{:S(2)}) collective-permute-start(bf16[2,128,1088]{1,2,0:T(8,128)(2,1)} %bitcast.303), channel_id=1, source_target_pairs={{0,2},{1,3},{2,0},{3,1},{4,6},{5,7},{6,4},{7,5},{8,10},{9,11},{10,... | collective-permute-start | bytes 1671176 | tf_op jit(solution)/shard_map/ppermute | solution.py:396
  22.7 23.1 %collective-permute-start = (bf16[2,128,1088]{1,2,0:T(8,128)(2,1)}, bf16[2,128,1088]{1,2,0:T(8,128)(2,1)S(1)}, u32[]{:S(2)}, u32[]{:S(2)}) collective-permute-start(bf16[2,128,1088]{1,2,0:T(8,128)(2,1)} %bitcast.304), channel_id=1, source_target_pairs={{0,1},{1,0},{2,3},{3,2},{4,5},{5,4},{6,7},{7,6},{8,9},{9,8},{10,11... | collective-permute-start | bytes 1671176 | tf_op jit(solution)/shard_map/ppermute | solution.py:396
  54.1 119.8 %all-gather.11.cloned.1.call-start = ((), (), s32[]{:S(2)}) async-start(), calls=%async_computation.8 | async-start | bytes 1658880 | tf_op jit(solution)/shard_map/all_gather | solution.py:630
  70.6 30.3 %collective-permute-start.7 = (bf16[2,2,144,1088]{3,2,1,0:T(8,128)(2,1)S(1)}, bf16[2,2,144,1088]{3,2,1,0:T(8,128)(2,1)}, u32[]{:S(2)}, u32[]{:S(2)}) collective-permute-start(bf16[2,2,144,1088]{3,2,1,0:T(8,128)(2,1)S(1)} %pad_maximum_fusion.2.refs_0_), channel_id=1, source_target_pairs={{0,2},{1,3},{2,0},{3,1},{4,6},{5,7},{6,4},{7,5},{8,10},{9,11},{10,... | collective-permute-start | bytes 3760136 | tf_op jit(solution)/shard_map/ppermute | solution.py:396
  73.6 30.0 %collective-permute-start.9 = (bf16[2,2,144,1088]{3,2,1,0:T(8,128)(2,1)S(1)}, bf16[2,2,144,1088]{3,2,1,0:T(8,128)(2,1)}, u32[]{:S(2)}, u32[]{:S(2)}) collective-permute-start(bf16[2,2,144,1088]{3,2,1,0:T(8,128)(2,1)S(1)} %pad_maximum_fusion.3.refs_1_), channel_id=1, source_target_pairs={{0,4},{4,0},{1,5},{5,1},{2,6},{6,2},{3,7},{7,3},{8,12},{12,8},{9,1... | collective-permute-start | bytes 3760136 | tf_op jit(solution)/shard_map/ppermute | solution.py:396
  75.0 36.0 %collective-permute-start.5 = (bf16[2,2,144,1088]{3,2,1,0:T(8,128)(2,1)S(1)}, bf16[2,2,144,1088]{3,2,1,0:T(8,128)(2,1)}, u32[]{:S(2)}, u32[]{:S(2)}) collective-permute-start(bf16[2,2,144,1088]{3,2,1,0:T(8,128)(2,1)S(1)} %pad_maximum_fusion.2.refs_0_), channel_id=1, source_target_pairs={{0,1},{1,0},{2,3},{3,2},{4,5},{5,4},{6,7},{7,6},{8,9},{9,8},{10,11... | collective-permute-start | bytes 3760136 | tf_op jit(solution)/shard_map/ppermute | solution.py:396
  75.9 39.6 %collective-permute-start.6 = (bf16[2,2,144,1088]{3,2,1,0:T(8,128)(2,1)S(1)}, bf16[2,2,144,1088]{3,2,1,0:T(8,128)(2,1)}, u32[]{:S(2)}, u32[]{:S(2)}) collective-permute-start(bf16[2,2,144,1088]{3,2,1,0:T(8,128)(2,1)S(1)} %pad_maximum_fusion.3.refs_1_), channel_id=1, source_target_pairs={{0,1},{1,0},{2,3},{3,2},{4,5},{5,4},{6,7},{7,6},{8,9},{9,8},{10,11... | collective-permute-start | bytes 3760136 | tf_op jit(solution)/shard_map/ppermute | solution.py:396
  106.1 21.7 %collective-permute-start.8 = (bf16[2,2,144,1088]{3,2,1,0:T(8,128)(2,1)}, bf16[2,2,144,1088]{3,2,1,0:T(8,128)(2,1)}, u32[]{:S(2)}, u32[]{:S(2)}) collective-permute-start(bf16[2,2,144,1088]{3,2,1,0:T(8,128)(2,1)} %collective-permute-done.7.refs_2_), channel_id=1, source_target_pairs={{0,1},{1,0},{2,3},{3,2},{4,5},{5,4},{6,7},{7,6},{8,9},{9,8},{10,11... | collective-permute-start | bytes 3760136 | tf_op jit(solution)/shard_map/ppermute | solution.py:396
  106.2 24.1 %collective-permute-start.10 = (bf16[2,2,144,1088]{3,2,1,0:T(8,128)(2,1)}, bf16[2,2,144,1088]{3,2,1,0:T(8,128)(2,1)}, u32[]{:S(2)}, u32[]{:S(2)}) collective-permute-start(bf16[2,2,144,1088]{3,2,1,0:T(8,128)(2,1)} %collective-permute-done.9.refs_3_), channel_id=1, source_target_pairs={{0,1},{1,0},{2,3},{3,2},{4,5},{5,4},{6,7},{7,6},{8,9},{9,8},{10,11... | collective-permute-start | bytes 3760136 | tf_op jit(solution)/shard_map/ppermute | solution.py:396
  112.5 437.4 %reduce-scatter.8.cloned.1.call-start = ((), (), s32[]{:S(2)}) async-start(), calls=%async_computation.5 | async-start | bytes 1658880 | tf_op jit(solution)/shard_map/reduce_scatter | solution.py:698
  134.3 34.0 %collective-permute-start.15 = (bf16[2,2,144,1088]{3,2,1,0:T(8,128)(2,1)S(1)}, bf16[2,2,144,1088]{3,2,1,0:T(8,128)(2,1)}, u32[]{:S(2)}, u32[]{:S(2)}) collective-permute-start(bf16[2,2,144,1088]{3,2,1,0:T(8,128)(2,1)S(1)} %maximum_select_fusion.1.refs_0_), channel_id=1, source_target_pairs={{0,2},{1,3},{2,0},{3,1},{4,6},{5,7},{6,4},{7,5},{8,10},{9,11},{10,... | collective-permute-start | bytes 3760136 | tf_op jit(solution)/shard_map/ppermute | solution.py:396
  137.1 33.7 %collective-permute-start.17 = (bf16[2,2,144,1088]{3,2,1,0:T(8,128)(2,1)}, bf16[2,2,144,1088]{3,2,1,0:T(8,128)(2,1)}, u32[]{:S(2)}, u32[]{:S(2)}) collective-permute-start(bf16[2,2,144,1088]{3,2,1,0:T(8,128)(2,1)} %maximum_select_fusion.2.refs_1_), channel_id=1, source_target_pairs={{0,4},{4,0},{1,5},{5,1},{2,6},{6,2},{3,7},{7,3},{8,12},{12,8},{9,1... | collective-permute-start | bytes 3760136 | tf_op jit(solution)/shard_map/ppermute | solution.py:396
  138.2 39.6 %collective-permute-start.13 = (bf16[2,2,144,1088]{3,2,1,0:T(8,128)(2,1)S(1)}, bf16[2,2,144,1088]{3,2,1,0:T(8,128)(2,1)S(1)}, u32[]{:S(2)}, u32[]{:S(2)}) collective-permute-start(bf16[2,2,144,1088]{3,2,1,0:T(8,128)(2,1)S(1)} %maximum_select_fusion.1.refs_0_), channel_id=1, source_target_pairs={{0,1},{1,0},{2,3},{3,2},{4,5},{5,4},{6,7},{7,6},{8,9},{9,8},{10,11... | collective-permute-start | bytes 3760136 | tf_op jit(solution)/shard_map/ppermute | solution.py:396
  140.1 46.2 %collective-permute-start.14 = (bf16[2,2,144,1088]{3,2,1,0:T(8,128)(2,1)}, bf16[2,2,144,1088]{3,2,1,0:T(8,128)(2,1)}, u32[]{:S(2)}, u32[]{:S(2)}) collective-permute-start(bf16[2,2,144,1088]{3,2,1,0:T(8,128)(2,1)} %maximum_select_fusion.2.refs_1_), channel_id=1, source_target_pairs={{0,1},{1,0},{2,3},{3,2},{4,5},{5,4},{6,7},{7,6},{8,9},{9,8},{10,11... | collective-permute-start | bytes 3760136 | tf_op jit(solution)/shard_map/ppermute | solution.py:396
  173.3 24.0 %collective-permute-start.16 = (bf16[2,2,144,1088]{3,2,1,0:T(8,128)(2,1)}, bf16[2,2,144,1088]{3,2,1,0:T(8,128)(2,1)}, u32[]{:S(2)}, u32[]{:S(2)}) collective-permute-start(bf16[2,2,144,1088]{3,2,1,0:T(8,128)(2,1)} %collective-permute-done.15.refs_2_), channel_id=1, source_target_pairs={{0,1},{1,0},{2,3},{3,2},{4,5},{5,4},{6,7},{7,6},{8,9},{9,8},{10,11... | collective-permute-start | bytes 3760136 | tf_op jit(solution)/shard_map/ppermute | solution.py:396
  173.4 26.4 %collective-permute-start.18 = (bf16[2,2,144,1088]{3,2,1,0:T(8,128)(2,1)}, bf16[2,2,144,1088]{3,2,1,0:T(8,128)(2,1)}, u32[]{:S(2)}, u32[]{:S(2)}) collective-permute-start(bf16[2,2,144,1088]{3,2,1,0:T(8,128)(2,1)} %collective-permute-done.17.refs_3_), channel_id=1, source_target_pairs={{0,1},{1,0},{2,3},{3,2},{4,5},{5,4},{6,7},{7,6},{8,9},{9,8},{10,11... | collective-permute-start | bytes 3760136 | tf_op jit(solution)/shard_map/ppermute | solution.py:396
  176.3 19.8 %collective-permute-start.19 = (bf16[2,144,1088]{2,1,0:T(8,128)(2,1)}, bf16[2,144,1088]{2,1,0:T(8,128)(2,1)}, u32[]{:S(2)}, u32[]{:S(2)}) collective-permute-start(bf16[2,144,1088]{2,1,0:T(8,128)(2,1)} %bitcast.31), channel_id=1, source_target_pairs={{0,4},{4,0},{1,5},{5,1},{2,6},{6,2},{3,7},{7,3},{8,12},{12,8},{9,1... | collective-permute-start | bytes 1880072 | tf_op jit(solution)/shard_map/ppermute | solution.py:396
  192.3 46.0 %collective-permute-start.25 = (bf16[2,128,1088]{1,2,0:T(8,128)(2,1)}, bf16[2,128,1088]{1,2,0:T(8,128)(2,1)}, u32[]{:S(2)}, u32[]{:S(2)}) collective-permute-start(bf16[2,128,1088]{1,2,0:T(8,128)(2,1)} %copy.144), channel_id=1, source_target_pairs={{0,3},{1,2},{2,1},{3,0},{4,7},{5,6},{6,5},{7,4},{8,11},{9,10},{10,... | collective-permute-start | bytes 1671176 | tf_op jit(solution)/shard_map/ppermute | solution.py:396
  196.1 43.6 %collective-permute-start.24 = (bf16[2,128,1088]{1,2,0:T(8,128)(2,1)}, bf16[2,128,1088]{1,2,0:T(8,128)(2,1)}, u32[]{:S(2)}, u32[]{:S(2)}) collective-permute-start(bf16[2,128,1088]{1,2,0:T(8,128)(2,1)} %copy.142), channel_id=1, source_target_pairs={{0,2},{1,3},{2,0},{3,1},{4,6},{5,7},{6,4},{7,5},{8,10},{9,11},{10,... | collective-permute-start | bytes 1671176 | tf_op jit(solution)/shard_map/ppermute | solution.py:396
  197.0 44.8 %collective-permute-start.23 = (bf16[2,128,1088]{1,2,0:T(8,128)(2,1)}, bf16[2,128,1088]{1,2,0:T(8,128)(2,1)}, u32[]{:S(2)}, u32[]{:S(2)}) collective-permute-start(bf16[2,128,1088]{1,2,0:T(8,128)(2,1)} %copy.140), channel_id=1, source_target_pairs={{0,1},{1,0},{2,3},{3,2},{4,5},{5,4},{6,7},{7,6},{8,9},{9,8},{10,11... | collective-permute-start | bytes 1671176 | tf_op jit(solution)/shard_map/ppermute | solution.py:396
  203.9 86.3 %collective-permute-start.21 = (bf16[2,2,144,1088]{3,2,1,0:T(8,128)(2,1)S(1)}, bf16[2,2,144,1088]{3,2,1,0:T(8,128)(2,1)}, u32[]{:S(2)}, u32[]{:S(2)}) collective-permute-start(bf16[2,2,144,1088]{3,2,1,0:T(8,128)(2,1)S(1)} %maximum_select_fusion.3.refs_0_), channel_id=1, source_target_pairs={{0,2},{1,3},{2,0},{3,1},{4,6},{5,7},{6,4},{7,5},{8,10},{9,11},{10,... | collective-permute-start | bytes 3760136 | tf_op jit(solution)/shard_map/ppermute | solution.py:396
  206.7 86.0 %collective-permute-start.22 = (bf16[2,2,144,1088]{3,2,1,0:T(8,128)(2,1)S(1)}, bf16[2,2,144,1088]{3,2,1,0:T(8,128)(2,1)}, u32[]{:S(2)}, u32[]{:S(2)}) collective-permute-start(bf16[2,2,144,1088]{3,2,1,0:T(8,128)(2,1)S(1)} %maximum_select_fusion.4.refs_1_), channel_id=1, source_target_pairs={{0,4},{4,0},{1,5},{5,1},{2,6},{6,2},{3,7},{7,3},{8,12},{12,8},{9,1... | collective-permute-start | bytes 3760136 | tf_op jit(solution)/shard_map/ppermute | solution.py:396
  317.0 46.6 %collective-permute-start.30 = (bf16[4,4,144,1088]{3,2,1,0:T(8,128)(2,1)}, bf16[4,4,144,1088]{3,2,1,0:T(8,128)(2,1)}, u32[]{:S(2)}, u32[]{:S(2)}) collective-permute-start(bf16[4,4,144,1088]{3,2,1,0:T(8,128)(2,1)} %broadcast_select_fusion.2), channel_id=1, source_target_pairs={{0,1},{1,0},{2,3},{3,2},{4,5},{5,4},{6,7},{7,6},{8,9},{9,8},{10,11... | collective-permute-start | bytes 15040520 | tf_op jit(solution)/shard_map/ppermute | solution.py:396
  372.9 45.2 %collective-permute-start.31 = (bf16[2,2,144,1088]{3,2,1,0:T(8,128)(2,1)}, bf16[2,2,144,1088]{3,2,1,0:T(8,128)(2,1)}, u32[]{:S(2)}, u32[]{:S(2)}) collective-permute-start(bf16[2,2,144,1088]{3,2,1,0:T(8,128)(2,1)} %get-tuple-element.181), channel_id=1, source_target_pairs={{0,4},{4,0},{1,5},{5,1},{2,6},{6,2},{3,7},{7,3},{8,12},{12,8},{9,1... | collective-permute-start | bytes 3760136 | tf_op jit(solution)/shard_map/ppermute | solution.py:396
  375.5 42.6 %collective-permute-start.32 = (bf16[2,2,144,1088]{3,2,1,0:T(8,128)(2,1)S(1)}, bf16[2,2,144,1088]{3,2,1,0:T(8,128)(2,1)}, u32[]{:S(2)}, u32[]{:S(2)}) collective-permute-start(bf16[2,2,144,1088]{3,2,1,0:T(8,128)(2,1)S(1)} %get-tuple-element.180), channel_id=1, source_target_pairs={{0,2},{1,3},{2,0},{3,1},{4,6},{5,7},{6,4},{7,5},{8,10},{9,11},{10,... | collective-permute-start | bytes 3760136 | tf_op jit(solution)/shard_map/ppermute | solution.py:396
  417.3 59.2 %collective-permute-start.35 = (bf16[4,4,144,1088]{3,2,1,0:T(8,128)(2,1)}, bf16[4,4,144,1088]{3,2,1,0:T(8,128)(2,1)}, u32[]{:S(2)}, u32[]{:S(2)}) collective-permute-start(bf16[4,4,144,1088]{3,2,1,0:T(8,128)(2,1)} %broadcast_select_fusion.1), channel_id=1, source_target_pairs={{0,1},{1,0},{2,3},{3,2},{4,5},{5,4},{6,7},{7,6},{8,9},{9,8},{10,11... | collective-permute-start | bytes 15040520 | tf_op jit(solution)/shard_map/ppermute | solution.py:396
  476.4 209.9 %reduce-scatter.6.cloned.1.call-start = ((), (), s32[]{:S(2)}) async-start(), calls=%async_computation.4 | async-start | bytes 1658880 | tf_op jit(solution)/shard_map/reduce_scatter | solution.py:698
  491.2 88.7 %collective-permute-start.42 = (bf16[2,2,144,1088]{3,2,1,0:T(8,128)(2,1)}, bf16[2,2,144,1088]{3,2,1,0:T(8,128)(2,1)}, u32[]{:S(2)}, u32[]{:S(2)}) collective-permute-start(bf16[2,2,144,1088]{3,2,1,0:T(8,128)(2,1)} %get-tuple-element.177), channel_id=1, source_target_pairs={{0,4},{4,0},{1,5},{5,1},{2,6},{6,2},{3,7},{7,3},{8,12},{12,8},{9,1... | collective-permute-start | bytes 3760136 | tf_op jit(solution)/shard_map/ppermute | solution.py:396
  491.5 88.9 %collective-permute-start.43 = (bf16[2,2,144,1088]{3,2,1,0:T(8,128)(2,1)}, bf16[2,2,144,1088]{3,2,1,0:T(8,128)(2,1)}, u32[]{:S(2)}, u32[]{:S(2)}) collective-permute-start(bf16[2,2,144,1088]{3,2,1,0:T(8,128)(2,1)} %get-tuple-element.176), channel_id=1, source_target_pairs={{0,2},{1,3},{2,0},{3,1},{4,6},{5,7},{6,4},{7,5},{8,10},{9,11},{10,... | collective-permute-start | bytes 3760136 | tf_op jit(solution)/shard_map/ppermute | solution.py:396
  498.2 63.7 %collective-permute-start.36 = (bf16[2,128,1088]{1,2,0:T(8,128)(2,1)}, bf16[2,128,1088]{1,2,0:T(8,128)(2,1)}, u32[]{:S(2)}, u32[]{:S(2)}) collective-permute-start(bf16[2,128,1088]{1,2,0:T(8,128)(2,1)} %copy.152), channel_id=1, source_target_pairs={{0,1},{1,0},{2,3},{3,2},{4,5},{5,4},{6,7},{7,6},{8,9},{9,8},{10,11... | collective-permute-start | bytes 1671176 | tf_op jit(solution)/shard_map/ppermute | solution.py:396
  500.3 66.2 %collective-permute-start.37 = (bf16[2,128,1088]{1,2,0:T(8,128)(2,1)}, bf16[2,128,1088]{1,2,0:T(8,128)(2,1)}, u32[]{:S(2)}, u32[]{:S(2)}) collective-permute-start(bf16[2,128,1088]{1,2,0:T(8,128)(2,1)} %copy.154), channel_id=1, source_target_pairs={{0,2},{1,3},{2,0},{3,1},{4,6},{5,7},{6,4},{7,5},{8,10},{9,11},{10,... | collective-permute-start | bytes 1671176 | tf_op jit(solution)/shard_map/ppermute | solution.py:396
  560.9 51.5 %collective-permute-start.39 = (bf16[4,4,144,1088]{3,2,1,0:T(8,128)(2,1)}, bf16[4,4,144,1088]{3,2,1,0:T(8,128)(2,1)}, u32[]{:S(2)}, u32[]{:S(2)}) collective-permute-start(bf16[4,4,144,1088]{3,2,1,0:T(8,128)(2,1)} %broadcast_select_fusion), channel_id=1, source_target_pairs={{0,1},{1,0},{2,3},{3,2},{4,5},{5,4},{6,7},{7,6},{8,9},{9,8},{10,11... | collective-permute-start | bytes 15040520 | tf_op jit(solution)/shard_map/ppermute | solution.py:396
  566.5 24.5 %collective-permute-start.38 = (bf16[2,128,1088]{1,2,0:T(8,128)(2,1)}, bf16[2,128,1088]{1,2,0:T(8,128)(2,1)}, u32[]{:S(2)}, u32[]{:S(2)}) collective-permute-start(bf16[2,128,1088]{1,2,0:T(8,128)(2,1)} %copy.156), channel_id=1, source_target_pairs={{0,3},{1,2},{2,1},{3,0},{4,7},{5,6},{6,5},{7,4},{8,11},{9,10},{10,... | collective-permute-start | bytes 1671176 | tf_op jit(solution)/shard_map/ppermute | solution.py:396
  579.9 20.2 %collective-permute-start.66 = (bf16[2,1,144,1088]{3,2,1,0:T(8,128)(2,1)}, bf16[2,1,144,1088]{3,2,1,0:T(8,128)(2,1)}, u32[]{:S(2)}, u32[]{:S(2)}) collective-permute-start(bf16[2,1,144,1088]{3,2,1,0:T(8,128)(2,1)} %pad_maximum_fusion.9.refs_0_), channel_id=1, source_target_pairs={{0,1},{1,0},{2,3},{3,2},{4,5},{5,4},{6,7},{7,6},{8,9},{9,8},{10,11... | collective-permute-start | bytes 1880072 | tf_op jit(solution)/shard_map/ppermute | solution.py:396
  579.9 20.2 %collective-permute-start.67 = (bf16[2,1,144,1088]{3,2,1,0:T(8,128)(2,1)}, bf16[2,1,144,1088]{3,2,1,0:T(8,128)(2,1)}, u32[]{:S(2)}, u32[]{:S(2)}) collective-permute-start(bf16[2,1,144,1088]{3,2,1,0:T(8,128)(2,1)} %collective-permute-done.65.refs_1_), channel_id=1, source_target_pairs={{0,1},{1,0},{2,3},{3,2},{4,5},{5,4},{6,7},{7,6},{8,9},{9,8},{10,11... | collective-permute-start | bytes 1880072 | tf_op jit(solution)/shard_map/ppermute | solution.py:396
  585.7 19.9 %collective-permute-start.44 = (bf16[2,144,1088]{2,1,0:T(8,128)(2,1)}, bf16[2,144,1088]{2,1,0:T(8,128)(2,1)}, u32[]{:S(2)}, u32[]{:S(2)}) collective-permute-start(bf16[2,144,1088]{2,1,0:T(8,128)(2,1)} %select_bitcast_fusion.3), channel_id=1, source_target_pairs={{0,2},{1,3},{2,0},{3,1},{4,6},{5,7},{6,4},{7,5},{8,10},{9,11},{10,... | collective-permute-start | bytes 1880072 | tf_op jit(solution)/shard_map/ppermute | solution.py:396
  619.2 31.0 %collective-permute-start.40 = (bf16[2,2,144,1088]{3,2,1,0:T(8,128)(2,1)S(1)}, bf16[2,2,144,1088]{3,2,1,0:T(8,128)(2,1)}, u32[]{:S(2)}, u32[]{:S(2)}) collective-permute-start(bf16[2,2,144,1088]{3,2,1,0:T(8,128)(2,1)S(1)} %get-tuple-element.175), channel_id=1, source_target_pairs={{0,4},{4,0},{1,5},{5,1},{2,6},{6,2},{3,7},{7,3},{8,12},{12,8},{9,1... | collective-permute-start | bytes 3760136 | tf_op jit(solution)/shard_map/ppermute | solution.py:396
  620.9 30.7 %collective-permute-start.41 = (bf16[2,2,144,1088]{3,2,1,0:T(8,128)(2,1)S(1)}, bf16[2,2,144,1088]{3,2,1,0:T(8,128)(2,1)}, u32[]{:S(2)}, u32[]{:S(2)}) collective-permute-start(bf16[2,2,144,1088]{3,2,1,0:T(8,128)(2,1)S(1)} %get-tuple-element.174), channel_id=1, source_target_pairs={{0,2},{1,3},{2,0},{3,1},{4,6},{5,7},{6,4},{7,5},{8,10},{9,11},{10,... | collective-permute-start | bytes 3760136 | tf_op jit(solution)/shard_map/ppermute | solution.py:396
  622.5 103.8 %reduce-scatter.4.cloned.1.call-start = ((), (), s32[]{:S(2)}) async-start(), calls=%async_computation.3 | async-start | bytes 1658880 | tf_op jit(solution)/shard_map/reduce_scatter | solution.py:698
  678.3 41.5 %collective-permute-start.48 = (bf16[2,128,1088]{1,2,0:T(8,128)(2,1)}, bf16[2,128,1088]{1,2,0:T(8,128)(2,1)}, u32[]{:S(2)}, u32[]{:S(2)}) collective-permute-start(bf16[2,128,1088]{1,2,0:T(8,128)(2,1)} %copy.160), channel_id=1, source_target_pairs={{0,1},{1,0},{2,3},{3,2},{4,5},{5,4},{6,7},{7,6},{8,9},{9,8},{10,11... | collective-permute-start | bytes 1671176 | tf_op jit(solution)/shard_map/ppermute | solution.py:396
  680.4 44.2 %collective-permute-start.49 = (bf16[2,128,1088]{1,2,0:T(8,128)(2,1)}, bf16[2,128,1088]{1,2,0:T(8,128)(2,1)}, u32[]{:S(2)}, u32[]{:S(2)}) collective-permute-start(bf16[2,128,1088]{1,2,0:T(8,128)(2,1)} %copy.162), channel_id=1, source_target_pairs={{0,2},{1,3},{2,0},{3,1},{4,6},{5,7},{6,4},{7,5},{8,10},{9,11},{10,... | collective-permute-start | bytes 1671176 | tf_op jit(solution)/shard_map/ppermute | solution.py:396
  683.2 42.8 %collective-permute-start.50 = (bf16[2,128,1088]{1,2,0:T(8,128)(2,1)}, bf16[2,128,1088]{1,2,0:T(8,128)(2,1)S(1)}, u32[]{:S(2)}, u32[]{:S(2)}) collective-permute-start(bf16[2,128,1088]{1,2,0:T(8,128)(2,1)} %copy.164), channel_id=1, source_target_pairs={{0,3},{1,2},{2,1},{3,0},{4,7},{5,6},{6,5},{7,4},{8,11},{9,10},{10,... | collective-permute-start | bytes 1671176 | tf_op jit(solution)/shard_map/ppermute | solution.py:396
  687.4 25.1 %collective-permute-start.60 = (bf16[1,144,1088]{2,1,0:T(8,128)(2,1)S(1)}, bf16[1,144,1088]{2,1,0:T(8,128)(2,1)S(1)}, u32[]{:S(2)}, u32[]{:S(2)}) collective-permute-start(bf16[1,144,1088]{2,1,0:T(8,128)(2,1)S(1)} %broadcast_select_fusion.13), channel_id=1, source_target_pairs={{0,4},{4,0},{1,5},{5,1},{2,6},{6,2},{3,7},{7,3},{8,12},{12,8},{9,1... | collective-permute-start | bytes 940040 | tf_op jit(solution)/shard_map/ppermute | solution.py:396
  719.6 27.9 %collective-permute-start.62 = (bf16[2,1,144,1088]{3,2,1,0:T(8,128)(2,1)S(1)}, bf16[2,1,144,1088]{3,2,1,0:T(8,128)(2,1)}, u32[]{:S(2)}, u32[]{:S(2)}) collective-permute-start(bf16[2,1,144,1088]{3,2,1,0:T(8,128)(2,1)S(1)} %pad_maximum_fusion.8.refs_0_), channel_id=1, source_target_pairs={{0,1},{1,0},{2,3},{3,2},{4,5},{5,4},{6,7},{7,6},{8,9},{9,8},{10,11... | collective-permute-start | bytes 1880072 | tf_op jit(solution)/shard_map/ppermute | solution.py:396
  719.7 26.5 %collective-permute-start.55 = (bf16[4,16,1088]{2,1,0:T(8,128)(2,1)S(1)}, bf16[4,16,1088]{2,1,0:T(8,128)(2,1)S(1)}, u32[]{:S(2)}, u32[]{:S(2)}) collective-permute-start(bf16[4,16,1088]{2,1,0:T(8,128)(2,1)S(1)} %add_convert_fusion.9), channel_id=1, source_target_pairs={{0,16},{8,24},{16,0},{24,8},{1,17},{9,25},{17,1},{25,9},{2,18},{10... | collective-permute-start | bytes 417800 | tf_op jit(solution)/shard_map/ppermute | solution.py:396
  729.0 18.6 %collective-permute-start.63 = (bf16[2,1,144,1088]{3,2,1,0:T(8,128)(2,1)S(1)}, bf16[2,1,144,1088]{3,2,1,0:T(8,128)(2,1)}, u32[]{:S(2)}, u32[]{:S(2)}) collective-permute-start(bf16[2,1,144,1088]{3,2,1,0:T(8,128)(2,1)S(1)} %collective-permute-done.61.refs_1_), channel_id=1, source_target_pairs={{0,1},{1,0},{2,3},{3,2},{4,5},{5,4},{6,7},{7,6},{8,9},{9,8},{10,11... | collective-permute-start | bytes 1880072 | tf_op jit(solution)/shard_map/ppermute | solution.py:396
  (81 other events, 1082.0 us)
Sparse Core Ops, SparseCore 0:
  10.2 35.6 all-gather.6
  54.3 34.8 all-gather.8
  112.6 32.3 all-gather.10
  476.6 30.9 reduce-scatter.7
  622.6 32.0 reduce-scatter.5
  686.5 33.9 reduce-scatter.3

commit v5 on v4

--- a/solution.py
+++ b/solution.py
@@ -58,7 +58,8 @@
     return key_at <= query_at
 
 
-def attention_forward_kernel(blocks, width, order_ref, q_ref, k_ref, v_ref, o_ref, lse_ref):
+def attention_forward_kernel(blocks, width, order_ref, q_ref, k_ref, v_ref, *refs):
+    o_ref, lse_ref = refs[-2:]
     count, local = k_ref.shape[1], k_ref.shape[3]
     tile = blocks * local
     keys = only_valid(sorted_rows(k_ref, (0,), order_ref, 0, count), width)
@@ -157,7 +158,7 @@
     return 2 if count % 2 == 0 else 1
 
 
-def attention_forward(joined, order):
+def attention_forward(joined, order, ties=()):
     _, count, seqs, local, width = joined.shape
     length = count * local
     pairs = pl.cdiv(width, LANES)
@@ -169,7 +170,8 @@
         grid_spec=pltpu.PrefetchScalarGridSpec(
             num_scalar_prefetch=1,
             grid=(seqs, pairs),
-            in_specs=[spec(0), spec(1), spec(2)],
+            in_specs=[spec(0), spec(1), spec(2)]
+            + [pl.BlockSpec(memory_space=pl.ANY)] * len(ties),
             out_specs=[
                 pl.BlockSpec((count, 1, local, LANES), lambda s, h, order: (0, s, 0, h)),
                 pl.BlockSpec((1, 1, 8, length), lambda s, h, order: (s, h, 0, 0)),
@@ -185,7 +187,7 @@
             bytes_accessed=8 * seqs * length * width // COST_SCALE,
             transcendentals=0,
         ),
-    )(order, joined, joined, joined)
+    )(order, joined, joined, joined, *ties)
 
 
 def attention_backward(joined, mixed, grad_mixed, lse, order, ties=()):
@@ -276,7 +278,8 @@
     low_ref[...] = (standard * row(small_ref, G_TWO) + row(small_ref, B_TWO)).astype(BF16)
 
 
-def hidden_kernel(low_ref, w_ref, bias_ref, act_ref, slope_ref):
+def hidden_kernel(low_ref, w_ref, bias_ref, *refs):
+    act_ref, slope_ref = refs[-2:]
     low = low_ref[...]
     scale = 0.7978845608028654
     for which in range(w_ref.shape[0]):
@@ -415,29 +418,30 @@
 def to_sequences(values, count, *earlier):
     seqs, local, width = values.shape
     own = lax.axis_index("ctx")
-    parts = values.reshape(count, seqs // count, local, width)
+    parts = values.swapaxes(1, 2).reshape(count, seqs // count, width, local)
     pieces = []
     for offset in range(count):
         piece = lax.dynamic_index_in_dim(parts, own ^ offset, keepdims=False)
         if earlier:
             piece = held(piece, *earlier)
-        pieces.append(swap(piece, "ctx", offset) if offset else piece)
-    return row_major(jnp.stack(pieces))
+        pieces.append(row_major(swap(row_major(piece), "ctx", offset)) if offset else piece)
+    return row_major(row_major(jnp.stack(pieces)).swapaxes(2, 3))
 
 
 def to_blocks(values, kind, *earlier):
     count, share, local, width = values.shape
     own = lax.axis_index("ctx")
-    out = row_major(jnp.zeros((count, share, local, width), kind))
+    values = values.swapaxes(2, 3)
+    if earlier:
+        values = held(values, *earlier)
+    values = row_major(values)
+    out = row_major(jnp.zeros((count, share, width, local), kind))
     for offset in range(count):
-        piece = values[offset]
-        if earlier:
-            piece = held(piece, *earlier)
-        piece = row_major(piece)
+        piece = row_major(values[offset])
         if offset:
             piece = row_major(swap(piece, "ctx", offset))
         out = lax.dynamic_update_index_in_dim(out, piece.astype(kind), own ^ offset, 0)
-    return row_major(out).reshape(count * share, local, width)
+    return row_major(out).reshape(count * share, width, local).swapaxes(1, 2)
 
 
 class Windows:
@@ -575,7 +579,7 @@
     low_sum = add_pair(pick(win.y, *low), low_received)
     high_sum = add_pair(pick(win.x, *high), high_received)
     sums = jnp.concatenate([low_sum, high_sum], axis=0)
-    return sums, [corner(low_sent), corner(high_sent)], [corner(sums)]
+    return sums, [corner(low_sent)], [corner(sums)]
 
 
 def reduce_vectors(values):
@@ -643,7 +647,7 @@
         other_a = spread_cores(own_a)
         full_a = place(win, own_a, other_a, owned_rows, shards)
         vector_part = part_b[:, win.size : win.size + vector_rows]
-        own_b = spread_chips(held(part_b[:, : win.size], *own_a[-2:]), hold=other_a)
+        own_b = spread_chips(held(part_b[:, : win.size], own_a[2]), hold=[full_a])
     else:
         vector_part = gather_z(vector_tile)[:, :vector_rows]
         full_a, full_b, full_c = [
@@ -669,30 +673,30 @@
     if pairwise:
         other_b = spread_cores(own_b)
         full_b = place(win, own_b, other_b, owned_rows, shards)
-        own_c = spread_chips(held(part_c, joined, *own_b[-2:]), hold=other_b)
-        steps = [corner(array[1]) for array in own_c[:2]]
+        own_c = spread_chips(held(part_c, joined), hold=[full_b])
+        steps = [corner(own_c[0][1]), corner(own_c[1][1]), corner(own_c[2]), corner(own_c[3])]
     else:
-        steps = []
-    mixed, lse = attention_forward(joined, order)
+        steps = [corner(joined[0, 0])] * 4
+    mixed, lse = attention_forward(joined, order, ties=steps[:2])
     attended = mixed.reshape(rows, width)
     middle, low_two = by_rows(
         attended_kernel,
         [low_inputs, attended],
         [(w_a, 3, 1), small],
         [((), F32), ((), BF16)],
-        ties=steps,
     )
     w_fc = full_b.reshape(wide, width, width)
     low_act, slope = by_rows(
-        hidden_kernel, [low_two], [w_fc, bias_fc], [((wide,), BF16), ((wide,), BF16)]
+        hidden_kernel,
+        [low_two],
+        [w_fc, bias_fc],
+        [((wide,), BF16), ((wide,), BF16)],
+        ties=steps[2:],
     )
     if pairwise:
         full_c = place(win, own_c, spread_cores(own_c), owned_rows, shards, transposed=True)
     w_proj = full_c.reshape(wide, width, width)
-    low_grad_out = to_sequences(cotangent, count, *(own_b[-2:] if pairwise else ()))
-    if pairwise:
-        low_grad_out = held(low_grad_out, *own_c[-2:])
-    low_grad_out = low_grad_out.reshape(rows, width)
+    low_grad_out = to_sequences(cotangent, count, joined).reshape(rows, width)
 
     def finish_units(sums, *earlier):
         sums = lax.psum_scatter(sums, "shard", scatter_dimension=0, tiled=False)
@@ -745,7 +749,7 @@
         ties=[corner(grad_fc), *proj_marks[1]],
     )
     layer_out = to_blocks(
-        outputs.reshape(blocked), BF16, low_grad_middle, *proj_marks[2], *fc_marks[0]
+        outputs.reshape(blocked), BF16, *fc_marks[0][:1]
     )
     grad_out_weight = dot_tn(attended, low_grad_middle).astype(BF16)
     grad_joined = attention_backward(

time: 792 us -> 825 us (1.042)
  waiting for transfers between devices: 160 us -> 256 us
  local copies, waits for them, and re-layouts: 146 us -> 94.6 us
  between operations: 44.1 us -> 25.9 us
    ppermute x68, waiting for transfers between devices: 159 us -> 256 us  [swap(): lax.ppermute(values, axis, [(index, index ^ offset) for index in range(co...]
    unnamed x114 -> x130, local copies, waits for them, and re-layouts: 31.6 us -> 13.9 us
    ppermute x12 -> x0, local copies, waits for them, and re-layouts: 15.6 us -> none  [swap(): lax.ppermute(values, axis, [(index, index ^ offset) for index in range(co...]
    slice x22 -> x8, local copies, waits for them, and re-layouts: 23.4 us -> 8.1 us  [held(): entry = array[(0,) * array.ndim]]
    select_n x18 -> x17, other arithmetic: 23.1 us -> 20.4 us  [pick(): return jnp.where(bit == 0, on_zero, on_one)]
    select_n x15 -> x14, other arithmetic: 16.7 us -> 17.5 us  [held(): return jnp.where(wrong, jnp.zeros_like(values), values)]
  transfers between devices with their start and end apart: 74 -> 74, of which waited for: 29 -> 32; matrix products, arithmetic and copies ran while one was open for 29% -> 22% of each run, Pallas kernels for 30% -> 24%
where the time goes in v5:
time: 825 us; the launch traced here: 819 us
  waiting for transfers between devices  256 us (31%)
  Pallas kernels  239 us (29%)
  other arithmetic  98.2 us (12%)
  local copies, waits for them, and re-layouts  94.6 us (11%)
  starting transfers between devices  58.7 us (7%)
  matrix products  45.9 us (6%)
  between operations  25.9 us (3%)
    ppermute x68, waiting for transfers between devices, swap(): lax.ppermute(values, axis, [(index, index ^ offset) for index in range(co...  256 us
    pallas_call x7, Pallas kernels, by_rows(): pl.pallas_call(kernel, grid=(rows // tile,), in_specs=in_specs, out_specs...  140 us
    ppermute x68, starting transfers between devices, swap(): lax.ppermute(values, axis, [(index, index ^ offset) for index in range(co...  58.3 us
    pallas_call x6, Pallas kernels, assemble(): pl.pallas_call(functools.partial(assemble_kernel, groups, win.start, win....  39.5 us
    convert_element_type x16, other arithmetic, add_pair(): return (kept.astype(F32) + received.astype(F32)).astype(BF16)  36.1 us
    pallas_call x1, Pallas kernels, attention_forward(): pl.pallas_call(functools.partial(attention_forward_kernel, query_blocks(c...  31.1 us
    pallas_call x1, Pallas kernels, attention_backward(): pl.pallas_call(functools.partial(attention_backward_kernel, query_blocks(...  28.9 us
    select_n x17, other arithmetic, pick(): return jnp.where(bit == 0, on_zero, on_one)  20.4 us
  transfers between devices with their start and end apart: 74, of which 32 were waited for; matrix products, arithmetic and copies ran while one was open for 22% of the time, Pallas kernels for 24%

profile of v5, /device:TPU:0, one launch (start us, length us, event | category | flops | bytes accessed | tf_op | source)
XLA Modules:
  0.0 818.8 jit_solution(6556396639944696326)
XLA Ops:
  17.8 11.1 %collective-permute-done.2 = bf16[2,1088,128]{2,1,0:T(8,128)(2,1)S(1)} collective-permute-done((bf16[2,1088,128]{2,1,0:T(8,128)(2,1)}, bf16[2,1088,128]{2,1,0:T(8,128)(2,1)S(1)}, u32[]{:S(2)}, u32[]{:S(2)}) %collective-permute-start.2) | collective-permute-done | bytes 557088 | tf_op jit(solution)/shard_map/ppermute | solution.py:399
  28.9 12.1 %collective-permute-done.1 = bf16[2,1088,128]{2,1,0:T(8,128)(2,1)} collective-permute-done((bf16[2,1088,128]{2,1,0:T(8,128)(2,1)}, bf16[2,1088,128]{2,1,0:T(8,128)(2,1)}, u32[]{:S(2)}, u32[]{:S(2)}) %collective-permute-start.1) | collective-permute-done | bytes 557088 | tf_op jit(solution)/shard_map/ppermute | solution.py:399
  51.4 13.3 %collective-permute-done.3 = bf16[2,144,1088]{2,1,0:T(8,128)(2,1)S(1)} collective-permute-done((bf16[2,144,1088]{2,1,0:T(8,128)(2,1)}, bf16[2,144,1088]{2,1,0:T(8,128)(2,1)S(1)}, u32[]{:S(2)}, u32[]{:S(2)}) %collective-permute-start.3) | collective-permute-done | bytes 626720 | tf_op jit(solution)/shard_map/ppermute | solution.py:399
  72.8 25.1 %collective-permute-done.5.refs_2_ = bf16[2,2,144,1088]{3,2,1,0:T(8,128)(2,1)} collective-permute-done((bf16[2,2,144,1088]{3,2,1,0:T(8,128)(2,1)S(1)}, bf16[2,2,144,1088]{3,2,1,0:T(8,128)(2,1)}, u32[]{:S(2)}, u32[]{:S(2)}) %collective-permute-start.5) | collective-permute-done | bytes 1253408 | tf_op jit(solution)/shard_map/ppermute | solution.py:399
  105.9 12.8 %collective-permute-done.14 = bf16[2,144,1088]{2,1,0:T(8,128)(2,1)} collective-permute-done((bf16[2,144,1088]{2,1,0:T(8,128)(2,1)}, bf16[2,144,1088]{2,1,0:T(8,128)(2,1)}, u32[]{:S(2)}, u32[]{:S(2)}) %collective-permute-start.14) | collective-permute-done | bytes 626720 | tf_op jit(solution)/shard_map/ppermute | solution.py:399
  122.7 10.6 %collective-permute-done.15 = bf16[2,144,1088]{2,1,0:T(8,128)(2,1)} collective-permute-done((bf16[2,144,1088]{2,1,0:T(8,128)(2,1)}, bf16[2,144,1088]{2,1,0:T(8,128)(2,1)}, u32[]{:S(2)}, u32[]{:S(2)}) %collective-permute-start.15) | collective-permute-done | bytes 626720 | tf_op jit(solution)/shard_map/ppermute | solution.py:399
  133.3 8.6 %shard_map.271 = bf16[4,4,272,1088]{3,2,1,0:T(8,128)(2,1)} custom-call(s32[3]{0:T(128)} %pad_add_fusion.here_ref, bf16[2,2,144,1088]{3,2,1,0:T(8,128)(2,1)} %copy-done.18, bf16[2,2,144,1088]{3,2,1,0:T(8,128)(2,1)} %copy-done.19, bf16[2,2,144,1088]{3,2,1,0:T(8,128)(2,1)} %collective-permute-done.5.refs_2_, ...), custom_call_target="tpu_custom_call" | custom-call | bytes 18939904 | tf_op jit(solution)/shard_map/pallas_call | solution.py:494
  143.1 16.7 %shard_map.272 = (bf16[3,1024,1088]{2,1,0:T(8,128)(2,1)}, bf16[1024,1088]{1,0:T(8,128)(2,1)}) custom-call(bf16[1024,1088]{1,0:T(8,128)(2,1)} %bitcast.280, bf16[4,1088,1088]{2,1,0:T(8,128)(2,1)} %bitcast.260, f32[8,1088]{1,0:T(8,128)} %reshape.205.small_ref), custom_call_target="tpu_custom_call" | custom-call | flops 1363673088 | bytes 2580736 | tf_op jit(solution)/shard_map/pallas_call | solution.py:378
  176.4 32.8 %collective-permute-done.13 = bf16[2,1088,128]{2,1,0:T(8,128)(2,1)S(1)} collective-permute-done((bf16[2,1088,128]{2,1,0:T(8,128)(2,1)S(1)}, bf16[2,1088,128]{2,1,0:T(8,128)(2,1)S(1)}, u32[]{:S(2)}, u32[]{:S(2)}) %collective-permute-start.13) | collective-permute-done | bytes 557088 | tf_op jit(solution)/shard_map/ppermute | solution.py:399
  211.2 6.6 collective-permute-done.12
  218.8 7.8 collective-permute-done.22
  233.8 9.9 %collective-permute-done.23 = bf16[2,144,1088]{2,1,0:T(8,128)(2,1)} collective-permute-done((bf16[2,144,1088]{2,1,0:T(8,128)(2,1)S(1)}, bf16[2,144,1088]{2,1,0:T(8,128)(2,1)}, u32[]{:S(2)}, u32[]{:S(2)}) %collective-permute-start.23) | collective-permute-done | bytes 626720 | tf_op jit(solution)/shard_map/ppermute | solution.py:399
  243.7 8.6 %shard_map.273 = bf16[4,4,272,1088]{3,2,1,0:T(8,128)(2,1)} custom-call(s32[3]{0:T(128)} %pad_add_fusion.here_ref, bf16[2,2,144,1088]{3,2,1,0:T(8,128)(2,1)} %maximum_select_fusion.refs_0_, bf16[2,2,144,1088]{3,2,1,0:T(8,128)(2,1)} %maximum_select_fusion.1.refs_1_, bf16[2,2,144,1088]{3,2,1,0:T(8,128)(2,1)} %collective-permute-done.16.refs_2_, ...), custom_call_target="tpu_custom_call" | custom-call | bytes 18939904 | tf_op jit(solution)/shard_map/pallas_call | solution.py:494
  260.5 31.1 %shard_map.274 = (bf16[4,2,128,1088]{3,2,1,0:T(8,128)(2,1)}, f32[2,9,8,512]{3,2,1,0:T(8,128)}) custom-call(s32[4]{0:T(128)} %broadcast_xor_fusion.order_ref, bf16[3,4,2,128,1088]{4,3,2,1,0:T(8,128)(2,1)} %bitcast.254, bf16[3,4,2,128,1088]{4,3,2,1,0:T(8,128)(2,1)} %bitcast.255, bf16[3,4,2,128,1088]{4,3,2,1,0:T(8,128)(2,1)} %bitcast.256, ...), custom_call_target="tpu_custom_call" | custom-call | flops 1207959552 | bytes 1114112 | tf_op jit(solution)/shard_map/pallas_call | solution.py:168
  291.5 8.5 %shard_map.275 = (f32[1024,1088]{1,0:T(8,128)}, bf16[1024,1088]{1,0:T(8,128)(2,1)}) custom-call(bf16[1024,1088]{1,0:T(8,128)(2,1)} %bitcast.281, bf16[1024,1088]{1,0:T(8,128)(2,1)} %bitcast.291, bf16[4,1088,1088]{2,1,0:T(8,128)(2,1)} %bitcast.261, f32[8,1088]{1,0:T(8,128)} %reshape.205.small_ref), custom_call_target="tpu_custom_call" | custom-call | flops 454557696 | bytes 2580736 | tf_op jit(solution)/shard_map/pallas_call | solution.py:378
  302.4 27.8 %shard_map.276 = (bf16[4,1024,1088]{2,1,0:T(8,128)(2,1)}, bf16[4,1024,1088]{2,1,0:T(8,128)(2,1)}) custom-call(bf16[1024,1088]{1,0:T(8,128)(2,1)} %get-tuple-element.69.low_ref, bf16[4,1088,1088]{2,1,0:T(8,128)(2,1)} %bitcast.264, f32[4,1,1088]{2,1,0:T(1,128)} %reshape.211.bias_ref, bf16[16,128]{1,0:T(8,128)(2,1)} %slice.564.refs_0_, ...), custom_call_target="tpu_custom_call" | custom-call | flops 1818230784 | bytes 3693696 | tf_op jit(solution)/shard_map/pallas_call | solution.py:378
  330.2 14.8 %convolution_convert_fusion.1 = bf16[4,1088,1088]{2,1,0:T(8,128)(2,1)S(1)} fusion(bf16[4,1024,1088]{2,1,0:T(8,128)(2,1)} %get-tuple-element.72.act_ref, bf16[1024,1088,1]{1,0,2:T(8,128)(2,1)S(1)} %bitcast.286), kind=kOutput, calls=%fused_computation.1 | convolution fusion | flops 9701965824 | bytes 20611072 | tf_op jit(solution)/shard_map/ctx,td->cxd/dot_general | solution.py:722
  354.5 6.1 collective-permute-done.26.refs_4_
  360.6 5.7 collective-permute-done.27.refs_5_
  367.8 8.6 %shard_map.277 = bf16[4,4,272,1088]{3,2,1,0:T(8,128)(2,1)} custom-call(s32[3]{0:T(128)} %pad_add_fusion.here_ref, bf16[2,2,144,1088]{3,2,1,0:T(8,128)(2,1)} %copy-done.14, bf16[2,2,144,1088]{3,2,1,0:T(8,128)(2,1)} %copy-done.16, bf16[2,2,144,1088]{3,2,1,0:T(8,128)(2,1)} %copy-done.34, bf16[2,2,144,1088]{3,2,1,0:T(8,128)(2,1)} %collective-permute-done.25.refs_3_, ...), custom_call_target="tpu_custom_call" | custom-call | bytes 18939904 | tf_op jit(solution)/shard_map/pallas_call | solution.py:494
  376.4 19.8 %shard_map.278 = bf16[1024,1088]{1,0:T(8,128)(2,1)} custom-call(f32[1024,1088]{1,0:T(8,128)} %get-tuple-element.71.middle_ref, bf16[4,1024,1088]{2,1,0:T(8,128)(2,1)} %get-tuple-element.72.act_ref, bf16[4,1088,1088]{2,1,0:T(8,128)(2,1)} %bitcast.266, f32[8,1088]{1,0:T(8,128)} %reshape.205.small_ref, bf16[16,128]{1,0:T(8,128)(2,1)} %slice.568.refs_0_), custom_call_target="tpu_custom_call" | custom-call | flops 1818230784 | bytes 3138304 | tf_op jit(solution)/shard_map/pallas_call | solution.py:378
  397.5 6.6 add_convert_fusion.2
  410.8 20.9 %shard_map.279 = (bf16[4,1024,1088]{2,1,0:T(8,128)(2,1)}, f32[8,1088]{1,0:T(8,128)}) custom-call(bf16[1024,1088]{1,0:T(8,128)(2,1)} %bitcast.287, bf16[4,1024,1088]{2,1,0:T(8,128)(2,1)} %get-tuple-element.70.slope_ref, bf16[4,1088,1088]{2,1,0:T(8,128)(2,1)} %bitcast.267, bf16[16,128]{1,0:T(8,128)(2,1)} %slice.569.refs_0_, bf16[16,128]{1,0:T(8,128)(2,1)} %slice.575.refs_1_, ...), custom_call_target="tpu_custom_call" | custom-call | flops 1818230784 | bytes 3696384 | tf_op jit(solution)/shard_map/pallas_call | solution.py:378
  431.7 13.4 %convolution_convert_fusion = bf16[4,1088,1088]{1,2,0:T(8,128)(2,1)S(1)} fusion(bf16[4,1024,1088]{2,1,0:T(8,128)(2,1)} %get-tuple-element.73.hidden_ref, bf16[1024,1088]{1,0:T(8,128)(2,1)S(1)} %copy-done.32), kind=kOutput, calls=%fused_computation | convolution fusion | flops 9701965824 | bytes 20611072 | tf_op jit(solution)/shard_map/td,ctx->cdx/dot_general | solution.py:740
  459.8 27.4 %shard_map.280 = (f32[1024,1088]{1,0:T(8,128)}, bf16[1024,1088]{1,0:T(8,128)(2,1)}, bf16[1024,1088]{1,0:T(8,128)(2,1)}, f32[8,1088]{1,0:T(8,128)}) custom-call(bf16[4,1024,1088]{2,1,0:T(8,128)(2,1)} %get-tuple-element.73.hidden_ref, bf16[1024,1088]{1,0:T(8,128)(2,1)} %bitcast.288, f32[1024,1088]{1,0:T(8,128)} %get-tuple-element.71.middle_ref, ...), custom_call_target="tpu_custom_call" | custom-call | flops 2272788480 | bytes 5441024 | tf_op jit(solution)/shard_map/pallas_call | solution.py:378
  487.2 5.5 convolution_convert_fusion.3
  495.8 6.6 add_convert_fusion.1
  522.3 28.9 %shard_map.281 = bf16[3,4,2,128,1088]{4,3,2,1,0:T(8,128)(2,1)} custom-call(s32[4]{0:T(128)} %broadcast_xor_fusion.order_ref, bf16[3,4,2,128,1088]{4,3,2,1,0:T(8,128)(2,1)} %bitcast.257, bf16[3,4,2,128,1088]{4,3,2,1,0:T(8,128)(2,1)} %bitcast.258, bf16[3,4,2,128,1088]{4,3,2,1,0:T(8,128)(2,1)} %bitcast.259, bf16[4,2,128,1088]{3,2,1,0:T(8,128)(2,1)} %get-tuple-element.68.o_ref, ...), custom_call_target="tpu_custom_call" | custom-call | flops 1509949440 | bytes 2228224 | tf_op jit(solution)/shard_map/pallas_call | solution.py:201
  552.3 12.3 %convolution_convert_fusion.2 = bf16[3,1088,1088]{1,2,0:T(8,128)(2,1)S(1)} fusion(bf16[3,1024,1088]{2,1,0:T(8,128)(2,1)} %bitcast.284, bf16[1024,1088]{1,0:T(8,128)(2,1)S(1)} %copy-done.59), kind=kOutput, calls=%fused_computation.2 | convolution fusion | flops 7276474368 | bytes 16015360 | tf_op jit(solution)/shard_map/td,ctx->cdx/dot_general | solution.py:763
  564.6 4.4 broadcast_select_fusion
  574.9 7.0 collective-permute-done.64
  588.6 11.3 %collective-permute-done.65.refs_1_ = bf16[2,1,144,1088]{3,2,1,0:T(8,128)(2,1)S(1)} collective-permute-done((bf16[2,1,144,1088]{3,2,1,0:T(8,128)(2,1)S(1)}, bf16[2,1,144,1088]{3,2,1,0:T(8,128)(2,1)S(1)}, u32[]{:S(2)}, u32[]{:S(2)}) %collective-permute-start.65) | collective-permute-done | bytes 626720 | tf_op jit(solution)/shard_map/ppermute | solution.py:399
  607.0 4.9 collective-permute-done.33
  612.4 9.5 %collective-permute-done.34 = bf16[2,1088,128]{2,1,0:T(8,128)(2,1)S(1)} collective-permute-done((bf16[2,1088,128]{2,1,0:T(8,128)(2,1)S(1)}, bf16[2,1088,128]{2,1,0:T(8,128)(2,1)S(1)}, u32[]{:S(2)}, u32[]{:S(2)}) %collective-permute-start.34) | collective-permute-done | bytes 557088 | tf_op jit(solution)/shard_map/ppermute | solution.py:399
  626.2 5.1 shard_map.285
  631.2 5.1 collective-permute-done.44
  643.1 4.6 add_convert_fusion
  656.3 18.5 %shard_map.282 = (bf16[1024,1088]{1,0:T(8,128)(2,1)}, f32[8,1088]{1,0:T(8,128)}) custom-call(bf16[3,1024,1088]{2,1,0:T(8,128)(2,1)} %bitcast.285, f32[1024,1088]{1,0:T(8,128)} %get-tuple-element.82.grad_middle_ref, bf16[1024,1088]{1,0:T(8,128)(2,1)} %bitcast.282, bf16[4,1088,1088]{2,1,0:T(8,128)(2,1)} %bitcast.263, f32[8,1088]{1,0:T(8,128)} %reshape.205.small_ref, ...), custom_call_target="tpu_custom_call" | custom-call | flops 1363673088 | bytes 3144192 | tf_op jit(solution)/shard_map/pallas_call | solution.py:378
  677.3 4.4 collective-permute-done.40
  689.9 13.5 %collective-permute-done.46 = bf16[2,144,1088]{2,1,0:T(8,128)(2,1)} collective-permute-done((bf16[2,144,1088]{2,1,0:T(8,128)(2,1)}, bf16[2,144,1088]{2,1,0:T(8,128)(2,1)}, u32[]{:S(2)}, u32[]{:S(2)}) %collective-permute-start.46) | collective-permute-done | bytes 626720 | tf_op jit(solution)/shard_map/ppermute | solution.py:399
  733.1 13.9 %collective-permute-done.53 = bf16[4,16,1088]{2,1,0:T(8,128)(2,1)S(1)} collective-permute-done((bf16[4,16,1088]{2,1,0:T(8,128)(2,1)S(1)}, bf16[4,16,1088]{2,1,0:T(8,128)(2,1)S(1)}, u32[]{:S(2)}, u32[]{:S(2)}) %collective-permute-start.53) | collective-permute-done | bytes 139296 | tf_op jit(solution)/shard_map/ppermute | solution.py:399
  750.1 6.3 collective-permute-done.54
  765.1 6.4 collective-permute-done.56
  778.4 4.3 shard_map.284
  782.7 6.3 collective-permute-done.57.refs_1_
  793.2 5.8 concatenate.42
  799.0 4.3 shard_map.283
  803.3 4.3 slice_bitcast_fusion.7
  (405 shorter events, 233.2 us)
Async XLA Ops:
  7.2 38.7 %all-gather.7.cloned.1.call-start = ((), (), s32[]{:S(2)}) async-start(), calls=%async_computation.6 | async-start | bytes 1658880 | tf_op jit(solution)/shard_map/all_gather | solution.py:634
  9.8 90.6 %all-gather.9.cloned.1.call-start = ((), (), s32[]{:S(2)}) async-start(), calls=%async_computation.7 | async-start | bytes 1843200 | tf_op jit(solution)/shard_map/all_gather | solution.py:634
  15.5 25.4 %collective-permute-start.1 = (bf16[2,1088,128]{2,1,0:T(8,128)(2,1)}, bf16[2,1088,128]{2,1,0:T(8,128)(2,1)}, u32[]{:S(2)}, u32[]{:S(2)}) collective-permute-start(bf16[2,1088,128]{2,1,0:T(8,128)(2,1)} %get-tuple-element.128), channel_id=1, source_target_pairs={{0,2},{1,3},{2,0},{3,1},{4,6},{5,7},{6,4},{7,5},{8,10},{9,11},{10,... | collective-permute-start | bytes 1671176 | tf_op jit(solution)/shard_map/ppermute | solution.py:399
  16.1 24.8 %collective-permute-start = (bf16[2,1088,128]{2,1,0:T(8,128)(2,1)}, bf16[2,1088,128]{2,1,0:T(8,128)(2,1)}, u32[]{:S(2)}, u32[]{:S(2)}) collective-permute-start(bf16[2,1088,128]{2,1,0:T(8,128)(2,1)} %get-tuple-element.129), channel_id=1, source_target_pairs={{0,1},{1,0},{2,3},{3,2},{4,5},{5,4},{6,7},{7,6},{8,9},{9,8},{10,11... | collective-permute-start | bytes 1671176 | tf_op jit(solution)/shard_map/ppermute | solution.py:399
  51.3 123.5 %all-gather.11.cloned.1.call-start = ((), (), s32[]{:S(2)}) async-start(), calls=%async_computation.8 | async-start | bytes 1658880 | tf_op jit(solution)/shard_map/all_gather | solution.py:634
  67.7 30.3 %collective-permute-start.5 = (bf16[2,2,144,1088]{3,2,1,0:T(8,128)(2,1)S(1)}, bf16[2,2,144,1088]{3,2,1,0:T(8,128)(2,1)}, u32[]{:S(2)}, u32[]{:S(2)}) collective-permute-start(bf16[2,2,144,1088]{3,2,1,0:T(8,128)(2,1)S(1)} %pad_maximum_fusion.3.refs_0_), channel_id=1, source_target_pairs={{0,2},{1,3},{2,0},{3,1},{4,6},{5,7},{6,4},{7,5},{8,10},{9,11},{10,... | collective-permute-start | bytes 3760136 | tf_op jit(solution)/shard_map/ppermute | solution.py:399
  70.9 34.3 %collective-permute-start.6 = (bf16[2,2,144,1088]{3,2,1,0:T(8,128)(2,1)S(1)}, bf16[2,2,144,1088]{3,2,1,0:T(8,128)(2,1)}, u32[]{:S(2)}, u32[]{:S(2)}) collective-permute-start(bf16[2,2,144,1088]{3,2,1,0:T(8,128)(2,1)S(1)} %pad_maximum_fusion.4.refs_1_), channel_id=1, source_target_pairs={{0,4},{4,0},{1,5},{5,1},{2,6},{6,2},{3,7},{7,3},{8,12},{12,8},{9,1... | collective-permute-start | bytes 3760136 | tf_op jit(solution)/shard_map/ppermute | solution.py:399
  104.7 28.6 %collective-permute-start.7 = (bf16[2,2,144,1088]{3,2,1,0:T(8,128)(2,1)S(1)}, bf16[2,2,144,1088]{3,2,1,0:T(8,128)(2,1)}, u32[]{:S(2)}, u32[]{:S(2)}) collective-permute-start(bf16[2,2,144,1088]{3,2,1,0:T(8,128)(2,1)S(1)} %pad_maximum_fusion.3.refs_0_), channel_id=1, source_target_pairs={{0,1},{1,0},{2,3},{3,2},{4,5},{5,4},{6,7},{7,6},{8,9},{9,8},{10,11... | collective-permute-start | bytes 3760136 | tf_op jit(solution)/shard_map/ppermute | solution.py:399
  104.7 28.6 %collective-permute-start.8 = (bf16[2,2,144,1088]{3,2,1,0:T(8,128)(2,1)S(1)}, bf16[2,2,144,1088]{3,2,1,0:T(8,128)(2,1)}, u32[]{:S(2)}, u32[]{:S(2)}) collective-permute-start(bf16[2,2,144,1088]{3,2,1,0:T(8,128)(2,1)S(1)} %pad_maximum_fusion.4.refs_1_), channel_id=1, source_target_pairs={{0,1},{1,0},{2,3},{3,2},{4,5},{5,4},{6,7},{7,6},{8,9},{9,8},{10,11... | collective-permute-start | bytes 3760136 | tf_op jit(solution)/shard_map/ppermute | solution.py:399
  105.2 28.1 %collective-permute-start.9 = (bf16[2,2,144,1088]{3,2,1,0:T(8,128)(2,1)}, bf16[2,2,144,1088]{3,2,1,0:T(8,128)(2,1)}, u32[]{:S(2)}, u32[]{:S(2)}) collective-permute-start(bf16[2,2,144,1088]{3,2,1,0:T(8,128)(2,1)} %collective-permute-done.5.refs_2_), channel_id=1, source_target_pairs={{0,1},{1,0},{2,3},{3,2},{4,5},{5,4},{6,7},{7,6},{8,9},{9,8},{10,11... | collective-permute-start | bytes 3760136 | tf_op jit(solution)/shard_map/ppermute | solution.py:399
  105.2 28.0 %collective-permute-start.10 = (bf16[2,2,144,1088]{3,2,1,0:T(8,128)(2,1)}, bf16[2,2,144,1088]{3,2,1,0:T(8,128)(2,1)}, u32[]{:S(2)}, u32[]{:S(2)}) collective-permute-start(bf16[2,2,144,1088]{3,2,1,0:T(8,128)(2,1)} %collective-permute-done.6.refs_3_), channel_id=1, source_target_pairs={{0,1},{1,0},{2,3},{3,2},{4,5},{5,4},{6,7},{7,6},{8,9},{9,8},{10,11... | collective-permute-start | bytes 3760136 | tf_op jit(solution)/shard_map/ppermute | solution.py:399
  105.7 465.3 %reduce-scatter.8.cloned.1.call-start = ((), (), s32[]{:S(2)}) async-start(), calls=%async_computation.5 | async-start | bytes 1658880 | tf_op jit(solution)/shard_map/reduce_scatter | solution.py:702
  166.1 52.2 %collective-permute-start.16 = (bf16[2,2,144,1088]{3,2,1,0:T(8,128)(2,1)}, bf16[2,2,144,1088]{3,2,1,0:T(8,128)(2,1)}, u32[]{:S(2)}, u32[]{:S(2)}) collective-permute-start(bf16[2,2,144,1088]{3,2,1,0:T(8,128)(2,1)} %maximum_select_fusion.refs_0_), channel_id=1, source_target_pairs={{0,2},{1,3},{2,0},{3,1},{4,6},{5,7},{6,4},{7,5},{8,10},{9,11},{10,... | collective-permute-start | bytes 3760136 | tf_op jit(solution)/shard_map/ppermute | solution.py:399
  169.8 48.6 %collective-permute-start.17 = (bf16[2,2,144,1088]{3,2,1,0:T(8,128)(2,1)}, bf16[2,2,144,1088]{3,2,1,0:T(8,128)(2,1)}, u32[]{:S(2)}, u32[]{:S(2)}) collective-permute-start(bf16[2,2,144,1088]{3,2,1,0:T(8,128)(2,1)} %maximum_select_fusion.1.refs_1_), channel_id=1, source_target_pairs={{0,4},{4,0},{1,5},{5,1},{2,6},{6,2},{3,7},{7,3},{8,12},{12,8},{9,1... | collective-permute-start | bytes 3760136 | tf_op jit(solution)/shard_map/ppermute | solution.py:399
  172.9 36.2 %collective-permute-start.13 = (bf16[2,1088,128]{2,1,0:T(8,128)(2,1)S(1)}, bf16[2,1088,128]{2,1,0:T(8,128)(2,1)S(1)}, u32[]{:S(2)}, u32[]{:S(2)}) collective-permute-start(bf16[2,1088,128]{2,1,0:T(8,128)(2,1)S(1)} %get-tuple-element.123), channel_id=1, source_target_pairs={{0,3},{1,2},{2,1},{3,0},{4,7},{5,6},{6,5},{7,4},{8,11},{9,10},{10,... | collective-permute-start | bytes 1671176 | tf_op jit(solution)/shard_map/ppermute | solution.py:399
  172.9 44.8 %collective-permute-start.12 = (bf16[2,1088,128]{2,1,0:T(8,128)(2,1)}, bf16[2,1088,128]{2,1,0:T(8,128)(2,1)S(1)}, u32[]{:S(2)}, u32[]{:S(2)}) collective-permute-start(bf16[2,1088,128]{2,1,0:T(8,128)(2,1)} %get-tuple-element.124), channel_id=1, source_target_pairs={{0,2},{1,3},{2,0},{3,1},{4,6},{5,7},{6,4},{7,5},{8,10},{9,11},{10,... | collective-permute-start | bytes 1671176 | tf_op jit(solution)/shard_map/ppermute | solution.py:399
  173.7 44.0 %collective-permute-start.11 = (bf16[2,1088,128]{2,1,0:T(8,128)(2,1)}, bf16[2,1088,128]{2,1,0:T(8,128)(2,1)}, u32[]{:S(2)}, u32[]{:S(2)}) collective-permute-start(bf16[2,1088,128]{2,1,0:T(8,128)(2,1)} %get-tuple-element.125), channel_id=1, source_target_pairs={{0,1},{1,0},{2,3},{3,2},{4,5},{5,4},{6,7},{7,6},{8,9},{9,8},{10,11... | collective-permute-start | bytes 1671176 | tf_op jit(solution)/shard_map/ppermute | solution.py:399
  217.7 25.9 %collective-permute-start.18 = (bf16[2,2,144,1088]{3,2,1,0:T(8,128)(2,1)}, bf16[2,2,144,1088]{3,2,1,0:T(8,128)(2,1)}, u32[]{:S(2)}, u32[]{:S(2)}) collective-permute-start(bf16[2,2,144,1088]{3,2,1,0:T(8,128)(2,1)} %maximum_select_fusion.refs_0_), channel_id=1, source_target_pairs={{0,1},{1,0},{2,3},{3,2},{4,5},{5,4},{6,7},{7,6},{8,9},{9,8},{10,11... | collective-permute-start | bytes 3760136 | tf_op jit(solution)/shard_map/ppermute | solution.py:399
  217.7 25.9 %collective-permute-start.19 = (bf16[2,2,144,1088]{3,2,1,0:T(8,128)(2,1)}, bf16[2,2,144,1088]{3,2,1,0:T(8,128)(2,1)}, u32[]{:S(2)}, u32[]{:S(2)}) collective-permute-start(bf16[2,2,144,1088]{3,2,1,0:T(8,128)(2,1)} %maximum_select_fusion.1.refs_1_), channel_id=1, source_target_pairs={{0,1},{1,0},{2,3},{3,2},{4,5},{5,4},{6,7},{7,6},{8,9},{9,8},{10,11... | collective-permute-start | bytes 3760136 | tf_op jit(solution)/shard_map/ppermute | solution.py:399
  218.3 25.4 %collective-permute-start.20 = (bf16[2,2,144,1088]{3,2,1,0:T(8,128)(2,1)}, bf16[2,2,144,1088]{3,2,1,0:T(8,128)(2,1)}, u32[]{:S(2)}, u32[]{:S(2)}) collective-permute-start(bf16[2,2,144,1088]{3,2,1,0:T(8,128)(2,1)} %collective-permute-done.16.refs_2_), channel_id=1, source_target_pairs={{0,1},{1,0},{2,3},{3,2},{4,5},{5,4},{6,7},{7,6},{8,9},{9,8},{10,11... | collective-permute-start | bytes 3760136 | tf_op jit(solution)/shard_map/ppermute | solution.py:399
  218.3 25.4 %collective-permute-start.21 = (bf16[2,2,144,1088]{3,2,1,0:T(8,128)(2,1)}, bf16[2,2,144,1088]{3,2,1,0:T(8,128)(2,1)}, u32[]{:S(2)}, u32[]{:S(2)}) collective-permute-start(bf16[2,2,144,1088]{3,2,1,0:T(8,128)(2,1)} %collective-permute-done.17.refs_3_), channel_id=1, source_target_pairs={{0,1},{1,0},{2,3},{3,2},{4,5},{5,4},{6,7},{7,6},{8,9},{9,8},{10,11... | collective-permute-start | bytes 3760136 | tf_op jit(solution)/shard_map/ppermute | solution.py:399
  255.0 45.1 %collective-permute-start.24 = (bf16[2,2,144,1088]{3,2,1,0:T(8,128)(2,1)S(1)}, bf16[2,2,144,1088]{3,2,1,0:T(8,128)(2,1)S(1)}, u32[]{:S(2)}, u32[]{:S(2)}) collective-permute-start(bf16[2,2,144,1088]{3,2,1,0:T(8,128)(2,1)S(1)} %maximum_select_fusion.2.refs_0_), channel_id=1, source_target_pairs={{0,2},{1,3},{2,0},{3,1},{4,6},{5,7},{6,4},{7,5},{8,10},{9,11},{10,... | collective-permute-start | bytes 3760136 | tf_op jit(solution)/shard_map/ppermute | solution.py:399
  257.1 43.7 %collective-permute-start.25 = (bf16[2,2,144,1088]{3,2,1,0:T(8,128)(2,1)S(1)}, bf16[2,2,144,1088]{3,2,1,0:T(8,128)(2,1)}, u32[]{:S(2)}, u32[]{:S(2)}) collective-permute-start(bf16[2,2,144,1088]{3,2,1,0:T(8,128)(2,1)S(1)} %maximum_select_fusion.3.refs_1_), channel_id=1, source_target_pairs={{0,4},{4,0},{1,5},{5,1},{2,6},{6,2},{3,7},{7,3},{8,12},{12,8},{9,1... | collective-permute-start | bytes 3760136 | tf_op jit(solution)/shard_map/ppermute | solution.py:399
  350.9 46.6 %collective-permute-start.30 = (bf16[4,4,144,1088]{3,2,1,0:T(8,128)(2,1)}, bf16[4,4,144,1088]{3,2,1,0:T(8,128)(2,1)}, u32[]{:S(2)}, u32[]{:S(2)}) collective-permute-start(bf16[4,4,144,1088]{3,2,1,0:T(8,128)(2,1)} %broadcast_select_fusion.2), channel_id=1, source_target_pairs={{0,1},{1,0},{2,3},{3,2},{4,5},{5,4},{6,7},{7,6},{8,9},{9,8},{10,11... | collective-permute-start | bytes 15040520 | tf_op jit(solution)/shard_map/ppermute | solution.py:399
  406.8 45.2 %collective-permute-start.35 = (bf16[2,2,144,1088]{3,2,1,0:T(8,128)(2,1)}, bf16[2,2,144,1088]{3,2,1,0:T(8,128)(2,1)}, u32[]{:S(2)}, u32[]{:S(2)}) collective-permute-start(bf16[2,2,144,1088]{3,2,1,0:T(8,128)(2,1)} %get-tuple-element.106), channel_id=1, source_target_pairs={{0,4},{4,0},{1,5},{5,1},{2,6},{6,2},{3,7},{7,3},{8,12},{12,8},{9,1... | collective-permute-start | bytes 3760136 | tf_op jit(solution)/shard_map/ppermute | solution.py:399
  408.1 44.0 %collective-permute-start.36 = (bf16[2,2,144,1088]{3,2,1,0:T(8,128)(2,1)S(1)}, bf16[2,2,144,1088]{3,2,1,0:T(8,128)(2,1)}, u32[]{:S(2)}, u32[]{:S(2)}) collective-permute-start(bf16[2,2,144,1088]{3,2,1,0:T(8,128)(2,1)S(1)} %get-tuple-element.105), channel_id=1, source_target_pairs={{0,2},{1,3},{2,0},{3,1},{4,6},{5,7},{6,4},{7,5},{8,10},{9,11},{10,... | collective-permute-start | bytes 3760136 | tf_op jit(solution)/shard_map/ppermute | solution.py:399
  448.4 47.4 %collective-permute-start.31 = (bf16[4,4,144,1088]{3,2,1,0:T(8,128)(2,1)}, bf16[4,4,144,1088]{3,2,1,0:T(8,128)(2,1)}, u32[]{:S(2)}, u32[]{:S(2)}) collective-permute-start(bf16[4,4,144,1088]{3,2,1,0:T(8,128)(2,1)} %broadcast_select_fusion.1), channel_id=1, source_target_pairs={{0,1},{1,0},{2,3},{3,2},{4,5},{5,4},{6,7},{7,6},{8,9},{9,8},{10,11... | collective-permute-start | bytes 15040520 | tf_op jit(solution)/shard_map/ppermute | solution.py:399
  457.1 36.1 %collective-permute-start.37 = (bf16[2,144,1088]{2,1,0:T(8,128)(2,1)S(1)}, bf16[2,144,1088]{2,1,0:T(8,128)(2,1)S(1)}, u32[]{:S(2)}, u32[]{:S(2)}) collective-permute-start(bf16[2,144,1088]{2,1,0:T(8,128)(2,1)S(1)} %fusion.22), channel_id=1, source_target_pairs={{0,2},{1,3},{2,0},{3,1},{4,6},{5,7},{6,4},{7,5},{8,10},{9,11},{10,... | collective-permute-start | bytes 1880072 | tf_op jit(solution)/shard_map/ppermute | solution.py:399
  457.8 35.5 %collective-permute-start.38 = (bf16[2,144,1088]{2,1,0:T(8,128)(2,1)S(1)}, bf16[2,144,1088]{2,1,0:T(8,128)(2,1)S(1)}, u32[]{:S(2)}, u32[]{:S(2)}) collective-permute-start(bf16[2,144,1088]{2,1,0:T(8,128)(2,1)S(1)} %select_bitcast_fusion.4), channel_id=1, source_target_pairs={{0,4},{4,0},{1,5},{5,1},{2,6},{6,2},{3,7},{7,3},{8,12},{12,8},{9,1... | collective-permute-start | bytes 1880072 | tf_op jit(solution)/shard_map/ppermute | solution.py:399
  495.7 229.1 %reduce-scatter.6.cloned.1.call-start = ((), (), s32[]{:S(2)}) async-start(), calls=%async_computation.4 | async-start | bytes 1658880 | tf_op jit(solution)/shard_map/reduce_scatter | solution.py:702
  507.9 92.0 %collective-permute-start.42 = (bf16[2,2,144,1088]{3,2,1,0:T(8,128)(2,1)}, bf16[2,2,144,1088]{3,2,1,0:T(8,128)(2,1)}, u32[]{:S(2)}, u32[]{:S(2)}) collective-permute-start(bf16[2,2,144,1088]{3,2,1,0:T(8,128)(2,1)} %get-tuple-element.102), channel_id=1, source_target_pairs={{0,4},{4,0},{1,5},{5,1},{2,6},{6,2},{3,7},{7,3},{8,12},{12,8},{9,1... | collective-permute-start | bytes 3760136 | tf_op jit(solution)/shard_map/ppermute | solution.py:399
  509.1 91.5 %collective-permute-start.43 = (bf16[2,2,144,1088]{3,2,1,0:T(8,128)(2,1)}, bf16[2,2,144,1088]{3,2,1,0:T(8,128)(2,1)}, u32[]{:S(2)}, u32[]{:S(2)}) collective-permute-start(bf16[2,2,144,1088]{3,2,1,0:T(8,128)(2,1)} %get-tuple-element.101), channel_id=1, source_target_pairs={{0,2},{1,3},{2,0},{3,1},{4,6},{5,7},{6,4},{7,5},{8,10},{9,11},{10,... | collective-permute-start | bytes 3760136 | tf_op jit(solution)/shard_map/ppermute | solution.py:399
  521.7 63.6 %collective-permute-start.32 = (bf16[2,1088,128]{2,1,0:T(8,128)(2,1)}, bf16[2,1088,128]{2,1,0:T(8,128)(2,1)}, u32[]{:S(2)}, u32[]{:S(2)}) collective-permute-start(bf16[2,1088,128]{2,1,0:T(8,128)(2,1)} %get-tuple-element.120), channel_id=1, source_target_pairs={{0,1},{1,0},{2,3},{3,2},{4,5},{5,4},{6,7},{7,6},{8,9},{9,8},{10,11... | collective-permute-start | bytes 1671176 | tf_op jit(solution)/shard_map/ppermute | solution.py:399
  569.2 73.9 %collective-permute-start.39 = (bf16[4,4,144,1088]{3,2,1,0:T(8,128)(2,1)}, bf16[4,4,144,1088]{3,2,1,0:T(8,128)(2,1)}, u32[]{:S(2)}, u32[]{:S(2)}) collective-permute-start(bf16[4,4,144,1088]{3,2,1,0:T(8,128)(2,1)} %broadcast_select_fusion), channel_id=1, source_target_pairs={{0,1},{1,0},{2,3},{3,2},{4,5},{5,4},{6,7},{7,6},{8,9},{9,8},{10,11... | collective-permute-start | bytes 15040520 | tf_op jit(solution)/shard_map/ppermute | solution.py:399
  585.2 26.6 %collective-permute-start.33 = (bf16[2,1088,128]{2,1,0:T(8,128)(2,1)S(1)}, bf16[2,1088,128]{2,1,0:T(8,128)(2,1)S(1)}, u32[]{:S(2)}, u32[]{:S(2)}) collective-permute-start(bf16[2,1088,128]{2,1,0:T(8,128)(2,1)S(1)} %copy-done.47), channel_id=1, source_target_pairs={{0,2},{1,3},{2,0},{3,1},{4,6},{5,7},{6,4},{7,5},{8,10},{9,11},{10,... | collective-permute-start | bytes 1671176 | tf_op jit(solution)/shard_map/ppermute | solution.py:399
  599.9 21.9 %collective-permute-start.34 = (bf16[2,1088,128]{2,1,0:T(8,128)(2,1)S(1)}, bf16[2,1088,128]{2,1,0:T(8,128)(2,1)S(1)}, u32[]{:S(2)}, u32[]{:S(2)}) collective-permute-start(bf16[2,1088,128]{2,1,0:T(8,128)(2,1)S(1)} %copy-done.46), channel_id=1, source_target_pairs={{0,3},{1,2},{2,1},{3,0},{4,7},{5,6},{6,5},{7,4},{8,11},{9,10},{10,... | collective-permute-start | bytes 1671176 | tf_op jit(solution)/shard_map/ppermute | solution.py:399
  600.0 25.3 %collective-permute-start.66 = (bf16[2,1,144,1088]{3,2,1,0:T(8,128)(2,1)S(1)}, bf16[2,1,144,1088]{3,2,1,0:T(8,128)(2,1)S(1)}, u32[]{:S(2)}, u32[]{:S(2)}) collective-permute-start(bf16[2,1,144,1088]{3,2,1,0:T(8,128)(2,1)S(1)} %pad_maximum_fusion.10.refs_0_), channel_id=1, source_target_pairs={{0,1},{1,0},{2,3},{3,2},{4,5},{5,4},{6,7},{7,6},{8,9},{9,8},{10,11... | collective-permute-start | bytes 1880072 | tf_op jit(solution)/shard_map/ppermute | solution.py:399
  600.6 25.6 %collective-permute-start.67 = (bf16[2,1,144,1088]{3,2,1,0:T(8,128)(2,1)S(1)}, bf16[2,1,144,1088]{3,2,1,0:T(8,128)(2,1)}, u32[]{:S(2)}, u32[]{:S(2)}) collective-permute-start(bf16[2,1,144,1088]{3,2,1,0:T(8,128)(2,1)S(1)} %collective-permute-done.65.refs_1_), channel_id=1, source_target_pairs={{0,1},{1,0},{2,3},{3,2},{4,5},{5,4},{6,7},{7,6},{8,9},{9,8},{10,11... | collective-permute-start | bytes 1880072 | tf_op jit(solution)/shard_map/ppermute | solution.py:399
  611.9 24.5 %collective-permute-start.44 = (bf16[2,144,1088]{2,1,0:T(8,128)(2,1)}, bf16[2,144,1088]{2,1,0:T(8,128)(2,1)}, u32[]{:S(2)}, u32[]{:S(2)}) collective-permute-start(bf16[2,144,1088]{2,1,0:T(8,128)(2,1)} %select_bitcast_fusion.3), channel_id=1, source_target_pairs={{0,2},{1,3},{2,0},{3,1},{4,6},{5,7},{6,4},{7,5},{8,10},{9,11},{10,... | collective-permute-start | bytes 1880072 | tf_op jit(solution)/shard_map/ppermute | solution.py:399
  649.9 31.7 %collective-permute-start.40 = (bf16[2,2,144,1088]{3,2,1,0:T(8,128)(2,1)S(1)}, bf16[2,2,144,1088]{3,2,1,0:T(8,128)(2,1)}, u32[]{:S(2)}, u32[]{:S(2)}) collective-permute-start(bf16[2,2,144,1088]{3,2,1,0:T(8,128)(2,1)S(1)} %get-tuple-element.100), channel_id=1, source_target_pairs={{0,4},{4,0},{1,5},{5,1},{2,6},{6,2},{3,7},{7,3},{8,12},{12,8},{9,1... | collective-permute-start | bytes 3760136 | tf_op jit(solution)/shard_map/ppermute | solution.py:399
  651.7 31.4 %collective-permute-start.41 = (bf16[2,2,144,1088]{3,2,1,0:T(8,128)(2,1)S(1)}, bf16[2,2,144,1088]{3,2,1,0:T(8,128)(2,1)}, u32[]{:S(2)}, u32[]{:S(2)}) collective-permute-start(bf16[2,2,144,1088]{3,2,1,0:T(8,128)(2,1)S(1)} %get-tuple-element.99), channel_id=1, source_target_pairs={{0,2},{1,3},{2,0},{3,1},{4,6},{5,7},{6,4},{7,5},{8,10},{9,11},{10,... | collective-permute-start | bytes 3760136 | tf_op jit(solution)/shard_map/ppermute | solution.py:399
  655.0 106.4 %reduce-scatter.4.cloned.1.call-start = ((), (), s32[]{:S(2)}) async-start(), calls=%async_computation.3 | async-start | bytes 1658880 | tf_op jit(solution)/shard_map/reduce_scatter | solution.py:702
  716.9 39.5 %collective-permute-start.48 = (bf16[2,1088,128]{2,1,0:T(8,128)(2,1)S(1)}, bf16[2,1088,128]{2,1,0:T(8,128)(2,1)}, u32[]{:S(2)}, u32[]{:S(2)}) collective-permute-start(bf16[2,1088,128]{2,1,0:T(8,128)(2,1)S(1)} %get-tuple-element.117), channel_id=1, source_target_pairs={{0,1},{1,0},{2,3},{3,2},{4,5},{5,4},{6,7},{7,6},{8,9},{9,8},{10,11... | collective-permute-start | bytes 1671176 | tf_op jit(solution)/shard_map/ppermute | solution.py:399
  716.9 44.4 %collective-permute-start.49 = (bf16[2,1088,128]{2,1,0:T(8,128)(2,1)S(1)}, bf16[2,1088,128]{2,1,0:T(8,128)(2,1)}, u32[]{:S(2)}, u32[]{:S(2)}) collective-permute-start(bf16[2,1088,128]{2,1,0:T(8,128)(2,1)S(1)} %get-tuple-element.116), channel_id=1, source_target_pairs={{0,2},{1,3},{2,0},{3,1},{4,6},{5,7},{6,4},{7,5},{8,10},{9,11},{10,... | collective-permute-start | bytes 1671176 | tf_op jit(solution)/shard_map/ppermute | solution.py:399
  718.1 55.9 %collective-permute-start.50 = (bf16[2,1088,128]{2,1,0:T(8,128)(2,1)}, bf16[2,1088,128]{2,1,0:T(8,128)(2,1)}, u32[]{:S(2)}, u32[]{:S(2)}) collective-permute-start(bf16[2,1088,128]{2,1,0:T(8,128)(2,1)} %get-tuple-element.115), channel_id=1, source_target_pairs={{0,3},{1,2},{2,1},{3,0},{4,7},{5,6},{6,5},{7,4},{8,11},{9,10},{10,... | collective-permute-start | bytes 1671176 | tf_op jit(solution)/shard_map/ppermute | solution.py:399
  725.8 22.8 %collective-permute-start.60 = (bf16[1,144,1088]{2,1,0:T(8,128)(2,1)S(1)}, bf16[1,144,1088]{2,1,0:T(8,128)(2,1)S(1)}, u32[]{:S(2)}, u32[]{:S(2)}) collective-permute-start(bf16[1,144,1088]{2,1,0:T(8,128)(2,1)S(1)} %broadcast_select_fusion.14), channel_id=1, source_target_pairs={{0,4},{4,0},{1,5},{5,1},{2,6},{6,2},{3,7},{7,3},{8,12},{12,8},{9,1... | collective-permute-start | bytes 940040 | tf_op jit(solution)/shard_map/ppermute | solution.py:399
  756.4 21.1 %collective-permute-start.62 = (bf16[2,1,144,1088]{3,2,1,0:T(8,128)(2,1)S(1)}, bf16[2,1,144,1088]{3,2,1,0:T(8,128)(2,1)S(1)}, u32[]{:S(2)}, u32[]{:S(2)}) collective-permute-start(bf16[2,1,144,1088]{3,2,1,0:T(8,128)(2,1)S(1)} %pad_maximum_fusion.9.refs_0_), channel_id=1, source_target_pairs={{0,1},{1,0},{2,3},{3,2},{4,5},{5,4},{6,7},{7,6},{8,9},{9,8},{10,11... | collective-permute-start | bytes 1880072 | tf_op jit(solution)/shard_map/ppermute | solution.py:399
  756.4 19.7 %collective-permute-start.55 = (bf16[4,16,1088]{2,1,0:T(8,128)(2,1)S(1)}, bf16[4,16,1088]{2,1,0:T(8,128)(2,1)S(1)}, u32[]{:S(2)}, u32[]{:S(2)}) collective-permute-start(bf16[4,16,1088]{2,1,0:T(8,128)(2,1)S(1)} %add_convert_fusion.9), channel_id=1, source_target_pairs={{0,16},{8,24},{16,0},{24,8},{1,17},{9,25},{17,1},{25,9},{2,18},{10... | collective-permute-start | bytes 417800 | tf_op jit(solution)/shard_map/ppermute | solution.py:399
  (91 other events, 1341.2 us)
Sparse Core Ops, SparseCore 0:
  10.2 35.6 all-gather.6
  51.4 34.8 all-gather.8
  105.8 33.5 all-gather.10
  495.8 31.9 reduce-scatter.7
  655.1 30.9 reduce-scatter.5
  724.2 34.6 reduce-scatter.3

commit v6 on v5

--- a/solution.py
+++ b/solution.py
@@ -259,7 +259,8 @@
     return small_ref[index : index + 1, :]
 
 
-def qkv_kernel(x_ref, w_ref, small_ref, joined_ref, low_ref):
+def qkv_kernel(x_ref, w_ref, small_ref, *refs):
+    joined_ref, low_ref = refs[-2:]
     standard, _ = standardize(x_ref[...].astype(F32))
     low = (standard * row(small_ref, G_ONE) + row(small_ref, B_ONE)).astype(BF16)
     low_ref[...] = low
@@ -404,6 +405,8 @@
 
 
 def held(values, *earlier):
+    if not earlier:
+        return values
     wrong = jnp.zeros((), jnp.bool_)
     for array in earlier:
         entry = array[(0,) * array.ndim]
@@ -415,33 +418,29 @@
     return jnp.where(bit == 0, on_zero, on_one)
 
 
-def to_sequences(values, count, *earlier):
+def to_sequences(values, count, start=(), finish=()):
     seqs, local, width = values.shape
     own = lax.axis_index("ctx")
     parts = values.swapaxes(1, 2).reshape(count, seqs // count, width, local)
-    pieces = []
-    for offset in range(count):
-        piece = lax.dynamic_index_in_dim(parts, own ^ offset, keepdims=False)
-        if earlier:
-            piece = held(piece, *earlier)
-        pieces.append(row_major(swap(row_major(piece), "ctx", offset)) if offset else piece)
-    return row_major(row_major(jnp.stack(pieces)).swapaxes(2, 3))
-
-
-def to_blocks(values, kind, *earlier):
+    mine = [lax.dynamic_index_in_dim(parts, own ^ i, keepdims=False) for i in range(count)]
+    far = row_major(held(jnp.stack(mine[2:]), *start))
+    far = row_major(swap(far, "ctx", 2))
+    near = row_major(swap(row_major(jnp.stack([mine[1], far[1]])), "ctx", 1))
+    whole = row_major(jnp.stack([mine[0], near[0], far[0], near[1]]))
+    return row_major(held(whole, *finish).swapaxes(2, 3))
+
+
+def to_blocks(values, kind, *start):
     count, share, local, width = values.shape
     own = lax.axis_index("ctx")
-    values = values.swapaxes(2, 3)
-    if earlier:
-        values = held(values, *earlier)
-    values = row_major(values)
+    values = row_major(held(values.swapaxes(2, 3), *start))
+    far = row_major(swap(row_major(values[2:]), "ctx", 2))
+    near = row_major(swap(row_major(jnp.stack([values[1], far[1]])), "ctx", 1))
     out = row_major(jnp.zeros((count, share, width, local), kind))
-    for offset in range(count):
-        piece = row_major(values[offset])
-        if offset:
-            piece = row_major(swap(piece, "ctx", offset))
+    for offset, piece in enumerate([values[0], near[0], far[0], near[1]]):
         out = lax.dynamic_update_index_in_dim(out, piece.astype(kind), own ^ offset, 0)
-    return row_major(out).reshape(count * share, width, local).swapaxes(1, 2)
+    out = row_major(out).reshape(count * share, width, local).swapaxes(1, 2)
+    return out, near
 
 
 class Windows:
@@ -504,7 +503,7 @@
     )(here, *own, *other)
 
 
-def spread_chips(mine, hold=()):
+def spread_chips(mine):
     shards = mine.shape[0]
     if shards == 1:
         first = jnp.stack([mine, swap(mine, "replica", 1)])
@@ -512,9 +511,10 @@
     split = shards // 2
     low, high = mine[:split], mine[split:]
     low_there, high_there = after(swap(low, "replica", 1), swap(high, "ctx", 2))
-    first = held(jnp.stack([low, low_there]), *hold)
-    second = held(jnp.stack([high, high_there]), *hold)
-    return [first, second, swap(first, "ctx", 2), swap(second, "replica", 1)]
+    first = jnp.stack([low, low_there])
+    second = jnp.stack([high, high_there])
+    third, fourth = after(swap(first, "ctx", 2), swap(second, "replica", 1))
+    return [first, second, third, fourth]
 
 
 def chip_groups(shards):
@@ -583,7 +583,6 @@
 
 
 def reduce_vectors(values):
-    values = add_pair(values, swap(values, "ctx", 1))
     values = add_pair(values, swap(values, "replica", 1))
     values = add_pair(values, swap(values, "ctx", 2))
     step = 1
@@ -647,7 +646,7 @@
         other_a = spread_cores(own_a)
         full_a = place(win, own_a, other_a, owned_rows, shards)
         vector_part = part_b[:, win.size : win.size + vector_rows]
-        own_b = spread_chips(held(part_b[:, : win.size], own_a[2]), hold=[full_a])
+        own_b = spread_chips(held(part_b[:, : win.size], own_a[2]))
     else:
         vector_part = gather_z(vector_tile)[:, :vector_rows]
         full_a, full_b, full_c = [
@@ -666,14 +665,15 @@
     held_by = jnp.sum(jnp.where(block_order[None, :] == index[:, None], index[None, :], 0), axis=1)
     order = (held_by ^ lax.axis_index("ctx")).astype(jnp.int32)
 
+    steps = [corner(own_b[0][1]), corner(own_b[1][1])] if pairwise else []
     joined, low_one = by_rows(
-        qkv_kernel, [low_inputs], [(w_a, 0, 3), small], [((3,), BF16), ((), BF16)]
+        qkv_kernel, [low_inputs], [(w_a, 0, 3), small], [((3,), BF16), ((), BF16)], ties=steps
     )
     joined = joined.reshape((3,) + blocked)
     if pairwise:
         other_b = spread_cores(own_b)
         full_b = place(win, own_b, other_b, owned_rows, shards)
-        own_c = spread_chips(held(part_c, joined), hold=[full_b])
+        own_c = spread_chips(held(part_c, own_b[2], joined))
         steps = [corner(own_c[0][1]), corner(own_c[1][1]), corner(own_c[2]), corner(own_c[3])]
     else:
         steps = [corner(joined[0, 0])] * 4
@@ -696,12 +696,18 @@
     if pairwise:
         full_c = place(win, own_c, spread_cores(own_c), owned_rows, shards, transposed=True)
     w_proj = full_c.reshape(wide, width, width)
-    low_grad_out = to_sequences(cotangent, count, joined).reshape(rows, width)
-
-    def finish_units(sums, *earlier):
-        sums = lax.psum_scatter(sums, "shard", scatter_dimension=0, tiled=False)
-        own = spread_chips(held(sums[None], *earlier))
-        return place(win, own, spread_cores(own), owned_rows, 1, kind=F32)[:, 0]
+    start, finish = ((own_c[2], mixed), (full_c,)) if pairwise else ((), ())
+    low_grad_out = to_sequences(cotangent, count, start, finish).reshape(rows, width)
+
+    def finish_units(groups, *earlier):
+        sums = [
+            lax.psum_scatter(group, "shard", scatter_dimension=0, tiled=False)
+            for group in groups
+        ]
+        own = spread_chips(held(jnp.stack(sums), *earlier))
+        return place(
+            win, own, spread_cores(own), owned_rows, len(sums), transposed=True, kind=F32
+        )
 
     def reduce_whole(grads, transposed=False):
         if transposed:
@@ -740,6 +746,7 @@
     grad_fc = jnp.einsum("td,ctx->cdx", low_two, grad_hidden, preferred_element_type=F32)
     grad_fc = grad_fc.astype(BF16)
     partial_fc, fc_marks = start_units(by_shard(grad_fc))
+    layer_out, returned = to_blocks(outputs.reshape(blocked), BF16, *proj_marks[1])
     grad_middle, low_grad_middle, grad_mixed, sums_middle = by_rows(
         middle_back_kernel,
         [grad_hidden, low_grad_out, middle],
@@ -748,9 +755,6 @@
         sums=8,
         ties=[corner(grad_fc), *proj_marks[1]],
     )
-    layer_out = to_blocks(
-        outputs.reshape(blocked), BF16, *fc_marks[0][:1]
-    )
     grad_out_weight = dot_tn(attended, low_grad_middle).astype(BF16)
     grad_joined = attention_backward(
         joined,
@@ -758,7 +762,7 @@
         grad_mixed.reshape(blocked),
         lse,
         order,
-        ties=[corner(grad_out_weight), *proj_marks[2], *fc_marks[0]],
+        ties=[corner(grad_out_weight), corner(returned), *proj_marks[2], *fc_marks[0]],
     ).reshape(3, rows, width)
     grad_qkv = jnp.einsum("td,ctx->cdx", low_one, grad_joined, preferred_element_type=F32)
     grad_qkv = grad_qkv.astype(BF16)
@@ -776,9 +780,6 @@
     )
     if pairwise:
         partial_a, _, _ = reduce_second(win, halves, grad_inputs)
-    earlier = (partial_a,) if pairwise else ()
-    input_grad = to_blocks(grad_inputs.reshape(blocked), F32, *earlier)
-
     small_grads = sums_middle + sums_input
     grad_fc_bias = sums_hidden[:wide]
     vector_grads = jnp.concatenate(
@@ -794,16 +795,18 @@
         vector_grads.reshape(shards, vector_rows, width),
         ((0, 0), (0, -vector_rows % 16), (0, 0)),
     )
+    blocked_grads = grad_inputs.reshape(blocked)
     if pairwise:
-        owned_proj = finish_units(partial_proj, grad_joined)
-        owned_a = finish_units(partial_a)
-        owned_fc = finish_units(partial_fc, partial_a)
+        vector_grads = held(vector_grads, partial_a)
+        vector_grads = add_pair(vector_grads, swap(vector_grads, "ctx", 1))
+        (owned_a,) = finish_units([partial_a])
+        owned_proj, owned_fc = finish_units([partial_proj, partial_fc], vector_grads)
+        input_grad, _ = to_blocks(blocked_grads, F32, vector_grads)
         owned_vectors = lax.dynamic_index_in_dim(
-            reduce_vectors(held(vector_grads, partial_a)),
-            lax.axis_index("shard"),
-            keepdims=False,
+            reduce_vectors(vector_grads), lax.axis_index("shard"), keepdims=False
         )
     else:
+        input_grad, _ = to_blocks(blocked_grads, F32)
         owned_proj = reduce_whole(partial_proj, transposed=True)
         owned_a, owned_fc = reduce_whole(partial_a), reduce_whole(partial_fc)
         owned_vectors = lax.psum_scatter(

time: 825 us -> 737 us (0.89)
  waiting for transfers between devices: 256 us -> 184 us
  other arithmetic: 98.2 us -> 82.4 us
  starting transfers between devices: 58.7 us -> 50 us
  local copies, waits for them, and re-layouts: 94.6 us -> 103 us
    ppermute x68 -> x64, waiting for transfers between devices: 256 us -> 163 us  [swap(): lax.ppermute(values, axis, [(index, index ^ offset) for index in range(co...]
    all_gather x3, waiting for transfers between devices: 0.73 us -> 21.4 us  [gather_z(): return lax.all_gather(values, 'shard', axis=0, tiled=False)]
    ppermute x68 -> x64, starting transfers between devices: 58.3 us -> 49.6 us  [swap(): lax.ppermute(values, axis, [(index, index ^ offset) for index in range(co...]
    select_n x14 -> x10, other arithmetic: 17.5 us -> 12.4 us  [held(): return jnp.where(wrong, jnp.zeros_like(values), values)]
    unnamed x130 -> x122, local copies, waits for them, and re-layouts: 13.9 us -> 18.5 us
    pallas_call x6 -> x5, Pallas kernels: 39.5 us -> 37.2 us  [assemble(): pl.pallas_call(functools.partial(assemble_kernel, groups, win.start, win....]
  transfers between devices with their start and end apart: 74 -> 70, of which waited for: 32 -> 25; matrix products, arithmetic and copies ran while one was open for 22% -> 22% of each run, Pallas kernels for 24% -> 32%
where the time goes in v6:
time: 737 us; the launch traced here: 731 us
  Pallas kernels  237 us (32%)
  waiting for transfers between devices  184 us (25%)
  local copies, waits for them, and re-layouts  103 us (14%)
  other arithmetic  82.4 us (11%)
  starting transfers between devices  50 us (7%)
  matrix products  45.8 us (6%)
  between operations  28.6 us (4%)
    ppermute x64, waiting for transfers between devices, swap(): lax.ppermute(values, axis, [(index, index ^ offset) for index in range(co...  163 us
    pallas_call x7, Pallas kernels, by_rows(): pl.pallas_call(kernel, grid=(rows // tile,), in_specs=in_specs, out_specs...  140 us
    ppermute x64, starting transfers between devices, swap(): lax.ppermute(values, axis, [(index, index ^ offset) for index in range(co...  49.6 us
    pallas_call x5, Pallas kernels, assemble(): pl.pallas_call(functools.partial(assemble_kernel, groups, win.start, win....  37.2 us
    convert_element_type x16, other arithmetic, add_pair(): return (kept.astype(F32) + received.astype(F32)).astype(BF16)  31.4 us
    pallas_call x1, Pallas kernels, attention_forward(): pl.pallas_call(functools.partial(attention_forward_kernel, query_blocks(c...  31.2 us
    pallas_call x1, Pallas kernels, attention_backward(): pl.pallas_call(functools.partial(attention_backward_kernel, query_blocks(...  28.7 us
    all_gather x3, waiting for transfers between devices, gather_z(): return lax.all_gather(values, 'shard', axis=0, tiled=False)  21.4 us
  transfers between devices with their start and end apart: 70, of which 25 were waited for; matrix products, arithmetic and copies ran while one was open for 22% of the time, Pallas kernels for 32%

profile of v6, /device:TPU:0, one launch (start us, length us, event | category | flops | bytes accessed | tf_op | source)
XLA Modules:
  0.0 731.0 jit_solution(3334589303054356555)
XLA Ops:
  7.2 3.7 constant_dynamic-slice_fusion.3
  12.1 3.0 collective-permute-start
  18.1 21.7 %collective-permute-done = bf16[2,2,1088,128]{3,2,1,0:T(8,128)(2,1)S(1)} collective-permute-done((bf16[2,2,1088,128]{3,2,1,0:T(8,128)(2,1)}, bf16[2,2,1088,128]{3,2,1,0:T(8,128)(2,1)S(1)}, u32[]{:S(2)}, u32[]{:S(2)}) %collective-permute-start) | collective-permute-done | bytes 1114144 | tf_op jit(solution)/shard_map/ppermute | solution.py:400
  42.8 8.4 %all-gather.7.cloned.1.call-done = bf16[576,1088]{1,0:T(8,128)(2,1)} async-done(((bf16[144,1088]{1,0:T(8,128)(2,1)}), bf16[576,1088]{1,0:T(8,128)(2,1)}) %all-gather.7.cloned.1.call-update) | async-done | bytes 1253392 | tf_op jit(solution)/shard_map/all_gather | solution.py:633
  58.5 13.2 %collective-permute-done.2 = bf16[2,144,1088]{2,1,0:T(8,128)(2,1)S(1)} collective-permute-done((bf16[2,144,1088]{2,1,0:T(8,128)(2,1)}, bf16[2,144,1088]{2,1,0:T(8,128)(2,1)S(1)}, u32[]{:S(2)}, u32[]{:S(2)}) %collective-permute-start.2) | collective-permute-done | bytes 626720 | tf_op jit(solution)/shard_map/ppermute | solution.py:400
  78.2 13.0 %all-gather.9.cloned.1.call-done = bf16[640,1088]{1,0:T(8,128)(2,1)} async-done(((bf16[160,1088]{1,0:T(8,128)(2,1)}), bf16[640,1088]{1,0:T(8,128)(2,1)}) %all-gather.9.cloned.1.call-update) | async-done | bytes 1392656 | tf_op jit(solution)/shard_map/all_gather | solution.py:633
  91.2 12.1 %collective-permute-done.4.refs_2_ = bf16[2,2,144,1088]{3,2,1,0:T(8,128)(2,1)S(1)} collective-permute-done((bf16[2,2,144,1088]{3,2,1,0:T(8,128)(2,1)}, bf16[2,2,144,1088]{3,2,1,0:T(8,128)(2,1)S(1)}, u32[]{:S(2)}, u32[]{:S(2)}) %collective-permute-start.4) | collective-permute-done | bytes 1253408 | tf_op jit(solution)/shard_map/ppermute | solution.py:400
  112.8 11.3 %collective-permute-done.10 = bf16[2,144,1088]{2,1,0:T(8,128)(2,1)S(1)} collective-permute-done((bf16[2,144,1088]{2,1,0:T(8,128)(2,1)}, bf16[2,144,1088]{2,1,0:T(8,128)(2,1)S(1)}, u32[]{:S(2)}, u32[]{:S(2)}) %collective-permute-start.10) | collective-permute-done | bytes 626720 | tf_op jit(solution)/shard_map/ppermute | solution.py:400
  131.9 8.7 %shard_map.271 = bf16[4,4,272,1088]{3,2,1,0:T(8,128)(2,1)} custom-call(s32[3]{0:T(128)} %pad_add_fusion.here_ref, bf16[2,2,144,1088]{3,2,1,0:T(8,128)(2,1)} %pad_maximum_fusion.3.refs_0_, bf16[2,2,144,1088]{3,2,1,0:T(8,128)(2,1)} %pad_maximum_fusion.4.refs_1_, bf16[2,2,144,1088]{3,2,1,0:T(8,128)(2,1)} %copy-done.35, bf16[2,2,144,1088]{3,2,1,0:T(8,128)(2,1)} %copy-done.36, ...), custom_call_target="tpu_custom_call" | custom-call | bytes 18939904 | tf_op jit(solution)/shard_map/pallas_call | solution.py:493
  140.6 16.7 %shard_map.272 = (bf16[3,1024,1088]{2,1,0:T(8,128)(2,1)}, bf16[1024,1088]{1,0:T(8,128)(2,1)}) custom-call(bf16[1024,1088]{1,0:T(8,128)(2,1)} %bitcast.235, bf16[4,1088,1088]{2,1,0:T(8,128)(2,1)} %bitcast.217, f32[8,1088]{1,0:T(8,128)} %reshape.196.small_ref, bf16[16,128]{1,0:T(8,128)(2,1)} %slice.645.refs_0_, bf16[16,128]{1,0:T(8,128)(2,1)} %slice.646.refs_1_), custom_call_target="tpu_custom_call" | custom-call | flops 1363673088 | bytes 2581760 | tf_op jit(solution)/shard_map/pallas_call | solution.py:379
  165.9 14.5 %collective-permute-done.14 = bf16[2,144,1088]{2,1,0:T(8,128)(2,1)S(1)} collective-permute-done((bf16[2,144,1088]{2,1,0:T(8,128)(2,1)S(1)}, bf16[2,144,1088]{2,1,0:T(8,128)(2,1)S(1)}, u32[]{:S(2)}, u32[]{:S(2)}) %collective-permute-start.14) | collective-permute-done | bytes 626720 | tf_op jit(solution)/shard_map/ppermute | solution.py:400
  185.8 31.2 %shard_map.273 = (bf16[4,2,128,1088]{3,2,1,0:T(8,128)(2,1)}, f32[2,9,8,512]{3,2,1,0:T(8,128)}) custom-call(s32[4]{0:T(128)} %broadcast_xor_fusion.order_ref, bf16[3,4,2,128,1088]{4,3,2,1,0:T(8,128)(2,1)} %bitcast.211, bf16[3,4,2,128,1088]{4,3,2,1,0:T(8,128)(2,1)} %bitcast.212, bf16[3,4,2,128,1088]{4,3,2,1,0:T(8,128)(2,1)} %bitcast.213, ...), custom_call_target="tpu_custom_call" | custom-call | flops 1207959552 | bytes 1114112 | tf_op jit(solution)/shard_map/pallas_call | solution.py:168
  225.4 8.5 %shard_map.274 = (f32[1024,1088]{1,0:T(8,128)}, bf16[1024,1088]{1,0:T(8,128)(2,1)}) custom-call(bf16[1024,1088]{1,0:T(8,128)(2,1)} %bitcast.236, bf16[1024,1088]{1,0:T(8,128)(2,1)} %bitcast.245, bf16[4,1088,1088]{2,1,0:T(8,128)(2,1)} %bitcast.218, f32[8,1088]{1,0:T(8,128)} %reshape.196.small_ref), custom_call_target="tpu_custom_call" | custom-call | flops 454557696 | bytes 2580736 | tf_op jit(solution)/shard_map/pallas_call | solution.py:379
  234.5 8.6 %shard_map.275 = bf16[4,4,272,1088]{3,2,1,0:T(8,128)(2,1)} custom-call(s32[3]{0:T(128)} %pad_add_fusion.here_ref, bf16[2,2,144,1088]{3,2,1,0:T(8,128)(2,1)} %copy-done.12, bf16[2,2,144,1088]{3,2,1,0:T(8,128)(2,1)} %copy-done.13, bf16[2,2,144,1088]{3,2,1,0:T(8,128)(2,1)} %collective-permute-done.12.refs_2_, ...), custom_call_target="tpu_custom_call" | custom-call | bytes 18939904 | tf_op jit(solution)/shard_map/pallas_call | solution.py:493
  243.6 6.8 collective-permute-done.26
  256.0 27.8 %shard_map.276 = (bf16[4,1024,1088]{2,1,0:T(8,128)(2,1)}, bf16[4,1024,1088]{2,1,0:T(8,128)(2,1)}) custom-call(bf16[1024,1088]{1,0:T(8,128)(2,1)} %get-tuple-element.82.low_ref, bf16[4,1088,1088]{2,1,0:T(8,128)(2,1)} %bitcast.221, f32[4,1,1088]{2,1,0:T(1,128)} %reshape.200.bias_ref, bf16[16,128]{1,0:T(8,128)(2,1)} %slice.653.refs_0_, ...), custom_call_target="tpu_custom_call" | custom-call | flops 1818230784 | bytes 3693696 | tf_op jit(solution)/shard_map/pallas_call | solution.py:379
  285.7 8.6 %shard_map.277 = bf16[4,4,272,1088]{3,2,1,0:T(8,128)(2,1)} custom-call(s32[3]{0:T(128)} %pad_add_fusion.here_ref, bf16[2,2,144,1088]{3,2,1,0:T(8,128)(2,1)} %copy-done.14, bf16[2,2,144,1088]{3,2,1,0:T(8,128)(2,1)} %copy-done.15, bf16[2,2,144,1088]{3,2,1,0:T(8,128)(2,1)} %collective-permute-done.20.refs_2_, ...), custom_call_target="tpu_custom_call" | custom-call | bytes 18939904 | tf_op jit(solution)/shard_map/pallas_call | solution.py:493
  301.8 15.2 %convolution_convert_fusion.1 = bf16[4,1088,1088]{2,1,0:T(8,128)(2,1)S(1)} fusion(bf16[4,1024,1088]{2,1,0:T(8,128)(2,1)} %get-tuple-element.86.act_ref, bf16[1024,1088,1]{1,0,2:T(8,128)(2,1)S(1)} %bitcast.240), kind=kOutput, calls=%fused_computation.1 | convolution fusion | flops 9701965824 | bytes 20611072 | tf_op jit(solution)/shard_map/ctx,td->cxd/dot_general | solution.py:728
  317.0 3.3 broadcast_select_fusion.2
  325.4 19.8 %shard_map.278 = bf16[1024,1088]{1,0:T(8,128)(2,1)} custom-call(f32[1024,1088]{1,0:T(8,128)} %get-tuple-element.88.middle_ref, bf16[4,1024,1088]{2,1,0:T(8,128)(2,1)} %get-tuple-element.86.act_ref, bf16[4,1088,1088]{2,1,0:T(8,128)(2,1)} %bitcast.223, f32[8,1088]{1,0:T(8,128)} %reshape.196.small_ref, bf16[16,128]{1,0:T(8,128)(2,1)} %slice.669.refs_0_), custom_call_target="tpu_custom_call" | custom-call | flops 1818230784 | bytes 3138304 | tf_op jit(solution)/shard_map/pallas_call | solution.py:379
  346.4 6.6 add_convert_fusion.2
  360.5 21.1 %shard_map.279 = (bf16[4,1024,1088]{2,1,0:T(8,128)(2,1)}, f32[8,1088]{1,0:T(8,128)}) custom-call(bf16[1024,1088]{1,0:T(8,128)(2,1)} %bitcast.241, bf16[4,1024,1088]{2,1,0:T(8,128)(2,1)} %get-tuple-element.89.slope_ref, bf16[4,1088,1088]{2,1,0:T(8,128)(2,1)} %bitcast.224, bf16[16,128]{1,0:T(8,128)(2,1)} %slice.677.refs_0_, bf16[16,128]{1,0:T(8,128)(2,1)} %slice.679.refs_1_, ...), custom_call_target="tpu_custom_call" | custom-call | flops 1818230784 | bytes 3696384 | tf_op jit(solution)/shard_map/pallas_call | solution.py:379
  381.6 13.2 %convolution_convert_fusion = bf16[4,1088,1088]{1,2,0:T(8,128)(2,1)S(1)} fusion(bf16[4,1024,1088]{2,1,0:T(8,128)(2,1)} %get-tuple-element.90.hidden_ref, bf16[1024,1088]{1,0:T(8,128)(2,1)S(1)} %copy-done.22), kind=kOutput, calls=%fused_computation | convolution fusion | flops 9701965824 | bytes 20611072 | tf_op jit(solution)/shard_map/td,ctx->cdx/dot_general | solution.py:746
  395.8 3.3 broadcast_select_fusion.1
  400.9 4.3 add_convert_fusion.7
  410.2 4.2 copy.66
  419.7 27.2 %shard_map.280 = (f32[1024,1088]{1,0:T(8,128)}, bf16[1024,1088]{1,0:T(8,128)(2,1)}, bf16[1024,1088]{1,0:T(8,128)(2,1)}, f32[8,1088]{1,0:T(8,128)}) custom-call(bf16[4,1024,1088]{2,1,0:T(8,128)(2,1)} %get-tuple-element.90.hidden_ref, bf16[1024,1088]{1,0:T(8,128)(2,1)} %bitcast.242, f32[1024,1088]{1,0:T(8,128)} %get-tuple-element.88.middle_ref, ...), custom_call_target="tpu_custom_call" | custom-call | flops 2272788480 | bytes 5441024 | tf_op jit(solution)/shard_map/pallas_call | solution.py:379
  446.9 4.8 convolution_convert_fusion.3
  454.4 2.8 collective-permute-done.33
  466.5 7.3 add_convert_fusion.1
  480.6 28.7 %shard_map.281 = bf16[3,4,2,128,1088]{4,3,2,1,0:T(8,128)(2,1)} custom-call(s32[4]{0:T(128)} %broadcast_xor_fusion.order_ref, bf16[3,4,2,128,1088]{4,3,2,1,0:T(8,128)(2,1)} %bitcast.214, bf16[3,4,2,128,1088]{4,3,2,1,0:T(8,128)(2,1)} %bitcast.215, bf16[3,4,2,128,1088]{4,3,2,1,0:T(8,128)(2,1)} %bitcast.216, bf16[4,2,128,1088]{3,2,1,0:T(8,128)(2,1)} %get-tuple-element.81.o_ref, ...), custom_call_target="tpu_custom_call" | custom-call | flops 1509949440 | bytes 2228224 | tf_op jit(solution)/shard_map/pallas_call | solution.py:201
  509.4 12.7 %convolution_convert_fusion.2 = bf16[3,1088,1088]{1,2,0:T(8,128)(2,1)S(1)} fusion(bf16[3,1024,1088]{2,1,0:T(8,128)(2,1)} %bitcast.238, bf16[1024,1088]{1,0:T(8,128)(2,1)} %get-tuple-element.96), kind=kOutput, calls=%fused_computation.2 | convolution fusion | flops 7276474368 | bytes 16015360 | tf_op jit(solution)/shard_map/td,ctx->cdx/dot_general | solution.py:767
  524.7 3.5 add_convert_fusion.4
  531.7 14.0 %collective-permute-done.41 = bf16[2,144,1088]{2,1,0:T(8,128)(2,1)S(1)} collective-permute-done((bf16[2,144,1088]{2,1,0:T(8,128)(2,1)S(1)}, bf16[2,144,1088]{2,1,0:T(8,128)(2,1)S(1)}, u32[]{:S(2)}, u32[]{:S(2)}) %collective-permute-start.41) | collective-permute-done | bytes 626720 | tf_op jit(solution)/shard_map/ppermute | solution.py:400
  556.9 18.6 %shard_map.282 = (bf16[1024,1088]{1,0:T(8,128)(2,1)}, f32[8,1088]{1,0:T(8,128)}) custom-call(bf16[3,1024,1088]{2,1,0:T(8,128)(2,1)} %bitcast.239, f32[1024,1088]{1,0:T(8,128)} %get-tuple-element.98.grad_middle_ref, bf16[1024,1088]{1,0:T(8,128)(2,1)} %bitcast.237, bf16[4,1088,1088]{2,1,0:T(8,128)(2,1)} %bitcast.220, f32[8,1088]{1,0:T(8,128)} %reshape.196.small_ref, ...), custom_call_target="tpu_custom_call" | custom-call | flops 1363673088 | bytes 3144192 | tf_op jit(solution)/shard_map/pallas_call | solution.py:379
  578.0 4.8 collective-permute-done.37
  583.7 2.7 add_convert_fusion.3
  590.4 12.4 %collective-permute-done.43 = bf16[2,144,1088]{2,1,0:T(8,128)(2,1)} collective-permute-done((bf16[2,144,1088]{2,1,0:T(8,128)(2,1)}, bf16[2,144,1088]{2,1,0:T(8,128)(2,1)}, u32[]{:S(2)}, u32[]{:S(2)}) %collective-permute-start.43) | collective-permute-done | bytes 626720 | tf_op jit(solution)/shard_map/ppermute | solution.py:400
  625.4 24.7 %collective-permute-done.49 = bf16[4,16,1088]{2,1,0:T(8,128)(2,1)S(1)} collective-permute-done((bf16[4,16,1088]{2,1,0:T(8,128)(2,1)S(1)}, bf16[4,16,1088]{2,1,0:T(8,128)(2,1)S(1)}, u32[]{:S(2)}, u32[]{:S(2)}) %collective-permute-start.49) | collective-permute-done | bytes 139296 | tf_op jit(solution)/shard_map/ppermute | solution.py:400
  652.4 4.2 collective-permute-done.57
  659.5 3.2 collective-permute-start.51
  665.1 7.9 %collective-permute-done.58.refs_2_ = bf16[2,1,144,1088]{3,2,1,0:T(8,128)(2,1)} collective-permute-done((bf16[2,1,144,1088]{3,2,1,0:T(8,128)(2,1)S(1)}, bf16[2,1,144,1088]{3,2,1,0:T(8,128)(2,1)}, u32[]{:S(2)}, u32[]{:S(2)}) %collective-permute-start.58) | collective-permute-done | bytes 626720 | tf_op jit(solution)/shard_map/ppermute | solution.py:400
  680.2 7.0 shard_map.284
  688.9 4.4 slice_bitcast_fusion.3
  697.8 5.8 concatenate.43
  711.2 4.3 shard_map.283
  715.5 4.3 slice_bitcast_fusion.7
  719.8 4.1 concatenate.40
  (408 shorter events, 184.4 us)
Async XLA Ops:
  7.2 44.0 %all-gather.7.cloned.1.call-start = ((), (), s32[]{:S(2)}) async-start(), calls=%async_computation.6 | async-start | bytes 1658880 | tf_op jit(solution)/shard_map/all_gather | solution.py:633
  12.1 27.7 %collective-permute-start = (bf16[2,2,1088,128]{3,2,1,0:T(8,128)(2,1)}, bf16[2,2,1088,128]{3,2,1,0:T(8,128)(2,1)S(1)}, u32[]{:S(2)}, u32[]{:S(2)}) collective-permute-start(bf16[2,2,1088,128]{3,2,1,0:T(8,128)(2,1)} %pad_maximum_fusion.12), channel_id=1, source_target_pairs={{0,2},{1,3},{2,0},{3,1},{4,6},{5,7},{6,4},{7,5},{8,10},{9,11},{10,... | collective-permute-start | bytes 3342344 | tf_op jit(solution)/shard_map/ppermute | solution.py:400
  17.7 73.5 %all-gather.9.cloned.1.call-start = ((), (), s32[]{:S(2)}) async-start(), calls=%async_computation.7 | async-start | bytes 1843200 | tf_op jit(solution)/shard_map/all_gather | solution.py:633
  58.4 103.9 %all-gather.11.cloned.1.call-start = ((), (), s32[]{:S(2)}) async-start(), calls=%async_computation.8 | async-start | bytes 1658880 | tf_op jit(solution)/shard_map/all_gather | solution.py:633
  74.1 29.3 %collective-permute-start.4 = (bf16[2,2,144,1088]{3,2,1,0:T(8,128)(2,1)}, bf16[2,2,144,1088]{3,2,1,0:T(8,128)(2,1)S(1)}, u32[]{:S(2)}, u32[]{:S(2)}) collective-permute-start(bf16[2,2,144,1088]{3,2,1,0:T(8,128)(2,1)} %pad_maximum_fusion.3.refs_0_), channel_id=1, source_target_pairs={{0,2},{1,3},{2,0},{3,1},{4,6},{5,7},{6,4},{7,5},{8,10},{9,11},{10,... | collective-permute-start | bytes 3760136 | tf_op jit(solution)/shard_map/ppermute | solution.py:400
  76.8 29.0 %collective-permute-start.5 = (bf16[2,2,144,1088]{3,2,1,0:T(8,128)(2,1)}, bf16[2,2,144,1088]{3,2,1,0:T(8,128)(2,1)S(1)}, u32[]{:S(2)}, u32[]{:S(2)}) collective-permute-start(bf16[2,2,144,1088]{3,2,1,0:T(8,128)(2,1)} %pad_maximum_fusion.4.refs_1_), channel_id=1, source_target_pairs={{0,4},{4,0},{1,5},{5,1},{2,6},{6,2},{3,7},{7,3},{8,12},{12,8},{9,1... | collective-permute-start | bytes 3760136 | tf_op jit(solution)/shard_map/ppermute | solution.py:400
  78.2 48.2 %collective-permute-start.6 = (bf16[2,2,144,1088]{3,2,1,0:T(8,128)(2,1)}, bf16[2,2,144,1088]{3,2,1,0:T(8,128)(2,1)}, u32[]{:S(2)}, u32[]{:S(2)}) collective-permute-start(bf16[2,2,144,1088]{3,2,1,0:T(8,128)(2,1)} %pad_maximum_fusion.3.refs_0_), channel_id=1, source_target_pairs={{0,1},{1,0},{2,3},{3,2},{4,5},{5,4},{6,7},{7,6},{8,9},{9,8},{10,11... | collective-permute-start | bytes 3760136 | tf_op jit(solution)/shard_map/ppermute | solution.py:400
  112.0 20.0 %collective-permute-start.7 = (bf16[2,2,144,1088]{3,2,1,0:T(8,128)(2,1)}, bf16[2,2,144,1088]{3,2,1,0:T(8,128)(2,1)}, u32[]{:S(2)}, u32[]{:S(2)}) collective-permute-start(bf16[2,2,144,1088]{3,2,1,0:T(8,128)(2,1)} %pad_maximum_fusion.4.refs_1_), channel_id=1, source_target_pairs={{0,1},{1,0},{2,3},{3,2},{4,5},{5,4},{6,7},{7,6},{8,9},{9,8},{10,11... | collective-permute-start | bytes 3760136 | tf_op jit(solution)/shard_map/ppermute | solution.py:400
  112.0 508.7 %reduce-scatter.6.cloned.1.call-start = ((), (), s32[]{:S(2)}) async-start(), calls=%async_computation.4 | async-start | bytes 1658880 | tf_op jit(solution)/shard_map/reduce_scatter | solution.py:704
  112.2 19.7 %collective-permute-start.8 = (bf16[2,2,144,1088]{3,2,1,0:T(8,128)(2,1)}, bf16[2,2,144,1088]{3,2,1,0:T(8,128)(2,1)}, u32[]{:S(2)}, u32[]{:S(2)}) collective-permute-start(bf16[2,2,144,1088]{3,2,1,0:T(8,128)(2,1)} %copy-done.35), channel_id=1, source_target_pairs={{0,1},{1,0},{2,3},{3,2},{4,5},{5,4},{6,7},{7,6},{8,9},{9,8},{10,11... | collective-permute-start | bytes 3760136 | tf_op jit(solution)/shard_map/ppermute | solution.py:400
  125.3 34.5 %collective-permute-start.12 = (bf16[2,2,144,1088]{3,2,1,0:T(8,128)(2,1)S(1)}, bf16[2,2,144,1088]{3,2,1,0:T(8,128)(2,1)}, u32[]{:S(2)}, u32[]{:S(2)}) collective-permute-start(bf16[2,2,144,1088]{3,2,1,0:T(8,128)(2,1)S(1)} %pad_maximum_fusion.5.refs_0_), channel_id=1, source_target_pairs={{0,2},{1,3},{2,0},{3,1},{4,6},{5,7},{6,4},{7,5},{8,10},{9,11},{10,... | collective-permute-start | bytes 3760136 | tf_op jit(solution)/shard_map/ppermute | solution.py:400
  126.4 33.4 %collective-permute-start.13 = (bf16[2,2,144,1088]{3,2,1,0:T(8,128)(2,1)S(1)}, bf16[2,2,144,1088]{3,2,1,0:T(8,128)(2,1)}, u32[]{:S(2)}, u32[]{:S(2)}) collective-permute-start(bf16[2,2,144,1088]{3,2,1,0:T(8,128)(2,1)S(1)} %pad_maximum_fusion.6.refs_1_), channel_id=1, source_target_pairs={{0,4},{4,0},{1,5},{5,1},{2,6},{6,2},{3,7},{7,3},{8,12},{12,8},{9,1... | collective-permute-start | bytes 3760136 | tf_op jit(solution)/shard_map/ppermute | solution.py:400
  164.6 16.6 %collective-permute-start.15 = (bf16[2,144,1088]{2,1,0:T(8,128)(2,1)S(1)}, bf16[2,144,1088]{2,1,0:T(8,128)(2,1)S(1)}, u32[]{:S(2)}, u32[]{:S(2)}) collective-permute-start(bf16[2,144,1088]{2,1,0:T(8,128)(2,1)S(1)} %bitcast.256), channel_id=1, source_target_pairs={{0,2},{1,3},{2,0},{3,1},{4,6},{5,7},{6,4},{7,5},{8,10},{9,11},{10,... | collective-permute-start | bytes 1880072 | tf_op jit(solution)/shard_map/ppermute | solution.py:400
  181.4 38.1 %collective-permute-start.20 = (bf16[2,2,144,1088]{3,2,1,0:T(8,128)(2,1)S(1)}, bf16[2,2,144,1088]{3,2,1,0:T(8,128)(2,1)}, u32[]{:S(2)}, u32[]{:S(2)}) collective-permute-start(bf16[2,2,144,1088]{3,2,1,0:T(8,128)(2,1)S(1)} %pad_maximum_fusion.7.refs_0_), channel_id=1, source_target_pairs={{0,2},{1,3},{2,0},{3,1},{4,6},{5,7},{6,4},{7,5},{8,10},{9,11},{10,... | collective-permute-start | bytes 3760136 | tf_op jit(solution)/shard_map/ppermute | solution.py:400
  182.5 37.5 %collective-permute-start.21 = (bf16[2,2,144,1088]{3,2,1,0:T(8,128)(2,1)S(1)}, bf16[2,2,144,1088]{3,2,1,0:T(8,128)(2,1)}, u32[]{:S(2)}, u32[]{:S(2)}) collective-permute-start(bf16[2,2,144,1088]{3,2,1,0:T(8,128)(2,1)S(1)} %pad_maximum_fusion.8.refs_1_), channel_id=1, source_target_pairs={{0,4},{4,0},{1,5},{5,1},{2,6},{6,2},{3,7},{7,3},{8,12},{12,8},{9,1... | collective-permute-start | bytes 3760136 | tf_op jit(solution)/shard_map/ppermute | solution.py:400
  183.9 49.9 %collective-permute-start.16 = (bf16[2,2,144,1088]{3,2,1,0:T(8,128)(2,1)S(1)}, bf16[2,2,144,1088]{3,2,1,0:T(8,128)(2,1)}, u32[]{:S(2)}, u32[]{:S(2)}) collective-permute-start(bf16[2,2,144,1088]{3,2,1,0:T(8,128)(2,1)S(1)} %pad_maximum_fusion.5.refs_0_), channel_id=1, source_target_pairs={{0,1},{1,0},{2,3},{3,2},{4,5},{5,4},{6,7},{7,6},{8,9},{9,8},{10,11... | collective-permute-start | bytes 3760136 | tf_op jit(solution)/shard_map/ppermute | solution.py:400
  183.9 50.0 %collective-permute-start.17 = (bf16[2,2,144,1088]{3,2,1,0:T(8,128)(2,1)S(1)}, bf16[2,2,144,1088]{3,2,1,0:T(8,128)(2,1)}, u32[]{:S(2)}, u32[]{:S(2)}) collective-permute-start(bf16[2,2,144,1088]{3,2,1,0:T(8,128)(2,1)S(1)} %pad_maximum_fusion.6.refs_1_), channel_id=1, source_target_pairs={{0,1},{1,0},{2,3},{3,2},{4,5},{5,4},{6,7},{7,6},{8,9},{9,8},{10,11... | collective-permute-start | bytes 3760136 | tf_op jit(solution)/shard_map/ppermute | solution.py:400
  184.5 50.0 %collective-permute-start.18 = (bf16[2,2,144,1088]{3,2,1,0:T(8,128)(2,1)}, bf16[2,2,144,1088]{3,2,1,0:T(8,128)(2,1)}, u32[]{:S(2)}, u32[]{:S(2)}) collective-permute-start(bf16[2,2,144,1088]{3,2,1,0:T(8,128)(2,1)} %collective-permute-done.12.refs_2_), channel_id=1, source_target_pairs={{0,1},{1,0},{2,3},{3,2},{4,5},{5,4},{6,7},{7,6},{8,9},{9,8},{10,11... | collective-permute-start | bytes 3760136 | tf_op jit(solution)/shard_map/ppermute | solution.py:400
  223.6 26.9 %collective-permute-start.26 = (bf16[2,2,1088,128]{3,2,1,0:T(8,128)(2,1)}, bf16[2,2,1088,128]{3,2,1,0:T(8,128)(2,1)}, u32[]{:S(2)}, u32[]{:S(2)}) collective-permute-start(bf16[2,2,1088,128]{3,2,1,0:T(8,128)(2,1)} %maximum_select_fusion), channel_id=1, source_target_pairs={{0,2},{1,3},{2,0},{3,1},{4,6},{5,7},{6,4},{7,5},{8,10},{9,11},{10,... | collective-permute-start | bytes 3342344 | tf_op jit(solution)/shard_map/ppermute | solution.py:400
  233.9 49.9 %collective-permute-start.22 = (bf16[2,2,144,1088]{3,2,1,0:T(8,128)(2,1)S(1)}, bf16[2,2,144,1088]{3,2,1,0:T(8,128)(2,1)S(1)}, u32[]{:S(2)}, u32[]{:S(2)}) collective-permute-start(bf16[2,2,144,1088]{3,2,1,0:T(8,128)(2,1)S(1)} %pad_maximum_fusion.7.refs_0_), channel_id=1, source_target_pairs={{0,1},{1,0},{2,3},{3,2},{4,5},{5,4},{6,7},{7,6},{8,9},{9,8},{10,11... | collective-permute-start | bytes 3760136 | tf_op jit(solution)/shard_map/ppermute | solution.py:400
  234.0 49.8 %collective-permute-start.23 = (bf16[2,2,144,1088]{3,2,1,0:T(8,128)(2,1)S(1)}, bf16[2,2,144,1088]{3,2,1,0:T(8,128)(2,1)S(1)}, u32[]{:S(2)}, u32[]{:S(2)}) collective-permute-start(bf16[2,2,144,1088]{3,2,1,0:T(8,128)(2,1)S(1)} %pad_maximum_fusion.8.refs_1_), channel_id=1, source_target_pairs={{0,1},{1,0},{2,3},{3,2},{4,5},{5,4},{6,7},{7,6},{8,9},{9,8},{10,11... | collective-permute-start | bytes 3760136 | tf_op jit(solution)/shard_map/ppermute | solution.py:400
  243.1 40.7 %collective-permute-start.24 = (bf16[2,2,144,1088]{3,2,1,0:T(8,128)(2,1)}, bf16[2,2,144,1088]{3,2,1,0:T(8,128)(2,1)S(1)}, u32[]{:S(2)}, u32[]{:S(2)}) collective-permute-start(bf16[2,2,144,1088]{3,2,1,0:T(8,128)(2,1)} %collective-permute-done.20.refs_2_), channel_id=1, source_target_pairs={{0,1},{1,0},{2,3},{3,2},{4,5},{5,4},{6,7},{7,6},{8,9},{9,8},{10,11... | collective-permute-start | bytes 3760136 | tf_op jit(solution)/shard_map/ppermute | solution.py:400
  243.2 40.7 %collective-permute-start.25 = (bf16[2,2,144,1088]{3,2,1,0:T(8,128)(2,1)}, bf16[2,2,144,1088]{3,2,1,0:T(8,128)(2,1)}, u32[]{:S(2)}, u32[]{:S(2)}) collective-permute-start(bf16[2,2,144,1088]{3,2,1,0:T(8,128)(2,1)} %collective-permute-done.21.refs_3_), channel_id=1, source_target_pairs={{0,1},{1,0},{2,3},{3,2},{4,5},{5,4},{6,7},{7,6},{8,9},{9,8},{10,11... | collective-permute-start | bytes 3760136 | tf_op jit(solution)/shard_map/ppermute | solution.py:400
  252.8 44.1 %collective-permute-start.27 = (bf16[2,2,1088,128]{3,2,1,0:T(8,128)(2,1)}, bf16[2,2,1088,128]{3,2,1,0:T(8,128)(2,1)S(1)}, u32[]{:S(2)}, u32[]{:S(2)}) collective-permute-start(bf16[2,2,1088,128]{3,2,1,0:T(8,128)(2,1)} %pad_maximum_fusion.14), channel_id=1, source_target_pairs={{0,1},{1,0},{2,3},{3,2},{4,5},{5,4},{6,7},{7,6},{8,9},{9,8},{10,11... | collective-permute-start | bytes 3342344 | tf_op jit(solution)/shard_map/ppermute | solution.py:400
  322.4 24.1 %collective-permute-start.28 = (bf16[4,4,144,1088]{3,2,1,0:T(8,128)(2,1)}, bf16[4,4,144,1088]{3,2,1,0:T(8,128)(2,1)}, u32[]{:S(2)}, u32[]{:S(2)}) collective-permute-start(bf16[4,4,144,1088]{3,2,1,0:T(8,128)(2,1)} %broadcast_select_fusion.2), channel_id=1, source_target_pairs={{0,1},{1,0},{2,3},{3,2},{4,5},{5,4},{6,7},{7,6},{8,9},{9,8},{10,11... | collective-permute-start | bytes 15040520 | tf_op jit(solution)/shard_map/ppermute | solution.py:400
  355.8 45.1 %collective-permute-start.29 = (bf16[2,2,144,1088]{3,2,1,0:T(8,128)(2,1)}, bf16[2,2,144,1088]{3,2,1,0:T(8,128)(2,1)}, u32[]{:S(2)}, u32[]{:S(2)}) collective-permute-start(bf16[2,2,144,1088]{3,2,1,0:T(8,128)(2,1)} %get-tuple-element.130), channel_id=1, source_target_pairs={{0,4},{4,0},{1,5},{5,1},{2,6},{6,2},{3,7},{7,3},{8,12},{12,8},{9,1... | collective-permute-start | bytes 3760136 | tf_op jit(solution)/shard_map/ppermute | solution.py:400
  358.0 42.9 %collective-permute-start.30 = (bf16[2,2,144,1088]{3,2,1,0:T(8,128)(2,1)S(1)}, bf16[2,2,144,1088]{3,2,1,0:T(8,128)(2,1)}, u32[]{:S(2)}, u32[]{:S(2)}) collective-permute-start(bf16[2,2,144,1088]{3,2,1,0:T(8,128)(2,1)S(1)} %get-tuple-element.129), channel_id=1, source_target_pairs={{0,2},{1,3},{2,0},{3,1},{4,6},{5,7},{6,4},{7,5},{8,10},{9,11},{10,... | collective-permute-start | bytes 3760136 | tf_op jit(solution)/shard_map/ppermute | solution.py:400
  400.1 66.4 %collective-permute-start.35 = (bf16[4,4,144,1088]{3,2,1,0:T(8,128)(2,1)}, bf16[4,4,144,1088]{3,2,1,0:T(8,128)(2,1)}, u32[]{:S(2)}, u32[]{:S(2)}) collective-permute-start(bf16[4,4,144,1088]{3,2,1,0:T(8,128)(2,1)} %broadcast_select_fusion.1), channel_id=1, source_target_pairs={{0,1},{1,0},{2,3},{3,2},{4,5},{5,4},{6,7},{7,6},{8,9},{9,8},{10,11... | collective-permute-start | bytes 15040520 | tf_op jit(solution)/shard_map/ppermute | solution.py:400
  415.8 42.7 %collective-permute-start.31 = (bf16[2,2,1088,128]{3,2,1,0:T(8,128)(2,1)S(1)}, bf16[2,2,1088,128]{3,2,1,0:T(8,128)(2,1)S(1)}, u32[]{:S(2)}, u32[]{:S(2)}) collective-permute-start(bf16[2,2,1088,128]{3,2,1,0:T(8,128)(2,1)S(1)} %slice.672), channel_id=1, source_target_pairs={{0,2},{1,3},{2,0},{3,1},{4,6},{5,7},{6,4},{7,5},{8,10},{9,11},{10,... | collective-permute-start | bytes 3342344 | tf_op jit(solution)/shard_map/ppermute | solution.py:400
  416.7 40.4 %collective-permute-start.33 = (bf16[2,144,1088]{2,1,0:T(8,128)(2,1)}, bf16[2,144,1088]{2,1,0:T(8,128)(2,1)}, u32[]{:S(2)}, u32[]{:S(2)}) collective-permute-start(bf16[2,144,1088]{2,1,0:T(8,128)(2,1)} %fusion.25), channel_id=1, source_target_pairs={{0,2},{1,3},{2,0},{3,1},{4,6},{5,7},{6,4},{7,5},{8,10},{9,11},{10,... | collective-permute-start | bytes 1880072 | tf_op jit(solution)/shard_map/ppermute | solution.py:400
  418.8 38.4 %collective-permute-start.34 = (bf16[2,144,1088]{2,1,0:T(8,128)(2,1)}, bf16[2,144,1088]{2,1,0:T(8,128)(2,1)S(1)}, u32[]{:S(2)}, u32[]{:S(2)}) collective-permute-start(bf16[2,144,1088]{2,1,0:T(8,128)(2,1)} %select_bitcast_fusion.4), channel_id=1, source_target_pairs={{0,4},{4,0},{1,5},{5,1},{2,6},{6,2},{3,7},{7,3},{8,12},{12,8},{9,1... | collective-permute-start | bytes 1880072 | tf_op jit(solution)/shard_map/ppermute | solution.py:400
  462.0 158.7 %reduce-scatter.8.cloned.1.call-start = ((), (), s32[]{:S(2)}) async-start(), calls=%async_computation.5 | async-start | bytes 1658880 | tf_op jit(solution)/shard_map/reduce_scatter | solution.py:704
  476.6 48.1 %collective-permute-start.39 = (bf16[2,2,144,1088]{3,2,1,0:T(8,128)(2,1)}, bf16[2,2,144,1088]{3,2,1,0:T(8,128)(2,1)}, u32[]{:S(2)}, u32[]{:S(2)}) collective-permute-start(bf16[2,2,144,1088]{3,2,1,0:T(8,128)(2,1)} %get-tuple-element.126), channel_id=1, source_target_pairs={{0,4},{4,0},{1,5},{5,1},{2,6},{6,2},{3,7},{7,3},{8,12},{12,8},{9,1... | collective-permute-start | bytes 3760136 | tf_op jit(solution)/shard_map/ppermute | solution.py:400
  478.5 46.2 %collective-permute-start.40 = (bf16[2,2,144,1088]{3,2,1,0:T(8,128)(2,1)}, bf16[2,2,144,1088]{3,2,1,0:T(8,128)(2,1)}, u32[]{:S(2)}, u32[]{:S(2)}) collective-permute-start(bf16[2,2,144,1088]{3,2,1,0:T(8,128)(2,1)} %get-tuple-element.125), channel_id=1, source_target_pairs={{0,2},{1,3},{2,0},{3,1},{4,6},{5,7},{6,4},{7,5},{8,10},{9,11},{10,... | collective-permute-start | bytes 3760136 | tf_op jit(solution)/shard_map/ppermute | solution.py:400
  523.5 24.3 %collective-permute-start.36 = (bf16[4,4,144,1088]{3,2,1,0:T(8,128)(2,1)S(1)}, bf16[4,4,144,1088]{3,2,1,0:T(8,128)(2,1)S(1)}, u32[]{:S(2)}, u32[]{:S(2)}) collective-permute-start(bf16[4,4,144,1088]{3,2,1,0:T(8,128)(2,1)S(1)} %broadcast_select_fusion), channel_id=1, source_target_pairs={{0,1},{1,0},{2,3},{3,2},{4,5},{5,4},{6,7},{7,6},{8,9},{9,8},{10,11... | collective-permute-start | bytes 15040520 | tf_op jit(solution)/shard_map/ppermute | solution.py:400
  528.3 17.4 %collective-permute-start.41 = (bf16[2,144,1088]{2,1,0:T(8,128)(2,1)S(1)}, bf16[2,144,1088]{2,1,0:T(8,128)(2,1)S(1)}, u32[]{:S(2)}, u32[]{:S(2)}) collective-permute-start(bf16[2,144,1088]{2,1,0:T(8,128)(2,1)S(1)} %select_bitcast_fusion.3), channel_id=1, source_target_pairs={{0,2},{1,3},{2,0},{3,1},{4,6},{5,7},{6,4},{7,5},{8,10},{9,11},{10,... | collective-permute-start | bytes 1880072 | tf_op jit(solution)/shard_map/ppermute | solution.py:400
  529.6 17.1 %collective-permute-start.42 = (bf16[2,144,1088]{2,1,0:T(8,128)(2,1)S(1)}, bf16[2,144,1088]{2,1,0:T(8,128)(2,1)S(1)}, u32[]{:S(2)}, u32[]{:S(2)}) collective-permute-start(bf16[2,144,1088]{2,1,0:T(8,128)(2,1)S(1)} %select_bitcast_fusion.2), channel_id=1, source_target_pairs={{0,4},{4,0},{1,5},{5,1},{2,6},{6,2},{3,7},{7,3},{8,12},{12,8},{9,1... | collective-permute-start | bytes 1880072 | tf_op jit(solution)/shard_map/ppermute | solution.py:400
  552.3 30.5 %collective-permute-start.37 = (bf16[2,2,144,1088]{3,2,1,0:T(8,128)(2,1)S(1)}, bf16[2,2,144,1088]{3,2,1,0:T(8,128)(2,1)}, u32[]{:S(2)}, u32[]{:S(2)}) collective-permute-start(bf16[2,2,144,1088]{3,2,1,0:T(8,128)(2,1)S(1)} %get-tuple-element.124), channel_id=1, source_target_pairs={{0,4},{4,0},{1,5},{5,1},{2,6},{6,2},{3,7},{7,3},{8,12},{12,8},{9,1... | collective-permute-start | bytes 3760136 | tf_op jit(solution)/shard_map/ppermute | solution.py:400
  553.5 30.2 %collective-permute-start.38 = (bf16[2,2,144,1088]{3,2,1,0:T(8,128)(2,1)S(1)}, bf16[2,2,144,1088]{3,2,1,0:T(8,128)(2,1)}, u32[]{:S(2)}, u32[]{:S(2)}) collective-permute-start(bf16[2,2,144,1088]{3,2,1,0:T(8,128)(2,1)S(1)} %get-tuple-element.123), channel_id=1, source_target_pairs={{0,2},{1,3},{2,0},{3,1},{4,6},{5,7},{6,4},{7,5},{8,10},{9,11},{10,... | collective-permute-start | bytes 3760136 | tf_op jit(solution)/shard_map/ppermute | solution.py:400
  555.6 122.0 %reduce-scatter.4.cloned.1.call-start = ((), (), s32[]{:S(2)}) async-start(), calls=%async_computation.3 | async-start | bytes 1658880 | tf_op jit(solution)/shard_map/reduce_scatter | solution.py:704
  619.4 56.8 %collective-permute-start.46 = (bf16[2,2,1088,128]{3,2,1,0:T(8,128)(2,1)}, bf16[2,2,1088,128]{3,2,1,0:T(8,128)(2,1)S(1)}, u32[]{:S(2)}, u32[]{:S(2)}) collective-permute-start(bf16[2,2,1088,128]{3,2,1,0:T(8,128)(2,1)} %slice.724), channel_id=1, source_target_pairs={{0,2},{1,3},{2,0},{3,1},{4,6},{5,7},{6,4},{7,5},{8,10},{9,11},{10,... | collective-permute-start | bytes 3342344 | tf_op jit(solution)/shard_map/ppermute | solution.py:400
  621.9 28.3 %collective-permute-start.49 = (bf16[4,16,1088]{2,1,0:T(8,128)(2,1)S(1)}, bf16[4,16,1088]{2,1,0:T(8,128)(2,1)S(1)}, u32[]{:S(2)}, u32[]{:S(2)}) collective-permute-start(bf16[4,16,1088]{2,1,0:T(8,128)(2,1)S(1)} %add_convert_fusion.11), channel_id=1, source_target_pairs={{0,2},{1,3},{2,0},{3,1},{4,6},{5,7},{6,4},{7,5},{8,10},{9,11},{10,... | collective-permute-start | bytes 417800 | tf_op jit(solution)/shard_map/ppermute | solution.py:400
  622.8 29.6 %collective-permute-start.56 = (bf16[1,144,1088]{2,1,0:T(8,128)(2,1)S(1)}, bf16[1,144,1088]{2,1,0:T(8,128)(2,1)S(1)}, u32[]{:S(2)}, u32[]{:S(2)}) collective-permute-start(bf16[1,144,1088]{2,1,0:T(8,128)(2,1)S(1)} %get-tuple-element.166), channel_id=1, source_target_pairs={{0,4},{4,0},{1,5},{5,1},{2,6},{6,2},{3,7},{7,3},{8,12},{12,8},{9,1... | collective-permute-start | bytes 940040 | tf_op jit(solution)/shard_map/ppermute | solution.py:400
  624.1 32.4 %collective-permute-start.57 = (bf16[1,144,1088]{2,1,0:T(8,128)(2,1)S(1)}, bf16[1,144,1088]{2,1,0:T(8,128)(2,1)S(1)}, u32[]{:S(2)}, u32[]{:S(2)}) collective-permute-start(bf16[1,144,1088]{2,1,0:T(8,128)(2,1)S(1)} %get-tuple-element.165), channel_id=1, source_target_pairs={{0,2},{1,3},{2,0},{3,1},{4,6},{5,7},{6,4},{7,5},{8,10},{9,11},{10,... | collective-permute-start | bytes 940040 | tf_op jit(solution)/shard_map/ppermute | solution.py:400
  658.0 19.6 %collective-permute-start.60 = (bf16[2,1,144,1088]{3,2,1,0:T(8,128)(2,1)S(1)}, bf16[2,1,144,1088]{3,2,1,0:T(8,128)(2,1)}, u32[]{:S(2)}, u32[]{:S(2)}) collective-permute-start(bf16[2,1,144,1088]{3,2,1,0:T(8,128)(2,1)S(1)} %pad_maximum_fusion.18.refs_0_), channel_id=1, source_target_pairs={{0,1},{1,0},{2,3},{3,2},{4,5},{5,4},{6,7},{7,6},{8,9},{9,8},{10,11... | collective-permute-start | bytes 1880072 | tf_op jit(solution)/shard_map/ppermute | solution.py:400
  658.1 17.5 %collective-permute-start.59 = (bf16[2,1,144,1088]{3,2,1,0:T(8,128)(2,1)S(1)}, bf16[2,1,144,1088]{3,2,1,0:T(8,128)(2,1)}, u32[]{:S(2)}, u32[]{:S(2)}) collective-permute-start(bf16[2,1,144,1088]{3,2,1,0:T(8,128)(2,1)S(1)} %pad_maximum_fusion.19.refs_1_), channel_id=1, source_target_pairs={{0,4},{4,0},{1,5},{5,1},{2,6},{6,2},{3,7},{7,3},{8,12},{12,8},{9,1... | collective-permute-start | bytes 1880072 | tf_op jit(solution)/shard_map/ppermute | solution.py:400
  677.6 26.1 %collective-permute-start.47 = (bf16[2,2,1088,128]{3,2,1,0:T(8,128)(2,1)}, bf16[2,2,1088,128]{3,2,1,0:T(8,128)(2,1)}, u32[]{:S(2)}, u32[]{:S(2)}) collective-permute-start(bf16[2,2,1088,128]{3,2,1,0:T(8,128)(2,1)} %pad_maximum_fusion.16), channel_id=1, source_target_pairs={{0,1},{1,0},{2,3},{3,2},{4,5},{5,4},{6,7},{7,6},{8,9},{9,8},{10,11... | collective-permute-start | bytes 3342344 | tf_op jit(solution)/shard_map/ppermute | solution.py:400
  688.1 17.8 %collective-permute-start.53 = (bf16[2,1,144,1088]{3,2,1,0:T(8,128)(2,1)S(1)}, bf16[2,1,144,1088]{3,2,1,0:T(8,128)(2,1)}, u32[]{:S(2)}, u32[]{:S(2)}) collective-permute-start(bf16[2,1,144,1088]{3,2,1,0:T(8,128)(2,1)S(1)} %pad_maximum_fusion.17.refs_0_), channel_id=1, source_target_pairs={{0,2},{1,3},{2,0},{3,1},{4,6},{5,7},{6,4},{7,5},{8,10},{9,11},{10,... | collective-permute-start | bytes 1880072 | tf_op jit(solution)/shard_map/ppermute | solution.py:400
  (83 other events, 833.4 us)
Sparse Core Ops, SparseCore 0:
  17.8 33.2 all-gather.6
  58.6 32.6 all-gather.8
  112.1 33.7 all-gather.10
  462.1 32.1 reduce-scatter.5
  555.7 32.3 reduce-scatter.7
  610.1 32.5 reduce-scatter.3

commit v7 on v6

--- a/solution.py
+++ b/solution.py
@@ -536,6 +536,61 @@
     return assemble(win, chip_groups(shards), own, other, owned_rows, shards, transposed, kind)
 
 
+def grads_kernel(groups, start, size, forms, here_ref, *refs):
+    total = sum(len(form) for form in forms)
+    arrays, outs = refs[:-total], refs[-total:]
+    x, y, core = here_ref[0], here_ref[1], here_ref[2]
+
+    def put(form, targets, block, row, values):
+        width = values.shape[-1]
+        if form == (0,):
+            owned = targets[0].shape[0] // 4
+            at = pl.multiple_of(block * owned + row, 16)
+            targets[0][pl.ds(at, size), :] = values
+            return
+        first = 0
+        for wide, ref in zip(form, targets):
+            for i in range(wide):
+
+                @pl.when(block == first + i)
+                def _():
+                    ref[pl.ds(row, size), i * width : (i + 1) * width] = values
+
+            first += wide
+
+    for turn in range(2):
+        row = pl.multiple_of((core ^ turn) * start, 16)
+        for (places, first), ref in zip(groups, arrays[turn * len(groups) :]):
+            for i, (dx, dy) in enumerate(places):
+                block = 2 * (x ^ dx) + (y ^ dy)
+                for s in range(ref.shape[1]):
+                    before = sum(len(form) for form in forms[: first + s])
+                    targets = outs[before : before + len(forms[first + s])]
+                    put(forms[first + s], targets, block, row, ref[i, s].astype(F32))
+
+
+def place_grads(win, own, other, owned_rows, forms):
+    width = own[0].shape[-1]
+    here = jnp.stack([win.x, win.y, win.core]).astype(jnp.int32)
+    shapes = [
+        (owned_rows, wide * width) if wide else (4 * owned_rows, width)
+        for form in forms
+        for wide in form
+    ]
+    groups = chip_groups(len(forms))
+    return pl.pallas_call(
+        functools.partial(grads_kernel, groups, win.start, win.size, forms),
+        in_specs=[pl.BlockSpec(memory_space=pltpu.SMEM)]
+        + [pl.BlockSpec(memory_space=pltpu.VMEM)] * (2 * len(groups)),
+        out_specs=[pl.BlockSpec(memory_space=pltpu.VMEM)] * len(shapes),
+        out_shape=[jax.ShapeDtypeStruct(shape, F32) for shape in shapes],
+        compiler_params=pltpu.CompilerParams(vmem_limit_bytes=VMEM_LIMIT),
+        cost_estimate=pl.CostEstimate(
+            flops=0, bytes_accessed=4 * owned_rows * width * len(forms), transcendentals=0
+        ),
+    )(here, *own, *other)
+
+
 def add_pair(kept, received):
     return (kept.astype(F32) + received.astype(F32)).astype(BF16)
 
@@ -583,8 +638,8 @@
 
 
 def reduce_vectors(values):
+    values = add_pair(values, swap(values, "ctx", 1))
     values = add_pair(values, swap(values, "replica", 1))
-    values = add_pair(values, swap(values, "ctx", 2))
     step = 1
     while step < lax.axis_size("shard"):
         values = add_pair(values, swap(values, "shard", step))
@@ -699,15 +754,13 @@
     start, finish = ((own_c[2], mixed), (full_c,)) if pairwise else ((), ())
     low_grad_out = to_sequences(cotangent, count, start, finish).reshape(rows, width)
 
-    def finish_units(groups, *earlier):
+    def finish_units(groups, forms, *earlier):
         sums = [
             lax.psum_scatter(group, "shard", scatter_dimension=0, tiled=False)
             for group in groups
         ]
         own = spread_chips(held(jnp.stack(sums), *earlier))
-        return place(
-            win, own, spread_cores(own), owned_rows, len(sums), transposed=True, kind=F32
-        )
+        return own, place_grads(win, own, spread_cores(own), owned_rows, forms)
 
     def reduce_whole(grads, transposed=False):
         if transposed:
@@ -798,10 +851,12 @@
     blocked_grads = grad_inputs.reshape(blocked)
     if pairwise:
         vector_grads = held(vector_grads, partial_a)
-        vector_grads = add_pair(vector_grads, swap(vector_grads, "ctx", 1))
-        (owned_a,) = finish_units([partial_a])
-        owned_proj, owned_fc = finish_units([partial_proj, partial_fc], vector_grads)
-        input_grad, _ = to_blocks(blocked_grads, F32, vector_grads)
+        vector_grads = add_pair(vector_grads, swap(vector_grads, "ctx", 2))
+        _, (qkv_grad, out_grad) = finish_units([partial_a], ((3, 1),))
+        own, (proj_grad, fc_grad) = finish_units(
+            [partial_proj, partial_fc], ((0,), (wide,)), vector_grads
+        )
+        input_grad, _ = to_blocks(blocked_grads, F32, own[0][1], own[1][1])
         owned_vectors = lax.dynamic_index_in_dim(
             reduce_vectors(vector_grads), lax.axis_index("shard"), keepdims=False
         )
@@ -813,10 +868,12 @@
             vector_grads, "shard", scatter_dimension=0, tiled=False
         )
         owned_vectors = lax.psum(owned_vectors, ("replica", "ctx"))
+        side_by_side = lambda blocks: jnp.concatenate(list(blocks), axis=1)
+        qkv_grad, out_grad = side_by_side(owned_a[:3]), owned_a[3]
+        fc_grad = side_by_side(owned_fc)
+        proj_grad = owned_proj.reshape(wide * owned_rows, width)
     owned_vectors = owned_vectors[:vector_rows].reshape(-1).astype(F32)
     vec = [owned_vectors[i * owned_rows : (i + 1) * owned_rows] for i in range(8)]
-    qkv_grad = jnp.concatenate([owned_a[i] for i in range(3)], axis=1)
-    fc_grad = jnp.concatenate([owned_fc[i] for i in range(wide)], axis=1)
     return (
         layer_out,
         input_grad,
@@ -825,13 +882,13 @@
         qkv_grad,
         vec[2],
         vec[3],
-        owned_a[3],
+        out_grad,
         vec[4],
         vec[5],
         vec[6],
         fc_grad,
         owned_vectors[8 * owned_rows :],
-        owned_proj.reshape(wide * owned_rows, width),
+        proj_grad,
         vec[7],
     )
 

time: 737 us -> 720 us (0.977)
  local copies, waits for them, and re-layouts: 103 us -> 81.5 us
    pallas_call x0 -> x2, Pallas kernels: none -> 13.1 us  [place_grads(): pl.pallas_call(functools.partial(grads_kernel, groups, win.start, win.siz...]
    pallas_call x5 -> x3, Pallas kernels: 37.2 us -> 25.9 us  [assemble(): pl.pallas_call(functools.partial(assemble_kernel, groups, win.start, win....]
    concatenate x2 -> x0, local copies, waits for them, and re-layouts: 9.92 us -> none  [the longest x1 5.84 us: per_device(): fc_grad = jnp.concatenate([owned_fc[i] for i in range(wide)], axis=1)]
    squeeze x2 -> x0, local copies, waits for them, and re-layouts: 8.66 us -> none  [the longest x1 4.35 us: per_device(): fc_grad = jnp.concatenate([owned_fc[i] for i in range(wide)], axis=1)]
    unnamed x122 -> x134, local copies, waits for them, and re-layouts: 18.5 us -> 16 us
  transfers between devices with their start and end apart: 70 -> 70, of which waited for: 25 -> 27; matrix products, arithmetic and copies ran while one was open for 22% -> 21% of each run, Pallas kernels for 32% -> 33%
where the time goes in v7:
time: 720 us; the launch traced here: 714 us
  Pallas kernels  239 us (33%)
  waiting for transfers between devices  186 us (26%)
  other arithmetic  81.7 us (11%)
  local copies, waits for them, and re-layouts  81.5 us (11%)
  starting transfers between devices  49.5 us (7%)
  matrix products  45.8 us (6%)
  between operations  31.3 us (4%)
    ppermute x64, waiting for transfers between devices, swap(): lax.ppermute(values, axis, [(index, index ^ offset) for index in range(co...  163 us
    pallas_call x7, Pallas kernels, by_rows(): pl.pallas_call(kernel, grid=(rows // tile,), in_specs=in_specs, out_specs...  140 us
    ppermute x64, starting transfers between devices, swap(): lax.ppermute(values, axis, [(index, index ^ offset) for index in range(co...  49.1 us
    convert_element_type x16, other arithmetic, add_pair(): return (kept.astype(F32) + received.astype(F32)).astype(BF16)  32.1 us
    pallas_call x1, Pallas kernels, attention_forward(): pl.pallas_call(functools.partial(attention_forward_kernel, query_blocks(c...  31.2 us
    pallas_call x1, Pallas kernels, attention_backward(): pl.pallas_call(functools.partial(attention_backward_kernel, query_blocks(...  28.7 us
    pallas_call x3, Pallas kernels, assemble(): pl.pallas_call(functools.partial(assemble_kernel, groups, win.start, win....  25.9 us
    all_gather x3, waiting for transfers between devices, gather_z(): return lax.all_gather(values, 'shard', axis=0, tiled=False)  22.8 us
  transfers between devices with their start and end apart: 70, of which 27 were waited for; matrix products, arithmetic and copies ran while one was open for 21% of the time, Pallas kernels for 33%

profile of v7, /device:TPU:0, one launch (start us, length us, event | category | flops | bytes accessed | tf_op | source)
XLA Modules:
  0.0 714.2 jit_solution(12572324450734282687)
XLA Ops:
  7.2 3.7 constant_dynamic-slice_fusion.3
  12.1 3.0 collective-permute-start
  18.1 21.7 %collective-permute-done = bf16[2,2,1088,128]{3,2,1,0:T(8,128)(2,1)S(1)} collective-permute-done((bf16[2,2,1088,128]{3,2,1,0:T(8,128)(2,1)}, bf16[2,2,1088,128]{3,2,1,0:T(8,128)(2,1)S(1)}, u32[]{:S(2)}, u32[]{:S(2)}) %collective-permute-start) | collective-permute-done | bytes 1114144 | tf_op jit(solution)/shard_map/ppermute | solution.py:400
  41.4 9.8 %all-gather.7.cloned.1.call-done = bf16[576,1088]{1,0:T(8,128)(2,1)} async-done(((bf16[144,1088]{1,0:T(8,128)(2,1)}), bf16[576,1088]{1,0:T(8,128)(2,1)}) %all-gather.7.cloned.1.call-update) | async-done | bytes 1253392 | tf_op jit(solution)/shard_map/all_gather | solution.py:688
  51.6 2.7 copy.60
  58.5 13.2 %collective-permute-done.2 = bf16[2,144,1088]{2,1,0:T(8,128)(2,1)S(1)} collective-permute-done((bf16[2,144,1088]{2,1,0:T(8,128)(2,1)}, bf16[2,144,1088]{2,1,0:T(8,128)(2,1)S(1)}, u32[]{:S(2)}, u32[]{:S(2)}) %collective-permute-start.2) | collective-permute-done | bytes 626720 | tf_op jit(solution)/shard_map/ppermute | solution.py:400
  78.2 13.0 %all-gather.9.cloned.1.call-done = bf16[640,1088]{1,0:T(8,128)(2,1)} async-done(((bf16[160,1088]{1,0:T(8,128)(2,1)}), bf16[640,1088]{1,0:T(8,128)(2,1)}) %all-gather.9.cloned.1.call-update) | async-done | bytes 1392656 | tf_op jit(solution)/shard_map/all_gather | solution.py:688
  91.3 12.1 %collective-permute-done.4.refs_2_ = bf16[2,2,144,1088]{3,2,1,0:T(8,128)(2,1)S(1)} collective-permute-done((bf16[2,2,144,1088]{3,2,1,0:T(8,128)(2,1)}, bf16[2,2,144,1088]{3,2,1,0:T(8,128)(2,1)S(1)}, u32[]{:S(2)}, u32[]{:S(2)}) %collective-permute-start.4) | collective-permute-done | bytes 1253408 | tf_op jit(solution)/shard_map/ppermute | solution.py:400
  103.4 2.4 collective-permute-done.5.refs_3_
  112.8 11.3 %collective-permute-done.10 = bf16[2,144,1088]{2,1,0:T(8,128)(2,1)S(1)} collective-permute-done((bf16[2,144,1088]{2,1,0:T(8,128)(2,1)}, bf16[2,144,1088]{2,1,0:T(8,128)(2,1)S(1)}, u32[]{:S(2)}, u32[]{:S(2)}) %collective-permute-start.10) | collective-permute-done | bytes 626720 | tf_op jit(solution)/shard_map/ppermute | solution.py:400
  132.9 8.7 %shard_map.271 = bf16[4,4,272,1088]{3,2,1,0:T(8,128)(2,1)} custom-call(s32[3]{0:T(128)} %pad_add_fusion.here_ref, bf16[2,2,144,1088]{3,2,1,0:T(8,128)(2,1)} %pad_maximum_fusion.3.refs_0_, bf16[2,2,144,1088]{3,2,1,0:T(8,128)(2,1)} %pad_maximum_fusion.4.refs_1_, bf16[2,2,144,1088]{3,2,1,0:T(8,128)(2,1)} %copy-done.36, bf16[2,2,144,1088]{3,2,1,0:T(8,128)(2,1)} %copy-done.37, ...), custom_call_target="tpu_custom_call" | custom-call | bytes 18939904 | tf_op jit(solution)/shard_map/pallas_call | solution.py:493
  141.6 16.7 %shard_map.272 = (bf16[3,1024,1088]{2,1,0:T(8,128)(2,1)}, bf16[1024,1088]{1,0:T(8,128)(2,1)}) custom-call(bf16[1024,1088]{1,0:T(8,128)(2,1)} %bitcast.219, bf16[4,1088,1088]{2,1,0:T(8,128)(2,1)} %bitcast.201, f32[8,1088]{1,0:T(8,128)} %reshape.183.small_ref, bf16[16,128]{1,0:T(8,128)(2,1)} %slice.608.refs_0_, bf16[16,128]{1,0:T(8,128)(2,1)} %slice.609.refs_1_), custom_call_target="tpu_custom_call" | custom-call | flops 1363673088 | bytes 2581760 | tf_op jit(solution)/shard_map/pallas_call | solution.py:379
  166.9 14.2 %collective-permute-done.14 = bf16[2,144,1088]{2,1,0:T(8,128)(2,1)S(1)} collective-permute-done((bf16[2,144,1088]{2,1,0:T(8,128)(2,1)S(1)}, bf16[2,144,1088]{2,1,0:T(8,128)(2,1)S(1)}, u32[]{:S(2)}, u32[]{:S(2)}) %collective-permute-start.14) | collective-permute-done | bytes 626720 | tf_op jit(solution)/shard_map/ppermute | solution.py:400
  186.5 31.2 %shard_map.273 = (bf16[4,2,128,1088]{3,2,1,0:T(8,128)(2,1)}, f32[2,9,8,512]{3,2,1,0:T(8,128)}) custom-call(s32[4]{0:T(128)} %broadcast_xor_fusion.order_ref, bf16[3,4,2,128,1088]{4,3,2,1,0:T(8,128)(2,1)} %bitcast.195, bf16[3,4,2,128,1088]{4,3,2,1,0:T(8,128)(2,1)} %bitcast.196, bf16[3,4,2,128,1088]{4,3,2,1,0:T(8,128)(2,1)} %bitcast.197, ...), custom_call_target="tpu_custom_call" | custom-call | flops 1207959552 | bytes 1114112 | tf_op jit(solution)/shard_map/pallas_call | solution.py:168
  226.1 8.5 %shard_map.274 = (f32[1024,1088]{1,0:T(8,128)}, bf16[1024,1088]{1,0:T(8,128)(2,1)}) custom-call(bf16[1024,1088]{1,0:T(8,128)(2,1)} %bitcast.220, bf16[1024,1088]{1,0:T(8,128)(2,1)} %bitcast.229, bf16[4,1088,1088]{2,1,0:T(8,128)(2,1)} %bitcast.202, f32[8,1088]{1,0:T(8,128)} %reshape.183.small_ref), custom_call_target="tpu_custom_call" | custom-call | flops 454557696 | bytes 2580736 | tf_op jit(solution)/shard_map/pallas_call | solution.py:379
  235.2 8.6 %shard_map.275 = bf16[4,4,272,1088]{3,2,1,0:T(8,128)(2,1)} custom-call(s32[3]{0:T(128)} %pad_add_fusion.here_ref, bf16[2,2,144,1088]{3,2,1,0:T(8,128)(2,1)} %copy-done.11, bf16[2,2,144,1088]{3,2,1,0:T(8,128)(2,1)} %copy-done.12, bf16[2,2,144,1088]{3,2,1,0:T(8,128)(2,1)} %collective-permute-done.12.refs_2_, ...), custom_call_target="tpu_custom_call" | custom-call | bytes 18939904 | tf_op jit(solution)/shard_map/pallas_call | solution.py:493
  244.3 6.8 collective-permute-done.26
  256.7 27.8 %shard_map.276 = (bf16[4,1024,1088]{2,1,0:T(8,128)(2,1)}, bf16[4,1024,1088]{2,1,0:T(8,128)(2,1)}) custom-call(bf16[1024,1088]{1,0:T(8,128)(2,1)} %get-tuple-element.86.low_ref, bf16[4,1088,1088]{2,1,0:T(8,128)(2,1)} %bitcast.205, f32[4,1,1088]{2,1,0:T(1,128)} %reshape.187.bias_ref, bf16[16,128]{1,0:T(8,128)(2,1)} %slice.616.refs_0_, ...), custom_call_target="tpu_custom_call" | custom-call | flops 1818230784 | bytes 3693696 | tf_op jit(solution)/shard_map/pallas_call | solution.py:379
  286.5 8.6 %shard_map.277 = bf16[4,4,272,1088]{3,2,1,0:T(8,128)(2,1)} custom-call(s32[3]{0:T(128)} %pad_add_fusion.here_ref, bf16[2,2,144,1088]{3,2,1,0:T(8,128)(2,1)} %copy-done.13, bf16[2,2,144,1088]{3,2,1,0:T(8,128)(2,1)} %copy-done.14, bf16[2,2,144,1088]{3,2,1,0:T(8,128)(2,1)} %collective-permute-done.20.refs_2_, ...), custom_call_target="tpu_custom_call" | custom-call | bytes 18939904 | tf_op jit(solution)/shard_map/pallas_call | solution.py:493
  298.1 2.7 copy.62
  302.6 15.2 %convolution_convert_fusion.1 = bf16[4,1088,1088]{2,1,0:T(8,128)(2,1)S(1)} fusion(bf16[4,1024,1088]{2,1,0:T(8,128)(2,1)} %get-tuple-element.90.act_ref, bf16[1024,1088,1]{1,0,2:T(8,128)(2,1)S(1)} %bitcast.224), kind=kOutput, calls=%fused_computation.1 | convolution fusion | flops 9701965824 | bytes 20611072 | tf_op jit(solution)/shard_map/ctx,td->cxd/dot_general | solution.py:781
  317.9 3.3 broadcast_select_fusion.2
  326.2 19.8 %shard_map.278 = bf16[1024,1088]{1,0:T(8,128)(2,1)} custom-call(f32[1024,1088]{1,0:T(8,128)} %get-tuple-element.92.middle_ref, bf16[4,1024,1088]{2,1,0:T(8,128)(2,1)} %get-tuple-element.90.act_ref, bf16[4,1088,1088]{2,1,0:T(8,128)(2,1)} %bitcast.207, f32[8,1088]{1,0:T(8,128)} %reshape.183.small_ref, bf16[16,128]{1,0:T(8,128)(2,1)} %slice.632.refs_0_), custom_call_target="tpu_custom_call" | custom-call | flops 1818230784 | bytes 3138304 | tf_op jit(solution)/shard_map/pallas_call | solution.py:379
  347.2 6.6 add_convert_fusion.2
  361.5 21.1 %shard_map.279 = (bf16[4,1024,1088]{2,1,0:T(8,128)(2,1)}, f32[8,1088]{1,0:T(8,128)}) custom-call(bf16[1024,1088]{1,0:T(8,128)(2,1)} %bitcast.225, bf16[4,1024,1088]{2,1,0:T(8,128)(2,1)} %get-tuple-element.93.slope_ref, bf16[4,1088,1088]{2,1,0:T(8,128)(2,1)} %bitcast.208, bf16[16,128]{1,0:T(8,128)(2,1)} %slice.640.refs_0_, bf16[16,128]{1,0:T(8,128)(2,1)} %slice.642.refs_1_, ...), custom_call_target="tpu_custom_call" | custom-call | flops 1818230784 | bytes 3696384 | tf_op jit(solution)/shard_map/pallas_call | solution.py:379
  382.6 13.2 %convolution_convert_fusion = bf16[4,1088,1088]{1,2,0:T(8,128)(2,1)S(1)} fusion(bf16[4,1024,1088]{2,1,0:T(8,128)(2,1)} %get-tuple-element.94.hidden_ref, bf16[1024,1088]{1,0:T(8,128)(2,1)S(1)} %copy-done.23), kind=kOutput, calls=%fused_computation | convolution fusion | flops 9701965824 | bytes 20611072 | tf_op jit(solution)/shard_map/td,ctx->cdx/dot_general | solution.py:799
  396.8 3.3 broadcast_select_fusion.1
  402.0 4.3 add_convert_fusion.7
  411.3 4.2 copy.66
  420.5 27.2 %shard_map.280 = (f32[1024,1088]{1,0:T(8,128)}, bf16[1024,1088]{1,0:T(8,128)(2,1)}, bf16[1024,1088]{1,0:T(8,128)(2,1)}, f32[8,1088]{1,0:T(8,128)}) custom-call(bf16[4,1024,1088]{2,1,0:T(8,128)(2,1)} %get-tuple-element.94.hidden_ref, bf16[1024,1088]{1,0:T(8,128)(2,1)} %bitcast.226, f32[1024,1088]{1,0:T(8,128)} %get-tuple-element.92.middle_ref, ...), custom_call_target="tpu_custom_call" | custom-call | flops 2272788480 | bytes 5441024 | tf_op jit(solution)/shard_map/pallas_call | solution.py:379
  447.8 4.8 convolution_convert_fusion.3
  455.2 3.0 collective-permute-done.33
  467.5 7.3 %add_convert_fusion.1 = bf16[4,4,144,1088]{3,2,1,0:T(8,128)(2,1)S(1)} fusion(bf16[4,4,144,1088]{3,2,1,0:T(8,128)(2,1)} %collective-permute-done.35, pred[]{:T(512)S(6)} %eq.16, bf16[4,4,272,1088]{3,2,1,0:T(8,128)(2,1)} %bitcast.211), kind=kLoop, calls=%fused_computation.4 | loop fusion | flops 12533760 | bytes 20054016 | tf_op jit(solution)/shard_map/convert_element_type | solution.py:595
  481.4 28.7 %shard_map.281 = bf16[3,4,2,128,1088]{4,3,2,1,0:T(8,128)(2,1)} custom-call(s32[4]{0:T(128)} %broadcast_xor_fusion.order_ref, bf16[3,4,2,128,1088]{4,3,2,1,0:T(8,128)(2,1)} %bitcast.198, bf16[3,4,2,128,1088]{4,3,2,1,0:T(8,128)(2,1)} %bitcast.199, bf16[3,4,2,128,1088]{4,3,2,1,0:T(8,128)(2,1)} %bitcast.200, bf16[4,2,128,1088]{3,2,1,0:T(8,128)(2,1)} %get-tuple-element.85.o_ref, ...), custom_call_target="tpu_custom_call" | custom-call | flops 1509949440 | bytes 2228224 | tf_op jit(solution)/shard_map/pallas_call | solution.py:201
  510.1 12.7 %convolution_convert_fusion.2 = bf16[3,1088,1088]{1,2,0:T(8,128)(2,1)S(1)} fusion(bf16[3,1024,1088]{2,1,0:T(8,128)(2,1)} %bitcast.222, bf16[1024,1088]{1,0:T(8,128)(2,1)} %get-tuple-element.100), kind=kOutput, calls=%fused_computation.2 | convolution fusion | flops 7276474368 | bytes 16015360 | tf_op jit(solution)/shard_map/td,ctx->cdx/dot_general | solution.py:820
  525.5 3.5 add_convert_fusion.4
  532.7 13.7 %collective-permute-done.41 = bf16[2,144,1088]{2,1,0:T(8,128)(2,1)S(1)} collective-permute-done((bf16[2,144,1088]{2,1,0:T(8,128)(2,1)S(1)}, bf16[2,144,1088]{2,1,0:T(8,128)(2,1)S(1)}, u32[]{:S(2)}, u32[]{:S(2)}) %collective-permute-start.41) | collective-permute-done | bytes 626720 | tf_op jit(solution)/shard_map/ppermute | solution.py:400
  557.8 18.6 %shard_map.282 = (bf16[1024,1088]{1,0:T(8,128)(2,1)}, f32[8,1088]{1,0:T(8,128)}) custom-call(bf16[3,1024,1088]{2,1,0:T(8,128)(2,1)} %bitcast.223, f32[1024,1088]{1,0:T(8,128)} %get-tuple-element.102.grad_middle_ref, bf16[1024,1088]{1,0:T(8,128)(2,1)} %bitcast.221, bf16[4,1088,1088]{2,1,0:T(8,128)(2,1)} %bitcast.204, f32[8,1088]{1,0:T(8,128)} %reshape.183.small_ref, ...), custom_call_target="tpu_custom_call" | custom-call | flops 1363673088 | bytes 3144192 | tf_op jit(solution)/shard_map/pallas_call | solution.py:379
  578.9 4.7 collective-permute-done.37
  584.8 2.7 add_convert_fusion.3
  591.1 12.7 %collective-permute-done.43 = bf16[2,144,1088]{2,1,0:T(8,128)(2,1)} collective-permute-done((bf16[2,144,1088]{2,1,0:T(8,128)(2,1)}, bf16[2,144,1088]{2,1,0:T(8,128)(2,1)}, u32[]{:S(2)}, u32[]{:S(2)}) %collective-permute-start.43) | collective-permute-done | bytes 626720 | tf_op jit(solution)/shard_map/ppermute | solution.py:400
  620.9 7.2 %collective-permute-done.46 = bf16[1,144,1088]{2,1,0:T(8,128)(2,1)S(1)} collective-permute-done((bf16[1,144,1088]{2,1,0:T(8,128)(2,1)S(1)}, bf16[1,144,1088]{2,1,0:T(8,128)(2,1)S(1)}, u32[]{:S(2)}, u32[]{:S(2)}) %collective-permute-start.46) | collective-permute-done | bytes 313376 | tf_op jit(solution)/shard_map/ppermute | solution.py:400
  633.6 2.4 copy.73
  648.3 16.8 %collective-permute-done.48 = bf16[2,2,1088,128]{3,2,1,0:T(8,128)(2,1)S(1)} collective-permute-done((bf16[2,2,1088,128]{3,2,1,0:T(8,128)(2,1)S(1)}, bf16[2,2,1088,128]{3,2,1,0:T(8,128)(2,1)S(1)}, u32[]{:S(2)}, u32[]{:S(2)}) %collective-permute-start.48) | collective-permute-done | bytes 1114144 | tf_op jit(solution)/shard_map/ppermute | solution.py:400
  671.1 6.8 collective-permute-done.58.refs_2_
  683.6 8.2 %shard_map.284 = (f32[1088,1088]{1,0:T(8,128)}, f32[272,4352]{1,0:T(8,128)}) custom-call(s32[3]{0:T(128)} %pad_add_fusion.here_ref, bf16[2,1,144,1088]{3,2,1,0:T(8,128)(2,1)} %copy-done.20, bf16[2,1,144,1088]{3,2,1,0:T(8,128)(2,1)} %copy-done.21, bf16[2,1,144,1088]{3,2,1,0:T(8,128)(2,1)} %collective-permute-done.58.refs_2_, ...), custom_call_target="tpu_custom_call" | custom-call | bytes 2367488 | tf_op jit(solution)/shard_map/pallas_call | solution.py:581
  693.0 5.5 collective-permute-done.55.refs_1_
  702.3 4.9 shard_map.283
  (417 shorter events, 173.7 us)
Async XLA Ops:
  7.2 44.0 %all-gather.7.cloned.1.call-start = ((), (), s32[]{:S(2)}) async-start(), calls=%async_computation.6 | async-start | bytes 1658880 | tf_op jit(solution)/shard_map/all_gather | solution.py:688
  12.1 27.7 %collective-permute-start = (bf16[2,2,1088,128]{3,2,1,0:T(8,128)(2,1)}, bf16[2,2,1088,128]{3,2,1,0:T(8,128)(2,1)S(1)}, u32[]{:S(2)}, u32[]{:S(2)}) collective-permute-start(bf16[2,2,1088,128]{3,2,1,0:T(8,128)(2,1)} %pad_maximum_fusion.12), channel_id=1, source_target_pairs={{0,2},{1,3},{2,0},{3,1},{4,6},{5,7},{6,4},{7,5},{8,10},{9,11},{10,... | collective-permute-start | bytes 3342344 | tf_op jit(solution)/shard_map/ppermute | solution.py:400
  17.7 73.5 %all-gather.9.cloned.1.call-start = ((), (), s32[]{:S(2)}) async-start(), calls=%async_computation.7 | async-start | bytes 1843200 | tf_op jit(solution)/shard_map/all_gather | solution.py:688
  58.5 104.8 %all-gather.11.cloned.1.call-start = ((), (), s32[]{:S(2)}) async-start(), calls=%async_computation.8 | async-start | bytes 1658880 | tf_op jit(solution)/shard_map/all_gather | solution.py:688
  74.1 29.3 %collective-permute-start.4 = (bf16[2,2,144,1088]{3,2,1,0:T(8,128)(2,1)}, bf16[2,2,144,1088]{3,2,1,0:T(8,128)(2,1)S(1)}, u32[]{:S(2)}, u32[]{:S(2)}) collective-permute-start(bf16[2,2,144,1088]{3,2,1,0:T(8,128)(2,1)} %pad_maximum_fusion.3.refs_0_), channel_id=1, source_target_pairs={{0,2},{1,3},{2,0},{3,1},{4,6},{5,7},{6,4},{7,5},{8,10},{9,11},{10,... | collective-permute-start | bytes 3760136 | tf_op jit(solution)/shard_map/ppermute | solution.py:400
  76.8 29.0 %collective-permute-start.5 = (bf16[2,2,144,1088]{3,2,1,0:T(8,128)(2,1)}, bf16[2,2,144,1088]{3,2,1,0:T(8,128)(2,1)S(1)}, u32[]{:S(2)}, u32[]{:S(2)}) collective-permute-start(bf16[2,2,144,1088]{3,2,1,0:T(8,128)(2,1)} %pad_maximum_fusion.4.refs_1_), channel_id=1, source_target_pairs={{0,4},{4,0},{1,5},{5,1},{2,6},{6,2},{3,7},{7,3},{8,12},{12,8},{9,1... | collective-permute-start | bytes 3760136 | tf_op jit(solution)/shard_map/ppermute | solution.py:400
  78.2 48.2 %collective-permute-start.6 = (bf16[2,2,144,1088]{3,2,1,0:T(8,128)(2,1)}, bf16[2,2,144,1088]{3,2,1,0:T(8,128)(2,1)}, u32[]{:S(2)}, u32[]{:S(2)}) collective-permute-start(bf16[2,2,144,1088]{3,2,1,0:T(8,128)(2,1)} %pad_maximum_fusion.3.refs_0_), channel_id=1, source_target_pairs={{0,1},{1,0},{2,3},{3,2},{4,5},{5,4},{6,7},{7,6},{8,9},{9,8},{10,11... | collective-permute-start | bytes 3760136 | tf_op jit(solution)/shard_map/ppermute | solution.py:400
  111.9 21.0 %collective-permute-start.7 = (bf16[2,2,144,1088]{3,2,1,0:T(8,128)(2,1)}, bf16[2,2,144,1088]{3,2,1,0:T(8,128)(2,1)}, u32[]{:S(2)}, u32[]{:S(2)}) collective-permute-start(bf16[2,2,144,1088]{3,2,1,0:T(8,128)(2,1)} %pad_maximum_fusion.4.refs_1_), channel_id=1, source_target_pairs={{0,1},{1,0},{2,3},{3,2},{4,5},{5,4},{6,7},{7,6},{8,9},{9,8},{10,11... | collective-permute-start | bytes 3760136 | tf_op jit(solution)/shard_map/ppermute | solution.py:400
  111.9 503.5 %reduce-scatter.4.cloned.1.call-start = ((), (), s32[]{:S(2)}) async-start(), calls=%async_computation.3 | async-start | bytes 1658880 | tf_op jit(solution)/shard_map/reduce_scatter | solution.py:759
  112.2 20.7 %collective-permute-start.8 = (bf16[2,2,144,1088]{3,2,1,0:T(8,128)(2,1)}, bf16[2,2,144,1088]{3,2,1,0:T(8,128)(2,1)}, u32[]{:S(2)}, u32[]{:S(2)}) collective-permute-start(bf16[2,2,144,1088]{3,2,1,0:T(8,128)(2,1)} %copy-done.36), channel_id=1, source_target_pairs={{0,1},{1,0},{2,3},{3,2},{4,5},{5,4},{6,7},{7,6},{8,9},{9,8},{10,11... | collective-permute-start | bytes 3760136 | tf_op jit(solution)/shard_map/ppermute | solution.py:400
  125.3 35.4 %collective-permute-start.12 = (bf16[2,2,144,1088]{3,2,1,0:T(8,128)(2,1)S(1)}, bf16[2,2,144,1088]{3,2,1,0:T(8,128)(2,1)}, u32[]{:S(2)}, u32[]{:S(2)}) collective-permute-start(bf16[2,2,144,1088]{3,2,1,0:T(8,128)(2,1)S(1)} %pad_maximum_fusion.5.refs_0_), channel_id=1, source_target_pairs={{0,2},{1,3},{2,0},{3,1},{4,6},{5,7},{6,4},{7,5},{8,10},{9,11},{10,... | collective-permute-start | bytes 3760136 | tf_op jit(solution)/shard_map/ppermute | solution.py:400
  126.4 34.3 %collective-permute-start.13 = (bf16[2,2,144,1088]{3,2,1,0:T(8,128)(2,1)S(1)}, bf16[2,2,144,1088]{3,2,1,0:T(8,128)(2,1)}, u32[]{:S(2)}, u32[]{:S(2)}) collective-permute-start(bf16[2,2,144,1088]{3,2,1,0:T(8,128)(2,1)S(1)} %pad_maximum_fusion.6.refs_1_), channel_id=1, source_target_pairs={{0,4},{4,0},{1,5},{5,1},{2,6},{6,2},{3,7},{7,3},{8,12},{12,8},{9,1... | collective-permute-start | bytes 3760136 | tf_op jit(solution)/shard_map/ppermute | solution.py:400
  164.8 16.2 %collective-permute-start.14 = (bf16[2,144,1088]{2,1,0:T(8,128)(2,1)S(1)}, bf16[2,144,1088]{2,1,0:T(8,128)(2,1)S(1)}, u32[]{:S(2)}, u32[]{:S(2)}) collective-permute-start(bf16[2,144,1088]{2,1,0:T(8,128)(2,1)S(1)} %bitcast.241), channel_id=1, source_target_pairs={{0,4},{4,0},{1,5},{5,1},{2,6},{6,2},{3,7},{7,3},{8,12},{12,8},{9,1... | collective-permute-start | bytes 1880072 | tf_op jit(solution)/shard_map/ppermute | solution.py:400
  165.6 16.6 %collective-permute-start.15 = (bf16[2,144,1088]{2,1,0:T(8,128)(2,1)S(1)}, bf16[2,144,1088]{2,1,0:T(8,128)(2,1)S(1)}, u32[]{:S(2)}, u32[]{:S(2)}) collective-permute-start(bf16[2,144,1088]{2,1,0:T(8,128)(2,1)S(1)} %bitcast.239), channel_id=1, source_target_pairs={{0,2},{1,3},{2,0},{3,1},{4,6},{5,7},{6,4},{7,5},{8,10},{9,11},{10,... | collective-permute-start | bytes 1880072 | tf_op jit(solution)/shard_map/ppermute | solution.py:400
  182.4 37.8 %collective-permute-start.20 = (bf16[2,2,144,1088]{3,2,1,0:T(8,128)(2,1)S(1)}, bf16[2,2,144,1088]{3,2,1,0:T(8,128)(2,1)}, u32[]{:S(2)}, u32[]{:S(2)}) collective-permute-start(bf16[2,2,144,1088]{3,2,1,0:T(8,128)(2,1)S(1)} %pad_maximum_fusion.7.refs_0_), channel_id=1, source_target_pairs={{0,2},{1,3},{2,0},{3,1},{4,6},{5,7},{6,4},{7,5},{8,10},{9,11},{10,... | collective-permute-start | bytes 3760136 | tf_op jit(solution)/shard_map/ppermute | solution.py:400
  183.4 37.3 %collective-permute-start.21 = (bf16[2,2,144,1088]{3,2,1,0:T(8,128)(2,1)S(1)}, bf16[2,2,144,1088]{3,2,1,0:T(8,128)(2,1)}, u32[]{:S(2)}, u32[]{:S(2)}) collective-permute-start(bf16[2,2,144,1088]{3,2,1,0:T(8,128)(2,1)S(1)} %pad_maximum_fusion.8.refs_1_), channel_id=1, source_target_pairs={{0,4},{4,0},{1,5},{5,1},{2,6},{6,2},{3,7},{7,3},{8,12},{12,8},{9,1... | collective-permute-start | bytes 3760136 | tf_op jit(solution)/shard_map/ppermute | solution.py:400
  184.7 50.0 %collective-permute-start.16 = (bf16[2,2,144,1088]{3,2,1,0:T(8,128)(2,1)S(1)}, bf16[2,2,144,1088]{3,2,1,0:T(8,128)(2,1)}, u32[]{:S(2)}, u32[]{:S(2)}) collective-permute-start(bf16[2,2,144,1088]{3,2,1,0:T(8,128)(2,1)S(1)} %pad_maximum_fusion.5.refs_0_), channel_id=1, source_target_pairs={{0,1},{1,0},{2,3},{3,2},{4,5},{5,4},{6,7},{7,6},{8,9},{9,8},{10,11... | collective-permute-start | bytes 3760136 | tf_op jit(solution)/shard_map/ppermute | solution.py:400
  184.7 50.1 %collective-permute-start.17 = (bf16[2,2,144,1088]{3,2,1,0:T(8,128)(2,1)S(1)}, bf16[2,2,144,1088]{3,2,1,0:T(8,128)(2,1)}, u32[]{:S(2)}, u32[]{:S(2)}) collective-permute-start(bf16[2,2,144,1088]{3,2,1,0:T(8,128)(2,1)S(1)} %pad_maximum_fusion.6.refs_1_), channel_id=1, source_target_pairs={{0,1},{1,0},{2,3},{3,2},{4,5},{5,4},{6,7},{7,6},{8,9},{9,8},{10,11... | collective-permute-start | bytes 3760136 | tf_op jit(solution)/shard_map/ppermute | solution.py:400
  185.2 50.1 %collective-permute-start.18 = (bf16[2,2,144,1088]{3,2,1,0:T(8,128)(2,1)}, bf16[2,2,144,1088]{3,2,1,0:T(8,128)(2,1)}, u32[]{:S(2)}, u32[]{:S(2)}) collective-permute-start(bf16[2,2,144,1088]{3,2,1,0:T(8,128)(2,1)} %collective-permute-done.12.refs_2_), channel_id=1, source_target_pairs={{0,1},{1,0},{2,3},{3,2},{4,5},{5,4},{6,7},{7,6},{8,9},{9,8},{10,11... | collective-permute-start | bytes 3760136 | tf_op jit(solution)/shard_map/ppermute | solution.py:400
  224.3 26.9 %collective-permute-start.26 = (bf16[2,2,1088,128]{3,2,1,0:T(8,128)(2,1)}, bf16[2,2,1088,128]{3,2,1,0:T(8,128)(2,1)}, u32[]{:S(2)}, u32[]{:S(2)}) collective-permute-start(bf16[2,2,1088,128]{3,2,1,0:T(8,128)(2,1)} %maximum_select_fusion), channel_id=1, source_target_pairs={{0,2},{1,3},{2,0},{3,1},{4,6},{5,7},{6,4},{7,5},{8,10},{9,11},{10,... | collective-permute-start | bytes 3342344 | tf_op jit(solution)/shard_map/ppermute | solution.py:400
  234.6 49.9 %collective-permute-start.22 = (bf16[2,2,144,1088]{3,2,1,0:T(8,128)(2,1)S(1)}, bf16[2,2,144,1088]{3,2,1,0:T(8,128)(2,1)S(1)}, u32[]{:S(2)}, u32[]{:S(2)}) collective-permute-start(bf16[2,2,144,1088]{3,2,1,0:T(8,128)(2,1)S(1)} %pad_maximum_fusion.7.refs_0_), channel_id=1, source_target_pairs={{0,1},{1,0},{2,3},{3,2},{4,5},{5,4},{6,7},{7,6},{8,9},{9,8},{10,11... | collective-permute-start | bytes 3760136 | tf_op jit(solution)/shard_map/ppermute | solution.py:400
  234.7 49.8 %collective-permute-start.23 = (bf16[2,2,144,1088]{3,2,1,0:T(8,128)(2,1)S(1)}, bf16[2,2,144,1088]{3,2,1,0:T(8,128)(2,1)S(1)}, u32[]{:S(2)}, u32[]{:S(2)}) collective-permute-start(bf16[2,2,144,1088]{3,2,1,0:T(8,128)(2,1)S(1)} %pad_maximum_fusion.8.refs_1_), channel_id=1, source_target_pairs={{0,1},{1,0},{2,3},{3,2},{4,5},{5,4},{6,7},{7,6},{8,9},{9,8},{10,11... | collective-permute-start | bytes 3760136 | tf_op jit(solution)/shard_map/ppermute | solution.py:400
  243.8 40.8 %collective-permute-start.24 = (bf16[2,2,144,1088]{3,2,1,0:T(8,128)(2,1)}, bf16[2,2,144,1088]{3,2,1,0:T(8,128)(2,1)S(1)}, u32[]{:S(2)}, u32[]{:S(2)}) collective-permute-start(bf16[2,2,144,1088]{3,2,1,0:T(8,128)(2,1)} %collective-permute-done.20.refs_2_), channel_id=1, source_target_pairs={{0,1},{1,0},{2,3},{3,2},{4,5},{5,4},{6,7},{7,6},{8,9},{9,8},{10,11... | collective-permute-start | bytes 3760136 | tf_op jit(solution)/shard_map/ppermute | solution.py:400
  243.9 40.7 %collective-permute-start.25 = (bf16[2,2,144,1088]{3,2,1,0:T(8,128)(2,1)}, bf16[2,2,144,1088]{3,2,1,0:T(8,128)(2,1)}, u32[]{:S(2)}, u32[]{:S(2)}) collective-permute-start(bf16[2,2,144,1088]{3,2,1,0:T(8,128)(2,1)} %collective-permute-done.21.refs_3_), channel_id=1, source_target_pairs={{0,1},{1,0},{2,3},{3,2},{4,5},{5,4},{6,7},{7,6},{8,9},{9,8},{10,11... | collective-permute-start | bytes 3760136 | tf_op jit(solution)/shard_map/ppermute | solution.py:400
  253.5 44.1 %collective-permute-start.27 = (bf16[2,2,1088,128]{3,2,1,0:T(8,128)(2,1)}, bf16[2,2,1088,128]{3,2,1,0:T(8,128)(2,1)S(1)}, u32[]{:S(2)}, u32[]{:S(2)}) collective-permute-start(bf16[2,2,1088,128]{3,2,1,0:T(8,128)(2,1)} %pad_maximum_fusion.14), channel_id=1, source_target_pairs={{0,1},{1,0},{2,3},{3,2},{4,5},{5,4},{6,7},{7,6},{8,9},{9,8},{10,11... | collective-permute-start | bytes 3342344 | tf_op jit(solution)/shard_map/ppermute | solution.py:400
  323.2 24.1 %collective-permute-start.28 = (bf16[4,4,144,1088]{3,2,1,0:T(8,128)(2,1)}, bf16[4,4,144,1088]{3,2,1,0:T(8,128)(2,1)}, u32[]{:S(2)}, u32[]{:S(2)}) collective-permute-start(bf16[4,4,144,1088]{3,2,1,0:T(8,128)(2,1)} %broadcast_select_fusion.2), channel_id=1, source_target_pairs={{0,1},{1,0},{2,3},{3,2},{4,5},{5,4},{6,7},{7,6},{8,9},{9,8},{10,11... | collective-permute-start | bytes 15040520 | tf_op jit(solution)/shard_map/ppermute | solution.py:400
  356.6 45.3 %collective-permute-start.29 = (bf16[2,2,144,1088]{3,2,1,0:T(8,128)(2,1)}, bf16[2,2,144,1088]{3,2,1,0:T(8,128)(2,1)}, u32[]{:S(2)}, u32[]{:S(2)}) collective-permute-start(bf16[2,2,144,1088]{3,2,1,0:T(8,128)(2,1)} %get-tuple-element.134), channel_id=1, source_target_pairs={{0,4},{4,0},{1,5},{5,1},{2,6},{6,2},{3,7},{7,3},{8,12},{12,8},{9,1... | collective-permute-start | bytes 3760136 | tf_op jit(solution)/shard_map/ppermute | solution.py:400
  359.0 42.9 %collective-permute-start.30 = (bf16[2,2,144,1088]{3,2,1,0:T(8,128)(2,1)S(1)}, bf16[2,2,144,1088]{3,2,1,0:T(8,128)(2,1)}, u32[]{:S(2)}, u32[]{:S(2)}) collective-permute-start(bf16[2,2,144,1088]{3,2,1,0:T(8,128)(2,1)S(1)} %get-tuple-element.133), channel_id=1, source_target_pairs={{0,2},{1,3},{2,0},{3,1},{4,6},{5,7},{6,4},{7,5},{8,10},{9,11},{10,... | collective-permute-start | bytes 3760136 | tf_op jit(solution)/shard_map/ppermute | solution.py:400
  401.2 66.3 %collective-permute-start.35 = (bf16[4,4,144,1088]{3,2,1,0:T(8,128)(2,1)}, bf16[4,4,144,1088]{3,2,1,0:T(8,128)(2,1)}, u32[]{:S(2)}, u32[]{:S(2)}) collective-permute-start(bf16[4,4,144,1088]{3,2,1,0:T(8,128)(2,1)} %broadcast_select_fusion.1), channel_id=1, source_target_pairs={{0,1},{1,0},{2,3},{3,2},{4,5},{5,4},{6,7},{7,6},{8,9},{9,8},{10,11... | collective-permute-start | bytes 15040520 | tf_op jit(solution)/shard_map/ppermute | solution.py:400
  416.9 42.7 %collective-permute-start.31 = (bf16[2,2,1088,128]{3,2,1,0:T(8,128)(2,1)S(1)}, bf16[2,2,1088,128]{3,2,1,0:T(8,128)(2,1)S(1)}, u32[]{:S(2)}, u32[]{:S(2)}) collective-permute-start(bf16[2,2,1088,128]{3,2,1,0:T(8,128)(2,1)S(1)} %slice.635), channel_id=1, source_target_pairs={{0,2},{1,3},{2,0},{3,1},{4,6},{5,7},{6,4},{7,5},{8,10},{9,11},{10,... | collective-permute-start | bytes 3342344 | tf_op jit(solution)/shard_map/ppermute | solution.py:400
  417.8 40.5 %collective-permute-start.33 = (bf16[2,144,1088]{2,1,0:T(8,128)(2,1)}, bf16[2,144,1088]{2,1,0:T(8,128)(2,1)}, u32[]{:S(2)}, u32[]{:S(2)}) collective-permute-start(bf16[2,144,1088]{2,1,0:T(8,128)(2,1)} %fusion.25), channel_id=1, source_target_pairs={{0,2},{1,3},{2,0},{3,1},{4,6},{5,7},{6,4},{7,5},{8,10},{9,11},{10,... | collective-permute-start | bytes 1880072 | tf_op jit(solution)/shard_map/ppermute | solution.py:400
  419.9 38.4 %collective-permute-start.34 = (bf16[2,144,1088]{2,1,0:T(8,128)(2,1)}, bf16[2,144,1088]{2,1,0:T(8,128)(2,1)S(1)}, u32[]{:S(2)}, u32[]{:S(2)}) collective-permute-start(bf16[2,144,1088]{2,1,0:T(8,128)(2,1)} %select_bitcast_fusion.4), channel_id=1, source_target_pairs={{0,4},{4,0},{1,5},{5,1},{2,6},{6,2},{3,7},{7,3},{8,12},{12,8},{9,1... | collective-permute-start | bytes 1880072 | tf_op jit(solution)/shard_map/ppermute | solution.py:400
  463.0 152.4 %reduce-scatter.6.cloned.1.call-start = ((), (), s32[]{:S(2)}) async-start(), calls=%async_computation.4 | async-start | bytes 1658880 | tf_op jit(solution)/shard_map/reduce_scatter | solution.py:759
  477.7 47.8 %collective-permute-start.39 = (bf16[2,2,144,1088]{3,2,1,0:T(8,128)(2,1)}, bf16[2,2,144,1088]{3,2,1,0:T(8,128)(2,1)}, u32[]{:S(2)}, u32[]{:S(2)}) collective-permute-start(bf16[2,2,144,1088]{3,2,1,0:T(8,128)(2,1)} %get-tuple-element.130), channel_id=1, source_target_pairs={{0,4},{4,0},{1,5},{5,1},{2,6},{6,2},{3,7},{7,3},{8,12},{12,8},{9,1... | collective-permute-start | bytes 3760136 | tf_op jit(solution)/shard_map/ppermute | solution.py:400
  479.3 46.2 %collective-permute-start.40 = (bf16[2,2,144,1088]{3,2,1,0:T(8,128)(2,1)}, bf16[2,2,144,1088]{3,2,1,0:T(8,128)(2,1)}, u32[]{:S(2)}, u32[]{:S(2)}) collective-permute-start(bf16[2,2,144,1088]{3,2,1,0:T(8,128)(2,1)} %get-tuple-element.129), channel_id=1, source_target_pairs={{0,2},{1,3},{2,0},{3,1},{4,6},{5,7},{6,4},{7,5},{8,10},{9,11},{10,... | collective-permute-start | bytes 3760136 | tf_op jit(solution)/shard_map/ppermute | solution.py:400
  524.2 24.4 %collective-permute-start.36 = (bf16[4,4,144,1088]{3,2,1,0:T(8,128)(2,1)S(1)}, bf16[4,4,144,1088]{3,2,1,0:T(8,128)(2,1)S(1)}, u32[]{:S(2)}, u32[]{:S(2)}) collective-permute-start(bf16[4,4,144,1088]{3,2,1,0:T(8,128)(2,1)S(1)} %broadcast_select_fusion), channel_id=1, source_target_pairs={{0,1},{1,0},{2,3},{3,2},{4,5},{5,4},{6,7},{7,6},{8,9},{9,8},{10,11... | collective-permute-start | bytes 15040520 | tf_op jit(solution)/shard_map/ppermute | solution.py:400
  529.0 17.4 %collective-permute-start.41 = (bf16[2,144,1088]{2,1,0:T(8,128)(2,1)S(1)}, bf16[2,144,1088]{2,1,0:T(8,128)(2,1)S(1)}, u32[]{:S(2)}, u32[]{:S(2)}) collective-permute-start(bf16[2,144,1088]{2,1,0:T(8,128)(2,1)S(1)} %select_bitcast_fusion.3), channel_id=1, source_target_pairs={{0,2},{1,3},{2,0},{3,1},{4,6},{5,7},{6,4},{7,5},{8,10},{9,11},{10,... | collective-permute-start | bytes 1880072 | tf_op jit(solution)/shard_map/ppermute | solution.py:400
  530.4 17.1 %collective-permute-start.42 = (bf16[2,144,1088]{2,1,0:T(8,128)(2,1)S(1)}, bf16[2,144,1088]{2,1,0:T(8,128)(2,1)S(1)}, u32[]{:S(2)}, u32[]{:S(2)}) collective-permute-start(bf16[2,144,1088]{2,1,0:T(8,128)(2,1)S(1)} %select_bitcast_fusion.2), channel_id=1, source_target_pairs={{0,4},{4,0},{1,5},{5,1},{2,6},{6,2},{3,7},{7,3},{8,12},{12,8},{9,1... | collective-permute-start | bytes 1880072 | tf_op jit(solution)/shard_map/ppermute | solution.py:400
  553.0 30.5 %collective-permute-start.37 = (bf16[2,2,144,1088]{3,2,1,0:T(8,128)(2,1)S(1)}, bf16[2,2,144,1088]{3,2,1,0:T(8,128)(2,1)}, u32[]{:S(2)}, u32[]{:S(2)}) collective-permute-start(bf16[2,2,144,1088]{3,2,1,0:T(8,128)(2,1)S(1)} %get-tuple-element.128), channel_id=1, source_target_pairs={{0,4},{4,0},{1,5},{5,1},{2,6},{6,2},{3,7},{7,3},{8,12},{12,8},{9,1... | collective-permute-start | bytes 3760136 | tf_op jit(solution)/shard_map/ppermute | solution.py:400
  554.5 30.2 %collective-permute-start.38 = (bf16[2,2,144,1088]{3,2,1,0:T(8,128)(2,1)S(1)}, bf16[2,2,144,1088]{3,2,1,0:T(8,128)(2,1)}, u32[]{:S(2)}, u32[]{:S(2)}) collective-permute-start(bf16[2,2,144,1088]{3,2,1,0:T(8,128)(2,1)S(1)} %get-tuple-element.127), channel_id=1, source_target_pairs={{0,2},{1,3},{2,0},{3,1},{4,6},{5,7},{6,4},{7,5},{8,10},{9,11},{10,... | collective-permute-start | bytes 3760136 | tf_op jit(solution)/shard_map/ppermute | solution.py:400
  556.5 110.8 %reduce-scatter.8.cloned.1.call-start = ((), (), s32[]{:S(2)}) async-start(), calls=%async_computation.5 | async-start | bytes 1658880 | tf_op jit(solution)/shard_map/reduce_scatter | solution.py:759
  619.4 19.5 %collective-permute-start.51 = (bf16[4,16,1088]{2,1,0:T(8,128)(2,1)S(1)}, bf16[4,16,1088]{2,1,0:T(8,128)(2,1)S(1)}, u32[]{:S(2)}, u32[]{:S(2)}) collective-permute-start(bf16[4,16,1088]{2,1,0:T(8,128)(2,1)S(1)} %add_convert_fusion.11), channel_id=1, source_target_pairs={{0,4},{4,0},{1,5},{5,1},{2,6},{6,2},{3,7},{7,3},{8,12},{12,8},{9,1... | collective-permute-start | bytes 417800 | tf_op jit(solution)/shard_map/ppermute | solution.py:400
  637.6 27.6 %collective-permute-start.48 = (bf16[2,2,1088,128]{3,2,1,0:T(8,128)(2,1)S(1)}, bf16[2,2,1088,128]{3,2,1,0:T(8,128)(2,1)S(1)}, u32[]{:S(2)}, u32[]{:S(2)}) collective-permute-start(bf16[2,2,1088,128]{3,2,1,0:T(8,128)(2,1)S(1)} %slice.689), channel_id=1, source_target_pairs={{0,2},{1,3},{2,0},{3,1},{4,6},{5,7},{6,4},{7,5},{8,10},{9,11},{10,... | collective-permute-start | bytes 3342344 | tf_op jit(solution)/shard_map/ppermute | solution.py:400
  641.3 36.6 %collective-permute-start.58 = (bf16[2,1,144,1088]{3,2,1,0:T(8,128)(2,1)S(1)}, bf16[2,1,144,1088]{3,2,1,0:T(8,128)(2,1)}, u32[]{:S(2)}, u32[]{:S(2)}) collective-permute-start(bf16[2,1,144,1088]{3,2,1,0:T(8,128)(2,1)S(1)} %pad_maximum_fusion.18.refs_0_), channel_id=1, source_target_pairs={{0,2},{1,3},{2,0},{3,1},{4,6},{5,7},{6,4},{7,5},{8,10},{9,11},{10,... | collective-permute-start | bytes 1880072 | tf_op jit(solution)/shard_map/ppermute | solution.py:400
  642.3 35.6 %collective-permute-start.59 = (bf16[2,1,144,1088]{3,2,1,0:T(8,128)(2,1)S(1)}, bf16[2,1,144,1088]{3,2,1,0:T(8,128)(2,1)}, u32[]{:S(2)}, u32[]{:S(2)}) collective-permute-start(bf16[2,1,144,1088]{3,2,1,0:T(8,128)(2,1)S(1)} %pad_maximum_fusion.19.refs_1_), channel_id=1, source_target_pairs={{0,4},{4,0},{1,5},{5,1},{2,6},{6,2},{3,7},{7,3},{8,12},{12,8},{9,1... | collective-permute-start | bytes 1880072 | tf_op jit(solution)/shard_map/ppermute | solution.py:400
  646.0 32.4 %collective-permute-start.53 = (bf16[4,16,1088]{2,1,0:T(8,128)(2,1)}, bf16[4,16,1088]{2,1,0:T(8,128)(2,1)}, u32[]{:S(2)}, u32[]{:S(2)}) collective-permute-start(bf16[4,16,1088]{2,1,0:T(8,128)(2,1)} %add_convert_fusion.9), channel_id=1, source_target_pairs={{0,16},{8,24},{16,0},{24,8},{1,17},{9,25},{17,1},{25,9},{2,18},{10... | collective-permute-start | bytes 417800 | tf_op jit(solution)/shard_map/ppermute | solution.py:400
  667.3 24.5 %collective-permute-start.49 = (bf16[2,2,1088,128]{3,2,1,0:T(8,128)(2,1)}, bf16[2,2,1088,128]{3,2,1,0:T(8,128)(2,1)}, u32[]{:S(2)}, u32[]{:S(2)}) collective-permute-start(bf16[2,2,1088,128]{3,2,1,0:T(8,128)(2,1)} %pad_maximum_fusion.16), channel_id=1, source_target_pairs={{0,1},{1,0},{2,3},{3,2},{4,5},{5,4},{6,7},{7,6},{8,9},{9,8},{10,11... | collective-permute-start | bytes 3342344 | tf_op jit(solution)/shard_map/ppermute | solution.py:400
  681.6 17.0 %collective-permute-start.55 = (bf16[2,1,144,1088]{3,2,1,0:T(8,128)(2,1)S(1)}, bf16[2,1,144,1088]{3,2,1,0:T(8,128)(2,1)S(1)}, u32[]{:S(2)}, u32[]{:S(2)}) collective-permute-start(bf16[2,1,144,1088]{3,2,1,0:T(8,128)(2,1)S(1)} %pad_maximum_fusion.17.refs_0_), channel_id=1, source_target_pairs={{0,2},{1,3},{2,0},{3,1},{4,6},{5,7},{6,4},{7,5},{8,10},{9,11},{10,... | collective-permute-start | bytes 1880072 | tf_op jit(solution)/shard_map/ppermute | solution.py:400
  (89 other events, 918.2 us)
Sparse Core Ops, SparseCore 0:
  17.9 33.2 all-gather.6
  58.6 32.6 all-gather.8
  112.0 33.7 all-gather.10
  463.1 31.8 reduce-scatter.3
  556.6 32.1 reduce-scatter.5
  612.4 31.6 reduce-scatter.7

commit v8 on v7

--- a/solution.py
+++ b/solution.py
@@ -158,36 +158,38 @@
     return 2 if count % 2 == 0 else 1
 
 
-def attention_forward(joined, order, ties=()):
+def attention_forward(joined, order, first, last, into=(), ties=()):
     _, count, seqs, local, width = joined.shape
     length = count * local
     pairs = pl.cdiv(width, LANES)
     spec = lambda which: pl.BlockSpec(
-        (1, count, 1, local, LANES), lambda s, h, order: (which, 0, s, 0, h)
-    )
+        (1, count, 1, local, LANES), lambda s, h, order: (which, 0, s + first, 0, h)
+    )
+    extra = list(into) + list(ties)
     return pl.pallas_call(
         functools.partial(attention_forward_kernel, query_blocks(count), width),
         grid_spec=pltpu.PrefetchScalarGridSpec(
             num_scalar_prefetch=1,
-            grid=(seqs, pairs),
+            grid=(last - first, pairs),
             in_specs=[spec(0), spec(1), spec(2)]
-            + [pl.BlockSpec(memory_space=pl.ANY)] * len(ties),
+            + [pl.BlockSpec(memory_space=pl.ANY)] * len(extra),
             out_specs=[
-                pl.BlockSpec((count, 1, local, LANES), lambda s, h, order: (0, s, 0, h)),
-                pl.BlockSpec((1, 1, 8, length), lambda s, h, order: (s, h, 0, 0)),
+                pl.BlockSpec((count, 1, local, LANES), lambda s, h, order: (0, s + first, 0, h)),
+                pl.BlockSpec((1, 1, 8, length), lambda s, h, order: (s + first, h, 0, 0)),
             ],
         ),
         out_shape=[
             jax.ShapeDtypeStruct((count, seqs, local, width), BF16),
             jax.ShapeDtypeStruct((seqs, pairs, 8, length), F32),
         ],
+        input_output_aliases={4 + i: i for i in range(len(into))},
         compiler_params=pltpu.CompilerParams(vmem_limit_bytes=VMEM_LIMIT),
         cost_estimate=pl.CostEstimate(
-            flops=seqs * pairs * 16 * length * length * LANES // COST_SCALE,
-            bytes_accessed=8 * seqs * length * width // COST_SCALE,
+            flops=(last - first) * pairs * 16 * length * length * LANES // COST_SCALE,
+            bytes_accessed=8 * (last - first) * length * width // COST_SCALE,
             transcendentals=0,
         ),
-    )(order, joined, joined, joined, *ties)
+    )(order, joined, joined, joined, *extra)
 
 
 def attention_backward(joined, mixed, grad_mixed, lse, order, ties=()):
@@ -418,14 +420,15 @@
     return jnp.where(bit == 0, on_zero, on_one)
 
 
-def to_sequences(values, count, start=(), finish=()):
+def to_sequences(values, count, start=(), then=(), finish=()):
     seqs, local, width = values.shape
     own = lax.axis_index("ctx")
     parts = values.swapaxes(1, 2).reshape(count, seqs // count, width, local)
     mine = [lax.dynamic_index_in_dim(parts, own ^ i, keepdims=False) for i in range(count)]
     far = row_major(held(jnp.stack(mine[2:]), *start))
     far = row_major(swap(far, "ctx", 2))
-    near = row_major(swap(row_major(jnp.stack([mine[1], far[1]])), "ctx", 1))
+    near = row_major(held(jnp.stack([mine[1], far[1]]), *then))
+    near = row_major(swap(near, "ctx", 1))
     whole = row_major(jnp.stack([mine[0], near[0], far[0], near[1]]))
     return row_major(held(whole, *finish).swapaxes(2, 3))
 
@@ -503,7 +506,7 @@
     )(here, *own, *other)
 
 
-def spread_chips(mine):
+def spread_chips(mine, hold=()):
     shards = mine.shape[0]
     if shards == 1:
         first = jnp.stack([mine, swap(mine, "replica", 1)])
@@ -511,8 +514,8 @@
     split = shards // 2
     low, high = mine[:split], mine[split:]
     low_there, high_there = after(swap(low, "replica", 1), swap(high, "ctx", 2))
-    first = jnp.stack([low, low_there])
-    second = jnp.stack([high, high_there])
+    first = held(jnp.stack([low, low_there]), *hold)
+    second = held(jnp.stack([high, high_there]), *hold)
     third, fourth = after(swap(first, "ctx", 2), swap(second, "replica", 1))
     return [first, second, third, fourth]
 
@@ -725,14 +728,16 @@
         qkv_kernel, [low_inputs], [(w_a, 0, 3), small], [((3,), BF16), ((), BF16)], ties=steps
     )
     joined = joined.reshape((3,) + blocked)
+    middle_seq = share // 2
+    begun = attention_forward(joined, order, 0, middle_seq)
     if pairwise:
         other_b = spread_cores(own_b)
         full_b = place(win, own_b, other_b, owned_rows, shards)
-        own_c = spread_chips(held(part_c, own_b[2], joined))
+        own_c = spread_chips(held(part_c, own_b[2], joined), hold=[begun[0]])
         steps = [corner(own_c[0][1]), corner(own_c[1][1]), corner(own_c[2]), corner(own_c[3])]
     else:
         steps = [corner(joined[0, 0])] * 4
-    mixed, lse = attention_forward(joined, order, ties=steps[:2])
+    mixed, lse = attention_forward(joined, order, middle_seq, share, begun, steps[:2])
     attended = mixed.reshape(rows, width)
     middle, low_two = by_rows(
         attended_kernel,
@@ -751,8 +756,8 @@
     if pairwise:
         full_c = place(win, own_c, spread_cores(own_c), owned_rows, shards, transposed=True)
     w_proj = full_c.reshape(wide, width, width)
-    start, finish = ((own_c[2], mixed), (full_c,)) if pairwise else ((), ())
-    low_grad_out = to_sequences(cotangent, count, start, finish).reshape(rows, width)
+    holds = ((own_c[2], low_two), (low_act,), (full_c,)) if pairwise else ((), (), ())
+    low_grad_out = to_sequences(cotangent, count, *holds).reshape(rows, width)
 
     def finish_units(groups, forms, *earlier):
         sums = [
@@ -760,7 +765,7 @@
             for group in groups
         ]
         own = spread_chips(held(jnp.stack(sums), *earlier))
-        return own, place_grads(win, own, spread_cores(own), owned_rows, forms)
+        return place_grads(win, own, spread_cores(own), owned_rows, forms)
 
     def reduce_whole(grads, transposed=False):
         if transposed:
@@ -829,7 +834,7 @@
         [(w_a, 0, 3), small],
         [((), BF16)],
         sums=8,
-        ties=[corner(grad_qkv), *mark, *fc_marks[2]],
+        ties=[*mark, *fc_marks[2]],
     )
     if pairwise:
         partial_a, _, _ = reduce_second(win, halves, grad_inputs)
@@ -852,11 +857,11 @@
     if pairwise:
         vector_grads = held(vector_grads, partial_a)
         vector_grads = add_pair(vector_grads, swap(vector_grads, "ctx", 2))
-        _, (qkv_grad, out_grad) = finish_units([partial_a], ((3, 1),))
-        own, (proj_grad, fc_grad) = finish_units(
+        qkv_grad, out_grad = finish_units([partial_a], ((3, 1),))
+        proj_grad, fc_grad = finish_units(
             [partial_proj, partial_fc], ((0,), (wide,)), vector_grads
         )
-        input_grad, _ = to_blocks(blocked_grads, F32, own[0][1], own[1][1])
+        input_grad, _ = to_blocks(blocked_grads, F32, vector_grads)
         owned_vectors = lax.dynamic_index_in_dim(
             reduce_vectors(vector_grads), lax.axis_index("shard"), keepdims=False
         )

time: 720 us -> 721 us (level)
  waiting for transfers between devices: 186 us -> 166 us
  other arithmetic: 81.7 us -> 90.4 us
  local copies, waits for them, and re-layouts: 81.5 us -> 89.5 us
    ppermute x64, waiting for transfers between devices: 163 us -> 145 us  [swap(): lax.ppermute(values, axis, [(index, index ^ offset) for index in range(co...]
    pallas_call x1 -> x2, Pallas kernels: 31.2 us -> 33.3 us  [attention_forward(): pl.pallas_call(functools.partial(attention_forward_kernel, query_blocks(c...]
  transfers between devices with their start and end apart: 70 -> 70, of which waited for: 27 -> 25; matrix products, arithmetic and copies ran while one was open for 21% -> 22% of each run, Pallas kernels for 33% -> 33%
where the time goes in v8:
time: 721 us; the launch traced here: 714 us
  Pallas kernels  241 us (33%)
  waiting for transfers between devices  166 us (23%)
  other arithmetic  90.4 us (13%)
  local copies, waits for them, and re-layouts  89.5 us (12%)
  starting transfers between devices  50.5 us (7%)
  matrix products  46.2 us (6%)
  between operations  31.2 us (4%)
    ppermute x64, waiting for transfers between devices, swap(): lax.ppermute(values, axis, [(index, index ^ offset) for index in range(co...  145 us
    pallas_call x7, Pallas kernels, by_rows(): pl.pallas_call(kernel, grid=(rows // tile,), in_specs=in_specs, out_specs...  140 us
    ppermute x64, starting transfers between devices, swap(): lax.ppermute(values, axis, [(index, index ^ offset) for index in range(co...  50.1 us
    pallas_call x2, Pallas kernels, attention_forward(): pl.pallas_call(functools.partial(attention_forward_kernel, query_blocks(c...  33.3 us
    convert_element_type x16, other arithmetic, add_pair(): return (kept.astype(F32) + received.astype(F32)).astype(BF16)  32.3 us
    pallas_call x1, Pallas kernels, attention_backward(): pl.pallas_call(functools.partial(attention_backward_kernel, query_blocks(...  28.8 us
    pallas_call x3, Pallas kernels, assemble(): pl.pallas_call(functools.partial(assemble_kernel, groups, win.start, win....  25.8 us
    select_n x17, other arithmetic, pick(): return jnp.where(bit == 0, on_zero, on_one)  21 us
  transfers between devices with their start and end apart: 70, of which 25 were waited for; matrix products, arithmetic and copies ran while one was open for 22% of the time, Pallas kernels for 33%

profile of v8, /device:TPU:0, one launch (start us, length us, event | category | flops | bytes accessed | tf_op | source)
XLA Modules:
  0.0 714.4 jit_solution(1987026560304585634)
XLA Ops:
  7.2 3.8 constant_dynamic-slice_fusion.3
  12.1 3.0 collective-permute-start
  18.1 21.7 %collective-permute-done = bf16[2,2,1088,128]{3,2,1,0:T(8,128)(2,1)S(1)} collective-permute-done((bf16[2,2,1088,128]{3,2,1,0:T(8,128)(2,1)}, bf16[2,2,1088,128]{3,2,1,0:T(8,128)(2,1)S(1)}, u32[]{:S(2)}, u32[]{:S(2)}) %collective-permute-start) | collective-permute-done | bytes 1114144 | tf_op jit(solution)/shard_map/ppermute | solution.py:402
  42.8 8.4 %all-gather.7.cloned.1.call-done = bf16[576,1088]{1,0:T(8,128)(2,1)} async-done(((bf16[144,1088]{1,0:T(8,128)(2,1)}), bf16[576,1088]{1,0:T(8,128)(2,1)}) %all-gather.7.cloned.1.call-update) | async-done | bytes 1253392 | tf_op jit(solution)/shard_map/all_gather | solution.py:691
  59.6 13.2 %collective-permute-done.2 = bf16[2,144,1088]{2,1,0:T(8,128)(2,1)S(1)} collective-permute-done((bf16[2,144,1088]{2,1,0:T(8,128)(2,1)}, bf16[2,144,1088]{2,1,0:T(8,128)(2,1)S(1)}, u32[]{:S(2)}, u32[]{:S(2)}) %collective-permute-start.2) | collective-permute-done | bytes 626720 | tf_op jit(solution)/shard_map/ppermute | solution.py:402
  80.1 12.2 %all-gather.9.cloned.1.call-done = bf16[640,1088]{1,0:T(8,128)(2,1)} async-done(((bf16[160,1088]{1,0:T(8,128)(2,1)}), bf16[640,1088]{1,0:T(8,128)(2,1)}) %all-gather.9.cloned.1.call-update) | async-done | bytes 1392656 | tf_op jit(solution)/shard_map/all_gather | solution.py:691
  92.4 12.2 %collective-permute-done.4.refs_2_ = bf16[2,2,144,1088]{3,2,1,0:T(8,128)(2,1)} collective-permute-done((bf16[2,2,144,1088]{3,2,1,0:T(8,128)(2,1)S(1)}, bf16[2,2,144,1088]{3,2,1,0:T(8,128)(2,1)}, u32[]{:S(2)}, u32[]{:S(2)}) %collective-permute-start.4) | collective-permute-done | bytes 1253408 | tf_op jit(solution)/shard_map/ppermute | solution.py:402
  116.5 9.9 %collective-permute-done.10 = bf16[2,144,1088]{2,1,0:T(8,128)(2,1)} collective-permute-done((bf16[2,144,1088]{2,1,0:T(8,128)(2,1)}, bf16[2,144,1088]{2,1,0:T(8,128)(2,1)}, u32[]{:S(2)}, u32[]{:S(2)}) %collective-permute-start.10) | collective-permute-done | bytes 626720 | tf_op jit(solution)/shard_map/ppermute | solution.py:402
  139.4 8.6 %shard_map.271 = bf16[4,4,272,1088]{3,2,1,0:T(8,128)(2,1)} custom-call(s32[3]{0:T(128)} %pad_add_fusion.here_ref, bf16[2,2,144,1088]{3,2,1,0:T(8,128)(2,1)} %copy-done.15, bf16[2,2,144,1088]{3,2,1,0:T(8,128)(2,1)} %copy-done.16, bf16[2,2,144,1088]{3,2,1,0:T(8,128)(2,1)} %collective-permute-done.4.refs_2_, ...), custom_call_target="tpu_custom_call" | custom-call | bytes 18939904 | tf_op jit(solution)/shard_map/pallas_call | solution.py:496
  148.0 16.7 %shard_map.272 = (bf16[3,1024,1088]{2,1,0:T(8,128)(2,1)}, bf16[1024,1088]{1,0:T(8,128)(2,1)}) custom-call(bf16[1024,1088]{1,0:T(8,128)(2,1)} %bitcast.221, bf16[4,1088,1088]{2,1,0:T(8,128)(2,1)} %bitcast.204, f32[8,1088]{1,0:T(8,128)} %reshape.185.small_ref, bf16[16,128]{1,0:T(8,128)(2,1)} %slice.608.refs_0_, bf16[16,128]{1,0:T(8,128)(2,1)} %slice.609.refs_1_), custom_call_target="tpu_custom_call" | custom-call | flops 1363673088 | bytes 2581760 | tf_op jit(solution)/shard_map/pallas_call | solution.py:381
  174.4 16.6 %shard_map.273 = (bf16[4,2,128,1088]{3,2,1,0:T(8,128)(2,1)}, f32[2,9,8,512]{3,2,1,0:T(8,128)}) custom-call(s32[4]{0:T(128)} %broadcast_xor_fusion.order_ref, bf16[3,4,2,128,1088]{4,3,2,1,0:T(8,128)(2,1)} %bitcast.195, bf16[3,4,2,128,1088]{4,3,2,1,0:T(8,128)(2,1)} %bitcast.196, bf16[3,4,2,128,1088]{4,3,2,1,0:T(8,128)(2,1)} %bitcast.197), custom_call_target="tpu_custom_call" | custom-call | flops 603979776 | bytes 557056 | tf_op jit(solution)/shard_map/pallas_call | solution.py:169
  198.4 16.7 %shard_map.274 = (bf16[4,2,128,1088]{3,2,1,0:T(8,128)(2,1)}, f32[2,9,8,512]{3,2,1,0:T(8,128)}) custom-call(s32[4]{0:T(128)} %broadcast_xor_fusion.order_ref, bf16[3,4,2,128,1088]{4,3,2,1,0:T(8,128)(2,1)} %bitcast.198, bf16[3,4,2,128,1088]{4,3,2,1,0:T(8,128)(2,1)} %bitcast.199, ...), custom_call_target="tpu_custom_call", output_to_operand_aliasing={{0}: (4, {}), {1}: (5, {})} | custom-call | flops 603979776 | bytes 557056 | tf_op jit(solution)/shard_map/pallas_call | solution.py:169
  215.0 8.5 %shard_map.275 = (f32[1024,1088]{1,0:T(8,128)}, bf16[1024,1088]{1,0:T(8,128)(2,1)}) custom-call(bf16[1024,1088]{1,0:T(8,128)(2,1)} %bitcast.222, bf16[1024,1088]{1,0:T(8,128)(2,1)} %bitcast.230, bf16[4,1088,1088]{2,1,0:T(8,128)(2,1)} %bitcast.205, f32[8,1088]{1,0:T(8,128)} %reshape.185.small_ref), custom_call_target="tpu_custom_call" | custom-call | flops 454557696 | bytes 2580736 | tf_op jit(solution)/shard_map/pallas_call | solution.py:381
  227.7 8.6 %shard_map.276 = bf16[4,4,272,1088]{3,2,1,0:T(8,128)(2,1)} custom-call(s32[3]{0:T(128)} %pad_add_fusion.here_ref, bf16[2,2,144,1088]{3,2,1,0:T(8,128)(2,1)} %pad_maximum_fusion.5.refs_0_, bf16[2,2,144,1088]{3,2,1,0:T(8,128)(2,1)} %pad_maximum_fusion.6.refs_1_, bf16[2,2,144,1088]{3,2,1,0:T(8,128)(2,1)} %collective-permute-done.12.refs_2_, ...), custom_call_target="tpu_custom_call" | custom-call | bytes 18939904 | tf_op jit(solution)/shard_map/pallas_call | solution.py:496
  244.4 27.9 %shard_map.277 = (bf16[4,1024,1088]{2,1,0:T(8,128)(2,1)}, bf16[4,1024,1088]{2,1,0:T(8,128)(2,1)}) custom-call(bf16[1024,1088]{1,0:T(8,128)(2,1)} %get-tuple-element.90.low_ref, bf16[4,1088,1088]{2,1,0:T(8,128)(2,1)} %bitcast.208, f32[4,1,1088]{2,1,0:T(1,128)} %reshape.189.bias_ref, bf16[16,128]{1,0:T(8,128)(2,1)} %slice.618.refs_0_, ...), custom_call_target="tpu_custom_call" | custom-call | flops 1818230784 | bytes 3693696 | tf_op jit(solution)/shard_map/pallas_call | solution.py:381
  278.8 8.6 %shard_map.278 = bf16[4,4,272,1088]{3,2,1,0:T(8,128)(2,1)} custom-call(s32[3]{0:T(128)} %pad_add_fusion.here_ref, bf16[2,2,144,1088]{3,2,1,0:T(8,128)(2,1)} %copy-done.13, bf16[2,2,144,1088]{3,2,1,0:T(8,128)(2,1)} %copy-done.14, bf16[2,2,144,1088]{3,2,1,0:T(8,128)(2,1)} %collective-permute-done.20.refs_2_, bf16[2,2,144,1088]{3,2,1,0:T(8,128)(2,1)} %copy-done.31, ...), custom_call_target="tpu_custom_call" | custom-call | bytes 18939904 | tf_op jit(solution)/shard_map/pallas_call | solution.py:496
  296.1 15.2 %convolution_convert_fusion.1 = bf16[4,1088,1088]{2,1,0:T(8,128)(2,1)S(1)} fusion(bf16[4,1024,1088]{2,1,0:T(8,128)(2,1)} %get-tuple-element.94.act_ref, bf16[1024,1088,1]{1,0,2:T(8,128)(2,1)S(1)} %bitcast.232), kind=kOutput, calls=%fused_computation.1 | convolution fusion | flops 9701965824 | bytes 20611072 | tf_op jit(solution)/shard_map/ctx,td->cxd/dot_general | solution.py:786
  311.3 3.3 broadcast_select_fusion.2
  319.2 19.8 %shard_map.279 = bf16[1024,1088]{1,0:T(8,128)(2,1)} custom-call(f32[1024,1088]{1,0:T(8,128)} %get-tuple-element.96.middle_ref, bf16[4,1024,1088]{2,1,0:T(8,128)(2,1)} %get-tuple-element.94.act_ref, bf16[4,1088,1088]{2,1,0:T(8,128)(2,1)} %bitcast.210, f32[8,1088]{1,0:T(8,128)} %reshape.185.small_ref, bf16[16,128]{1,0:T(8,128)(2,1)} %slice.634.refs_0_), custom_call_target="tpu_custom_call" | custom-call | flops 1818230784 | bytes 3138304 | tf_op jit(solution)/shard_map/pallas_call | solution.py:381
  340.3 6.6 add_convert_fusion.2
  354.8 21.1 %shard_map.280 = (bf16[4,1024,1088]{2,1,0:T(8,128)(2,1)}, f32[8,1088]{1,0:T(8,128)}) custom-call(bf16[1024,1088]{1,0:T(8,128)(2,1)} %bitcast.233, bf16[4,1024,1088]{2,1,0:T(8,128)(2,1)} %get-tuple-element.97.slope_ref, bf16[4,1088,1088]{2,1,0:T(8,128)(2,1)} %bitcast.211, bf16[16,128]{1,0:T(8,128)(2,1)} %slice.642.refs_0_, bf16[16,128]{1,0:T(8,128)(2,1)} %slice.644.refs_1_, ...), custom_call_target="tpu_custom_call" | custom-call | flops 1818230784 | bytes 3696384 | tf_op jit(solution)/shard_map/pallas_call | solution.py:381
  375.9 13.2 %convolution_convert_fusion = bf16[4,1088,1088]{1,2,0:T(8,128)(2,1)S(1)} fusion(bf16[4,1024,1088]{2,1,0:T(8,128)(2,1)} %get-tuple-element.98.hidden_ref, bf16[1024,1088]{1,0:T(8,128)(2,1)S(1)} %copy-done.25), kind=kOutput, calls=%fused_computation | convolution fusion | flops 9701965824 | bytes 20611072 | tf_op jit(solution)/shard_map/td,ctx->cdx/dot_general | solution.py:804
  390.1 3.3 broadcast_select_fusion.1
  395.3 4.3 add_convert_fusion.7
  403.7 4.2 copy.68
  413.6 27.2 %shard_map.281 = (f32[1024,1088]{1,0:T(8,128)}, bf16[1024,1088]{1,0:T(8,128)(2,1)}, bf16[1024,1088]{1,0:T(8,128)(2,1)}, f32[8,1088]{1,0:T(8,128)}) custom-call(bf16[4,1024,1088]{2,1,0:T(8,128)(2,1)} %get-tuple-element.98.hidden_ref, bf16[1024,1088]{1,0:T(8,128)(2,1)} %bitcast.234, f32[1024,1088]{1,0:T(8,128)} %get-tuple-element.96.middle_ref, ...), custom_call_target="tpu_custom_call" | custom-call | flops 2272788480 | bytes 5441024 | tf_op jit(solution)/shard_map/pallas_call | solution.py:381
  440.9 4.9 convolution_convert_fusion.3
  455.4 4.4 add_convert_fusion.1
  467.4 28.8 %shard_map.282 = bf16[3,4,2,128,1088]{4,3,2,1,0:T(8,128)(2,1)} custom-call(s32[4]{0:T(128)} %broadcast_xor_fusion.order_ref, bf16[3,4,2,128,1088]{4,3,2,1,0:T(8,128)(2,1)} %bitcast.201, bf16[3,4,2,128,1088]{4,3,2,1,0:T(8,128)(2,1)} %bitcast.202, bf16[3,4,2,128,1088]{4,3,2,1,0:T(8,128)(2,1)} %bitcast.203, bf16[4,2,128,1088]{3,2,1,0:T(8,128)(2,1)} %get-tuple-element.89.o_ref, ...), custom_call_target="tpu_custom_call" | custom-call | flops 1509949440 | bytes 2228224 | tf_op jit(solution)/shard_map/pallas_call | solution.py:203
  496.2 12.9 %convolution_convert_fusion.2 = bf16[3,1088,1088]{1,2,0:T(8,128)(2,1)S(1)} fusion(bf16[3,1024,1088]{2,1,0:T(8,128)(2,1)} %bitcast.228, bf16[1024,1088]{1,0:T(8,128)(2,1)S(1)} %copy-done.58), kind=kOutput, calls=%fused_computation.2 | convolution fusion | flops 7276474368 | bytes 16015360 | tf_op jit(solution)/shard_map/td,ctx->cdx/dot_general | solution.py:825
  509.2 4.4 broadcast_select_fusion
  516.9 4.4 add_convert_fusion.4
  526.2 12.6 %collective-permute-done.41 = bf16[2,144,1088]{2,1,0:T(8,128)(2,1)S(1)} collective-permute-done((bf16[2,144,1088]{2,1,0:T(8,128)(2,1)S(1)}, bf16[2,144,1088]{2,1,0:T(8,128)(2,1)S(1)}, u32[]{:S(2)}, u32[]{:S(2)}) %collective-permute-start.41) | collective-permute-done | bytes 626720 | tf_op jit(solution)/shard_map/ppermute | solution.py:402
  541.2 4.4 add_convert_fusion
  552.7 18.6 %shard_map.283 = (bf16[1024,1088]{1,0:T(8,128)(2,1)}, f32[8,1088]{1,0:T(8,128)}) custom-call(bf16[3,1024,1088]{2,1,0:T(8,128)(2,1)} %bitcast.229, f32[1024,1088]{1,0:T(8,128)} %get-tuple-element.106.grad_middle_ref, bf16[1024,1088]{1,0:T(8,128)(2,1)} %bitcast.223, bf16[4,1088,1088]{2,1,0:T(8,128)(2,1)} %bitcast.207, f32[8,1088]{1,0:T(8,128)} %reshape.185.small_ref, ...), custom_call_target="tpu_custom_call" | custom-call | flops 1363673088 | bytes 3143680 | tf_op jit(solution)/shard_map/pallas_call | solution.py:381
  573.8 4.7 collective-permute-done.37
  579.8 2.7 add_convert_fusion.3
  585.9 12.9 %collective-permute-done.43 = bf16[2,144,1088]{2,1,0:T(8,128)(2,1)} collective-permute-done((bf16[2,144,1088]{2,1,0:T(8,128)(2,1)}, bf16[2,144,1088]{2,1,0:T(8,128)(2,1)}, u32[]{:S(2)}, u32[]{:S(2)}) %collective-permute-start.43) | collective-permute-done | bytes 626720 | tf_op jit(solution)/shard_map/ppermute | solution.py:402
  623.7 3.7 collective-permute-done.49
  629.7 4.1 collective-permute-done.56
  633.8 18.7 %collective-permute-done.57 = bf16[1,144,1088]{2,1,0:T(8,128)(2,1)S(1)} collective-permute-done((bf16[1,144,1088]{2,1,0:T(8,128)(2,1)S(1)}, bf16[1,144,1088]{2,1,0:T(8,128)(2,1)S(1)}, u32[]{:S(2)}, u32[]{:S(2)}) %collective-permute-start.57) | collective-permute-done | bytes 313376 | tf_op jit(solution)/shard_map/ppermute | solution.py:402
  655.4 3.4 collective-permute-start.51
  664.9 4.4 collective-permute-done.58.refs_2_
  669.3 2.7 collective-permute-done.59.refs_3_
  672.5 5.0 collective-permute-done.52
  681.7 8.2 %shard_map.285 = (f32[1088,1088]{1,0:T(8,128)}, f32[272,4352]{1,0:T(8,128)}) custom-call(s32[3]{0:T(128)} %pad_add_fusion.here_ref, bf16[2,1,144,1088]{3,2,1,0:T(8,128)(2,1)} %copy-done.22, bf16[2,1,144,1088]{3,2,1,0:T(8,128)(2,1)} %copy-done.23, bf16[2,1,144,1088]{3,2,1,0:T(8,128)(2,1)} %collective-permute-done.58.refs_2_, ...), custom_call_target="tpu_custom_call" | custom-call | bytes 2367488 | tf_op jit(solution)/shard_map/pallas_call | solution.py:584
  691.3 6.3 collective-permute-done.53.refs_1_
  702.4 4.9 shard_map.284
  (418 shorter events, 191.1 us)
Async XLA Ops:
  7.2 44.0 %all-gather.7.cloned.1.call-start = ((), (), s32[]{:S(2)}) async-start(), calls=%async_computation.6 | async-start | bytes 1658880 | tf_op jit(solution)/shard_map/all_gather | solution.py:691
  12.1 27.7 %collective-permute-start = (bf16[2,2,1088,128]{3,2,1,0:T(8,128)(2,1)}, bf16[2,2,1088,128]{3,2,1,0:T(8,128)(2,1)S(1)}, u32[]{:S(2)}, u32[]{:S(2)}) collective-permute-start(bf16[2,2,1088,128]{3,2,1,0:T(8,128)(2,1)} %pad_maximum_fusion.10), channel_id=1, source_target_pairs={{0,2},{1,3},{2,0},{3,1},{4,6},{5,7},{6,4},{7,5},{8,10},{9,11},{10,... | collective-permute-start | bytes 3342344 | tf_op jit(solution)/shard_map/ppermute | solution.py:402
  17.8 74.6 %all-gather.9.cloned.1.call-start = ((), (), s32[]{:S(2)}) async-start(), calls=%async_computation.7 | async-start | bytes 1843200 | tf_op jit(solution)/shard_map/all_gather | solution.py:691
  59.6 110.2 %all-gather.11.cloned.1.call-start = ((), (), s32[]{:S(2)}) async-start(), calls=%async_computation.8 | async-start | bytes 1658880 | tf_op jit(solution)/shard_map/all_gather | solution.py:691
  75.3 29.3 %collective-permute-start.4 = (bf16[2,2,144,1088]{3,2,1,0:T(8,128)(2,1)S(1)}, bf16[2,2,144,1088]{3,2,1,0:T(8,128)(2,1)}, u32[]{:S(2)}, u32[]{:S(2)}) collective-permute-start(bf16[2,2,144,1088]{3,2,1,0:T(8,128)(2,1)S(1)} %pad_maximum_fusion.3.refs_0_), channel_id=1, source_target_pairs={{0,2},{1,3},{2,0},{3,1},{4,6},{5,7},{6,4},{7,5},{8,10},{9,11},{10,... | collective-permute-start | bytes 3760136 | tf_op jit(solution)/shard_map/ppermute | solution.py:402
  78.1 29.0 %collective-permute-start.5 = (bf16[2,2,144,1088]{3,2,1,0:T(8,128)(2,1)S(1)}, bf16[2,2,144,1088]{3,2,1,0:T(8,128)(2,1)}, u32[]{:S(2)}, u32[]{:S(2)}) collective-permute-start(bf16[2,2,144,1088]{3,2,1,0:T(8,128)(2,1)S(1)} %pad_maximum_fusion.4.refs_1_), channel_id=1, source_target_pairs={{0,4},{4,0},{1,5},{5,1},{2,6},{6,2},{3,7},{7,3},{8,12},{12,8},{9,1... | collective-permute-start | bytes 3760136 | tf_op jit(solution)/shard_map/ppermute | solution.py:402
  80.1 53.7 %collective-permute-start.6 = (bf16[2,2,144,1088]{3,2,1,0:T(8,128)(2,1)S(1)}, bf16[2,2,144,1088]{3,2,1,0:T(8,128)(2,1)}, u32[]{:S(2)}, u32[]{:S(2)}) collective-permute-start(bf16[2,2,144,1088]{3,2,1,0:T(8,128)(2,1)S(1)} %pad_maximum_fusion.3.refs_0_), channel_id=1, source_target_pairs={{0,1},{1,0},{2,3},{3,2},{4,5},{5,4},{6,7},{7,6},{8,9},{9,8},{10,11... | collective-permute-start | bytes 3760136 | tf_op jit(solution)/shard_map/ppermute | solution.py:402
  115.6 23.7 %collective-permute-start.7 = (bf16[2,2,144,1088]{3,2,1,0:T(8,128)(2,1)S(1)}, bf16[2,2,144,1088]{3,2,1,0:T(8,128)(2,1)}, u32[]{:S(2)}, u32[]{:S(2)}) collective-permute-start(bf16[2,2,144,1088]{3,2,1,0:T(8,128)(2,1)S(1)} %pad_maximum_fusion.4.refs_1_), channel_id=1, source_target_pairs={{0,1},{1,0},{2,3},{3,2},{4,5},{5,4},{6,7},{7,6},{8,9},{9,8},{10,11... | collective-permute-start | bytes 3760136 | tf_op jit(solution)/shard_map/ppermute | solution.py:402
  115.7 503.7 %reduce-scatter.6.cloned.1.call-start = ((), (), s32[]{:S(2)}) async-start(), calls=%async_computation.4 | async-start | bytes 1658880 | tf_op jit(solution)/shard_map/reduce_scatter | solution.py:764
  115.9 23.4 %collective-permute-start.8 = (bf16[2,2,144,1088]{3,2,1,0:T(8,128)(2,1)}, bf16[2,2,144,1088]{3,2,1,0:T(8,128)(2,1)}, u32[]{:S(2)}, u32[]{:S(2)}) collective-permute-start(bf16[2,2,144,1088]{3,2,1,0:T(8,128)(2,1)} %collective-permute-done.4.refs_2_), channel_id=1, source_target_pairs={{0,1},{1,0},{2,3},{3,2},{4,5},{5,4},{6,7},{7,6},{8,9},{9,8},{10,11... | collective-permute-start | bytes 3760136 | tf_op jit(solution)/shard_map/ppermute | solution.py:402
  130.3 36.9 %collective-permute-start.12 = (bf16[2,2,144,1088]{3,2,1,0:T(8,128)(2,1)}, bf16[2,2,144,1088]{3,2,1,0:T(8,128)(2,1)}, u32[]{:S(2)}, u32[]{:S(2)}) collective-permute-start(bf16[2,2,144,1088]{3,2,1,0:T(8,128)(2,1)} %pad_maximum_fusion.5.refs_0_), channel_id=1, source_target_pairs={{0,2},{1,3},{2,0},{3,1},{4,6},{5,7},{6,4},{7,5},{8,10},{9,11},{10,... | collective-permute-start | bytes 3760136 | tf_op jit(solution)/shard_map/ppermute | solution.py:402
  133.9 33.3 %collective-permute-start.13 = (bf16[2,2,144,1088]{3,2,1,0:T(8,128)(2,1)}, bf16[2,2,144,1088]{3,2,1,0:T(8,128)(2,1)}, u32[]{:S(2)}, u32[]{:S(2)}) collective-permute-start(bf16[2,2,144,1088]{3,2,1,0:T(8,128)(2,1)} %pad_maximum_fusion.6.refs_1_), channel_id=1, source_target_pairs={{0,4},{4,0},{1,5},{5,1},{2,6},{6,2},{3,7},{7,3},{8,12},{12,8},{9,1... | collective-permute-start | bytes 3760136 | tf_op jit(solution)/shard_map/ppermute | solution.py:402
  139.3 56.6 %collective-permute-start.16 = (bf16[2,2,144,1088]{3,2,1,0:T(8,128)(2,1)}, bf16[2,2,144,1088]{3,2,1,0:T(8,128)(2,1)}, u32[]{:S(2)}, u32[]{:S(2)}) collective-permute-start(bf16[2,2,144,1088]{3,2,1,0:T(8,128)(2,1)} %pad_maximum_fusion.5.refs_0_), channel_id=1, source_target_pairs={{0,1},{1,0},{2,3},{3,2},{4,5},{5,4},{6,7},{7,6},{8,9},{9,8},{10,11... | collective-permute-start | bytes 3760136 | tf_op jit(solution)/shard_map/ppermute | solution.py:402
  171.3 22.8 %collective-permute-start.14 = (bf16[2,144,1088]{2,1,0:T(8,128)(2,1)S(1)}, bf16[2,144,1088]{2,1,0:T(8,128)(2,1)S(1)}, u32[]{:S(2)}, u32[]{:S(2)}) collective-permute-start(bf16[2,144,1088]{2,1,0:T(8,128)(2,1)S(1)} %bitcast.247), channel_id=1, source_target_pairs={{0,4},{4,0},{1,5},{5,1},{2,6},{6,2},{3,7},{7,3},{8,12},{12,8},{9,1... | collective-permute-start | bytes 1880072 | tf_op jit(solution)/shard_map/ppermute | solution.py:402
  173.0 21.2 %collective-permute-start.15 = (bf16[2,144,1088]{2,1,0:T(8,128)(2,1)S(1)}, bf16[2,144,1088]{2,1,0:T(8,128)(2,1)S(1)}, u32[]{:S(2)}, u32[]{:S(2)}) collective-permute-start(bf16[2,144,1088]{2,1,0:T(8,128)(2,1)S(1)} %bitcast.245), channel_id=1, source_target_pairs={{0,2},{1,3},{2,0},{3,1},{4,6},{5,7},{6,4},{7,5},{8,10},{9,11},{10,... | collective-permute-start | bytes 1880072 | tf_op jit(solution)/shard_map/ppermute | solution.py:402
  174.4 51.7 %collective-permute-start.17 = (bf16[2,2,144,1088]{3,2,1,0:T(8,128)(2,1)}, bf16[2,2,144,1088]{3,2,1,0:T(8,128)(2,1)S(1)}, u32[]{:S(2)}, u32[]{:S(2)}) collective-permute-start(bf16[2,2,144,1088]{3,2,1,0:T(8,128)(2,1)} %pad_maximum_fusion.6.refs_1_), channel_id=1, source_target_pairs={{0,1},{1,0},{2,3},{3,2},{4,5},{5,4},{6,7},{7,6},{8,9},{9,8},{10,11... | collective-permute-start | bytes 3760136 | tf_op jit(solution)/shard_map/ppermute | solution.py:402
  193.5 32.7 %collective-permute-start.18 = (bf16[2,2,144,1088]{3,2,1,0:T(8,128)(2,1)}, bf16[2,2,144,1088]{3,2,1,0:T(8,128)(2,1)S(1)}, u32[]{:S(2)}, u32[]{:S(2)}) collective-permute-start(bf16[2,2,144,1088]{3,2,1,0:T(8,128)(2,1)} %collective-permute-done.12.refs_2_), channel_id=1, source_target_pairs={{0,1},{1,0},{2,3},{3,2},{4,5},{5,4},{6,7},{7,6},{8,9},{9,8},{10,11... | collective-permute-start | bytes 3760136 | tf_op jit(solution)/shard_map/ppermute | solution.py:402
  194.1 32.7 %collective-permute-start.19 = (bf16[2,2,144,1088]{3,2,1,0:T(8,128)(2,1)}, bf16[2,2,144,1088]{3,2,1,0:T(8,128)(2,1)}, u32[]{:S(2)}, u32[]{:S(2)}) collective-permute-start(bf16[2,2,144,1088]{3,2,1,0:T(8,128)(2,1)} %collective-permute-done.13.refs_3_), channel_id=1, source_target_pairs={{0,1},{1,0},{2,3},{3,2},{4,5},{5,4},{6,7},{7,6},{8,9},{9,8},{10,11... | collective-permute-start | bytes 3760136 | tf_op jit(solution)/shard_map/ppermute | solution.py:402
  194.4 41.9 %collective-permute-start.20 = (bf16[2,2,144,1088]{3,2,1,0:T(8,128)(2,1)S(1)}, bf16[2,2,144,1088]{3,2,1,0:T(8,128)(2,1)}, u32[]{:S(2)}, u32[]{:S(2)}) collective-permute-start(bf16[2,2,144,1088]{3,2,1,0:T(8,128)(2,1)S(1)} %maximum_select_fusion.refs_0_), channel_id=1, source_target_pairs={{0,2},{1,3},{2,0},{3,1},{4,6},{5,7},{6,4},{7,5},{8,10},{9,11},{10,... | collective-permute-start | bytes 3760136 | tf_op jit(solution)/shard_map/ppermute | solution.py:402
  195.9 40.3 %collective-permute-start.21 = (bf16[2,2,144,1088]{3,2,1,0:T(8,128)(2,1)S(1)}, bf16[2,2,144,1088]{3,2,1,0:T(8,128)(2,1)S(1)}, u32[]{:S(2)}, u32[]{:S(2)}) collective-permute-start(bf16[2,2,144,1088]{3,2,1,0:T(8,128)(2,1)S(1)} %maximum_select_fusion.1.refs_1_), channel_id=1, source_target_pairs={{0,4},{4,0},{1,5},{5,1},{2,6},{6,2},{3,7},{7,3},{8,12},{12,8},{9,1... | collective-permute-start | bytes 3760136 | tf_op jit(solution)/shard_map/ppermute | solution.py:402
  226.1 51.6 %collective-permute-start.22 = (bf16[2,2,144,1088]{3,2,1,0:T(8,128)(2,1)S(1)}, bf16[2,2,144,1088]{3,2,1,0:T(8,128)(2,1)}, u32[]{:S(2)}, u32[]{:S(2)}) collective-permute-start(bf16[2,2,144,1088]{3,2,1,0:T(8,128)(2,1)S(1)} %maximum_select_fusion.refs_0_), channel_id=1, source_target_pairs={{0,1},{1,0},{2,3},{3,2},{4,5},{5,4},{6,7},{7,6},{8,9},{9,8},{10,11... | collective-permute-start | bytes 3760136 | tf_op jit(solution)/shard_map/ppermute | solution.py:402
  226.2 51.5 %collective-permute-start.23 = (bf16[2,2,144,1088]{3,2,1,0:T(8,128)(2,1)S(1)}, bf16[2,2,144,1088]{3,2,1,0:T(8,128)(2,1)}, u32[]{:S(2)}, u32[]{:S(2)}) collective-permute-start(bf16[2,2,144,1088]{3,2,1,0:T(8,128)(2,1)S(1)} %maximum_select_fusion.1.refs_1_), channel_id=1, source_target_pairs={{0,1},{1,0},{2,3},{3,2},{4,5},{5,4},{6,7},{7,6},{8,9},{9,8},{10,11... | collective-permute-start | bytes 3760136 | tf_op jit(solution)/shard_map/ppermute | solution.py:402
  237.3 40.4 %collective-permute-start.24 = (bf16[2,2,144,1088]{3,2,1,0:T(8,128)(2,1)}, bf16[2,2,144,1088]{3,2,1,0:T(8,128)(2,1)}, u32[]{:S(2)}, u32[]{:S(2)}) collective-permute-start(bf16[2,2,144,1088]{3,2,1,0:T(8,128)(2,1)} %collective-permute-done.20.refs_2_), channel_id=1, source_target_pairs={{0,1},{1,0},{2,3},{3,2},{4,5},{5,4},{6,7},{7,6},{8,9},{9,8},{10,11... | collective-permute-start | bytes 3760136 | tf_op jit(solution)/shard_map/ppermute | solution.py:402
  241.3 33.6 %collective-permute-start.26 = (bf16[2,2,1088,128]{3,2,1,0:T(8,128)(2,1)S(1)}, bf16[2,2,1088,128]{3,2,1,0:T(8,128)(2,1)}, u32[]{:S(2)}, u32[]{:S(2)}) collective-permute-start(bf16[2,2,1088,128]{3,2,1,0:T(8,128)(2,1)S(1)} %maximum_select_fusion.2), channel_id=1, source_target_pairs={{0,2},{1,3},{2,0},{3,1},{4,6},{5,7},{6,4},{7,5},{8,10},{9,11},{10,... | collective-permute-start | bytes 3342344 | tf_op jit(solution)/shard_map/ppermute | solution.py:402
  243.7 34.0 %collective-permute-start.25 = (bf16[2,2,144,1088]{3,2,1,0:T(8,128)(2,1)S(1)}, bf16[2,2,144,1088]{3,2,1,0:T(8,128)(2,1)S(1)}, u32[]{:S(2)}, u32[]{:S(2)}) collective-permute-start(bf16[2,2,144,1088]{3,2,1,0:T(8,128)(2,1)S(1)} %copy-done.32), channel_id=1, source_target_pairs={{0,1},{1,0},{2,3},{3,2},{4,5},{5,4},{6,7},{7,6},{8,9},{9,8},{10,11... | collective-permute-start | bytes 3760136 | tf_op jit(solution)/shard_map/ppermute | solution.py:402
  316.7 23.6 %collective-permute-start.28 = (bf16[4,4,144,1088]{3,2,1,0:T(8,128)(2,1)}, bf16[4,4,144,1088]{3,2,1,0:T(8,128)(2,1)}, u32[]{:S(2)}, u32[]{:S(2)}) collective-permute-start(bf16[4,4,144,1088]{3,2,1,0:T(8,128)(2,1)} %broadcast_select_fusion.2), channel_id=1, source_target_pairs={{0,1},{1,0},{2,3},{3,2},{4,5},{5,4},{6,7},{7,6},{8,9},{9,8},{10,11... | collective-permute-start | bytes 15040520 | tf_op jit(solution)/shard_map/ppermute | solution.py:402
  349.7 45.6 %collective-permute-start.29 = (bf16[2,2,144,1088]{3,2,1,0:T(8,128)(2,1)}, bf16[2,2,144,1088]{3,2,1,0:T(8,128)(2,1)}, u32[]{:S(2)}, u32[]{:S(2)}) collective-permute-start(bf16[2,2,144,1088]{3,2,1,0:T(8,128)(2,1)} %get-tuple-element.138), channel_id=1, source_target_pairs={{0,4},{4,0},{1,5},{5,1},{2,6},{6,2},{3,7},{7,3},{8,12},{12,8},{9,1... | collective-permute-start | bytes 3760136 | tf_op jit(solution)/shard_map/ppermute | solution.py:402
  352.3 43.0 %collective-permute-start.30 = (bf16[2,2,144,1088]{3,2,1,0:T(8,128)(2,1)S(1)}, bf16[2,2,144,1088]{3,2,1,0:T(8,128)(2,1)}, u32[]{:S(2)}, u32[]{:S(2)}) collective-permute-start(bf16[2,2,144,1088]{3,2,1,0:T(8,128)(2,1)S(1)} %get-tuple-element.137), channel_id=1, source_target_pairs={{0,2},{1,3},{2,0},{3,1},{4,6},{5,7},{6,4},{7,5},{8,10},{9,11},{10,... | collective-permute-start | bytes 3760136 | tf_op jit(solution)/shard_map/ppermute | solution.py:402
  394.5 60.8 %collective-permute-start.35 = (bf16[4,4,144,1088]{3,2,1,0:T(8,128)(2,1)}, bf16[4,4,144,1088]{3,2,1,0:T(8,128)(2,1)}, u32[]{:S(2)}, u32[]{:S(2)}) collective-permute-start(bf16[4,4,144,1088]{3,2,1,0:T(8,128)(2,1)} %broadcast_select_fusion.1), channel_id=1, source_target_pairs={{0,1},{1,0},{2,3},{3,2},{4,5},{5,4},{6,7},{7,6},{8,9},{9,8},{10,11... | collective-permute-start | bytes 15040520 | tf_op jit(solution)/shard_map/ppermute | solution.py:402
  409.3 41.3 %collective-permute-start.31 = (bf16[2,2,1088,128]{3,2,1,0:T(8,128)(2,1)S(1)}, bf16[2,2,1088,128]{3,2,1,0:T(8,128)(2,1)S(1)}, u32[]{:S(2)}, u32[]{:S(2)}) collective-permute-start(bf16[2,2,1088,128]{3,2,1,0:T(8,128)(2,1)S(1)} %slice.637), channel_id=1, source_target_pairs={{0,2},{1,3},{2,0},{3,1},{4,6},{5,7},{6,4},{7,5},{8,10},{9,11},{10,... | collective-permute-start | bytes 3342344 | tf_op jit(solution)/shard_map/ppermute | solution.py:402
  411.0 39.5 %collective-permute-start.33 = (bf16[2,144,1088]{2,1,0:T(8,128)(2,1)}, bf16[2,144,1088]{2,1,0:T(8,128)(2,1)S(1)}, u32[]{:S(2)}, u32[]{:S(2)}) collective-permute-start(bf16[2,144,1088]{2,1,0:T(8,128)(2,1)} %fusion.25), channel_id=1, source_target_pairs={{0,2},{1,3},{2,0},{3,1},{4,6},{5,7},{6,4},{7,5},{8,10},{9,11},{10,... | collective-permute-start | bytes 1880072 | tf_op jit(solution)/shard_map/ppermute | solution.py:402
  413.2 37.4 %collective-permute-start.34 = (bf16[2,144,1088]{2,1,0:T(8,128)(2,1)}, bf16[2,144,1088]{2,1,0:T(8,128)(2,1)}, u32[]{:S(2)}, u32[]{:S(2)}) collective-permute-start(bf16[2,144,1088]{2,1,0:T(8,128)(2,1)} %select_bitcast_fusion.4), channel_id=1, source_target_pairs={{0,4},{4,0},{1,5},{5,1},{2,6},{6,2},{3,7},{7,3},{8,12},{12,8},{9,1... | collective-permute-start | bytes 1880072 | tf_op jit(solution)/shard_map/ppermute | solution.py:402
  463.9 53.1 %collective-permute-start.39 = (bf16[2,2,144,1088]{3,2,1,0:T(8,128)(2,1)}, bf16[2,2,144,1088]{3,2,1,0:T(8,128)(2,1)}, u32[]{:S(2)}, u32[]{:S(2)}) collective-permute-start(bf16[2,2,144,1088]{3,2,1,0:T(8,128)(2,1)} %get-tuple-element.134), channel_id=1, source_target_pairs={{0,4},{4,0},{1,5},{5,1},{2,6},{6,2},{3,7},{7,3},{8,12},{12,8},{9,1... | collective-permute-start | bytes 3760136 | tf_op jit(solution)/shard_map/ppermute | solution.py:402
  465.4 51.5 %collective-permute-start.40 = (bf16[2,2,144,1088]{3,2,1,0:T(8,128)(2,1)}, bf16[2,2,144,1088]{3,2,1,0:T(8,128)(2,1)}, u32[]{:S(2)}, u32[]{:S(2)}) collective-permute-start(bf16[2,2,144,1088]{3,2,1,0:T(8,128)(2,1)} %get-tuple-element.133), channel_id=1, source_target_pairs={{0,2},{1,3},{2,0},{3,1},{4,6},{5,7},{6,4},{7,5},{8,10},{9,11},{10,... | collective-permute-start | bytes 3760136 | tf_op jit(solution)/shard_map/ppermute | solution.py:402
  513.7 27.4 %collective-permute-start.36 = (bf16[4,4,144,1088]{3,2,1,0:T(8,128)(2,1)}, bf16[4,4,144,1088]{3,2,1,0:T(8,128)(2,1)}, u32[]{:S(2)}, u32[]{:S(2)}) collective-permute-start(bf16[4,4,144,1088]{3,2,1,0:T(8,128)(2,1)} %broadcast_select_fusion), channel_id=1, source_target_pairs={{0,1},{1,0},{2,3},{3,2},{4,5},{5,4},{6,7},{7,6},{8,9},{9,8},{10,11... | collective-permute-start | bytes 15040520 | tf_op jit(solution)/shard_map/ppermute | solution.py:402
  515.0 104.4 %reduce-scatter.8.cloned.1.call-start = ((), (), s32[]{:S(2)}) async-start(), calls=%async_computation.5 | async-start | bytes 1658880 | tf_op jit(solution)/shard_map/reduce_scatter | solution.py:764
  521.5 17.4 %collective-permute-start.41 = (bf16[2,144,1088]{2,1,0:T(8,128)(2,1)S(1)}, bf16[2,144,1088]{2,1,0:T(8,128)(2,1)S(1)}, u32[]{:S(2)}, u32[]{:S(2)}) collective-permute-start(bf16[2,144,1088]{2,1,0:T(8,128)(2,1)S(1)} %select_bitcast_fusion.3), channel_id=1, source_target_pairs={{0,2},{1,3},{2,0},{3,1},{4,6},{5,7},{6,4},{7,5},{8,10},{9,11},{10,... | collective-permute-start | bytes 1880072 | tf_op jit(solution)/shard_map/ppermute | solution.py:402
  522.9 17.1 %collective-permute-start.42 = (bf16[2,144,1088]{2,1,0:T(8,128)(2,1)S(1)}, bf16[2,144,1088]{2,1,0:T(8,128)(2,1)S(1)}, u32[]{:S(2)}, u32[]{:S(2)}) collective-permute-start(bf16[2,144,1088]{2,1,0:T(8,128)(2,1)S(1)} %select_bitcast_fusion.2), channel_id=1, source_target_pairs={{0,4},{4,0},{1,5},{5,1},{2,6},{6,2},{3,7},{7,3},{8,12},{12,8},{9,1... | collective-permute-start | bytes 1880072 | tf_op jit(solution)/shard_map/ppermute | solution.py:402
  547.9 30.7 %collective-permute-start.37 = (bf16[2,2,144,1088]{3,2,1,0:T(8,128)(2,1)S(1)}, bf16[2,2,144,1088]{3,2,1,0:T(8,128)(2,1)}, u32[]{:S(2)}, u32[]{:S(2)}) collective-permute-start(bf16[2,2,144,1088]{3,2,1,0:T(8,128)(2,1)S(1)} %get-tuple-element.132), channel_id=1, source_target_pairs={{0,4},{4,0},{1,5},{5,1},{2,6},{6,2},{3,7},{7,3},{8,12},{12,8},{9,1... | collective-permute-start | bytes 3760136 | tf_op jit(solution)/shard_map/ppermute | solution.py:402
  549.4 30.4 %collective-permute-start.38 = (bf16[2,2,144,1088]{3,2,1,0:T(8,128)(2,1)S(1)}, bf16[2,2,144,1088]{3,2,1,0:T(8,128)(2,1)}, u32[]{:S(2)}, u32[]{:S(2)}) collective-permute-start(bf16[2,2,144,1088]{3,2,1,0:T(8,128)(2,1)S(1)} %get-tuple-element.131), channel_id=1, source_target_pairs={{0,2},{1,3},{2,0},{3,1},{4,6},{5,7},{6,4},{7,5},{8,10},{9,11},{10,... | collective-permute-start | bytes 3760136 | tf_op jit(solution)/shard_map/ppermute | solution.py:402
  551.4 109.5 %reduce-scatter.4.cloned.1.call-start = ((), (), s32[]{:S(2)}) async-start(), calls=%async_computation.3 | async-start | bytes 1658880 | tf_op jit(solution)/shard_map/reduce_scatter | solution.py:764
  618.2 40.6 %collective-permute-start.46 = (bf16[2,2,1088,128]{3,2,1,0:T(8,128)(2,1)}, bf16[2,2,1088,128]{3,2,1,0:T(8,128)(2,1)}, u32[]{:S(2)}, u32[]{:S(2)}) collective-permute-start(bf16[2,2,1088,128]{3,2,1,0:T(8,128)(2,1)} %slice.687), channel_id=1, source_target_pairs={{0,2},{1,3},{2,0},{3,1},{4,6},{5,7},{6,4},{7,5},{8,10},{9,11},{10,... | collective-permute-start | bytes 3342344 | tf_op jit(solution)/shard_map/ppermute | solution.py:402
  622.9 29.5 %collective-permute-start.57 = (bf16[1,144,1088]{2,1,0:T(8,128)(2,1)S(1)}, bf16[1,144,1088]{2,1,0:T(8,128)(2,1)S(1)}, u32[]{:S(2)}, u32[]{:S(2)}) collective-permute-start(bf16[1,144,1088]{2,1,0:T(8,128)(2,1)S(1)} %get-tuple-element.169), channel_id=1, source_target_pairs={{0,2},{1,3},{2,0},{3,1},{4,6},{5,7},{6,4},{7,5},{8,10},{9,11},{10,... | collective-permute-start | bytes 940040 | tf_op jit(solution)/shard_map/ppermute | solution.py:402
  627.4 27.2 %collective-permute-start.50 = (bf16[4,16,1088]{2,1,0:T(8,128)(2,1)S(1)}, bf16[4,16,1088]{2,1,0:T(8,128)(2,1)S(1)}, u32[]{:S(2)}, u32[]{:S(2)}) collective-permute-start(bf16[4,16,1088]{2,1,0:T(8,128)(2,1)S(1)} %add_convert_fusion.10), channel_id=1, source_target_pairs={{0,8},{8,0},{16,24},{24,16},{1,9},{9,1},{17,25},{25,17},{2,10},{10... | collective-permute-start | bytes 417800 | tf_op jit(solution)/shard_map/ppermute | solution.py:402
  652.6 16.7 %collective-permute-start.58 = (bf16[2,1,144,1088]{3,2,1,0:T(8,128)(2,1)S(1)}, bf16[2,1,144,1088]{3,2,1,0:T(8,128)(2,1)}, u32[]{:S(2)}, u32[]{:S(2)}) collective-permute-start(bf16[2,1,144,1088]{3,2,1,0:T(8,128)(2,1)S(1)} %pad_maximum_fusion.15.refs_0_), channel_id=1, source_target_pairs={{0,2},{1,3},{2,0},{3,1},{4,6},{5,7},{6,4},{7,5},{8,10},{9,11},{10,... | collective-permute-start | bytes 1880072 | tf_op jit(solution)/shard_map/ppermute | solution.py:402
  654.0 18.0 %collective-permute-start.59 = (bf16[2,1,144,1088]{3,2,1,0:T(8,128)(2,1)S(1)}, bf16[2,1,144,1088]{3,2,1,0:T(8,128)(2,1)}, u32[]{:S(2)}, u32[]{:S(2)}) collective-permute-start(bf16[2,1,144,1088]{3,2,1,0:T(8,128)(2,1)S(1)} %pad_maximum_fusion.16.refs_1_), channel_id=1, source_target_pairs={{0,4},{4,0},{1,5},{5,1},{2,6},{6,2},{3,7},{7,3},{8,12},{12,8},{9,1... | collective-permute-start | bytes 1880072 | tf_op jit(solution)/shard_map/ppermute | solution.py:402
  660.9 29.0 %collective-permute-start.47 = (bf16[2,2,1088,128]{3,2,1,0:T(8,128)(2,1)}, bf16[2,2,1088,128]{3,2,1,0:T(8,128)(2,1)}, u32[]{:S(2)}, u32[]{:S(2)}) collective-permute-start(bf16[2,2,1088,128]{3,2,1,0:T(8,128)(2,1)} %pad_maximum_fusion.13), channel_id=1, source_target_pairs={{0,1},{1,0},{2,3},{3,2},{4,5},{5,4},{6,7},{7,6},{8,9},{9,8},{10,11... | collective-permute-start | bytes 3342344 | tf_op jit(solution)/shard_map/ppermute | solution.py:402
  680.2 17.4 %collective-permute-start.53 = (bf16[2,1,144,1088]{3,2,1,0:T(8,128)(2,1)S(1)}, bf16[2,1,144,1088]{3,2,1,0:T(8,128)(2,1)S(1)}, u32[]{:S(2)}, u32[]{:S(2)}) collective-permute-start(bf16[2,1,144,1088]{3,2,1,0:T(8,128)(2,1)S(1)} %pad_maximum_fusion.14.refs_0_), channel_id=1, source_target_pairs={{0,2},{1,3},{2,0},{3,1},{4,6},{5,7},{6,4},{7,5},{8,10},{9,11},{10,... | collective-permute-start | bytes 1880072 | tf_op jit(solution)/shard_map/ppermute | solution.py:402
  (89 other events, 785.1 us)
Sparse Core Ops, SparseCore 0:
  17.9 33.2 all-gather.6
  59.7 32.6 all-gather.8
  115.8 32.3 all-gather.10
  515.1 33.2 reduce-scatter.5
  551.5 32.1 reduce-scatter.7
  607.5 34.7 reduce-scatter.3
